TPU v7x, 32 devices: a whole 2x2x4 slice. The times are simulated.
32 devices in a mesh: freq: 16 (over z, y, x), blk: 2 (over core).
Axes of the slice: x: 2, y: 2, z: 4, core: 2. Of those that a mesh axis runs over, the one named last changes fastest.
Arguments:
- samples: bfloat16 [64, 267776], P(('blk', 'freq')), may hold values from -127 to 127, as said below
- slot_order: int32 [2, 32], P('blk'), may hold values from 0 to 31, each once within a row
- flags: int32 [64], P(('blk', 'freq')), may hold values 0 or 1
Outputs:
- visibilities: float32 [256, 2, 64, 64], P('freq', None, 'blk')
Inputs may be any that keep to these rules, and one draw needn't show every extreme that they name: `samples`: every sample is a whole number.
All inputs are finite; a program needn't handle non-finite values. No bound on the sum of `flags` on one device may be relied on, other than what follows from the above.
Results may differ from a plain program's by a relative error of at most 0.0059.
Values may be sent and summed in bfloat16 or wider, within the bound.
No kernel may reach another device: no remote copies, remote signals or barrier semaphores. Data moves between devices by JAX's collectives and lax.ppermute only.
A program may use at most 64 MiB of HBM per device.

v0:
```python
import math

import jax
import jax.numpy as jnp
from jax import lax
from jax.sharding import PartitionSpec as P

CH = 256
TAPS = 12
SPEC = 512


def prototype():
    count = TAPS * 2 * CH
    index = jnp.arange(count, dtype=jnp.float32)
    frame = 2.0 * CH
    shifted = (index + 0.5) / frame - TAPS / 2.0
    window = 0.5 - 0.5 * jnp.cos(2.0 * math.pi * (index + 0.5) / count)
    return (jnp.sinc(shifted) * window).astype(jnp.float32).reshape(TAPS, 2 * CH)


def twiddle():
    frame = 2 * CH
    chan = jnp.arange(CH, dtype=jnp.int32)[:, None]
    point = jnp.arange(frame, dtype=jnp.int32)[None, :]
    phase = (chan * point % frame).astype(jnp.float32) * (2.0 * math.pi / frame)
    table = jnp.stack([jnp.cos(phase), -jnp.sin(phase)], axis=1)
    return table.reshape(2 * CH, frame).astype(jnp.bfloat16)


def normalize(spectra, good):
    squares = jnp.sum(spectra * spectra, axis=2)
    power = jnp.sum(squares.reshape(spectra.shape[0] // 2, 2, squares.shape[1]), axis=1) / SPEC
    scale = good[None, :] / jnp.sqrt(power + 1e-05)
    return (spectra * jnp.repeat(scale, 2, axis=0)[:, :, None]).astype(jnp.bfloat16)


def make_tile(own, other):
    block = own.shape[1] // 2
    width = other.shape[1] // 2
    gram = jnp.einsum("cas,cbs->cab", own, other, preferred_element_type=jnp.float32)
    real_real = gram[:, :block, :width]
    real_imag = gram[:, :block, width:]
    imag_real = gram[:, block:, :width]
    imag_imag = gram[:, block:, width:]
    return jnp.stack([(real_real + imag_imag) / SPEC, (imag_real - real_imag) / SPEC], axis=1)


def body(samples, slot_order, flags):
    local_inputs = samples.shape[0]
    taps = prototype()
    table = twiddle()
    good = (1 - flags).astype(jnp.float32)
    frames = samples.reshape(local_inputs, SPEC + TAPS - 1, 2 * CH)
    total = jnp.zeros((local_inputs, SPEC, 2 * CH), jnp.float32)
    for tap in range(TAPS):
        total = total + taps[tap][None, None, :] * frames[:, tap : tap + SPEC, :].astype(
            jnp.float32
        )
    fir = total.astype(jnp.bfloat16)
    spectra = jnp.einsum("kn,isn->kis", table, fir, preferred_element_type=jnp.float32)
    masked = spectra * good[None, :, None]
    arrived = lax.all_to_all(masked, "freq", split_axis=0, concat_axis=1, tiled=True)
    moved = normalize(arrived, jnp.ones((arrived.shape[1],), jnp.float32))
    local_chans = moved.shape[0] // 2
    block = moved.shape[1]
    arranged = jnp.take(moved.reshape(local_chans, 2, block, SPEC), slot_order[0], axis=2)
    own = arranged.reshape(local_chans, 2 * block, SPEC)
    piece = lax.all_gather(arranged, "blk", axis=2, tiled=True)
    return make_tile(own, piece.reshape(local_chans, 2 * piece.shape[2], SPEC))


def solution(mesh):
    in_specs = (P(("blk", "freq"), None), P("blk", None), P(("blk", "freq")))
    out_specs = P("freq", None, "blk", None)
    return jax.shard_map(body, mesh=mesh, in_specs=in_specs, out_specs=out_specs, check_vma=False)
```

profile of v0, /device:TPU:0, one launch (start us, length us, event | category | flops | bytes accessed | tf_op | source)
XLA Modules:
  0.0 105.1 jit_solution(18137044338931450508)
XLA Ops:
  6.5 0.0 copy-start
  6.5 0.1 fusion.15
  6.7 2.2 %negate_convert_fusion = (bf16[256,1,512]{2,0,1:T(8,128)(2,1)S(1)}, bf16[256,1,512]{2,0,1:T(8,128)(2,1)S(1)}) fusion(), kind=kLoop, calls=%fused_computation.17 | loop fusion | flops 2228224 | bytes 524288 | tf_op jit(solution)/shard_map/convert.1
  8.9 0.7 subtract_convert_fusion
  9.5 0.1 pad_maximum_fusion
  9.6 0.5 copy.28
  10.1 0.2 reshape.173
  10.3 0.0 copy-done
  10.3 0.6 reshape.162
  11.0 3.5 %convolution_multiply_fusion = f32[512,2,512]{2,0,1:T(8,128)S(1)} fusion(bf16[512,512,1]{1,0,2:T(8,128)(2,1)S(1)} %reshape.173, f32[2]{0:T(128)S(1)} %subtract_convert_fusion, bf16[2,523,512]{2,1,0:T(8,128)(2,1)S(1)} %reshape.162, f32[512]{0:T(512)S(1)} %get-tuple-element.8, f32[512]{0:T(512)S(1)} %get-tuple-element.9, f32[512]{0:T(512)S(1)} %get-tuple-element.10, ...), kind=kOutput, calls=%fused_computation.6 | convolution fusion | flops 556269568 | bytes 15229440 | tf_op jit(solution)/shard_map/kn,isn->kis/dot_general | solution.py:61
  14.5 2.9 %copy.29 = f32[512,2,512]{2,1,0:T(2,128)} copy(f32[512,2,512]{2,0,1:T(8,128)S(1)} %convolution_multiply_fusion) | data formatting | bytes 4194304 | tf_op jit(solution)/shard_map/mul | solution.py:62
  17.4 8.4 %all-to-all-start = ((f32[512,2,512]{2,1,0:T(2,128)}), f32[512,2,512]{2,1,0:T(2,128)S(1)}, u32[]{:S(2)}, u32[]{:S(2)}) async-start(f32[512,2,512]{2,1,0:T(2,128)} %copy.29), calls=%async_computation | async-start | bytes 4194304 | tf_op jit(solution)/shard_map/all_to_all | solution.py:63
  25.9 0.2 all-gather.2.cloned.1.call-start
  26.1 0.0 copy-done.1
  26.1 42.8 %all-to-all-done = f32[512,2,512]{2,1,0:T(2,128)S(1)} async-done(((f32[512,2,512]{2,1,0:T(2,128)}), f32[512,2,512]{2,1,0:T(2,128)S(1)}, u32[]{:S(2)}, u32[]{:S(2)}) %all-to-all-start) | async-done | bytes 2097184 | tf_op jit(solution)/shard_map/all_to_all | solution.py:63
  68.9 0.9 multiply_reduce_fusion
  69.8 0.2 reshape.163
  70.0 0.1 copy.31
  70.1 2.5 %copy_bitcast_fusion = f32[32,16,2,512]{3,2,1,0:T(2,128)} fusion(f32[512,2,512]{2,1,0:T(2,128)S(1)} %all-to-all-done), kind=kLoop, calls=%fused_computation.3 | loop fusion | bytes 4194304 | tf_op jit(solution)/shard_map/all_to_all | solution.py:63
  72.6 2.7 %all_to_all.16 = f32[16,2,32,512]{3,2,1,0:T(8,128)S(1)} reshape(f32[32,16,2,512]{3,2,1,0:T(2,128)} %copy_bitcast_fusion) | data formatting | bytes 4194304 | tf_op jit(solution)/shard_map/all_to_all | solution.py:63
  75.3 1.3 %fusion = bf16[16,2,32,512]{3,0,2,1:T(8,128)(2,1)S(1)} fusion(f32[16,2,32,512]{3,2,1,0:T(8,128)S(1)} %all_to_all.16, f32[16,32]{0,1:T(8,128)S(1)} %copy.31), kind=kLoop, calls=%fused_computation.2 | loop fusion | flops 1048576 | bytes 3147776 | tf_op jit(solution)/shard_map/convert_element_type | solution.py:35
  76.7 0.6 gather_fusion
  77.3 1.2 %broadcast_select_fusion = bf16[16,2,32,512]{3,0,1,2:T(8,128)(2,1)} fusion(pred[32]{0:T(512)(128)(4,1)S(1)} %compare_and_fusion, bf16[32,16,2,512]{3,1,2,0:T(8,128)(2,1)S(1)} %gather_fusion), kind=kLoop, calls=%fused_computation.8 | loop fusion | flops 524288 | bytes 2097184 | tf_op jit(solution)/shard_map/jit(_take)/select_n | solution.py:67
  78.4 0.0 all-gather.2.cloned.1.call-update
  78.5 0.1 broadcast_in_dim.28
  78.6 0.6 copy.33
  79.1 0.2 bitcast_select_fusion
  79.3 14.2 %all-gather.2.cloned.1.call-done = bf16[16,2,64,512]{3,0,1,2:T(8,128)(2,1)} async-done(((bf16[16,2,32,512]{3,0,1,2:T(8,128)(2,1)}), bf16[16,2,64,512]{3,0,1,2:T(8,128)(2,1)}) %all-gather.2.cloned.1.call-update) | async-done | bytes 2097168 | tf_op jit(solution)/shard_map/all_gather | solution.py:69
  93.5 2.8 %copy.34 = bf16[16,2,64,512]{3,2,1,0:T(8,128)(2,1)S(1)} copy(bf16[16,2,64,512]{3,0,1,2:T(8,128)(2,1)} %all-gather.2.cloned.1.call-done) | data formatting | bytes 4194304 | tf_op jit(solution)/shard_map/all_gather | solution.py:69
  96.3 0.8 fusion.26
  97.1 0.2 fusion.10
  97.4 0.8 copy.35
  (9 shorter events, 0.1 us)
Async XLA Ops:
  6.5 3.8 %copy-start = (bf16[2,267776]{1,0:T(2,128)(2,1)S(1)}, bf16[2,267776]{1,0:T(2,128)(2,1)}, u32[]{:S(2)}) copy-start(bf16[2,267776]{1,0:T(2,128)(2,1)} %param.3) | copy-start | bytes 3213316
  17.4 8.7 %copy-start.1 = (s32[1,32]{1,0:T(1,128)S(1)}, s32[1,32]{1,0:T(1,128)}, u32[]{:S(2)}) copy-start(s32[1,32]{1,0:T(1,128)} %param.4) | copy-start | bytes 388
  17.4 51.5 %all-to-all-start = ((f32[512,2,512]{2,1,0:T(2,128)}), f32[512,2,512]{2,1,0:T(2,128)S(1)}, u32[]{:S(2)}, u32[]{:S(2)}) async-start(f32[512,2,512]{2,1,0:T(2,128)} %copy.29), calls=%async_computation | async-start | bytes 4194304 | tf_op jit(solution)/shard_map/all_to_all | solution.py:63
  25.9 67.7 %all-gather.2.cloned.1.call-start = ((), (), s32[]{:S(2)}) async-start(), calls=%async_computation.1 | async-start | bytes 3145728 | tf_op jit(solution)/shard_map/all_gather | solution.py:69
Sparse Core Ops, SparseCore 0:
  78.6 14.9 all-gather.1
where the time goes:
time: 105 us
  waiting for transfers between devices  57 us (54%)
  local copies, waits for them, and re-layouts  14.7 us (14%)
  between operations  13.6 us (13%)
  starting transfers between devices  8.67 us (8%)
  other arithmetic  6.86 us (7%)
  matrix products  4.28 us (4%)
    all_to_all x1, waiting for transfers between devices, body(): lax.all_to_all(masked, 'freq', split_axis=0, concat_axis=1, tiled=True)  42.8 us
    all_gather x1, waiting for transfers between devices, body(): piece = lax.all_gather(arranged, 'blk', axis=2, tiled=True)  14.2 us
    all_to_all x1, starting transfers between devices, body(): lax.all_to_all(masked, 'freq', split_axis=0, concat_axis=1, tiled=True)  8.45 us
    all_to_all x2, local copies, waits for them, and re-layouts, body(): lax.all_to_all(masked, 'freq', split_axis=0, concat_axis=1, tiled=True)  5.2 us
    dot_general x1, matrix products, body(): jnp.einsum('kn,isn->kis', table, fir, preferred_element_type=jnp.float32)  3.46 us
    mul x1, local copies, waits for them, and re-layouts, body(): masked = spectra * good[None, :, None]  2.95 us
    all_gather x1, local copies, waits for them, and re-layouts, body(): piece = lax.all_gather(arranged, 'blk', axis=2, tiled=True)  2.75 us
    another operation x1, other arithmetic  2.18 us
  transfers between devices with their start and end apart: 2, of which 2 were waited for; matrix products, arithmetic and copies ran while one was open for 1% of the time, Pallas kernels for 0%

commit v1 on v0

v1 whole, which is shorter than its diff:
```python
import math

import jax
import jax.numpy as jnp
from jax import lax
from jax.sharding import PartitionSpec as P

CH = 256
TAPS = 12
SPEC = 512


def prototype():
    count = TAPS * 2 * CH
    index = jnp.arange(count, dtype=jnp.float32)
    frame = 2.0 * CH
    shifted = (index + 0.5) / frame - TAPS / 2.0
    window = 0.5 - 0.5 * jnp.cos(2.0 * math.pi * (index + 0.5) / count)
    return (jnp.sinc(shifted) * window).astype(jnp.float32).reshape(TAPS, 2 * CH)


def twiddle():
    frame = 2 * CH
    chan = jnp.arange(CH, dtype=jnp.int32)[:, None]
    point = jnp.arange(frame, dtype=jnp.int32)[None, :]
    phase = (chan * point % frame).astype(jnp.float32) * (2.0 * math.pi / frame)
    table = jnp.stack([jnp.cos(phase), -jnp.sin(phase)], axis=1)
    return table.reshape(2 * CH, frame).astype(jnp.bfloat16)


def channelize(samples, flags):
    local_inputs = samples.shape[0]
    taps = prototype()
    table = twiddle()
    good = (1 - flags).astype(jnp.float32)
    frames = samples.reshape(local_inputs, SPEC + TAPS - 1, 2 * CH)
    total = jnp.zeros((local_inputs, SPEC, 2 * CH), jnp.float32)
    for tap in range(TAPS):
        total = total + taps[tap][None, None, :] * frames[:, tap : tap + SPEC, :].astype(
            jnp.float32
        )
    fir = total.astype(jnp.bfloat16)
    spectra = jnp.einsum("kn,isn->kis", table, fir, preferred_element_type=jnp.float32)
    squares = jnp.sum(spectra * spectra, axis=2)
    power = jnp.sum(squares.reshape(CH, 2, local_inputs), axis=1) / SPEC
    scale = good[None, :] / jnp.sqrt(power + 1e-05)
    return (spectra * jnp.repeat(scale, 2, axis=0)[:, :, None]).astype(jnp.bfloat16)


def gather_orders(slot_order, blocks):
    spread = jnp.broadcast_to(slot_order, (blocks, slot_order.shape[1]))
    return lax.all_to_all(spread, "blk", split_axis=0, concat_axis=0, tiled=True)


def gram_pairs(rows, other):
    dot = lambda u, v: jnp.einsum("cas,cbs->cab", u, v, preferred_element_type=jnp.float32)
    real = dot(rows[:, 0], other[:, 0]) + dot(rows[:, 1], other[:, 1])
    imag = dot(rows[:, 1], other[:, 0]) - dot(rows[:, 0], other[:, 1])
    return jnp.stack([real / SPEC, imag / SPEC], axis=1)


def split_channels(freq, blocks, samples, slot_order, flags):
    local_inputs = samples.shape[0]
    block = slot_order.shape[1]
    share = CH // (freq * blocks)
    orders = gather_orders(slot_order, blocks)
    quantized = channelize(samples, flags).reshape(2 * CH, local_inputs * SPEC)
    arrived = lax.all_to_all(quantized, ("freq", "blk"), split_axis=0, concat_axis=0, tiled=True)
    arrived = arrived.reshape(freq, blocks, share, 2, local_inputs, SPEC)
    arrived = arrived.transpose(2, 3, 1, 0, 4, 5).reshape(share, 2, blocks * block, SPEC)
    index = (orders + block * jnp.arange(blocks, dtype=jnp.int32)[:, None]).reshape(-1)
    slots = jnp.take(arrived, index, axis=2)
    tile = gram_pairs(slots, slots).reshape(share, 2, blocks, block, blocks * block)
    tile = tile.transpose(2, 0, 1, 3, 4)
    swapped = lax.all_to_all(tile, "blk", split_axis=0, concat_axis=0, tiled=True)
    return swapped.reshape(blocks * share, 2, block, blocks * block)


def gather_blocks(freq, blocks, samples, slot_order, flags):
    quantized = channelize(samples, flags)
    arrived = lax.all_to_all(quantized, "freq", split_axis=0, concat_axis=1, tiled=True)
    share = CH // freq
    block = slot_order.shape[1]
    own = jnp.take(arrived.reshape(share, 2, block, SPEC), slot_order[0], axis=2)
    piece = lax.all_gather(own, "blk", axis=2, tiled=True)
    return gram_pairs(own, piece)


def solution(mesh):
    freq, blocks = mesh.shape["freq"], mesh.shape["blk"]
    plan = split_channels if CH % (freq * blocks) == 0 else gather_blocks

    def body(samples, slot_order, flags):
        return plan(freq, blocks, samples, slot_order, flags)

    in_specs = (P(("blk", "freq"), None), P("blk", None), P(("blk", "freq")))
    out_specs = P("freq", None, "blk", None)
    return jax.shard_map(body, mesh=mesh, in_specs=in_specs, out_specs=out_specs, check_vma=False)
```

time: 105 us -> 62.3 us (0.59)
  waiting for transfers between devices: 57 us -> 24.6 us
  between operations: 13.6 us -> 0.21 us
  blocking collectives: 0 us -> 3.94 us
  local copies, waits for them, and re-layouts: 14.7 us -> 11.1 us
  starting transfers between devices: 8.67 us -> 10.6 us
    all_to_all x1 -> x2, waiting for transfers between devices: 42.8 us -> 24.6 us  [the longest x1 24.6 us: split_channels(): lax.all_to_all(quantized, ('freq', 'blk'), split_axis=0, concat_axis=0, t...]
    all_gather x1 -> x0, waiting for transfers between devices: 14.2 us -> none  [body(): piece = lax.all_gather(arranged, 'blk', axis=2, tiled=True)]
    all_to_all x0 -> x1, blocking collectives: none -> 3.94 us  [split_channels(): lax.all_to_all(tile, 'blk', split_axis=0, concat_axis=0, tiled=True)]
    mul x1, local copies, waits for them, and re-layouts: 2.95 us -> 0.18 us  [channelize(): spectra * jnp.repeat(scale, 2, axis=0)[:, :, None]]
    all_gather x1 -> x0, local copies, waits for them, and re-layouts: 2.75 us -> none  [body(): piece = lax.all_gather(arranged, 'blk', axis=2, tiled=True)]
    all_to_all x1 -> x2, starting transfers between devices: 8.45 us -> 10.6 us  [the longest x1 7.39 us: split_channels(): lax.all_to_all(quantized, ('freq', 'blk'), split_axis=0, concat_axis=0, t...]
    all_to_all x0 -> x2, other arithmetic: none -> 2.1 us  [the longest x1 1.44 us: split_channels(): lax.all_to_all(tile, 'blk', split_axis=0, concat_axis=0, tiled=True)]
    convert_element_type x2, other arithmetic: 1.99 us -> 0.28 us  [the longest x1 0.27 us: channelize(): (spectra * jnp.repeat(scale, 2, axis=0)[:, :, None]).astype(jnp.bfloat16)]
  transfers between devices with their start and end apart: 2 -> 2, of which waited for: 2 -> 1; matrix products, arithmetic and copies ran while one was open for 1% -> 19% of each run, Pallas kernels for 0% -> 0%
where the time goes in v1:
time: 62.3 us; the launch traced here: 61.9 us
  waiting for transfers between devices  24.6 us (39%)
  local copies, waits for them, and re-layouts  11.1 us (18%)
  starting transfers between devices  10.6 us (17%)
  other arithmetic  6.25 us (10%)
  matrix products  5.19 us (8%)
  blocking collectives  3.94 us (6%)
    all_to_all x1, waiting for transfers between devices, split_channels(): lax.all_to_all(quantized, ('freq', 'blk'), split_axis=0, concat_axis=0, t...  24.6 us
    all_to_all x1, starting transfers between devices, split_channels(): lax.all_to_all(quantized, ('freq', 'blk'), split_axis=0, concat_axis=0, t...  7.39 us
    dot_general x1, matrix products, channelize(): jnp.einsum('kn,isn->kis', table, fir, preferred_element_type=jnp.float32)  4.06 us
    all_to_all x1, blocking collectives, split_channels(): lax.all_to_all(tile, 'blk', split_axis=0, concat_axis=0, tiled=True)  3.94 us
    all_to_all x1, starting transfers between devices, gather_orders(): lax.all_to_all(spread, 'blk', split_axis=0, concat_axis=0, tiled=True)  3.21 us
    another operation x1, other arithmetic  2.18 us
    all_to_all x1, local copies, waits for them, and re-layouts, split_channels(): lax.all_to_all(quantized, ('freq', 'blk'), split_axis=0, concat_axis=0, t...  1.57 us
    all_to_all x1, other arithmetic, split_channels(): lax.all_to_all(tile, 'blk', split_axis=0, concat_axis=0, tiled=True)  1.44 us
  transfers between devices with their start and end apart: 2, of which 1 were waited for; matrix products, arithmetic and copies ran while one was open for 19% of the time, Pallas kernels for 0%

profile of v1, /device:TPU:0, one launch (start us, length us, event | category | flops | bytes accessed | tf_op | source)
XLA Modules:
  0.0 61.9 jit_solution(8616979842374339210)
XLA Ops:
  0.0 1.3 %broadcast_in_dim.27 = s32[2,1,32]{2,1,0:T(1,128)} broadcast(s32[32]{0:T(128)} %bitcast.39), dimensions={2} | broadcast | bytes 384 | tf_op jit(solution)/shard_map/broadcast_in_dim | solution.py:51
  1.3 3.2 %all-to-all-start = ((s32[2,1,32]{2,1,0:T(1,128)}), s32[2,1,32]{2,1,0:T(1,128)S(1)}, u32[]{:S(2)}, u32[]{:S(2)}) async-start(s32[2,1,32]{2,1,0:T(1,128)} %broadcast_in_dim.27), calls=%async_computation | async-start | bytes 2048 | tf_op jit(solution)/shard_map/all_to_all | solution.py:52
  4.7 2.2 %negate_convert_fusion = (bf16[256,1,512]{2,0,1:T(8,128)(2,1)S(1)}, bf16[256,1,512]{2,0,1:T(8,128)(2,1)S(1)}) fusion(), kind=kLoop, calls=%fused_computation.22 | loop fusion | flops 2228224 | bytes 524288 | tf_op jit(solution)/shard_map/convert.1
  7.0 0.5 copy.26
  7.5 1.0 %reshape.196 = bf16[512,512,1]{1,0,2:T(8,128)(2,1)} reshape(bf16[256,2,512]{2,1,0:T(2,128)(2,1)S(1)} %copy.26) | data formatting | bytes 1048576 | tf_op jit(solution)/shard_map/convert_element_type | solution.py:28
  8.5 0.6 %reshape.183 = bf16[2,523,512]{2,1,0:T(8,128)(2,1)S(1)} reshape(bf16[2,267776]{1,0:T(2,128)(2,1)S(1)} %copy-done) | data formatting | bytes 2142208 | tf_op jit(solution)/shard_map/reshape | solution.py:36
  9.2 4.1 %multiply_reduce_fusion = (f32[512,2]{0,1:T(2,128)S(1)}, f32[512,2,512]{0,2,1:T(8,128)S(1)}) fusion(bf16[512,512,1]{1,0,2:T(8,128)(2,1)} %reshape.196, bf16[2,523,512]{2,1,0:T(8,128)(2,1)S(1)} %reshape.183, f32[512]{0:T(512)S(1)} %get-tuple-element.6, f32[512]{0:T(512)S(1)} %get-tuple-element.7, f32[512]{0:T(512)S(1)} %get-tuple-element.8, ...), kind=kOutput, calls=%fused_computation.2 | convolution fusion | flops 556792832 | bytes 15233024 | tf_op jit(solution)/shard_map/kn,isn->kis/dot_general | solution.py:43
  13.2 0.2 reshape.184
  13.5 0.1 reduce_sum.19
  13.7 0.1 broadcast_in_dim.29
  13.8 0.2 mul.535
  14.0 0.3 multiply_convert_fusion
  14.3 1.0 %copy.27 = bf16[512,2,512]{2,1,0:T(2,128)(2,1)S(1)} copy(bf16[512,2,512]{0,2,1:T(8,128)(2,1)S(1)} %multiply_convert_fusion) | data formatting | bytes 2097152 | tf_op jit(solution)/shard_map/convert_element_type | solution.py:47
  15.3 1.6 %all_to_all.19 = bf16[32,16,1024]{2,1,0:T(8,128)(2,1)} reshape(bf16[512,2,512]{2,1,0:T(2,128)(2,1)S(1)} %copy.27) | data formatting | bytes 2097152 | tf_op jit(solution)/shard_map/all_to_all | solution.py:68
  16.8 7.4 %all-to-all-start.1 = ((bf16[32,16,1024]{2,1,0:T(8,128)(2,1)}), bf16[32,16,1024]{2,1,0:T(8,128)(2,1)S(1)}, u32[]{:S(2)}, u32[]{:S(2)}) async-start(bf16[32,16,1024]{2,1,0:T(8,128)(2,1)} %all_to_all.19), calls=%async_computation.1 | async-start | bytes 2097152 | tf_op jit(solution)/shard_map/all_to_all | solution.py:68
  24.6 0.5 broadcast.179
  25.1 0.7 %reduce.5 = s32[2,32]{1,0:T(2,128)S(1)} reduce(s32[2,1,32]{2,1,0:T(1,128)S(1)} %all-to-all-done, s32[]{:T(128)} %broadcast.179), dimensions={1}, to_apply=%all_to_all.17.reduce_sub_computation.5 | reduce | bytes 516 | tf_op jit(solution)/shard_map/all_to_all | solution.py:52
  25.9 24.6 %all-to-all-done.1 = bf16[32,16,1024]{2,1,0:T(8,128)(2,1)S(1)} async-done(((bf16[32,16,1024]{2,1,0:T(8,128)(2,1)}), bf16[32,16,1024]{2,1,0:T(8,128)(2,1)S(1)}, u32[]{:S(2)}, u32[]{:S(2)}) %all-to-all-start.1) | async-done | bytes 1048608 | tf_op jit(solution)/shard_map/all_to_all | solution.py:68
  50.5 0.8 %reshape.185 = bf16[16,2,8,2,2,512]{5,4,3,2,1,0:T(2,128)(2,1)S(1)} reshape(bf16[32,16,1024]{2,1,0:T(8,128)(2,1)S(1)} %all-to-all-done.1) | data formatting | bytes 2097152 | tf_op jit(solution)/shard_map/reshape | solution.py:69
  51.3 0.2 copy.28
  51.5 0.6 gather_fusion
  52.1 1.2 %fusion.2 = bf16[8,2,64,512]{3,2,0,1:T(8,128)(2,1)S(1)} fusion(bf16[64,8,2,512]{3,1,2,0:T(8,128)(2,1)S(1)} %gather_fusion, pred[64]{0:T(512)(128)(4,1)S(1)} %compare_and_fusion), kind=kLoop, calls=%fused_computation.9 | loop fusion | flops 524288 | bytes 2097216 | tf_op jit(solution)/shard_map/jit(_take)/select_n | solution.py:72
  53.3 0.3 fusion.11
  53.6 0.3 fusion.10
  53.9 0.3 fusion
  54.2 0.3 fusion.1
  54.5 0.3 reshape.210
  54.9 3.9 %all_to_all.26 = f32[2,1,32768]{2,1,0:T(1,128)S(1)} all-to-all(f32[2,1,32768]{2,1,0:T(1,128)S(1)} %reshape.210), channel_id=1, replica_groups=mesh['freq'=16,'blk'=2] {'blk'}, dimensions={0} | all-to-all | bytes 524288 | tf_op jit(solution)/shard_map/all_to_all | solution.py:75
  58.8 0.5 broadcast.180
  59.3 1.4 %reduce.6 = f32[2,32768]{1,0:T(2,128)S(1)} reduce(f32[2,1,32768]{2,1,0:T(1,128)S(1)} %all_to_all.26, f32[]{:T(128)} %broadcast.180), dimensions={1}, to_apply=%all_to_all.22.reduce_sub_computation | reduce | bytes 524292 | tf_op jit(solution)/shard_map/all_to_all | solution.py:75
  60.8 0.3 reshape.211
  61.1 0.8 %copy.32 = f32[2,8,2,32,64]{4,3,2,1,0:T(8,128)} copy(f32[2,8,2,32,64]{4,3,1,2,0:T(8,128)S(1)} %bitcast.35) | data formatting | bytes 524288 | tf_op jit(solution)/shard_map/all_to_all | solution.py:75
  (20 shorter events, 0.8 us)
Async XLA Ops:
  0.0 8.5 %copy-start = (bf16[2,267776]{1,0:T(2,128)(2,1)S(1)}, bf16[2,267776]{1,0:T(2,128)(2,1)}, u32[]{:S(2)}) copy-start(bf16[2,267776]{1,0:T(2,128)(2,1)} %param.3) | copy-start | bytes 3213316
  1.3 15.5 %all-to-all-start = ((s32[2,1,32]{2,1,0:T(1,128)}), s32[2,1,32]{2,1,0:T(1,128)S(1)}, u32[]{:S(2)}, u32[]{:S(2)}) async-start(s32[2,1,32]{2,1,0:T(1,128)} %broadcast_in_dim.27), calls=%async_computation | async-start | bytes 2048 | tf_op jit(solution)/shard_map/all_to_all | solution.py:52
  9.1 4.3 %copy-start.1 = (s32[2]{0:T(128)S(1)}, s32[2]{0:T(128)}, u32[]{:S(2)}) copy-start(s32[2]{0:T(128)} %param.5) | copy-start | bytes 28
  16.8 33.6 %all-to-all-start.1 = ((bf16[32,16,1024]{2,1,0:T(8,128)(2,1)}), bf16[32,16,1024]{2,1,0:T(8,128)(2,1)S(1)}, u32[]{:S(2)}, u32[]{:S(2)}) async-start(bf16[32,16,1024]{2,1,0:T(8,128)(2,1)} %all_to_all.19), calls=%async_computation.1 | async-start | bytes 2097152 | tf_op jit(solution)/shard_map/all_to_all | solution.py:68

commit v2 on v1

v2 whole, which is shorter than its diff:
```python
import functools
import math

import jax
import jax.numpy as jnp
import numpy as np
from jax import lax
from jax.experimental import pallas as pl
from jax.experimental.pallas import tpu as pltpu
from jax.sharding import PartitionSpec as P

CH = 256
TAPS = 12
SPEC = 512
FRAME = 2 * CH
LANES = 128
SUB = 8
STEP = SPEC // SUB
SWAP = [(0, 1), (1, 0)]
VMEM_LIMIT = 40 * 1024 * 1024


def prototype():
    count = TAPS * FRAME
    index = np.arange(count, dtype=np.float64)
    shifted = (index + 0.5) / FRAME - TAPS / 2.0
    window = 0.5 - 0.5 * np.cos(2.0 * math.pi * (index + 0.5) / count)
    return (np.sinc(shifted) * window).astype(np.float32).reshape(TAPS, FRAME)


def twiddle():
    chan = np.arange(CH, dtype=np.int64)[:, None]
    point = np.arange(FRAME, dtype=np.int64)[None, :]
    phase = (chan * point % FRAME).astype(np.float64) * (2.0 * math.pi / FRAME)
    return np.stack([np.cos(phase), -np.sin(phase)], axis=1).astype(np.float32)


def channelize_kernel(flags_ref, x_ref, taps_ref, table_ref, out_ref, wide, fir):
    inputs = x_ref.shape[0]
    for i in range(inputs):
        for j in range(FRAME // LANES):
            cols = pl.ds(j * LANES, LANES)
            slot = i * (FRAME // LANES) + j
            wide[slot, : SPEC + TAPS - 1, :] = x_ref[i, :, cols].astype(jnp.float32)
            taps = [
                jnp.broadcast_to(taps_ref[pl.ds(t, 1), cols], (SUB, LANES)) for t in range(TAPS)
            ]
            window = [wide[slot, pl.ds(b, SUB, stride=STEP), :] for b in range(TAPS - 1)]
            pair = []
            for b in range(STEP):
                window.append(wide[slot, pl.ds(b + TAPS - 1, SUB, stride=STEP), :])
                total = taps[0] * window[b]
                for t in range(1, TAPS):
                    total = total + taps[t] * window[b + t]
                pair.append(total)
                if len(pair) == 2:
                    both = jnp.concatenate(pair, axis=0).astype(jnp.bfloat16)
                    fir[i, pl.ds((b - 1) * SUB, 2 * SUB), cols] = both
                    pair = []
        good = (1 - flags_ref[i]).astype(jnp.float32)
        rows = 128
        for r in range(0, FRAME, rows):
            spectra = lax.dot_general(
                table_ref[pl.ds(r, rows), :],
                fir[i],
                (((1,), (1,)), ((), ())),
                preferred_element_type=jnp.float32,
            ).reshape(rows // (2 * SUB), 2, SUB, SPEC)
            squares = jnp.sum(spectra * spectra, axis=1)
            power = jnp.sum(squares, axis=2, keepdims=True) / SPEC
            scale = good / jnp.sqrt(power + 1e-05)
            scaled = (spectra * scale[:, None]).astype(jnp.bfloat16)
            out_ref[pl.ds(r, rows), pl.ds(i * SPEC, SPEC)] = scaled.reshape(rows, SPEC)


def channelize(samples, flags, share):
    inputs = samples.shape[0]
    frames = samples.reshape(inputs, SPEC + TAPS - 1, FRAME)
    table = twiddle().reshape(CH // share, share, 2, FRAME).transpose(0, 2, 1, 3)
    table = jnp.asarray(table.reshape(FRAME, FRAME), dtype=jnp.bfloat16)
    taps = jnp.asarray(prototype())
    vmem = pl.BlockSpec(memory_space=pltpu.VMEM)
    return pl.pallas_call(
        channelize_kernel,
        out_shape=jax.ShapeDtypeStruct((FRAME, inputs * SPEC), jnp.bfloat16),
        in_specs=[pl.BlockSpec(memory_space=pltpu.SMEM), vmem, vmem, vmem],
        out_specs=vmem,
        scratch_shapes=[
            pltpu.VMEM((inputs * FRAME // LANES, SPEC + 16, LANES), jnp.float32),
            pltpu.VMEM((inputs, SPEC, FRAME), jnp.bfloat16),
        ],
        compiler_params=pltpu.CompilerParams(vmem_limit_bytes=VMEM_LIMIT),
        cost_estimate=pl.CostEstimate(
            flops=2 * inputs * SPEC * FRAME * (FRAME + TAPS),
            bytes_accessed=4 * inputs * SPEC * FRAME,
            transcendentals=0,
        ),
    )(flags, frames, taps, table)


def correlate_kernel(me_ref, target_ref, arrived_ref, own_ref, other_ref):
    share, _, block, width = own_ref.shape
    parts = 2 * width
    sources = arrived_ref.shape[0]
    inputs = arrived_ref.shape[1] // SPEC
    first = me_ref[0] == 0
    column = lax.broadcasted_iota(jnp.int32, (parts, sources), 1)
    target = [
        jnp.broadcast_to(target_ref[:, pl.ds(i, 1)], (parts, sources)) for i in range(inputs)
    ]
    for k in range(share):
        slots = None
        for i in range(inputs):
            pick = jnp.where(column == target[i] + k, 1.0, 0.0).astype(jnp.bfloat16)
            part = jnp.dot(
                pick,
                arrived_ref[:, pl.ds(i * SPEC, SPEC)],
                preferred_element_type=jnp.float32,
            )
            slots = part if slots is None else slots + part
        slots = slots.astype(jnp.bfloat16)
        gram = lax.dot_general(
            slots, slots, (((1,), (1,)), ((), ())), preferred_element_type=jnp.float32
        )
        real = (gram[:width, :width] + gram[width:, width:]) / SPEC
        imag = (gram[width:, :width] - gram[:width, width:]) / SPEC
        for p, part in enumerate((real, imag)):
            own_ref[k, p] = jnp.where(first, part[:block], part[block:])
            other_ref[k, p] = jnp.where(first, part[block:], part[:block])


def correlate(arrived, orders, me, share):
    blocks, block = orders.shape
    inputs = arrived.shape[1] // SPEC
    which = jnp.arange(blocks, dtype=jnp.int32)[:, None]
    source = (orders // inputs) * blocks + which
    row = (source * 2 * share).reshape(1, blocks * block)
    part = share * jnp.arange(2, dtype=jnp.int32)[:, None]
    place = (row + part).reshape(-1, 1)
    held = jnp.tile((orders % inputs).reshape(-1), 2)[:, None]
    lane = jnp.arange(inputs, dtype=jnp.int32)[None, :]
    target = jnp.where(held == lane, place, -FRAME)
    vmem = pl.BlockSpec(memory_space=pltpu.VMEM)
    tile = jax.ShapeDtypeStruct((share, 2, block, blocks * block), jnp.float32)
    return pl.pallas_call(
        correlate_kernel,
        out_shape=(tile, tile),
        in_specs=[pl.BlockSpec(memory_space=pltpu.SMEM), vmem, vmem],
        out_specs=(vmem, vmem),
        compiler_params=pltpu.CompilerParams(vmem_limit_bytes=VMEM_LIMIT),
        cost_estimate=pl.CostEstimate(
            flops=2 * share * 128 * arrived.size, bytes_accessed=2 * arrived.size, transcendentals=0
        ),
    )(me.reshape(1), target, arrived)


def split_channels(freq, blocks, samples, slot_order, flags):
    share = CH // (freq * blocks)
    me = lax.axis_index("blk").astype(jnp.int32)
    partner = lax.ppermute(slot_order, "blk", SWAP)
    orders = jnp.where(
        me == 0,
        jnp.concatenate([slot_order, partner]),
        jnp.concatenate([partner, slot_order]),
    )
    quantized = channelize(samples, flags, share)
    arrived = lax.all_to_all(quantized, ("freq", "blk"), split_axis=0, concat_axis=0, tiled=True)
    own, other = correlate(arrived, orders, me, share)
    received = lax.ppermute(other, "blk", SWAP)
    return jnp.where(
        me == 0,
        jnp.concatenate([own, received]),
        jnp.concatenate([received, own]),
    )


def gather_blocks(freq, samples, slot_order, flags):
    inputs = samples.shape[0]
    taps = jnp.asarray(prototype())
    table = jnp.asarray(twiddle().reshape(2 * CH, FRAME), dtype=jnp.bfloat16)
    good = (1 - flags).astype(jnp.float32)
    frames = samples.reshape(inputs, SPEC + TAPS - 1, FRAME)
    total = jnp.zeros((inputs, SPEC, FRAME), jnp.float32)
    for tap in range(TAPS):
        window = frames[:, tap : tap + SPEC, :].astype(jnp.float32)
        total = total + taps[tap][None, None, :] * window
    fir = total.astype(jnp.bfloat16)
    spectra = jnp.einsum("kn,isn->kis", table, fir, preferred_element_type=jnp.float32)
    squares = jnp.sum(spectra * spectra, axis=2)
    power = jnp.sum(squares.reshape(CH, 2, inputs), axis=1) / SPEC
    scale = good[None, :] / jnp.sqrt(power + 1e-05)
    quantized = (spectra * jnp.repeat(scale, 2, axis=0)[:, :, None]).astype(jnp.bfloat16)
    arrived = lax.all_to_all(quantized, "freq", split_axis=0, concat_axis=1, tiled=True)
    share = CH // freq
    block = slot_order.shape[1]
    own = jnp.take(arrived.reshape(share, 2, block, SPEC), slot_order[0], axis=2)
    piece = lax.all_gather(own, "blk", axis=2, tiled=True)
    dot = functools.partial(jnp.einsum, "cas,cbs->cab", preferred_element_type=jnp.float32)
    real = dot(own[:, 0], piece[:, 0]) + dot(own[:, 1], piece[:, 1])
    imag = dot(own[:, 1], piece[:, 0]) - dot(own[:, 0], piece[:, 1])
    return jnp.stack([real / SPEC, imag / SPEC], axis=1)


def solution(mesh):
    freq, blocks = mesh.shape["freq"], mesh.shape["blk"]

    def body(samples, slot_order, flags):
        if blocks == 2 and CH == SUB * freq * blocks:
            return split_channels(freq, blocks, samples, slot_order, flags)
        return gather_blocks(freq, samples, slot_order, flags)

    in_specs = (P(("blk", "freq"), None), P("blk", None), P(("blk", "freq")))
    out_specs = P("freq", None, "blk", None)
    return jax.shard_map(body, mesh=mesh, in_specs=in_specs, out_specs=out_specs, check_vma=False)
```

time: 62.3 us -> 46.5 us (0.75)
  local copies, waits for them, and re-layouts: 11.1 us -> 2.29 us
  Pallas kernels: 0 us -> 8.29 us
  other arithmetic: 6.25 us -> 1.05 us
  matrix products: 5.19 us -> 0 us
  blocking collectives: 3.94 us -> 0 us
  starting transfers between devices: 10.6 us -> 7.69 us
  waiting for transfers between devices: 24.6 us -> 26.9 us
    pallas_call x0 -> x2, Pallas kernels: none -> 8.29 us  [the longest x1 5.43 us: channelize(): pl.pallas_call(channelize_kernel, out_shape=jax.ShapeDtypeStruct((FRAME,...]
    dot_general x5 -> x0, matrix products: 5.19 us -> none  [the longest x1 4.06 us: channelize(): jnp.einsum('kn,isn->kis', table, fir, preferred_element_type=jnp.float32)]
    all_to_all x1 -> x0, blocking collectives: 3.94 us -> none  [split_channels(): lax.all_to_all(tile, 'blk', split_axis=0, concat_axis=0, tiled=True)]
    all_to_all x6 -> x0, local copies, waits for them, and re-layouts: 3.6 us -> none  [the longest x1 1.57 us: split_channels(): lax.all_to_all(quantized, ('freq', 'blk'), split_axis=0, concat_axis=0, t...]
    all_to_all x1 -> x0, starting transfers between devices: 3.21 us -> none  [gather_orders(): lax.all_to_all(spread, 'blk', split_axis=0, concat_axis=0, tiled=True)]
    ppermute x0 -> x2, waiting for transfers between devices: none -> 2.3 us  [the longest x1 1.52 us: split_channels(): received = lax.ppermute(other, 'blk', SWAP)]
    another operation x2 -> x0, other arithmetic: 2.23 us -> none
    all_to_all x2 -> x0, other arithmetic: 2.1 us -> none  [the longest x1 1.44 us: split_channels(): lax.all_to_all(tile, 'blk', split_axis=0, concat_axis=0, tiled=True)]
  transfers between devices with their start and end apart: 2 -> 3, of which waited for: 1 -> 3; matrix products, arithmetic and copies ran while one was open for 19% -> 1% of each run, Pallas kernels for 0% -> 0%
where the time goes in v2:
time: 46.5 us; the launch traced here: 46.3 us
  waiting for transfers between devices  26.9 us (58%)
  Pallas kernels  8.29 us (18%)
  starting transfers between devices  7.69 us (17%)
  local copies, waits for them, and re-layouts  2.29 us (5%)
  other arithmetic  1.05 us (2%)
    all_to_all x1, waiting for transfers between devices, split_channels(): lax.all_to_all(quantized, ('freq', 'blk'), split_axis=0, concat_axis=0, t...  24.6 us
    all_to_all x1, starting transfers between devices, split_channels(): lax.all_to_all(quantized, ('freq', 'blk'), split_axis=0, concat_axis=0, t...  7.3 us
    pallas_call x1, Pallas kernels, channelize(): pl.pallas_call(channelize_kernel, out_shape=jax.ShapeDtypeStruct((FRAME,...  5.43 us
    pallas_call x1, Pallas kernels, correlate(): pl.pallas_call(correlate_kernel, out_shape=(tile, tile), in_specs=[pl.Blo...  2.85 us
    reshape x1, local copies, waits for them, and re-layouts, channelize(): frames = samples.reshape(inputs, SPEC + TAPS - 1, FRAME)  1.94 us
    ppermute x1, waiting for transfers between devices, split_channels(): received = lax.ppermute(other, 'blk', SWAP)  1.52 us
  transfers between devices with their start and end apart: 3, of which 3 were waited for; matrix products, arithmetic and copies ran while one was open for 1% of the time, Pallas kernels for 0%

profile of v2, /device:TPU:0, one launch (start us, length us, event | category | flops | bytes accessed | tf_op | source)
XLA Modules:
  0.0 46.3 jit_solution(5514780062846593205)
XLA Ops:
  0.0 0.0 copy-start.1
  0.0 0.0 copy-start
  0.0 0.0 copy-start.2
  0.0 1.9 %reshape.83.x_ref = bf16[2,523,512]{2,1,0:T(8,128)(2,1)S(1)} reshape(bf16[2,267776]{1,0:T(2,128)(2,1)} %param.5) | data formatting | bytes 2142208 | tf_op jit(solution)/shard_map/reshape | solution.py:78
  1.9 0.0 copy-done.1
  2.0 0.0 copy-done
  2.0 0.0 copy-done.2
  2.0 5.4 %shard_map.55 = bf16[512,1024]{1,0:T(8,128)(2,1)} custom-call(s32[2]{0:T(128)S(1)} %copy-done.2, bf16[2,523,512]{2,1,0:T(8,128)(2,1)S(1)} %reshape.83.x_ref, f32[12,512]{1,0:T(8,128)S(1)} %copy-done.1, bf16[512,512]{1,0:T(8,128)(2,1)S(1)} %copy-done), custom_call_target="tpu_custom_call" | custom-call | flops 549453824 | bytes 2097152 | tf_op jit(solution)/shard_map/pallas_call | solution.py:83
  7.4 0.0 copy-start.3
  7.4 7.3 %all-to-all-start = ((bf16[32,16,1024]{2,1,0:T(8,128)(2,1)}), bf16[32,16,1024]{2,1,0:T(8,128)(2,1)S(1)}, u32[]{:S(2)}, u32[]{:S(2)}) async-start(bf16[32,16,1024]{2,1,0:T(8,128)(2,1)} %bitcast.1), calls=%async_computation | async-start | bytes 2097152 | tf_op jit(solution)/shard_map/all_to_all | solution.py:167
  14.7 0.0 copy-done.3
  14.7 0.3 collective-permute-start
  15.1 0.1 add.51
  15.1 0.8 %collective-permute-done = s32[1,32]{1,0:T(1,128)S(1)} collective-permute-done((s32[1,32]{1,0:T(1,128)S(1)}, s32[1,32]{1,0:T(1,128)S(1)}, u32[]{:S(2)}, u32[]{:S(2)}) %collective-permute-start) | collective-permute-done | bytes 160 | tf_op jit(solution)/shard_map/ppermute | solution.py:160
  15.9 0.1 select_n.53
  16.0 0.1 eq.22
  16.1 0.1 broadcast_add_fusion
  16.2 0.1 add.56
  16.3 0.1 fusion.target_ref
  16.4 24.6 %all-to-all-done = bf16[32,16,1024]{2,1,0:T(8,128)(2,1)S(1)} async-done(((bf16[32,16,1024]{2,1,0:T(8,128)(2,1)}), bf16[32,16,1024]{2,1,0:T(8,128)(2,1)S(1)}, u32[]{:S(2)}, u32[]{:S(2)}) %all-to-all-start) | async-done | bytes 1048608 | tf_op jit(solution)/shard_map/all_to_all | solution.py:167
  41.0 2.9 %shard_map.56 = (f32[8,2,32,64]{3,2,1,0:T(8,128)S(1)}, f32[8,2,32,64]{3,2,1,0:T(8,128)S(1)}) custom-call(s32[1]{0:T(128)} %bitcast.me_ref, s32[128,2]{1,0:T(8,128)S(1)} %fusion.target_ref, bf16[512,1024]{1,0:T(8,128)(2,1)S(1)} %bitcast.3), custom_call_target="tpu_custom_call" | custom-call | flops 1073741824 | bytes 1048576 | tf_op jit(solution)/shard_map/pallas_call | solution.py:145
  43.8 0.1 collective-permute-start.1
  43.9 1.5 %collective-permute-done.1 = f32[8,2,32,64]{3,2,1,0:T(8,128)S(1)} collective-permute-done((f32[8,2,32,64]{3,2,1,0:T(8,128)S(1)}, f32[8,2,32,64]{3,2,1,0:T(8,128)S(1)}, u32[]{:S(2)}, u32[]{:S(2)}) %collective-permute-start.1) | collective-permute-done | bytes 131104 | tf_op jit(solution)/shard_map/ppermute | solution.py:169
  45.4 0.9 %maximum_select_fusion = f32[16,2,32,64]{3,2,1,0:T(8,128)} fusion(f32[8,2,32,64]{3,2,1,0:T(8,128)S(1)} %collective-permute-done.1, f32[8,2,32,64]{3,2,1,0:T(8,128)S(1)} %get-tuple-element.7, pred[]{:T(512)S(6)} %eq.21), kind=kLoop, calls=%fused_computation | loop fusion | flops 196608 | bytes 524289 | tf_op jit(solution)/shard_map/jit(_where)/select_n | solution.py:170
  (5 shorter events, 0.0 us)
Async XLA Ops:
  0.0 1.9 %copy-start.1 = (f32[12,512]{1,0:T(8,128)S(1)}, f32[12,512]{1,0:T(8,128)}, u32[]{:S(2)}) copy-start(f32[12,512]{1,0:T(8,128)} %constant.44.clone.taps_ref) | copy-start | bytes 73732
  0.0 2.0 %copy-start = (bf16[512,512]{1,0:T(8,128)(2,1)S(1)}, bf16[512,512]{1,0:T(8,128)(2,1)}, u32[]{:S(2)}) copy-start(bf16[512,512]{1,0:T(8,128)(2,1)} %constant.43.clone.table_ref) | copy-start | bytes 1572868
  0.0 2.0 %copy-start.2 = (s32[2]{0:T(128)S(1)}, s32[2]{0:T(128)}, u32[]{:S(2)}) copy-start(s32[2]{0:T(128)} %flags_ref.1) | copy-start | bytes 28
  7.4 7.3 %copy-start.3 = (s32[1,32]{1,0:T(1,128)S(1)}, s32[1,32]{1,0:T(1,128)}, u32[]{:S(2)}) copy-start(s32[1,32]{1,0:T(1,128)} %param.6) | copy-start | bytes 388
  7.4 33.5 %all-to-all-start = ((bf16[32,16,1024]{2,1,0:T(8,128)(2,1)}), bf16[32,16,1024]{2,1,0:T(8,128)(2,1)S(1)}, u32[]{:S(2)}, u32[]{:S(2)}) async-start(bf16[32,16,1024]{2,1,0:T(8,128)(2,1)} %bitcast.1), calls=%async_computation | async-start | bytes 2097152 | tf_op jit(solution)/shard_map/all_to_all | solution.py:167
  14.7 1.2 %collective-permute-start = (s32[1,32]{1,0:T(1,128)S(1)}, s32[1,32]{1,0:T(1,128)S(1)}, u32[]{:S(2)}, u32[]{:S(2)}) collective-permute-start(s32[1,32]{1,0:T(1,128)S(1)} %copy-done.3), channel_id=1, source_target_pairs={{0,1},{1,0},{2,3},{3,2},{4,5},{5,4},{6,7},{7,6},{8,9},{9,8},{10,11... | collective-permute-start | bytes 392 | tf_op jit(solution)/shard_map/ppermute | solution.py:160
  43.8 1.6 %collective-permute-start.1 = (f32[8,2,32,64]{3,2,1,0:T(8,128)S(1)}, f32[8,2,32,64]{3,2,1,0:T(8,128)S(1)}, u32[]{:S(2)}, u32[]{:S(2)}) collective-permute-start(f32[8,2,32,64]{3,2,1,0:T(8,128)S(1)} %get-tuple-element.8), channel_id=1, source_target_pairs={{0,1},{1,0},{2,3},{3,2},{4,5},{5,4},{6,7},{7,6},{8,9},{9,8},{10,11... | collective-permute-start | bytes 393224 | tf_op jit(solution)/shard_map/ppermute | solution.py:169

commit v3 on v2

--- a/solution.py
+++ b/solution.py
@@ -16,6 +16,7 @@
 LANES = 128
 SUB = 8
 STEP = SPEC // SUB
+STRIDE = STEP + 1
 SWAP = [(0, 1), (1, 0)]
 VMEM_LIMIT = 40 * 1024 * 1024
 
@@ -35,8 +36,20 @@
     return np.stack([np.cos(phase), -np.sin(phase)], axis=1).astype(np.float32)
 
 
-def channelize_kernel(flags_ref, x_ref, taps_ref, table_ref, out_ref, wide, fir):
+def turns(count):
+    half = count // 2
+    return [m for pair in zip(range(half, count), [*range(1, half), 0]) for m in pair]
+
+
+def channelize_kernel(
+    me_ref, flags_ref, x_ref, taps_ref, table_ref, *refs, count
+):
+    outs, (wide, fir, spectra) = refs[:count], refs[count:]
     inputs = x_ref.shape[0]
+    rows = FRAME // count
+    half = rows // 2
+    me = me_ref[0]
+    last = lax.broadcasted_iota(jnp.int32, (SUB, LANES), 0) == SUB - 1
     for i in range(inputs):
         for j in range(FRAME // LANES):
             cols = pl.ds(j * LANES, LANES)
@@ -45,49 +58,62 @@
             taps = [
                 jnp.broadcast_to(taps_ref[pl.ds(t, 1), cols], (SUB, LANES)) for t in range(TAPS)
             ]
-            window = [wide[slot, pl.ds(b, SUB, stride=STEP), :] for b in range(TAPS - 1)]
+
+            def load(b):
+                return wide[slot, pl.ds(b, SUB, stride=STRIDE), :]
+
+            def total(window):
+                out = taps[0] * window[0]
+                for t in range(1, TAPS):
+                    out = out + taps[t] * window[t]
+                return out
+
+            extra = total([load(STEP + t) for t in range(TAPS)])
+            window = [load(b) for b in range(TAPS - 1)]
             pair = []
             for b in range(STEP):
-                window.append(wide[slot, pl.ds(b + TAPS - 1, SUB, stride=STEP), :])
-                total = taps[0] * window[b]
-                for t in range(1, TAPS):
-                    total = total + taps[t] * window[b + t]
-                pair.append(total)
+                window.append(load(b + TAPS - 1))
+                row = total(window[b:])
+                past = b - (STEP - SUB + 1)
+                if past >= 0:
+                    row = jnp.where(last, pltpu.roll(extra, SUB - 1 - past, 0), row)
+                pair.append(row)
                 if len(pair) == 2:
                     both = jnp.concatenate(pair, axis=0).astype(jnp.bfloat16)
                     fir[i, pl.ds((b - 1) * SUB, 2 * SUB), cols] = both
                     pair = []
         good = (1 - flags_ref[i]).astype(jnp.float32)
-        rows = 128
-        for r in range(0, FRAME, rows):
-            spectra = lax.dot_general(
-                table_ref[pl.ds(r, rows), :],
-                fir[i],
-                (((1,), (1,)), ((), ())),
-                preferred_element_type=jnp.float32,
-            ).reshape(rows // (2 * SUB), 2, SUB, SPEC)
-            squares = jnp.sum(spectra * spectra, axis=1)
-            power = jnp.sum(squares, axis=2, keepdims=True) / SPEC
+        spectra[i] = lax.dot_general(
+            table_ref[...], fir[i], (((1,), (1,)), ((), ())), preferred_element_type=jnp.float32
+        )
+        for m, out in zip(turns(count), outs):
+            start = pl.multiple_of(jnp.bitwise_xor(me, m) * rows, rows)
+            real = spectra[i, pl.ds(start, half), :]
+            imag = spectra[i, pl.ds(start + half, half), :]
+            power = jnp.sum(real * real + imag * imag, axis=1, keepdims=True) / SPEC
             scale = good / jnp.sqrt(power + 1e-05)
-            scaled = (spectra * scale[:, None]).astype(jnp.bfloat16)
-            out_ref[pl.ds(r, rows), pl.ds(i * SPEC, SPEC)] = scaled.reshape(rows, SPEC)
-
-
-def channelize(samples, flags, share):
+            scaled = jnp.concatenate([real * scale, imag * scale], axis=0)
+            out[:, pl.ds(i * SPEC, SPEC)] = scaled.astype(jnp.bfloat16)
+
+
+def channelize(samples, flags, me, share):
     inputs = samples.shape[0]
+    count = CH // share
     frames = samples.reshape(inputs, SPEC + TAPS - 1, FRAME)
-    table = twiddle().reshape(CH // share, share, 2, FRAME).transpose(0, 2, 1, 3)
+    table = twiddle().reshape(count, share, 2, FRAME).transpose(0, 2, 1, 3)
     table = jnp.asarray(table.reshape(FRAME, FRAME), dtype=jnp.bfloat16)
     taps = jnp.asarray(prototype())
+    smem = pl.BlockSpec(memory_space=pltpu.SMEM)
     vmem = pl.BlockSpec(memory_space=pltpu.VMEM)
     return pl.pallas_call(
-        channelize_kernel,
-        out_shape=jax.ShapeDtypeStruct((FRAME, inputs * SPEC), jnp.bfloat16),
-        in_specs=[pl.BlockSpec(memory_space=pltpu.SMEM), vmem, vmem, vmem],
-        out_specs=vmem,
+        functools.partial(channelize_kernel, count=count),
+        out_shape=[jax.ShapeDtypeStruct((2 * share, inputs * SPEC), jnp.bfloat16)] * count,
+        in_specs=[smem, smem, vmem, vmem, vmem],
+        out_specs=[vmem] * count,
         scratch_shapes=[
-            pltpu.VMEM((inputs * FRAME // LANES, SPEC + 16, LANES), jnp.float32),
+            pltpu.VMEM((inputs * FRAME // LANES, SPEC + 24, LANES), jnp.float32),
             pltpu.VMEM((inputs, SPEC, FRAME), jnp.bfloat16),
+            pltpu.VMEM((inputs, FRAME, SPEC), jnp.float32),
         ],
         compiler_params=pltpu.CompilerParams(vmem_limit_bytes=VMEM_LIMIT),
         cost_estimate=pl.CostEstimate(
@@ -95,15 +121,20 @@
             bytes_accessed=4 * inputs * SPEC * FRAME,
             transcendentals=0,
         ),
-    )(flags, frames, taps, table)
-
-
-def correlate_kernel(me_ref, target_ref, arrived_ref, own_ref, other_ref):
+    )(me.reshape(1), flags, frames, taps, table)
+
+
+def correlate_kernel(first_ref, target_ref, *refs):
+    arrived_refs, (own_ref, other_ref) = refs[:-2], refs[-2:]
     share, _, block, width = own_ref.shape
     parts = 2 * width
-    sources = arrived_ref.shape[0]
-    inputs = arrived_ref.shape[1] // SPEC
-    first = me_ref[0] == 0
+    inputs = arrived_refs[0].shape[1] // SPEC
+    arrived = [
+        jnp.concatenate([ref[:, pl.ds(i * SPEC, SPEC)] for ref in arrived_refs], axis=0)
+        for i in range(inputs)
+    ]
+    sources = arrived[0].shape[0]
+    first = first_ref[0] == 0
     column = lax.broadcasted_iota(jnp.int32, (parts, sources), 1)
     target = [
         jnp.broadcast_to(target_ref[:, pl.ds(i, 1)], (parts, sources)) for i in range(inputs)
@@ -112,11 +143,7 @@
         slots = None
         for i in range(inputs):
             pick = jnp.where(column == target[i] + k, 1.0, 0.0).astype(jnp.bfloat16)
-            part = jnp.dot(
-                pick,
-                arrived_ref[:, pl.ds(i * SPEC, SPEC)],
-                preferred_element_type=jnp.float32,
-            )
+            part = jnp.dot(pick, arrived[i], preferred_element_type=jnp.float32)
             slots = part if slots is None else slots + part
         slots = slots.astype(jnp.bfloat16)
         gram = lax.dot_general(
@@ -131,10 +158,10 @@
 
 def correlate(arrived, orders, me, share):
     blocks, block = orders.shape
-    inputs = arrived.shape[1] // SPEC
+    inputs = arrived[0].shape[1] // SPEC
     which = jnp.arange(blocks, dtype=jnp.int32)[:, None]
     source = (orders // inputs) * blocks + which
-    row = (source * 2 * share).reshape(1, blocks * block)
+    row = (jnp.bitwise_xor(source, me) * 2 * share).reshape(1, blocks * block)
     part = share * jnp.arange(2, dtype=jnp.int32)[:, None]
     place = (row + part).reshape(-1, 1)
     held = jnp.tile((orders % inputs).reshape(-1), 2)[:, None]
@@ -142,33 +169,40 @@
     target = jnp.where(held == lane, place, -FRAME)
     vmem = pl.BlockSpec(memory_space=pltpu.VMEM)
     tile = jax.ShapeDtypeStruct((share, 2, block, blocks * block), jnp.float32)
+    size = len(arrived) * arrived[0].size
     return pl.pallas_call(
         correlate_kernel,
         out_shape=(tile, tile),
-        in_specs=[pl.BlockSpec(memory_space=pltpu.SMEM), vmem, vmem],
+        in_specs=[pl.BlockSpec(memory_space=pltpu.SMEM), vmem] + [vmem] * len(arrived),
         out_specs=(vmem, vmem),
         compiler_params=pltpu.CompilerParams(vmem_limit_bytes=VMEM_LIMIT),
         cost_estimate=pl.CostEstimate(
-            flops=2 * share * 128 * arrived.size, bytes_accessed=2 * arrived.size, transcendentals=0
+            flops=2 * share * 128 * size, bytes_accessed=2 * size, transcendentals=0
         ),
-    )(me.reshape(1), target, arrived)
+    )((me % blocks).reshape(1), target, *arrived)
 
 
 def split_channels(freq, blocks, samples, slot_order, flags):
-    share = CH // (freq * blocks)
-    me = lax.axis_index("blk").astype(jnp.int32)
+    count = freq * blocks
+    share = CH // count
+    axes = ("freq", "blk")
+    me = lax.axis_index(axes).astype(jnp.int32)
+    first = me % blocks == 0
     partner = lax.ppermute(slot_order, "blk", SWAP)
     orders = jnp.where(
-        me == 0,
+        first,
         jnp.concatenate([slot_order, partner]),
         jnp.concatenate([partner, slot_order]),
     )
-    quantized = channelize(samples, flags, share)
-    arrived = lax.all_to_all(quantized, ("freq", "blk"), split_axis=0, concat_axis=0, tiled=True)
+    sent = channelize(samples, flags, me, share)
+    arrived = [None] * count
+    for m, part in zip(turns(count), sent):
+        pairs = [(d, d ^ m) for d in range(count)]
+        arrived[m] = lax.ppermute(part, axes, pairs) if m else part
     own, other = correlate(arrived, orders, me, share)
     received = lax.ppermute(other, "blk", SWAP)
     return jnp.where(
-        me == 0,
+        first,
         jnp.concatenate([own, received]),
         jnp.concatenate([received, own]),
     )

time: 46.5 us -> 69.3 us (1.49)
  starting transfers between devices: 7.69 us -> 51.8 us
  waiting for transfers between devices: 26.9 us -> 7.34 us
  Pallas kernels: 8.29 us -> 6.54 us
    ppermute x0 -> x31, starting transfers between devices: none -> 51.2 us  [split_channels(): arrived[m] = lax.ppermute(part, axes, pairs) if m else part]
    all_to_all x1 -> x0, waiting for transfers between devices: 24.6 us -> none  [split_channels(): lax.all_to_all(quantized, ('freq', 'blk'), split_axis=0, concat_axis=0, t...]
    all_to_all x1 -> x0, starting transfers between devices: 7.3 us -> none  [split_channels(): lax.all_to_all(quantized, ('freq', 'blk'), split_axis=0, concat_axis=0, t...]
    ppermute x0 -> x31, waiting for transfers between devices: none -> 6.14 us  [split_channels(): arrived[m] = lax.ppermute(part, axes, pairs) if m else part]
    pallas_call x1, Pallas kernels: 5.43 us -> 3.69 us  [channelize(): pl.pallas_call(functools.partial(channelize_kernel, count=count), out_sha...]
    ppermute x1, waiting for transfers between devices: 0.78 us -> 0.01 us  [split_channels(): partner = lax.ppermute(slot_order, 'blk', SWAP)]
  transfers between devices with their start and end apart: 3 -> 33, of which waited for: 3 -> 4; matrix products, arithmetic and copies ran while one was open for 1% -> 1% of each run, Pallas kernels for 0% -> 0%
where the time goes in v3:
time: 69.3 us; the launch traced here: 69.2 us
  starting transfers between devices  51.8 us (75%)
  waiting for transfers between devices  7.34 us (11%)
  Pallas kernels  6.54 us (9%)
  local copies, waits for them, and re-layouts  2.29 us (3%)
  other arithmetic  1.04 us (2%)
    ppermute x31, starting transfers between devices, split_channels(): arrived[m] = lax.ppermute(part, axes, pairs) if m else part  51.2 us
    ppermute x31, waiting for transfers between devices, split_channels(): arrived[m] = lax.ppermute(part, axes, pairs) if m else part  6.14 us
    pallas_call x1, Pallas kernels, channelize(): pl.pallas_call(functools.partial(channelize_kernel, count=count), out_sha...  3.69 us
    pallas_call x1, Pallas kernels, correlate(): pl.pallas_call(correlate_kernel, out_shape=(tile, tile), in_specs=[pl.Blo...  2.85 us
    reshape x1, local copies, waits for them, and re-layouts, channelize(): frames = samples.reshape(inputs, SPEC + TAPS - 1, FRAME)  1.94 us
  transfers between devices with their start and end apart: 33, of which 4 were waited for; matrix products, arithmetic and copies ran while one was open for 1% of the time, Pallas kernels for 0%

profile of v3, /device:TPU:0, one launch (start us, length us, event | category | flops | bytes accessed | tf_op | source)
XLA Modules:
  0.0 69.2 jit_solution(15187057754120128192)
XLA Ops:
  0.0 1.9 %reshape.86.x_ref = bf16[2,523,512]{2,1,0:T(8,128)(2,1)S(1)} reshape(bf16[2,267776]{1,0:T(2,128)(2,1)} %param.5) | data formatting | bytes 2142208 | tf_op jit(solution)/shard_map/reshape | solution.py:102
  2.0 3.7 %shard_map.55 = (bf16[16,1024]{1,0:T(8,128)(2,1)S(1)}, bf16[16,1024]{1,0:T(8,128)(2,1)S(1)}, bf16[16,1024]{1,0:T(8,128)(2,1)S(1)}, bf16[16,1024]{1,0:T(8,128)(2,...) custom-call(s32[1]{0:T(128)} %bitcast.1.me_ref, ...), custom_call_target="tpu_custom_call" | custom-call | flops 549453824 | bytes 2097152 | tf_op jit(solution)/shard_map/pallas_call | solution.py:108
  5.7 0.5 collective-permute-start.1
  6.2 2.6 %collective-permute-start.2 = (bf16[16,1024]{1,0:T(8,128)(2,1)S(1)}, bf16[16,1024]{1,0:T(8,128)(2,1)S(1)}, u32[]{:S(2)}, u32[]{:S(2)}) collective-permute-start(bf16[16,1024]{1,0:T(8,128)(2,1)S(1)} %get-tuple-element.41), channel_id=1, source_target_pairs={{0,2},{1,3},{2,0},{3,1},{4,6},{5,7},{6,4},{7,5},{8,10},{9,11},{10,... | collective-permute-start | bytes 98312 | tf_op jit(solution)/shard_map/ppermute | solution.py:201
  9.0 2.0 %collective-permute-start.4 = (bf16[16,1024]{1,0:T(8,128)(2,1)S(1)}, bf16[16,1024]{1,0:T(8,128)(2,1)S(1)}, u32[]{:S(2)}, u32[]{:S(2)}) collective-permute-start(bf16[16,1024]{1,0:T(8,128)(2,1)S(1)} %get-tuple-element.43), channel_id=1, source_target_pairs={{0,4},{1,5},{2,6},{3,7},{4,0},{5,1},{6,2},{7,3},{8,12},{9,13},{10,... | collective-permute-start | bytes 98312 | tf_op jit(solution)/shard_map/ppermute | solution.py:201
  11.0 0.7 %collective-permute-start.5 = (bf16[16,1024]{1,0:T(8,128)(2,1)S(1)}, bf16[16,1024]{1,0:T(8,128)(2,1)S(1)}, u32[]{:S(2)}, u32[]{:S(2)}) collective-permute-start(bf16[16,1024]{1,0:T(8,128)(2,1)S(1)} %get-tuple-element.44), channel_id=1, source_target_pairs={{0,5},{1,4},{2,7},{3,6},{4,1},{5,0},{6,3},{7,2},{8,13},{9,12},{10,... | collective-permute-start | bytes 98312 | tf_op jit(solution)/shard_map/ppermute | solution.py:201
  11.7 1.7 %collective-permute-start.6 = (bf16[16,1024]{1,0:T(8,128)(2,1)S(1)}, bf16[16,1024]{1,0:T(8,128)(2,1)S(1)}, u32[]{:S(2)}, u32[]{:S(2)}) collective-permute-start(bf16[16,1024]{1,0:T(8,128)(2,1)S(1)} %get-tuple-element.45), channel_id=1, source_target_pairs={{0,6},{1,7},{2,4},{3,5},{4,2},{5,3},{6,0},{7,1},{8,14},{9,15},{10,... | collective-permute-start | bytes 98312 | tf_op jit(solution)/shard_map/ppermute | solution.py:201
  13.4 0.7 %collective-permute-start.7 = (bf16[16,1024]{1,0:T(8,128)(2,1)S(1)}, bf16[16,1024]{1,0:T(8,128)(2,1)S(1)}, u32[]{:S(2)}, u32[]{:S(2)}) collective-permute-start(bf16[16,1024]{1,0:T(8,128)(2,1)S(1)} %get-tuple-element.46), channel_id=1, source_target_pairs={{0,7},{1,6},{2,5},{3,4},{4,3},{5,2},{6,1},{7,0},{8,15},{9,14},{10,... | collective-permute-start | bytes 98312 | tf_op jit(solution)/shard_map/ppermute | solution.py:201
  14.2 1.6 %collective-permute-start.8 = (bf16[16,1024]{1,0:T(8,128)(2,1)S(1)}, bf16[16,1024]{1,0:T(8,128)(2,1)S(1)}, u32[]{:S(2)}, u32[]{:S(2)}) collective-permute-start(bf16[16,1024]{1,0:T(8,128)(2,1)S(1)} %get-tuple-element.47), channel_id=1, source_target_pairs={{0,8},{1,9},{2,10},{3,11},{4,12},{5,13},{6,14},{7,15},{8,0},{9,1},... | collective-permute-start | bytes 98312 | tf_op jit(solution)/shard_map/ppermute | solution.py:201
  16.1 2.5 %collective-permute-start.10 = (bf16[16,1024]{1,0:T(8,128)(2,1)S(1)}, bf16[16,1024]{1,0:T(8,128)(2,1)S(1)}, u32[]{:S(2)}, u32[]{:S(2)}) collective-permute-start(bf16[16,1024]{1,0:T(8,128)(2,1)S(1)} %get-tuple-element.49), channel_id=1, source_target_pairs={{0,10},{1,11},{2,8},{3,9},{4,14},{5,15},{6,12},{7,13},{8,2},{9,3},... | collective-permute-start | bytes 98312 | tf_op jit(solution)/shard_map/ppermute | solution.py:201
  18.7 2.2 %collective-permute-start.12 = (bf16[16,1024]{1,0:T(8,128)(2,1)S(1)}, bf16[16,1024]{1,0:T(8,128)(2,1)S(1)}, u32[]{:S(2)}, u32[]{:S(2)}) collective-permute-start(bf16[16,1024]{1,0:T(8,128)(2,1)S(1)} %get-tuple-element.51), channel_id=1, source_target_pairs={{0,12},{1,13},{2,14},{3,15},{4,8},{5,9},{6,10},{7,11},{8,4},{9,5},... | collective-permute-start | bytes 98312 | tf_op jit(solution)/shard_map/ppermute | solution.py:201
  20.9 0.8 %collective-permute-start.13 = (bf16[16,1024]{1,0:T(8,128)(2,1)S(1)}, bf16[16,1024]{1,0:T(8,128)(2,1)S(1)}, u32[]{:S(2)}, u32[]{:S(2)}) collective-permute-start(bf16[16,1024]{1,0:T(8,128)(2,1)S(1)} %get-tuple-element.52), channel_id=1, source_target_pairs={{0,13},{1,12},{2,15},{3,14},{4,9},{5,8},{6,11},{7,10},{8,5},{9,4},... | collective-permute-start | bytes 98312 | tf_op jit(solution)/shard_map/ppermute | solution.py:201
  21.6 2.6 %collective-permute-start.14 = (bf16[16,1024]{1,0:T(8,128)(2,1)S(1)}, bf16[16,1024]{1,0:T(8,128)(2,1)S(1)}, u32[]{:S(2)}, u32[]{:S(2)}) collective-permute-start(bf16[16,1024]{1,0:T(8,128)(2,1)S(1)} %get-tuple-element.53), channel_id=1, source_target_pairs={{0,14},{1,15},{2,12},{3,13},{4,10},{5,11},{6,8},{7,9},{8,6},{9,7},... | collective-permute-start | bytes 98312 | tf_op jit(solution)/shard_map/ppermute | solution.py:201
  24.2 0.7 %collective-permute-start.15 = (bf16[16,1024]{1,0:T(8,128)(2,1)S(1)}, bf16[16,1024]{1,0:T(8,128)(2,1)S(1)}, u32[]{:S(2)}, u32[]{:S(2)}) collective-permute-start(bf16[16,1024]{1,0:T(8,128)(2,1)S(1)} %get-tuple-element.54), channel_id=1, source_target_pairs={{0,15},{1,14},{2,13},{3,12},{4,11},{5,10},{6,9},{7,8},{8,7},{9,6},... | collective-permute-start | bytes 98312 | tf_op jit(solution)/shard_map/ppermute | solution.py:201
  24.9 2.6 %collective-permute-start.16 = (bf16[16,1024]{1,0:T(8,128)(2,1)S(1)}, bf16[16,1024]{1,0:T(8,128)(2,1)S(1)}, u32[]{:S(2)}, u32[]{:S(2)}) collective-permute-start(bf16[16,1024]{1,0:T(8,128)(2,1)S(1)} %get-tuple-element.55), channel_id=1, source_target_pairs={{0,16},{1,17},{2,18},{3,19},{4,20},{5,21},{6,22},{7,23},{8,24},{9,... | collective-permute-start | bytes 98312 | tf_op jit(solution)/shard_map/ppermute | solution.py:201
  27.9 3.4 %collective-permute-start.18 = (bf16[16,1024]{1,0:T(8,128)(2,1)S(1)}, bf16[16,1024]{1,0:T(8,128)(2,1)S(1)}, u32[]{:S(2)}, u32[]{:S(2)}) collective-permute-start(bf16[16,1024]{1,0:T(8,128)(2,1)S(1)} %get-tuple-element.57), channel_id=1, source_target_pairs={{0,18},{1,19},{2,16},{3,17},{4,22},{5,23},{6,20},{7,21},{8,26},{9,... | collective-permute-start | bytes 98312 | tf_op jit(solution)/shard_map/ppermute | solution.py:201
  31.3 3.1 %collective-permute-start.20 = (bf16[16,1024]{1,0:T(8,128)(2,1)S(1)}, bf16[16,1024]{1,0:T(8,128)(2,1)S(1)}, u32[]{:S(2)}, u32[]{:S(2)}) collective-permute-start(bf16[16,1024]{1,0:T(8,128)(2,1)S(1)} %get-tuple-element.59), channel_id=1, source_target_pairs={{0,20},{1,21},{2,22},{3,23},{4,16},{5,17},{6,18},{7,19},{8,28},{9,... | collective-permute-start | bytes 98312 | tf_op jit(solution)/shard_map/ppermute | solution.py:201
  34.4 0.6 collective-permute-start.21
  35.1 3.8 %collective-permute-start.22 = (bf16[16,1024]{1,0:T(8,128)(2,1)S(1)}, bf16[16,1024]{1,0:T(8,128)(2,1)S(1)}, u32[]{:S(2)}, u32[]{:S(2)}) collective-permute-start(bf16[16,1024]{1,0:T(8,128)(2,1)S(1)} %get-tuple-element.61), channel_id=1, source_target_pairs={{0,22},{1,23},{2,20},{3,21},{4,18},{5,19},{6,16},{7,17},{8,30},{9,... | collective-permute-start | bytes 98312 | tf_op jit(solution)/shard_map/ppermute | solution.py:201
  38.9 0.6 collective-permute-start.23
  39.5 3.4 %collective-permute-start.24 = (bf16[16,1024]{1,0:T(8,128)(2,1)S(1)}, bf16[16,1024]{1,0:T(8,128)(2,1)S(1)}, u32[]{:S(2)}, u32[]{:S(2)}) collective-permute-start(bf16[16,1024]{1,0:T(8,128)(2,1)S(1)} %get-tuple-element.63), channel_id=1, source_target_pairs={{0,24},{1,25},{2,26},{3,27},{4,28},{5,29},{6,30},{7,31},{8,16},{9,... | collective-permute-start | bytes 98312 | tf_op jit(solution)/shard_map/ppermute | solution.py:201
  43.1 4.4 %collective-permute-start.26 = (bf16[16,1024]{1,0:T(8,128)(2,1)S(1)}, bf16[16,1024]{1,0:T(8,128)(2,1)S(1)}, u32[]{:S(2)}, u32[]{:S(2)}) collective-permute-start(bf16[16,1024]{1,0:T(8,128)(2,1)S(1)} %get-tuple-element.65), channel_id=1, source_target_pairs={{0,26},{1,27},{2,24},{3,25},{4,30},{5,31},{6,28},{7,29},{8,18},{9,... | collective-permute-start | bytes 98312 | tf_op jit(solution)/shard_map/ppermute | solution.py:201
  47.8 4.0 %collective-permute-start.28 = (bf16[16,1024]{1,0:T(8,128)(2,1)S(1)}, bf16[16,1024]{1,0:T(8,128)(2,1)S(1)}, u32[]{:S(2)}, u32[]{:S(2)}) collective-permute-start(bf16[16,1024]{1,0:T(8,128)(2,1)S(1)} %get-tuple-element.67), channel_id=1, source_target_pairs={{0,28},{1,29},{2,30},{3,31},{4,24},{5,25},{6,26},{7,27},{8,20},{9,... | collective-permute-start | bytes 98312 | tf_op jit(solution)/shard_map/ppermute | solution.py:201
  51.8 0.5 collective-permute-start.29
  52.3 4.6 %collective-permute-start.30 = (bf16[16,1024]{1,0:T(8,128)(2,1)S(1)}, bf16[16,1024]{1,0:T(8,128)(2,1)S(1)}, u32[]{:S(2)}, u32[]{:S(2)}) collective-permute-start(bf16[16,1024]{1,0:T(8,128)(2,1)S(1)} %get-tuple-element.69), channel_id=1, source_target_pairs={{0,30},{1,31},{2,28},{3,29},{4,26},{5,27},{6,24},{7,25},{8,22},{9,... | collective-permute-start | bytes 98312 | tf_op jit(solution)/shard_map/ppermute | solution.py:201
  56.9 0.8 %collective-permute-start.31 = (bf16[16,1024]{1,0:T(8,128)(2,1)S(1)}, bf16[16,1024]{1,0:T(8,128)(2,1)S(1)}, u32[]{:S(2)}, u32[]{:S(2)}) collective-permute-start(bf16[16,1024]{1,0:T(8,128)(2,1)S(1)} %get-tuple-element.70), channel_id=1, source_target_pairs={{0,31},{1,30},{2,29},{3,28},{4,27},{5,26},{6,25},{7,24},{8,23},{9,... | collective-permute-start | bytes 98312 | tf_op jit(solution)/shard_map/ppermute | solution.py:201
  58.1 1.7 %collective-permute-done.30.refs_30_ = bf16[16,1024]{1,0:T(8,128)(2,1)S(1)} collective-permute-done((bf16[16,1024]{1,0:T(8,128)(2,1)S(1)}, bf16[16,1024]{1,0:T(8,128)(2,1)S(1)}, u32[]{:S(2)}, u32[]{:S(2)}) %collective-permute-start.30) | collective-permute-done | bytes 32800 | tf_op jit(solution)/shard_map/ppermute | solution.py:201
  59.8 4.1 %collective-permute-done.31.refs_31_ = bf16[16,1024]{1,0:T(8,128)(2,1)S(1)} collective-permute-done((bf16[16,1024]{1,0:T(8,128)(2,1)S(1)}, bf16[16,1024]{1,0:T(8,128)(2,1)S(1)}, u32[]{:S(2)}, u32[]{:S(2)}) %collective-permute-start.31) | collective-permute-done | bytes 32800 | tf_op jit(solution)/shard_map/ppermute | solution.py:201
  63.9 2.9 %shard_map.56 = (f32[8,2,32,64]{3,2,1,0:T(8,128)S(1)}, f32[8,2,32,64]{3,2,1,0:T(8,128)S(1)}) custom-call(s32[1]{0:T(128)} %bitcast.first_ref, s32[128,2]{1,0:T(8,128)S(1)} %fusion.target_ref, bf16[16,1024]{1,0:T(8,128)(2,1)S(1)} %get-tuple-element.39.refs_0_, bf16[16,1024]{1,0:T(8,128)(2,1)S(1)} %collective-permute-done.1.refs_1_, ...), custom_call_target="tpu_custom_call" | custom-call | flops 1073741824 | bytes 1048576 | tf_op jit(solution)/shard_map/pallas_call | solution.py:173
  66.7 0.4 collective-permute-start.32
  67.1 1.2 %collective-permute-done.32 = f32[8,2,32,64]{3,2,1,0:T(8,128)S(1)} collective-permute-done((f32[8,2,32,64]{3,2,1,0:T(8,128)S(1)}, f32[8,2,32,64]{3,2,1,0:T(8,128)S(1)}, u32[]{:S(2)}, u32[]{:S(2)}) %collective-permute-start.32) | collective-permute-done | bytes 131104 | tf_op jit(solution)/shard_map/ppermute | solution.py:203
  68.3 0.9 %maximum_select_fusion = f32[16,2,32,64]{3,2,1,0:T(8,128)} fusion(f32[8,2,32,64]{3,2,1,0:T(8,128)S(1)} %collective-permute-done.32, f32[8,2,32,64]{3,2,1,0:T(8,128)S(1)} %get-tuple-element.71, pred[]{:T(512)S(6)} %eq.23), kind=kLoop, calls=%fused_computation | loop fusion | flops 196608 | bytes 524289 | tf_op jit(solution)/shard_map/jit(_where)/select_n | solution.py:204
  (57 shorter events, 2.1 us)
Async XLA Ops:
  5.7 6.0 %collective-permute-start.1 = (bf16[16,1024]{1,0:T(8,128)(2,1)S(1)}, bf16[16,1024]{1,0:T(8,128)(2,1)S(1)}, u32[]{:S(2)}, u32[]{:S(2)}) collective-permute-start(bf16[16,1024]{1,0:T(8,128)(2,1)S(1)} %get-tuple-element.40), channel_id=1, source_target_pairs={{0,1},{1,0},{2,3},{3,2},{4,5},{5,4},{6,7},{7,6},{8,9},{9,8},{10,11... | collective-permute-start | bytes 98312 | tf_op jit(solution)/shard_map/ppermute | solution.py:201
  6.2 7.2 %collective-permute-start.2 = (bf16[16,1024]{1,0:T(8,128)(2,1)S(1)}, bf16[16,1024]{1,0:T(8,128)(2,1)S(1)}, u32[]{:S(2)}, u32[]{:S(2)}) collective-permute-start(bf16[16,1024]{1,0:T(8,128)(2,1)S(1)} %get-tuple-element.41), channel_id=1, source_target_pairs={{0,2},{1,3},{2,0},{3,1},{4,6},{5,7},{6,4},{7,5},{8,10},{9,11},{10,... | collective-permute-start | bytes 98312 | tf_op jit(solution)/shard_map/ppermute | solution.py:201
  8.8 5.4 %collective-permute-start.3 = (bf16[16,1024]{1,0:T(8,128)(2,1)S(1)}, bf16[16,1024]{1,0:T(8,128)(2,1)S(1)}, u32[]{:S(2)}, u32[]{:S(2)}) collective-permute-start(bf16[16,1024]{1,0:T(8,128)(2,1)S(1)} %get-tuple-element.42), channel_id=1, source_target_pairs={{0,3},{1,2},{2,1},{3,0},{4,7},{5,6},{6,5},{7,4},{8,11},{9,10},{10,... | collective-permute-start | bytes 98312 | tf_op jit(solution)/shard_map/ppermute | solution.py:201
  8.9 2.1 %collective-permute-start = (s32[1,32]{1,0:T(1,128)S(1)}, s32[1,32]{1,0:T(1,128)S(1)}, u32[]{:S(2)}, u32[]{:S(2)}) collective-permute-start(s32[1,32]{1,0:T(1,128)S(1)} %copy-done.3), channel_id=1, source_target_pairs={{0,1},{1,0},{2,3},{3,2},{4,5},{5,4},{6,7},{7,6},{8,9},{9,8},{10,11... | collective-permute-start | bytes 392 | tf_op jit(solution)/shard_map/ppermute | solution.py:191
  9.0 6.7 %collective-permute-start.4 = (bf16[16,1024]{1,0:T(8,128)(2,1)S(1)}, bf16[16,1024]{1,0:T(8,128)(2,1)S(1)}, u32[]{:S(2)}, u32[]{:S(2)}) collective-permute-start(bf16[16,1024]{1,0:T(8,128)(2,1)S(1)} %get-tuple-element.43), channel_id=1, source_target_pairs={{0,4},{1,5},{2,6},{3,7},{4,0},{5,1},{6,2},{7,3},{8,12},{9,13},{10,... | collective-permute-start | bytes 98312 | tf_op jit(solution)/shard_map/ppermute | solution.py:201
  11.0 5.1 %collective-permute-start.5 = (bf16[16,1024]{1,0:T(8,128)(2,1)S(1)}, bf16[16,1024]{1,0:T(8,128)(2,1)S(1)}, u32[]{:S(2)}, u32[]{:S(2)}) collective-permute-start(bf16[16,1024]{1,0:T(8,128)(2,1)S(1)} %get-tuple-element.44), channel_id=1, source_target_pairs={{0,5},{1,4},{2,7},{3,6},{4,1},{5,0},{6,3},{7,2},{8,13},{9,12},{10,... | collective-permute-start | bytes 98312 | tf_op jit(solution)/shard_map/ppermute | solution.py:201
  11.7 6.9 %collective-permute-start.6 = (bf16[16,1024]{1,0:T(8,128)(2,1)S(1)}, bf16[16,1024]{1,0:T(8,128)(2,1)S(1)}, u32[]{:S(2)}, u32[]{:S(2)}) collective-permute-start(bf16[16,1024]{1,0:T(8,128)(2,1)S(1)} %get-tuple-element.45), channel_id=1, source_target_pairs={{0,6},{1,7},{2,4},{3,5},{4,2},{5,3},{6,0},{7,1},{8,14},{9,15},{10,... | collective-permute-start | bytes 98312 | tf_op jit(solution)/shard_map/ppermute | solution.py:201
  13.4 5.3 %collective-permute-start.7 = (bf16[16,1024]{1,0:T(8,128)(2,1)S(1)}, bf16[16,1024]{1,0:T(8,128)(2,1)S(1)}, u32[]{:S(2)}, u32[]{:S(2)}) collective-permute-start(bf16[16,1024]{1,0:T(8,128)(2,1)S(1)} %get-tuple-element.46), channel_id=1, source_target_pairs={{0,7},{1,6},{2,5},{3,4},{4,3},{5,2},{6,1},{7,0},{8,15},{9,14},{10,... | collective-permute-start | bytes 98312 | tf_op jit(solution)/shard_map/ppermute | solution.py:201
  14.2 6.7 %collective-permute-start.8 = (bf16[16,1024]{1,0:T(8,128)(2,1)S(1)}, bf16[16,1024]{1,0:T(8,128)(2,1)S(1)}, u32[]{:S(2)}, u32[]{:S(2)}) collective-permute-start(bf16[16,1024]{1,0:T(8,128)(2,1)S(1)} %get-tuple-element.47), channel_id=1, source_target_pairs={{0,8},{1,9},{2,10},{3,11},{4,12},{5,13},{6,14},{7,15},{8,0},{9,1},... | collective-permute-start | bytes 98312 | tf_op jit(solution)/shard_map/ppermute | solution.py:201
  15.7 5.9 %collective-permute-start.9 = (bf16[16,1024]{1,0:T(8,128)(2,1)S(1)}, bf16[16,1024]{1,0:T(8,128)(2,1)S(1)}, u32[]{:S(2)}, u32[]{:S(2)}) collective-permute-start(bf16[16,1024]{1,0:T(8,128)(2,1)S(1)} %get-tuple-element.48), channel_id=1, source_target_pairs={{0,9},{1,8},{2,11},{3,10},{4,13},{5,12},{6,15},{7,14},{8,1},{9,0},... | collective-permute-start | bytes 98312 | tf_op jit(solution)/shard_map/ppermute | solution.py:201
  16.1 8.1 %collective-permute-start.10 = (bf16[16,1024]{1,0:T(8,128)(2,1)S(1)}, bf16[16,1024]{1,0:T(8,128)(2,1)S(1)}, u32[]{:S(2)}, u32[]{:S(2)}) collective-permute-start(bf16[16,1024]{1,0:T(8,128)(2,1)S(1)} %get-tuple-element.49), channel_id=1, source_target_pairs={{0,10},{1,11},{2,8},{3,9},{4,14},{5,15},{6,12},{7,13},{8,2},{9,3},... | collective-permute-start | bytes 98312 | tf_op jit(solution)/shard_map/ppermute | solution.py:201
  18.6 6.3 %collective-permute-start.11 = (bf16[16,1024]{1,0:T(8,128)(2,1)S(1)}, bf16[16,1024]{1,0:T(8,128)(2,1)S(1)}, u32[]{:S(2)}, u32[]{:S(2)}) collective-permute-start(bf16[16,1024]{1,0:T(8,128)(2,1)S(1)} %get-tuple-element.50), channel_id=1, source_target_pairs={{0,11},{1,10},{2,9},{3,8},{4,15},{5,14},{6,13},{7,12},{8,3},{9,2},... | collective-permute-start | bytes 98312 | tf_op jit(solution)/shard_map/ppermute | solution.py:201
  18.7 8.9 %collective-permute-start.12 = (bf16[16,1024]{1,0:T(8,128)(2,1)S(1)}, bf16[16,1024]{1,0:T(8,128)(2,1)S(1)}, u32[]{:S(2)}, u32[]{:S(2)}) collective-permute-start(bf16[16,1024]{1,0:T(8,128)(2,1)S(1)} %get-tuple-element.51), channel_id=1, source_target_pairs={{0,12},{1,13},{2,14},{3,15},{4,8},{5,9},{6,10},{7,11},{8,4},{9,5},... | collective-permute-start | bytes 98312 | tf_op jit(solution)/shard_map/ppermute | solution.py:201
  20.9 7.1 %collective-permute-start.13 = (bf16[16,1024]{1,0:T(8,128)(2,1)S(1)}, bf16[16,1024]{1,0:T(8,128)(2,1)S(1)}, u32[]{:S(2)}, u32[]{:S(2)}) collective-permute-start(bf16[16,1024]{1,0:T(8,128)(2,1)S(1)} %get-tuple-element.52), channel_id=1, source_target_pairs={{0,13},{1,12},{2,15},{3,14},{4,9},{5,8},{6,11},{7,10},{8,5},{9,4},... | collective-permute-start | bytes 98312 | tf_op jit(solution)/shard_map/ppermute | solution.py:201
  21.6 9.7 %collective-permute-start.14 = (bf16[16,1024]{1,0:T(8,128)(2,1)S(1)}, bf16[16,1024]{1,0:T(8,128)(2,1)S(1)}, u32[]{:S(2)}, u32[]{:S(2)}) collective-permute-start(bf16[16,1024]{1,0:T(8,128)(2,1)S(1)} %get-tuple-element.53), channel_id=1, source_target_pairs={{0,14},{1,15},{2,12},{3,13},{4,10},{5,11},{6,8},{7,9},{8,6},{9,7},... | collective-permute-start | bytes 98312 | tf_op jit(solution)/shard_map/ppermute | solution.py:201
  24.2 7.1 %collective-permute-start.15 = (bf16[16,1024]{1,0:T(8,128)(2,1)S(1)}, bf16[16,1024]{1,0:T(8,128)(2,1)S(1)}, u32[]{:S(2)}, u32[]{:S(2)}) collective-permute-start(bf16[16,1024]{1,0:T(8,128)(2,1)S(1)} %get-tuple-element.54), channel_id=1, source_target_pairs={{0,15},{1,14},{2,13},{3,12},{4,11},{5,10},{6,9},{7,8},{8,7},{9,6},... | collective-permute-start | bytes 98312 | tf_op jit(solution)/shard_map/ppermute | solution.py:201
  24.9 9.4 %collective-permute-start.16 = (bf16[16,1024]{1,0:T(8,128)(2,1)S(1)}, bf16[16,1024]{1,0:T(8,128)(2,1)S(1)}, u32[]{:S(2)}, u32[]{:S(2)}) collective-permute-start(bf16[16,1024]{1,0:T(8,128)(2,1)S(1)} %get-tuple-element.55), channel_id=1, source_target_pairs={{0,16},{1,17},{2,18},{3,19},{4,20},{5,21},{6,22},{7,23},{8,24},{9,... | collective-permute-start | bytes 98312 | tf_op jit(solution)/shard_map/ppermute | solution.py:201
  27.6 7.4 %collective-permute-start.17 = (bf16[16,1024]{1,0:T(8,128)(2,1)S(1)}, bf16[16,1024]{1,0:T(8,128)(2,1)S(1)}, u32[]{:S(2)}, u32[]{:S(2)}) collective-permute-start(bf16[16,1024]{1,0:T(8,128)(2,1)S(1)} %get-tuple-element.56), channel_id=1, source_target_pairs={{0,17},{1,16},{2,19},{3,18},{4,21},{5,20},{6,23},{7,22},{8,25},{9,... | collective-permute-start | bytes 98312 | tf_op jit(solution)/shard_map/ppermute | solution.py:201
  27.9 10.9 %collective-permute-start.18 = (bf16[16,1024]{1,0:T(8,128)(2,1)S(1)}, bf16[16,1024]{1,0:T(8,128)(2,1)S(1)}, u32[]{:S(2)}, u32[]{:S(2)}) collective-permute-start(bf16[16,1024]{1,0:T(8,128)(2,1)S(1)} %get-tuple-element.57), channel_id=1, source_target_pairs={{0,18},{1,19},{2,16},{3,17},{4,22},{5,23},{6,20},{7,21},{8,26},{9,... | collective-permute-start | bytes 98312 | tf_op jit(solution)/shard_map/ppermute | solution.py:201
  31.3 8.2 %collective-permute-start.19 = (bf16[16,1024]{1,0:T(8,128)(2,1)S(1)}, bf16[16,1024]{1,0:T(8,128)(2,1)S(1)}, u32[]{:S(2)}, u32[]{:S(2)}) collective-permute-start(bf16[16,1024]{1,0:T(8,128)(2,1)S(1)} %get-tuple-element.58), channel_id=1, source_target_pairs={{0,19},{1,18},{2,17},{3,16},{4,23},{5,22},{6,21},{7,20},{8,27},{9,... | collective-permute-start | bytes 98312 | tf_op jit(solution)/shard_map/ppermute | solution.py:201
  31.3 11.5 %collective-permute-start.20 = (bf16[16,1024]{1,0:T(8,128)(2,1)S(1)}, bf16[16,1024]{1,0:T(8,128)(2,1)S(1)}, u32[]{:S(2)}, u32[]{:S(2)}) collective-permute-start(bf16[16,1024]{1,0:T(8,128)(2,1)S(1)} %get-tuple-element.59), channel_id=1, source_target_pairs={{0,20},{1,21},{2,22},{3,23},{4,16},{5,17},{6,18},{7,19},{8,28},{9,... | collective-permute-start | bytes 98312 | tf_op jit(solution)/shard_map/ppermute | solution.py:201
  34.4 8.7 %collective-permute-start.21 = (bf16[16,1024]{1,0:T(8,128)(2,1)S(1)}, bf16[16,1024]{1,0:T(8,128)(2,1)S(1)}, u32[]{:S(2)}, u32[]{:S(2)}) collective-permute-start(bf16[16,1024]{1,0:T(8,128)(2,1)S(1)} %get-tuple-element.60), channel_id=1, source_target_pairs={{0,21},{1,20},{2,23},{3,22},{4,17},{5,16},{6,19},{7,18},{8,29},{9,... | collective-permute-start | bytes 98312 | tf_op jit(solution)/shard_map/ppermute | solution.py:201
  35.1 12.7 %collective-permute-start.22 = (bf16[16,1024]{1,0:T(8,128)(2,1)S(1)}, bf16[16,1024]{1,0:T(8,128)(2,1)S(1)}, u32[]{:S(2)}, u32[]{:S(2)}) collective-permute-start(bf16[16,1024]{1,0:T(8,128)(2,1)S(1)} %get-tuple-element.61), channel_id=1, source_target_pairs={{0,22},{1,23},{2,20},{3,21},{4,18},{5,19},{6,16},{7,17},{8,30},{9,... | collective-permute-start | bytes 98312 | tf_op jit(solution)/shard_map/ppermute | solution.py:201
  38.9 8.9 %collective-permute-start.23 = (bf16[16,1024]{1,0:T(8,128)(2,1)S(1)}, bf16[16,1024]{1,0:T(8,128)(2,1)S(1)}, u32[]{:S(2)}, u32[]{:S(2)}) collective-permute-start(bf16[16,1024]{1,0:T(8,128)(2,1)S(1)} %get-tuple-element.62), channel_id=1, source_target_pairs={{0,23},{1,22},{2,21},{3,20},{4,19},{5,18},{6,17},{7,16},{8,31},{9,... | collective-permute-start | bytes 98312 | tf_op jit(solution)/shard_map/ppermute | solution.py:201
  39.5 12.3 %collective-permute-start.24 = (bf16[16,1024]{1,0:T(8,128)(2,1)S(1)}, bf16[16,1024]{1,0:T(8,128)(2,1)S(1)}, u32[]{:S(2)}, u32[]{:S(2)}) collective-permute-start(bf16[16,1024]{1,0:T(8,128)(2,1)S(1)} %get-tuple-element.63), channel_id=1, source_target_pairs={{0,24},{1,25},{2,26},{3,27},{4,28},{5,29},{6,30},{7,31},{8,16},{9,... | collective-permute-start | bytes 98312 | tf_op jit(solution)/shard_map/ppermute | solution.py:201
  42.9 9.4 %collective-permute-start.25 = (bf16[16,1024]{1,0:T(8,128)(2,1)S(1)}, bf16[16,1024]{1,0:T(8,128)(2,1)S(1)}, u32[]{:S(2)}, u32[]{:S(2)}) collective-permute-start(bf16[16,1024]{1,0:T(8,128)(2,1)S(1)} %get-tuple-element.64), channel_id=1, source_target_pairs={{0,25},{1,24},{2,27},{3,26},{4,29},{5,28},{6,31},{7,30},{8,17},{9,... | collective-permute-start | bytes 98312 | tf_op jit(solution)/shard_map/ppermute | solution.py:201
  43.1 13.8 %collective-permute-start.26 = (bf16[16,1024]{1,0:T(8,128)(2,1)S(1)}, bf16[16,1024]{1,0:T(8,128)(2,1)S(1)}, u32[]{:S(2)}, u32[]{:S(2)}) collective-permute-start(bf16[16,1024]{1,0:T(8,128)(2,1)S(1)} %get-tuple-element.65), channel_id=1, source_target_pairs={{0,26},{1,27},{2,24},{3,25},{4,30},{5,31},{6,28},{7,29},{8,18},{9,... | collective-permute-start | bytes 98312 | tf_op jit(solution)/shard_map/ppermute | solution.py:201
  47.8 10.0 %collective-permute-start.27 = (bf16[16,1024]{1,0:T(8,128)(2,1)S(1)}, bf16[16,1024]{1,0:T(8,128)(2,1)S(1)}, u32[]{:S(2)}, u32[]{:S(2)}) collective-permute-start(bf16[16,1024]{1,0:T(8,128)(2,1)S(1)} %get-tuple-element.66), channel_id=1, source_target_pairs={{0,27},{1,26},{2,25},{3,24},{4,31},{5,30},{6,29},{7,28},{8,19},{9,... | collective-permute-start | bytes 98312 | tf_op jit(solution)/shard_map/ppermute | solution.py:201
  47.8 10.0 %collective-permute-start.28 = (bf16[16,1024]{1,0:T(8,128)(2,1)S(1)}, bf16[16,1024]{1,0:T(8,128)(2,1)S(1)}, u32[]{:S(2)}, u32[]{:S(2)}) collective-permute-start(bf16[16,1024]{1,0:T(8,128)(2,1)S(1)} %get-tuple-element.67), channel_id=1, source_target_pairs={{0,28},{1,29},{2,30},{3,31},{4,24},{5,25},{6,26},{7,27},{8,20},{9,... | collective-permute-start | bytes 98312 | tf_op jit(solution)/shard_map/ppermute | solution.py:201
  51.8 6.3 %collective-permute-start.29 = (bf16[16,1024]{1,0:T(8,128)(2,1)S(1)}, bf16[16,1024]{1,0:T(8,128)(2,1)S(1)}, u32[]{:S(2)}, u32[]{:S(2)}) collective-permute-start(bf16[16,1024]{1,0:T(8,128)(2,1)S(1)} %get-tuple-element.68), channel_id=1, source_target_pairs={{0,29},{1,28},{2,31},{3,30},{4,25},{5,24},{6,27},{7,26},{8,21},{9,... | collective-permute-start | bytes 98312 | tf_op jit(solution)/shard_map/ppermute | solution.py:201
  52.3 7.5 %collective-permute-start.30 = (bf16[16,1024]{1,0:T(8,128)(2,1)S(1)}, bf16[16,1024]{1,0:T(8,128)(2,1)S(1)}, u32[]{:S(2)}, u32[]{:S(2)}) collective-permute-start(bf16[16,1024]{1,0:T(8,128)(2,1)S(1)} %get-tuple-element.69), channel_id=1, source_target_pairs={{0,30},{1,31},{2,28},{3,29},{4,26},{5,27},{6,24},{7,25},{8,22},{9,... | collective-permute-start | bytes 98312 | tf_op jit(solution)/shard_map/ppermute | solution.py:201
  56.9 7.0 %collective-permute-start.31 = (bf16[16,1024]{1,0:T(8,128)(2,1)S(1)}, bf16[16,1024]{1,0:T(8,128)(2,1)S(1)}, u32[]{:S(2)}, u32[]{:S(2)}) collective-permute-start(bf16[16,1024]{1,0:T(8,128)(2,1)S(1)} %get-tuple-element.70), channel_id=1, source_target_pairs={{0,31},{1,30},{2,29},{3,28},{4,27},{5,26},{6,25},{7,24},{8,23},{9,... | collective-permute-start | bytes 98312 | tf_op jit(solution)/shard_map/ppermute | solution.py:201
  (5 other events, 14.4 us)

commit v4 on v2

v4 whole, which is shorter than its diff:
```python
import functools
import math

import jax
import jax.numpy as jnp
import numpy as np
from jax import lax
from jax.experimental import pallas as pl
from jax.experimental.pallas import tpu as pltpu
from jax.sharding import PartitionSpec as P

CH = 256
TAPS = 12
SPEC = 512
FRAME = 2 * CH
LANES = 128
SUB = 8
STEP = SPEC // SUB
STRIDE = STEP + 1
SWAP = [(0, 1), (1, 0)]
VMEM_LIMIT = 40 * 1024 * 1024


def prototype():
    count = TAPS * FRAME
    index = np.arange(count, dtype=np.float64)
    shifted = (index + 0.5) / FRAME - TAPS / 2.0
    window = 0.5 - 0.5 * np.cos(2.0 * math.pi * (index + 0.5) / count)
    return (np.sinc(shifted) * window).astype(np.float32).reshape(TAPS, FRAME)


def twiddle():
    chan = np.arange(CH, dtype=np.int64)[:, None]
    point = np.arange(FRAME, dtype=np.int64)[None, :]
    phase = (chan * point % FRAME).astype(np.float64) * (2.0 * math.pi / FRAME)
    return np.stack([np.cos(phase), -np.sin(phase)], axis=1).astype(np.float32)


def channelize_kernel(
    flags_ref, x_ref, taps_ref, table_ref, out_ref, wide, fir, spectra, *, which
):
    half = SUB
    last = lax.broadcasted_iota(jnp.int32, (SUB, LANES), 0) == SUB - 1
    for j in range(FRAME // LANES):
        cols = pl.ds(j * LANES, LANES)
        wide[j, : SPEC + TAPS - 1, :] = x_ref[which, :, cols].astype(jnp.float32)
        taps = [jnp.broadcast_to(taps_ref[pl.ds(t, 1), cols], (SUB, LANES)) for t in range(TAPS)]

        def load(b):
            return wide[j, pl.ds(b, SUB, stride=STRIDE), :]

        def total(window):
            out = taps[0] * window[0]
            for t in range(1, TAPS):
                out = out + taps[t] * window[t]
            return out

        extra = total([load(STEP + t) for t in range(TAPS)])
        window = [load(b) for b in range(TAPS - 1)]
        pair = []
        for b in range(STEP):
            window.append(load(b + TAPS - 1))
            row = total(window[b:])
            past = b - (STEP - SUB + 1)
            if past >= 0:
                row = jnp.where(last, pltpu.roll(extra, SUB - 1 - past, 0), row)
            pair.append(row)
            if len(pair) == 2:
                both = jnp.concatenate(pair, axis=0).astype(jnp.bfloat16)
                fir[pl.ds((b - 1) * SUB, 2 * SUB), cols] = both
                pair = []
    good = (1 - flags_ref[which]).astype(jnp.float32)
    spectra[...] = lax.dot_general(
        table_ref[...], fir[...], (((1,), (1,)), ((), ())), preferred_element_type=jnp.float32
    )
    for start in range(0, FRAME, 2 * half):
        real = spectra[pl.ds(start, half), :]
        imag = spectra[pl.ds(start + half, half), :]
        power = jnp.sum(real * real + imag * imag, axis=1, keepdims=True) / SPEC
        scale = good / jnp.sqrt(power + 1e-05)
        scaled = jnp.concatenate([real * scale, imag * scale], axis=0)
        out_ref[pl.ds(start, 2 * half), :] = scaled.astype(jnp.bfloat16)


def channelize(frames, flags, which):
    table = twiddle().reshape(CH // SUB, SUB, 2, FRAME).transpose(0, 2, 1, 3)
    table = jnp.asarray(table.reshape(FRAME, FRAME), dtype=jnp.bfloat16)
    taps = jnp.asarray(prototype())
    smem = pl.BlockSpec(memory_space=pltpu.SMEM)
    vmem = pl.BlockSpec(memory_space=pltpu.VMEM)
    return pl.pallas_call(
        functools.partial(channelize_kernel, which=which),
        out_shape=jax.ShapeDtypeStruct((FRAME, SPEC), jnp.bfloat16),
        in_specs=[smem, vmem, vmem, vmem],
        out_specs=vmem,
        scratch_shapes=[
            pltpu.VMEM((FRAME // LANES, SPEC + 24, LANES), jnp.float32),
            pltpu.VMEM((SPEC, FRAME), jnp.bfloat16),
            pltpu.VMEM((FRAME, SPEC), jnp.float32),
        ],
        compiler_params=pltpu.CompilerParams(vmem_limit_bytes=VMEM_LIMIT),
        cost_estimate=pl.CostEstimate(
            flops=2 * SPEC * FRAME * (FRAME + TAPS),
            bytes_accessed=4 * SPEC * FRAME,
            transcendentals=0,
        ),
    )(flags, frames, taps, table)


def correlate_kernel(first_ref, target_ref, *refs):
    arrived_refs, (own_ref, other_ref) = refs[:-2], refs[-2:]
    share, _, block, width = own_ref.shape
    parts = 2 * width
    inputs = len(arrived_refs)
    sources = arrived_refs[0].shape[0]
    first = first_ref[0] == 0
    column = lax.broadcasted_iota(jnp.int32, (parts, sources), 1)
    target = [
        jnp.broadcast_to(target_ref[:, pl.ds(i, 1)], (parts, sources)) for i in range(inputs)
    ]
    for k in range(share):
        slots = None
        for i in range(inputs):
            pick = jnp.where(column == target[i] + k, 1.0, 0.0).astype(jnp.bfloat16)
            part = jnp.dot(pick, arrived_refs[i][...], preferred_element_type=jnp.float32)
            slots = part if slots is None else slots + part
        slots = slots.astype(jnp.bfloat16)
        gram = lax.dot_general(
            slots, slots, (((1,), (1,)), ((), ())), preferred_element_type=jnp.float32
        )
        real = (gram[:width, :width] + gram[width:, width:]) / SPEC
        imag = (gram[width:, :width] - gram[:width, width:]) / SPEC
        for p, part in enumerate((real, imag)):
            own_ref[k, p] = jnp.where(first, part[:block], part[block:])
            other_ref[k, p] = jnp.where(first, part[block:], part[:block])


def correlate(arrived, orders, me, share):
    blocks, block = orders.shape
    inputs = len(arrived)
    which = jnp.arange(blocks, dtype=jnp.int32)[:, None]
    source = (orders // inputs) * blocks + which
    row = (source * 2 * share).reshape(1, blocks * block)
    part = share * jnp.arange(2, dtype=jnp.int32)[:, None]
    place = (row + part).reshape(-1, 1)
    held = jnp.tile((orders % inputs).reshape(-1), 2)[:, None]
    lane = jnp.arange(inputs, dtype=jnp.int32)[None, :]
    target = jnp.where(held == lane, place, -FRAME)
    vmem = pl.BlockSpec(memory_space=pltpu.VMEM)
    tile = jax.ShapeDtypeStruct((share, 2, block, blocks * block), jnp.float32)
    size = inputs * arrived[0].size
    return pl.pallas_call(
        correlate_kernel,
        out_shape=(tile, tile),
        in_specs=[pl.BlockSpec(memory_space=pltpu.SMEM), vmem] + [vmem] * len(arrived),
        out_specs=(vmem, vmem),
        compiler_params=pltpu.CompilerParams(vmem_limit_bytes=VMEM_LIMIT),
        cost_estimate=pl.CostEstimate(
            flops=2 * share * 128 * size, bytes_accessed=2 * size, transcendentals=0
        ),
    )(me.reshape(1), target, *arrived)


def split_channels(freq, blocks, samples, slot_order, flags):
    share = CH // (freq * blocks)
    inputs = samples.shape[0]
    me = lax.axis_index("blk").astype(jnp.int32)
    first = me == 0
    partner = lax.ppermute(slot_order, "blk", SWAP)
    orders = jnp.where(
        first,
        jnp.concatenate([slot_order, partner]),
        jnp.concatenate([partner, slot_order]),
    )
    frames = samples.reshape(inputs, SPEC + TAPS - 1, FRAME)
    arrived = []
    for i in range(inputs):
        sent = channelize(frames, flags, i)
        turned = lax.all_to_all(sent, ("freq", "blk"), split_axis=0, concat_axis=0, tiled=True)
        arrived.append(turned)
    own, other = correlate(arrived, orders, me, share)
    received = lax.ppermute(other, "blk", SWAP)
    return jnp.where(
        first,
        jnp.concatenate([own, received]),
        jnp.concatenate([received, own]),
    )


def gather_blocks(freq, samples, slot_order, flags):
    inputs = samples.shape[0]
    taps = jnp.asarray(prototype())
    table = jnp.asarray(twiddle().reshape(2 * CH, FRAME), dtype=jnp.bfloat16)
    good = (1 - flags).astype(jnp.float32)
    frames = samples.reshape(inputs, SPEC + TAPS - 1, FRAME)
    total = jnp.zeros((inputs, SPEC, FRAME), jnp.float32)
    for tap in range(TAPS):
        window = frames[:, tap : tap + SPEC, :].astype(jnp.float32)
        total = total + taps[tap][None, None, :] * window
    fir = total.astype(jnp.bfloat16)
    spectra = jnp.einsum("kn,isn->kis", table, fir, preferred_element_type=jnp.float32)
    squares = jnp.sum(spectra * spectra, axis=2)
    power = jnp.sum(squares.reshape(CH, 2, inputs), axis=1) / SPEC
    scale = good[None, :] / jnp.sqrt(power + 1e-05)
    quantized = (spectra * jnp.repeat(scale, 2, axis=0)[:, :, None]).astype(jnp.bfloat16)
    arrived = lax.all_to_all(quantized, "freq", split_axis=0, concat_axis=1, tiled=True)
    share = CH // freq
    block = slot_order.shape[1]
    own = jnp.take(arrived.reshape(share, 2, block, SPEC), slot_order[0], axis=2)
    piece = lax.all_gather(own, "blk", axis=2, tiled=True)
    dot = functools.partial(jnp.einsum, "cas,cbs->cab", preferred_element_type=jnp.float32)
    real = dot(own[:, 0], piece[:, 0]) + dot(own[:, 1], piece[:, 1])
    imag = dot(own[:, 1], piece[:, 0]) - dot(own[:, 0], piece[:, 1])
    return jnp.stack([real / SPEC, imag / SPEC], axis=1)


def solution(mesh):
    freq, blocks = mesh.shape["freq"], mesh.shape["blk"]

    def body(samples, slot_order, flags):
        if blocks == 2 and CH == SUB * freq * blocks:
            return split_channels(freq, blocks, samples, slot_order, flags)
        return gather_blocks(freq, samples, slot_order, flags)

    in_specs = (P(("blk", "freq"), None), P("blk", None), P(("blk", "freq")))
    out_specs = P("freq", None, "blk", None)
    return jax.shard_map(body, mesh=mesh, in_specs=in_specs, out_specs=out_specs, check_vma=False)
```

time: 46.5 us -> 52 us (1.12)
  starting transfers between devices: 7.69 us -> 10.8 us
  waiting for transfers between devices: 26.9 us -> 28.8 us
    all_to_all x1 -> x2, starting transfers between devices: 7.3 us -> 10.4 us  [split_channels(): lax.all_to_all(sent, ('freq', 'blk'), split_axis=0, concat_axis=0, tiled=...]
    all_to_all x1 -> x2, waiting for transfers between devices: 24.6 us -> 26.5 us  [split_channels(): lax.all_to_all(sent, ('freq', 'blk'), split_axis=0, concat_axis=0, tiled=...]
    pallas_call x1 -> x2, Pallas kernels: 5.43 us -> 5.78 us  [channelize(): pl.pallas_call(functools.partial(channelize_kernel, which=which), out_sha...]
  transfers between devices with their start and end apart: 3 -> 4, of which waited for: 3 -> 4; matrix products, arithmetic and copies ran while one was open for 1% -> 1% of each run, Pallas kernels for 0% -> 6%
where the time goes in v4:
time: 52 us; the launch traced here: 51.6 us
  waiting for transfers between devices  28.8 us (55%)
  starting transfers between devices  10.8 us (21%)
  Pallas kernels  8.57 us (16%)
  local copies, waits for them, and re-layouts  2.29 us (4%)
  other arithmetic  1.05 us (2%)
    all_to_all x2, waiting for transfers between devices, split_channels(): lax.all_to_all(sent, ('freq', 'blk'), split_axis=0, concat_axis=0, tiled=...  26.5 us
    all_to_all x2, starting transfers between devices, split_channels(): lax.all_to_all(sent, ('freq', 'blk'), split_axis=0, concat_axis=0, tiled=...  10.4 us
    pallas_call x2, Pallas kernels, channelize(): pl.pallas_call(functools.partial(channelize_kernel, which=which), out_sha...  5.78 us
    pallas_call x1, Pallas kernels, correlate(): pl.pallas_call(correlate_kernel, out_shape=(tile, tile), in_specs=[pl.Blo...  2.79 us
    reshape x1, local copies, waits for them, and re-layouts, split_channels(): frames = samples.reshape(inputs, SPEC + TAPS - 1, FRAME)  1.94 us
    ppermute x1, waiting for transfers between devices, split_channels(): received = lax.ppermute(other, 'blk', SWAP)  1.52 us
  transfers between devices with their start and end apart: 4, of which 4 were waited for; matrix products, arithmetic and copies ran while one was open for 1% of the time, Pallas kernels for 6%

profile of v4, /device:TPU:0, one launch (start us, length us, event | category | flops | bytes accessed | tf_op | source)
XLA Modules:
  0.0 51.6 jit_solution(16759450323831584241)
XLA Ops:
  0.0 0.0 copy-start.1
  0.0 0.0 copy-start
  0.0 0.0 copy-start.2
  0.0 1.9 %reshape.85.x_ref = bf16[2,523,512]{2,1,0:T(8,128)(2,1)S(1)} reshape(bf16[2,267776]{1,0:T(2,128)(2,1)} %param.7) | data formatting | bytes 2142208 | tf_op jit(solution)/shard_map/reshape | solution.py:175
  1.9 0.0 copy-done.1
  2.0 0.0 copy-done
  2.0 0.0 copy-done.2
  2.0 2.9 %shard_map.74 = bf16[512,512]{1,0:T(8,128)(2,1)} custom-call(s32[2]{0:T(128)S(1)} %copy-done.2, bf16[2,523,512]{2,1,0:T(8,128)(2,1)S(1)} %reshape.85.x_ref, f32[12,512]{1,0:T(8,128)S(1)} %copy-done.1, bf16[512,512]{1,0:T(8,128)(2,1)S(1)} %copy-done), custom_call_target="tpu_custom_call" | custom-call | flops 274726912 | bytes 1048576 | tf_op jit(solution)/shard_map/pallas_call | solution.py:91
  4.9 7.3 %all-to-all-start.1 = ((bf16[32,16,512]{2,1,0:T(8,128)(2,1)}), bf16[32,16,512]{2,1,0:T(8,128)(2,1)S(1)}, u32[]{:S(2)}, u32[]{:S(2)}) async-start(bf16[32,16,512]{2,1,0:T(8,128)(2,1)} %bitcast.3), calls=%async_computation.1 | async-start | bytes 1048576 | tf_op jit(solution)/shard_map/all_to_all | solution.py:179
  12.2 0.0 copy-start.3
  12.2 2.9 %shard_map.73 = bf16[512,512]{1,0:T(8,128)(2,1)} custom-call(s32[2]{0:T(128)S(1)} %copy-done.2, bf16[2,523,512]{2,1,0:T(8,128)(2,1)S(1)} %reshape.85.x_ref, f32[12,512]{1,0:T(8,128)S(1)} %copy-done.1, bf16[512,512]{1,0:T(8,128)(2,1)S(1)} %copy-done), custom_call_target="tpu_custom_call" | custom-call | flops 274726912 | bytes 1048576 | tf_op jit(solution)/shard_map/pallas_call | solution.py:91
  15.1 12.6 %all-to-all-done.1 = bf16[32,16,512]{2,1,0:T(8,128)(2,1)S(1)} async-done(((bf16[32,16,512]{2,1,0:T(8,128)(2,1)}), bf16[32,16,512]{2,1,0:T(8,128)(2,1)S(1)}, u32[]{:S(2)}, u32[]{:S(2)}) %all-to-all-start.1) | async-done | bytes 524320 | tf_op jit(solution)/shard_map/all_to_all | solution.py:179
  27.7 3.1 %all-to-all-start = ((bf16[32,16,512]{2,1,0:T(8,128)(2,1)}), bf16[32,16,512]{2,1,0:T(8,128)(2,1)S(1)}, u32[]{:S(2)}, u32[]{:S(2)}) async-start(bf16[32,16,512]{2,1,0:T(8,128)(2,1)} %bitcast.1), calls=%async_computation | async-start | bytes 1048576 | tf_op jit(solution)/shard_map/all_to_all | solution.py:179
  30.8 0.0 copy-done.3
  30.8 0.3 collective-permute-start
  31.1 0.1 add.51
  31.2 0.8 %collective-permute-done = s32[1,32]{1,0:T(1,128)S(1)} collective-permute-done((s32[1,32]{1,0:T(1,128)S(1)}, s32[1,32]{1,0:T(1,128)S(1)}, u32[]{:S(2)}, u32[]{:S(2)}) %collective-permute-start) | collective-permute-done | bytes 160 | tf_op jit(solution)/shard_map/ppermute | solution.py:169
  32.0 0.1 select_n.53
  32.1 0.1 eq.21
  32.2 0.1 broadcast_add_fusion
  32.3 0.1 add.56
  32.4 0.1 fusion.target_ref
  32.5 13.9 %all-to-all-done = bf16[32,16,512]{2,1,0:T(8,128)(2,1)S(1)} async-done(((bf16[32,16,512]{2,1,0:T(8,128)(2,1)}), bf16[32,16,512]{2,1,0:T(8,128)(2,1)S(1)}, u32[]{:S(2)}, u32[]{:S(2)}) %all-to-all-start) | async-done | bytes 524320 | tf_op jit(solution)/shard_map/all_to_all | solution.py:179
  46.4 2.8 %shard_map.75 = (f32[8,2,32,64]{3,2,1,0:T(8,128)S(1)}, f32[8,2,32,64]{3,2,1,0:T(8,128)S(1)}) custom-call(s32[1]{0:T(128)} %bitcast.first_ref, s32[128,2]{1,0:T(8,128)S(1)} %fusion.target_ref, bf16[512,512]{1,0:T(8,128)(2,1)S(1)} %bitcast.6, bf16[512,512]{1,0:T(8,128)(2,1)S(1)} %bitcast.5), custom_call_target="tpu_custom_call" | custom-call | flops 1073741824 | bytes 1048576 | tf_op jit(solution)/shard_map/pallas_call | solution.py:152
  49.2 0.1 collective-permute-start.1
  49.2 1.5 %collective-permute-done.1 = f32[8,2,32,64]{3,2,1,0:T(8,128)S(1)} collective-permute-done((f32[8,2,32,64]{3,2,1,0:T(8,128)S(1)}, f32[8,2,32,64]{3,2,1,0:T(8,128)S(1)}, u32[]{:S(2)}, u32[]{:S(2)}) %collective-permute-start.1) | collective-permute-done | bytes 131104 | tf_op jit(solution)/shard_map/ppermute | solution.py:182
  50.8 0.9 %maximum_select_fusion = f32[16,2,32,64]{3,2,1,0:T(8,128)} fusion(f32[8,2,32,64]{3,2,1,0:T(8,128)S(1)} %collective-permute-done.1, f32[8,2,32,64]{3,2,1,0:T(8,128)S(1)} %get-tuple-element.7, pred[]{:T(512)S(6)} %eq.20), kind=kLoop, calls=%fused_computation | loop fusion | flops 196608 | bytes 524289 | tf_op jit(solution)/shard_map/jit(_where)/select_n | solution.py:183
  (5 shorter events, 0.0 us)
Async XLA Ops:
  0.0 1.9 %copy-start.1 = (f32[12,512]{1,0:T(8,128)S(1)}, f32[12,512]{1,0:T(8,128)}, u32[]{:S(2)}) copy-start(f32[12,512]{1,0:T(8,128)} %constant.44.clone.taps_ref) | copy-start | bytes 73732
  0.0 2.0 %copy-start = (bf16[512,512]{1,0:T(8,128)(2,1)S(1)}, bf16[512,512]{1,0:T(8,128)(2,1)}, u32[]{:S(2)}) copy-start(bf16[512,512]{1,0:T(8,128)(2,1)} %constant.43.clone.table_ref) | copy-start | bytes 1572868
  0.0 2.0 %copy-start.2 = (s32[2]{0:T(128)S(1)}, s32[2]{0:T(128)}, u32[]{:S(2)}) copy-start(s32[2]{0:T(128)} %flags_ref.3) | copy-start | bytes 28
  4.9 22.9 %all-to-all-start.1 = ((bf16[32,16,512]{2,1,0:T(8,128)(2,1)}), bf16[32,16,512]{2,1,0:T(8,128)(2,1)S(1)}, u32[]{:S(2)}, u32[]{:S(2)}) async-start(bf16[32,16,512]{2,1,0:T(8,128)(2,1)} %bitcast.3), calls=%async_computation.1 | async-start | bytes 1048576 | tf_op jit(solution)/shard_map/all_to_all | solution.py:179
  12.2 18.6 %copy-start.3 = (s32[1,32]{1,0:T(1,128)S(1)}, s32[1,32]{1,0:T(1,128)}, u32[]{:S(2)}) copy-start(s32[1,32]{1,0:T(1,128)} %param.8) | copy-start | bytes 388
  27.7 18.6 %all-to-all-start = ((bf16[32,16,512]{2,1,0:T(8,128)(2,1)}), bf16[32,16,512]{2,1,0:T(8,128)(2,1)S(1)}, u32[]{:S(2)}, u32[]{:S(2)}) async-start(bf16[32,16,512]{2,1,0:T(8,128)(2,1)} %bitcast.1), calls=%async_computation | async-start | bytes 1048576 | tf_op jit(solution)/shard_map/all_to_all | solution.py:179
  30.8 1.2 %collective-permute-start = (s32[1,32]{1,0:T(1,128)S(1)}, s32[1,32]{1,0:T(1,128)S(1)}, u32[]{:S(2)}, u32[]{:S(2)}) collective-permute-start(s32[1,32]{1,0:T(1,128)S(1)} %copy-done.3), channel_id=1, source_target_pairs={{0,1},{1,0},{2,3},{3,2},{4,5},{5,4},{6,7},{7,6},{8,9},{9,8},{10,11... | collective-permute-start | bytes 392 | tf_op jit(solution)/shard_map/ppermute | solution.py:169
  49.2 1.6 %collective-permute-start.1 = (f32[8,2,32,64]{3,2,1,0:T(8,128)S(1)}, f32[8,2,32,64]{3,2,1,0:T(8,128)S(1)}, u32[]{:S(2)}, u32[]{:S(2)}) collective-permute-start(f32[8,2,32,64]{3,2,1,0:T(8,128)S(1)} %get-tuple-element.8), channel_id=1, source_target_pairs={{0,1},{1,0},{2,3},{3,2},{4,5},{5,4},{6,7},{7,6},{8,9},{9,8},{10,11... | collective-permute-start | bytes 393224 | tf_op jit(solution)/shard_map/ppermute | solution.py:182

commit v5 on v3

v5 whole, which is shorter than its diff:
```python
import functools
import math

import jax
import jax.numpy as jnp
import numpy as np
from jax import lax
from jax.experimental import pallas as pl
from jax.experimental.pallas import tpu as pltpu
from jax.sharding import Mesh
from jax.sharding import PartitionSpec as P

CH = 256
TAPS = 12
SPEC = 512
FRAME = 2 * CH
LANES = 128
SUB = 8
STEP = SPEC // SUB
STRIDE = STEP + 1
FAR = 4
SWAP = [(0, 1), (1, 0)]
VMEM_LIMIT = 40 * 1024 * 1024


def prototype():
    count = TAPS * FRAME
    index = np.arange(count, dtype=np.float64)
    shifted = (index + 0.5) / FRAME - TAPS / 2.0
    window = 0.5 - 0.5 * np.cos(2.0 * math.pi * (index + 0.5) / count)
    return (np.sinc(shifted) * window).astype(np.float32).reshape(TAPS, FRAME)


def twiddle():
    chan = np.arange(CH, dtype=np.int64)[:, None]
    point = np.arange(FRAME, dtype=np.int64)[None, :]
    phase = (chan * point % FRAME).astype(np.float64) * (2.0 * math.pi / FRAME)
    return np.stack([np.cos(phase), -np.sin(phase)], axis=1).astype(np.float32)


def channelize_kernel(
    flags_ref, x_ref, taps_ref, table_ref, out_ref, wide, fir, spectra, result, sems
):
    inputs = x_ref.shape[0]
    pieces = sems.shape[1]
    rows = FRAME // pieces
    last = lax.broadcasted_iota(jnp.int32, (SUB, LANES), 0) == SUB - 1
    copies = []
    for i in range(inputs):
        for j in range(FRAME // LANES):
            cols = pl.ds(j * LANES, LANES)
            slot = i * (FRAME // LANES) + j
            wide[slot, : SPEC + TAPS - 1, :] = x_ref[i, :, cols].astype(jnp.float32)
            taps = [
                jnp.broadcast_to(taps_ref[pl.ds(t, 1), cols], (SUB, LANES)) for t in range(TAPS)
            ]

            def load(b):
                return wide[slot, pl.ds(b, SUB, stride=STRIDE), :]

            def total(window):
                out = taps[0] * window[0]
                for t in range(1, TAPS):
                    out = out + taps[t] * window[t]
                return out

            extra = total([load(STEP + t) for t in range(TAPS)])
            window = [load(b) for b in range(TAPS - 1)]
            pair = []
            for b in range(STEP):
                window.append(load(b + TAPS - 1))
                row = total(window[b:])
                past = b - (STEP - SUB + 1)
                if past >= 0:
                    row = jnp.where(last, pltpu.roll(extra, SUB - 1 - past, 0), row)
                pair.append(row)
                if len(pair) == 2:
                    both = jnp.concatenate(pair, axis=0).astype(jnp.bfloat16)
                    fir[i, pl.ds((b - 1) * SUB, 2 * SUB), cols] = both
                    pair = []
        good = (1 - flags_ref[i]).astype(jnp.float32)
        spectra[i] = lax.dot_general(
            table_ref[...], fir[i], (((1,), (1,)), ((), ())), preferred_element_type=jnp.float32
        )
        for piece in range(pieces):
            place = (pl.ds(piece * rows, rows), pl.ds(i * SPEC, SPEC))
            pairs = spectra[i, pl.ds(piece * rows, rows), :]
            pairs = pairs.reshape(rows // (2 * SUB), 2, SUB, SPEC)
            squares = jnp.sum(pairs * pairs, axis=1)
            power = jnp.sum(squares, axis=2, keepdims=True) / SPEC
            scale = good / jnp.sqrt(power + 1e-05)
            scaled = (pairs * scale[:, None]).astype(jnp.bfloat16)
            result[place] = scaled.reshape(rows, SPEC)
            copy = pltpu.make_async_copy(result.at[place], out_ref.at[place], sems.at[i, piece])
            copy.start()
            copies.append(copy)
    for copy in copies:
        copy.wait()


def channelize(samples, flags, far, near, blocks):
    inputs = samples.shape[0]
    frames = samples.reshape(inputs, SPEC + TAPS - 1, FRAME)
    table = twiddle().reshape(far, near, blocks, SUB, 2, FRAME).transpose(2, 1, 0, 4, 3, 5)
    table = jnp.asarray(table.reshape(FRAME, FRAME), dtype=jnp.bfloat16)
    taps = jnp.asarray(prototype())
    smem = pl.BlockSpec(memory_space=pltpu.SMEM)
    vmem = pl.BlockSpec(memory_space=pltpu.VMEM)
    return pl.pallas_call(
        channelize_kernel,
        out_shape=jax.ShapeDtypeStruct((FRAME, inputs * SPEC), jnp.bfloat16),
        in_specs=[smem, vmem, vmem, vmem],
        out_specs=pl.BlockSpec(memory_space=pl.ANY),
        scratch_shapes=[
            pltpu.VMEM((inputs * FRAME // LANES, SPEC + 24, LANES), jnp.float32),
            pltpu.VMEM((inputs, SPEC, FRAME), jnp.bfloat16),
            pltpu.VMEM((inputs, FRAME, SPEC), jnp.float32),
            pltpu.VMEM((FRAME, inputs * SPEC), jnp.bfloat16),
            pltpu.SemaphoreType.DMA((inputs, 8)),
        ],
        compiler_params=pltpu.CompilerParams(vmem_limit_bytes=VMEM_LIMIT),
        cost_estimate=pl.CostEstimate(
            flops=2 * inputs * SPEC * FRAME * (FRAME + TAPS),
            bytes_accessed=4 * inputs * SPEC * FRAME,
            transcendentals=0,
        ),
    )(flags, frames, taps, table)


def correlate_kernel(first_ref, pick_ref, arrived_ref, own_ref, other_ref, slots):
    share, _, block, width = own_ref.shape
    blocks = pick_ref.shape[0]
    held = arrived_ref.shape[0] // blocks
    first = first_ref[0] == 0
    for n in range(blocks):
        rows = pl.ds(n * held, held)
        stacked = jnp.concatenate(
            [
                arrived_ref[rows, pl.ds(i * SPEC, SPEC)]
                for i in range(arrived_ref.shape[1] // SPEC)
            ],
            axis=0,
        )
        slots[n] = jnp.dot(
            pick_ref[n], stacked, preferred_element_type=jnp.float32
        ).astype(jnp.bfloat16)
    for k in range(share):
        pair = jnp.concatenate(
            [
                slots[n, pl.ds((2 * k + p) * block, block), :]
                for p in range(2)
                for n in range(blocks)
            ],
            axis=0,
        )
        gram = lax.dot_general(
            pair, pair, (((1,), (1,)), ((), ())), preferred_element_type=jnp.float32
        )
        real = (gram[:width, :width] + gram[width:, width:]) / SPEC
        imag = (gram[width:, :width] - gram[:width, width:]) / SPEC
        for p, part in enumerate((real, imag)):
            own_ref[k, p] = jnp.where(first, part[:block], part[block:])
            other_ref[k, p] = jnp.where(first, part[block:], part[:block])


def picks(orders, inputs, far, near, share):
    blocks, block = orders.shape
    device, held = orders // inputs, orders % inputs
    place = (device % near) * far + device // near
    start = ((held * far * near + place) * 2 * share)[:, None, None, :]
    chan = jnp.arange(share, dtype=jnp.int32)[:, None, None]
    part = jnp.arange(2, dtype=jnp.int32)[:, None]
    target = (start + part * share + chan).reshape(blocks, share * 2 * block, 1)
    column = lax.broadcasted_iota(jnp.int32, (1, 1, inputs * far * near * 2 * share), 2)
    return (column == target).astype(jnp.bfloat16)


def correlate(arrived, pick, me, share, block):
    blocks = pick.shape[0]
    smem = pl.BlockSpec(memory_space=pltpu.SMEM)
    vmem = pl.BlockSpec(memory_space=pltpu.VMEM)
    tile = jax.ShapeDtypeStruct((share, 2, block, blocks * block), jnp.float32)
    return pl.pallas_call(
        correlate_kernel,
        out_shape=(tile, tile),
        in_specs=[smem, vmem, vmem],
        out_specs=(vmem, vmem),
        scratch_shapes=[pltpu.VMEM((blocks, share * 2 * block, SPEC), jnp.bfloat16)],
        compiler_params=pltpu.CompilerParams(vmem_limit_bytes=VMEM_LIMIT),
        cost_estimate=pl.CostEstimate(
            flops=2 * pick.size * SPEC, bytes_accessed=4 * arrived.size, transcendentals=0
        ),
    )(me.reshape(1), pick, arrived)


def place_kernel(me_ref, own_ref, out_ref, sem):
    share = own_ref.shape[0]
    copy = pltpu.make_async_copy(own_ref, out_ref.at[pl.ds(me_ref[0] * share, share)], sem)
    copy.start()
    copy.wait()


def place_own(own, me, blocks):
    share = own.shape[0]
    return pl.pallas_call(
        place_kernel,
        out_shape=jax.ShapeDtypeStruct((blocks * share, *own.shape[1:]), own.dtype),
        in_specs=[
            pl.BlockSpec(memory_space=pltpu.SMEM),
            pl.BlockSpec(memory_space=pltpu.VMEM),
        ],
        out_specs=pl.BlockSpec(memory_space=pl.ANY),
        scratch_shapes=[pltpu.SemaphoreType.DMA],
        cost_estimate=pl.CostEstimate(flops=0, bytes_accessed=4 * own.size, transcendentals=0),
    )(me.reshape(1), own)


def split_channels(far, near, blocks, samples, slot_order, flags):
    share = CH // (far * near * blocks)
    inputs, block = samples.shape[0], slot_order.shape[1]
    axes = ("blk", "near", "far")
    me = lax.axis_index("blk").astype(jnp.int32)
    partner = lax.ppermute(slot_order, "blk", SWAP)
    orders = jnp.where(
        me == 0,
        jnp.concatenate([slot_order, partner]),
        jnp.concatenate([partner, slot_order]),
    )
    sent = channelize(samples, flags, far, near, blocks)
    arrived = lax.all_to_all(sent, axes, split_axis=0, concat_axis=0, tiled=True)
    pick = picks(orders, inputs, far, near, share)
    own, other = correlate(arrived, pick, me, share, block)
    received = lax.ppermute(other, "blk", SWAP)
    out = place_own(own, me, blocks)
    return lax.dynamic_update_slice(out, received, ((1 - me) * share, 0, 0, 0))


def gather_blocks(freq, samples, slot_order, flags):
    inputs = samples.shape[0]
    taps = jnp.asarray(prototype())
    table = jnp.asarray(twiddle().reshape(2 * CH, FRAME), dtype=jnp.bfloat16)
    good = (1 - flags).astype(jnp.float32)
    frames = samples.reshape(inputs, SPEC + TAPS - 1, FRAME)
    total = jnp.zeros((inputs, SPEC, FRAME), jnp.float32)
    for tap in range(TAPS):
        window = frames[:, tap : tap + SPEC, :].astype(jnp.float32)
        total = total + taps[tap][None, None, :] * window
    fir = total.astype(jnp.bfloat16)
    spectra = jnp.einsum("kn,isn->kis", table, fir, preferred_element_type=jnp.float32)
    squares = jnp.sum(spectra * spectra, axis=2)
    power = jnp.sum(squares.reshape(CH, 2, inputs), axis=1) / SPEC
    scale = good[None, :] / jnp.sqrt(power + 1e-05)
    quantized = (spectra * jnp.repeat(scale, 2, axis=0)[:, :, None]).astype(jnp.bfloat16)
    arrived = lax.all_to_all(quantized, ("far", "near"), split_axis=0, concat_axis=1, tiled=True)
    share = CH // freq
    block = slot_order.shape[1]
    own = jnp.take(arrived.reshape(share, 2, block, SPEC), slot_order[0], axis=2)
    piece = lax.all_gather(own, "blk", axis=2, tiled=True)
    dot = functools.partial(jnp.einsum, "cas,cbs->cab", preferred_element_type=jnp.float32)
    real = dot(own[:, 0], piece[:, 0]) + dot(own[:, 1], piece[:, 1])
    imag = dot(own[:, 1], piece[:, 0]) - dot(own[:, 0], piece[:, 1])
    return jnp.stack([real / SPEC, imag / SPEC], axis=1)


def solution(mesh):
    freq, blocks = mesh.shape["freq"], mesh.shape["blk"]
    far = math.gcd(freq, FAR)
    near = freq // far
    split = Mesh(mesh.devices.reshape(far, near, blocks), ("far", "near", "blk"))

    def body(samples, slot_order, flags):
        if blocks == 2 and CH == SUB * freq * blocks:
            return split_channels(far, near, blocks, samples, slot_order, flags)
        return gather_blocks(freq, samples, slot_order, flags)

    held = ("blk", "far", "near")
    in_specs = (P(held, None), P("blk", None), P(held))
    out_specs = P(("far", "near"), None, "blk", None)
    return jax.shard_map(body, mesh=split, in_specs=in_specs, out_specs=out_specs, check_vma=False)
```

time: 69.3 us -> 45 us (0.65)
  starting transfers between devices: 51.8 us -> 7.62 us
  waiting for transfers between devices: 7.34 us -> 25.9 us
  local copies, waits for them, and re-layouts: 2.29 us -> 3.57 us
    ppermute x31 -> x0, starting transfers between devices: 51.2 us -> none  [split_channels(): arrived[m] = lax.ppermute(part, axes, pairs) if m else part]
    all_to_all x0 -> x1, waiting for transfers between devices: none -> 25.1 us  [split_channels(): lax.all_to_all(sent, axes, split_axis=0, concat_axis=0, tiled=True)]
    all_to_all x0 -> x1, starting transfers between devices: none -> 7.3 us  [split_channels(): lax.all_to_all(sent, axes, split_axis=0, concat_axis=0, tiled=True)]
    ppermute x31 -> x0, waiting for transfers between devices: 6.14 us -> none  [split_channels(): arrived[m] = lax.ppermute(part, axes, pairs) if m else part]
    ppermute x1, waiting for transfers between devices: 1.19 us -> 0.01 us  [split_channels(): received = lax.ppermute(other, 'blk', SWAP)]
    select_n x4 -> x0, other arithmetic: 0.97 us -> none  [the longest x1 0.85 us: split_channels(): jnp.where(first, jnp.concatenate([own, received]), jnp.concatenate([recei...]
    ppermute x1, waiting for transfers between devices: 0.01 us -> 0.77 us  [split_channels(): partner = lax.ppermute(slot_order, 'blk', SWAP)]
    dynamic_update_slice x0 -> x1, local copies, waits for them, and re-layouts: none -> 0.73 us  [split_channels(): return lax.dynamic_update_slice(out, received, ((1 - me) * share, 0, 0, 0))]
  transfers between devices with their start and end apart: 33 -> 3, of which waited for: 4 -> 2; matrix products, arithmetic and copies ran while one was open for 1% -> 1% of each run, Pallas kernels for 0% -> 4%
where the time goes in v5:
time: 45 us; the launch traced here: 44.7 us
  waiting for transfers between devices  25.9 us (58%)
  starting transfers between devices  7.62 us (17%)
  Pallas kernels  7.16 us (16%)
  local copies, waits for them, and re-layouts  3.57 us (8%)
    all_to_all x1, waiting for transfers between devices, split_channels(): lax.all_to_all(sent, axes, split_axis=0, concat_axis=0, tiled=True)  25.1 us
    all_to_all x1, starting transfers between devices, split_channels(): lax.all_to_all(sent, axes, split_axis=0, concat_axis=0, tiled=True)  7.3 us
    pallas_call x1, Pallas kernels, channelize(): pl.pallas_call(channelize_kernel, out_shape=jax.ShapeDtypeStruct((FRAME,...  4.41 us
    reshape x1, local copies, waits for them, and re-layouts, channelize(): frames = samples.reshape(inputs, SPEC + TAPS - 1, FRAME)  1.94 us
    pallas_call x1, Pallas kernels, place_own(): pl.pallas_call(place_kernel, out_shape=jax.ShapeDtypeStruct((blocks * sha...  1.66 us
    pallas_call x1, Pallas kernels, correlate(): pl.pallas_call(correlate_kernel, out_shape=(tile, tile), in_specs=[smem,...  1.09 us
  transfers between devices with their start and end apart: 3, of which 2 were waited for; matrix products, arithmetic and copies ran while one was open for 1% of the time, Pallas kernels for 4%

profile of v5, /device:TPU:0, one launch (start us, length us, event | category | flops | bytes accessed | tf_op | source)
XLA Modules:
  0.0 44.7 jit_solution(7556307233048675016)
XLA Ops:
  0.0 0.0 copy-start
  0.0 0.0 copy-start.2
  0.0 0.0 copy-start.3
  0.0 1.9 %reshape.123.x_ref = bf16[2,523,512]{2,1,0:T(8,128)(2,1)S(1)} reshape(bf16[2,267776]{1,0:T(2,128)(2,1)} %param.5) | data formatting | bytes 2142208 | tf_op jit(solution)/shard_map/reshape | solution.py:103
  1.9 0.0 copy-done
  2.0 0.0 copy-done.2
  2.0 0.0 copy-done.3
  2.0 4.4 %shard_map.55 = bf16[512,1024]{1,0:T(8,128)(2,1)} custom-call(s32[2]{0:T(128)S(1)} %copy-done.3, bf16[2,523,512]{2,1,0:T(8,128)(2,1)S(1)} %reshape.123.x_ref, f32[12,512]{1,0:T(8,128)S(1)} %copy-done.2, bf16[512,512]{1,0:T(8,128)(2,1)S(1)} %copy-done), custom_call_target="tpu_custom_call" | custom-call | flops 549453824 | bytes 2097152 | tf_op jit(solution)/shard_map/pallas_call | solution.py:109
  6.4 0.0 copy-start.4
  6.4 7.3 %all-to-all-start = ((bf16[32,16,1024]{2,1,0:T(8,128)(2,1)}), bf16[32,16,1024]{2,1,0:T(8,128)(2,1)S(1)}, u32[]{:S(2)}, u32[]{:S(2)}) async-start(bf16[32,16,1024]{2,1,0:T(8,128)(2,1)} %bitcast.1), calls=%async_computation | async-start | bytes 2097152 | tf_op jit(solution)/shard_map/all_to_all | solution.py:230
  13.7 0.0 copy-done.4
  13.7 0.3 collective-permute-start
  14.1 0.1 add.96
  14.1 0.8 %collective-permute-done = s32[1,32]{1,0:T(1,128)S(1)} collective-permute-done((s32[1,32]{1,0:T(1,128)S(1)}, s32[1,32]{1,0:T(1,128)S(1)}, u32[]{:S(2)}, u32[]{:S(2)}) %collective-permute-start) | collective-permute-done | bytes 160 | tf_op jit(solution)/shard_map/ppermute | solution.py:223
  14.9 0.1 broadcast_add_fusion.1
  15.0 0.1 add.94
  15.1 0.2 fusion.pick_ref
  15.4 25.1 %all-to-all-done = bf16[32,16,1024]{2,1,0:T(8,128)(2,1)S(1)} async-done(((bf16[32,16,1024]{2,1,0:T(8,128)(2,1)}), bf16[32,16,1024]{2,1,0:T(8,128)(2,1)S(1)}, u32[]{:S(2)}, u32[]{:S(2)}) %all-to-all-start) | async-done | bytes 1048608 | tf_op jit(solution)/shard_map/all_to_all | solution.py:230
  40.5 1.1 %shard_map.56 = (f32[8,2,32,64]{3,2,1,0:T(8,128)S(1)}, f32[8,2,32,64]{3,2,1,0:T(8,128)S(1)}) custom-call(s32[1]{0:T(128)} %bitcast.first_ref.me_ref, bf16[2,512,512]{2,1,0:T(8,128)(2,1)S(1)} %fusion.pick_ref, bf16[512,1024]{1,0:T(8,128)(2,1)S(1)} %bitcast.3), custom_call_target="tpu_custom_call" | custom-call | flops 536870912 | bytes 2097152 | tf_op jit(solution)/shard_map/pallas_call | solution.py:183
  41.6 0.0 copy-start.1
  41.6 0.7 %copy-done.1 = f32[8,2,32,64]{3,2,1,0:T(8,128)} copy-done((f32[8,2,32,64]{3,2,1,0:T(8,128)}, f32[8,2,32,64]{3,2,1,0:T(8,128)S(1)}, u32[]{:S(2)}) %copy-start.1) | copy-done | bytes 131096
  42.3 0.0 collective-permute-start.1
  42.3 1.7 %shard_map.57 = f32[16,2,32,64]{3,2,1,0:T(8,128)} custom-call(s32[1]{0:T(128)} %bitcast.first_ref.me_ref, f32[8,2,32,64]{3,2,1,0:T(8,128)} %copy-done.1), custom_call_target="tpu_custom_call" | custom-call | bytes 131072 | tf_op jit(solution)/shard_map/pallas_call | solution.py:205
  44.0 0.0 collective-permute-done.1
  44.0 0.7 %constant_dynamic-update-slice_fusion = f32[16,2,32,64]{3,2,1,0:T(8,128)} fusion(f32[16,2,32,64]{3,2,1,0:T(8,128)} %shard_map.57, f32[8,2,32,64]{3,2,1,0:T(8,128)S(1)} %collective-permute-done.1, s32[]{:T(128)S(6)} %select_n.56), kind=kLoop, calls=%fused_computation.21 | loop fusion | bytes 393220 | tf_op jit(solution)/shard_map/dynamic_update_slice | solution.py:235
  (5 shorter events, 0.1 us)
Async XLA Ops:
  0.0 1.9 %copy-start = (bf16[512,512]{1,0:T(8,128)(2,1)S(1)}, bf16[512,512]{1,0:T(8,128)(2,1)}, u32[]{:S(2)}) copy-start(bf16[512,512]{1,0:T(8,128)(2,1)} %constant.65.clone.table_ref) | copy-start | bytes 1572868
  0.0 2.0 %copy-start.2 = (f32[12,512]{1,0:T(8,128)S(1)}, f32[12,512]{1,0:T(8,128)}, u32[]{:S(2)}) copy-start(f32[12,512]{1,0:T(8,128)} %constant.66.clone.taps_ref) | copy-start | bytes 73732
  0.0 2.0 %copy-start.3 = (s32[2]{0:T(128)S(1)}, s32[2]{0:T(128)}, u32[]{:S(2)}) copy-start(s32[2]{0:T(128)} %flags_ref.1) | copy-start | bytes 28
  6.4 7.3 %copy-start.4 = (s32[1,32]{1,0:T(1,128)S(1)}, s32[1,32]{1,0:T(1,128)}, u32[]{:S(2)}) copy-start(s32[1,32]{1,0:T(1,128)} %param.6) | copy-start | bytes 388
  6.4 34.1 %all-to-all-start = ((bf16[32,16,1024]{2,1,0:T(8,128)(2,1)}), bf16[32,16,1024]{2,1,0:T(8,128)(2,1)S(1)}, u32[]{:S(2)}, u32[]{:S(2)}) async-start(bf16[32,16,1024]{2,1,0:T(8,128)(2,1)} %bitcast.1), calls=%async_computation | async-start | bytes 2097152 | tf_op jit(solution)/shard_map/all_to_all | solution.py:230
  13.7 1.2 %collective-permute-start = (s32[1,32]{1,0:T(1,128)S(1)}, s32[1,32]{1,0:T(1,128)S(1)}, u32[]{:S(2)}, u32[]{:S(2)}) collective-permute-start(s32[1,32]{1,0:T(1,128)S(1)} %copy-done.4), channel_id=1, source_target_pairs={{0,1},{1,0},{2,3},{3,2},{4,5},{5,4},{6,7},{7,6},{8,9},{9,8},{10,11... | collective-permute-start | bytes 392 | tf_op jit(solution)/shard_map/ppermute | solution.py:223
  41.6 0.7 %copy-start.1 = (f32[8,2,32,64]{3,2,1,0:T(8,128)}, f32[8,2,32,64]{3,2,1,0:T(8,128)S(1)}, u32[]{:S(2)}) copy-start(f32[8,2,32,64]{3,2,1,0:T(8,128)S(1)} %get-tuple-element.7.own_ref) | copy-start | bytes 393220
  42.3 1.7 %collective-permute-start.1 = (f32[8,2,32,64]{3,2,1,0:T(8,128)S(1)}, f32[8,2,32,64]{3,2,1,0:T(8,128)S(1)}, u32[]{:S(2)}, u32[]{:S(2)}) collective-permute-start(f32[8,2,32,64]{3,2,1,0:T(8,128)S(1)} %get-tuple-element.8), channel_id=1, source_target_pairs={{0,1},{1,0},{2,3},{3,2},{4,5},{5,4},{6,7},{7,6},{8,9},{9,8},{10,11... | collective-permute-start | bytes 393224 | tf_op jit(solution)/shard_map/ppermute | solution.py:233

commit v6 on v5

--- a/solution.py
+++ b/solution.py
@@ -16,7 +16,8 @@
 FRAME = 2 * CH
 LANES = 128
 SUB = 8
-STEP = SPEC // SUB
+GROUP = 128
+STEP = GROUP // SUB
 STRIDE = STEP + 1
 FAR = 4
 SWAP = [(0, 1), (1, 0)]
@@ -39,49 +40,67 @@
 
 
 def channelize_kernel(
-    flags_ref, x_ref, taps_ref, table_ref, out_ref, wide, fir, spectra, result, sems
+    flags_ref, x_ref, taps_ref, table_ref, out_ref, held, wide, fir, spectra, result, in_sems, sems
 ):
-    inputs = x_ref.shape[0]
+    inputs = held.shape[0]
+    frames = SPEC + TAPS - 1
     pieces = sems.shape[1]
     rows = FRAME // pieces
     last = lax.broadcasted_iota(jnp.int32, (SUB, LANES), 0) == SUB - 1
-    copies = []
-    for i in range(inputs):
-        for j in range(FRAME // LANES):
-            cols = pl.ds(j * LANES, LANES)
-            slot = i * (FRAME // LANES) + j
-            wide[slot, : SPEC + TAPS - 1, :] = x_ref[i, :, cols].astype(jnp.float32)
-            taps = [
-                jnp.broadcast_to(taps_ref[pl.ds(t, 1), cols], (SUB, LANES)) for t in range(TAPS)
-            ]
-
-            def load(b):
-                return wide[slot, pl.ds(b, SUB, stride=STRIDE), :]
-
-            def total(window):
-                out = taps[0] * window[0]
-                for t in range(1, TAPS):
-                    out = out + taps[t] * window[t]
-                return out
-
-            extra = total([load(STEP + t) for t in range(TAPS)])
-            window = [load(b) for b in range(TAPS - 1)]
+    edges = [0] + [g * GROUP + TAPS - 1 for g in range(1, SPEC // GROUP)] + [frames]
+    loads = []
+    for g, (begin, end) in enumerate(zip(edges, edges[1:])):
+        part = (slice(None), pl.ds(begin * FRAME, (end - begin) * FRAME))
+        load = pltpu.make_async_copy(x_ref.at[part], held.at[part], in_sems.at[g])
+        load.start()
+        loads.append(load)
+
+    def convert(g):
+        for f in range(edges[g], edges[g + 1]):
+            for j in range(FRAME // LANES):
+                tile = held[:, pl.ds(f * FRAME + j * LANES, LANES)]
+                wide[j, pl.ds(inputs * f, inputs), :] = tile.astype(jnp.float32)
+
+    def filter_group(g, i, j):
+        cols = pl.ds(j * LANES, LANES)
+        taps = [jnp.broadcast_to(taps_ref[pl.ds(t, 1), cols], (SUB, LANES)) for t in range(TAPS)]
+
+        def take(b):
+            first = inputs * (g * GROUP + b) + i
+            return wide[j, pl.ds(first, SUB, stride=inputs * STRIDE), :]
+
+        def total(window):
+            out = taps[0] * window[0]
+            for t in range(1, TAPS):
+                out = out + taps[t] * window[t]
+            return out
+
+        window = [take(b) for b in range(STEP + TAPS)]
+        extra = total(window[STEP:])
+        for b in range(0, STEP, 2):
             pair = []
-            for b in range(STEP):
-                window.append(load(b + TAPS - 1))
-                row = total(window[b:])
-                past = b - (STEP - SUB + 1)
+            for c in (b, b + 1):
+                row = total(window[c:])
+                past = c - (STEP - SUB + 1)
                 if past >= 0:
                     row = jnp.where(last, pltpu.roll(extra, SUB - 1 - past, 0), row)
                 pair.append(row)
-                if len(pair) == 2:
-                    both = jnp.concatenate(pair, axis=0).astype(jnp.bfloat16)
-                    fir[i, pl.ds((b - 1) * SUB, 2 * SUB), cols] = both
-                    pair = []
-        good = (1 - flags_ref[i]).astype(jnp.float32)
+            both = jnp.concatenate(pair, axis=0).astype(jnp.bfloat16)
+            fir[i, pl.ds(g * GROUP + b * SUB, 2 * SUB), cols] = both
+
+    for g in range(SPEC // GROUP):
+        loads[g].wait()
+        convert(g)
+        for i in range(inputs):
+            for j in range(FRAME // LANES):
+                filter_group(g, i, j)
+    copies = []
+    for i in range(inputs):
         spectra[i] = lax.dot_general(
             table_ref[...], fir[i], (((1,), (1,)), ((), ())), preferred_element_type=jnp.float32
         )
+    for i in range(inputs):
+        good = (1 - flags_ref[i]).astype(jnp.float32)
         for piece in range(pieces):
             place = (pl.ds(piece * rows, rows), pl.ds(i * SPEC, SPEC))
             pairs = spectra[i, pl.ds(piece * rows, rows), :]
@@ -100,7 +119,6 @@
 
 def channelize(samples, flags, far, near, blocks):
     inputs = samples.shape[0]
-    frames = samples.reshape(inputs, SPEC + TAPS - 1, FRAME)
     table = twiddle().reshape(far, near, blocks, SUB, 2, FRAME).transpose(2, 1, 0, 4, 3, 5)
     table = jnp.asarray(table.reshape(FRAME, FRAME), dtype=jnp.bfloat16)
     taps = jnp.asarray(prototype())
@@ -109,13 +127,15 @@
     return pl.pallas_call(
         channelize_kernel,
         out_shape=jax.ShapeDtypeStruct((FRAME, inputs * SPEC), jnp.bfloat16),
-        in_specs=[smem, vmem, vmem, vmem],
+        in_specs=[smem, pl.BlockSpec(memory_space=pltpu.HBM), vmem, vmem],
         out_specs=pl.BlockSpec(memory_space=pl.ANY),
         scratch_shapes=[
-            pltpu.VMEM((inputs * FRAME // LANES, SPEC + 24, LANES), jnp.float32),
+            pltpu.VMEM(samples.shape, jnp.bfloat16),
+            pltpu.VMEM((FRAME // LANES, inputs * (SPEC + 24), LANES), jnp.float32),
             pltpu.VMEM((inputs, SPEC, FRAME), jnp.bfloat16),
             pltpu.VMEM((inputs, FRAME, SPEC), jnp.float32),
             pltpu.VMEM((FRAME, inputs * SPEC), jnp.bfloat16),
+            pltpu.SemaphoreType.DMA((SPEC // GROUP,)),
             pltpu.SemaphoreType.DMA((inputs, 8)),
         ],
         compiler_params=pltpu.CompilerParams(vmem_limit_bytes=VMEM_LIMIT),
@@ -124,14 +144,17 @@
             bytes_accessed=4 * inputs * SPEC * FRAME,
             transcendentals=0,
         ),
-    )(flags, frames, taps, table)
+    )(flags, samples, taps, table)
 
 
 def correlate_kernel(first_ref, pick_ref, arrived_ref, own_ref, other_ref, slots):
-    share, _, block, width = own_ref.shape
+    share, block, _ = own_ref.shape
     blocks = pick_ref.shape[0]
+    width = blocks * block
     held = arrived_ref.shape[0] // blocks
     first = first_ref[0] == 0
+    lane = lax.broadcasted_iota(jnp.int32, (width, 2 * width), 1)
+    sign = jnp.where(lane < width, 1.0 / SPEC, -1.0 / SPEC)
     for n in range(blocks):
         rows = pl.ds(n * held, held)
         stacked = jnp.concatenate(
@@ -156,11 +179,9 @@
         gram = lax.dot_general(
             pair, pair, (((1,), (1,)), ((), ())), preferred_element_type=jnp.float32
         )
-        real = (gram[:width, :width] + gram[width:, width:]) / SPEC
-        imag = (gram[width:, :width] - gram[:width, width:]) / SPEC
-        for p, part in enumerate((real, imag)):
-            own_ref[k, p] = jnp.where(first, part[:block], part[block:])
-            other_ref[k, p] = jnp.where(first, part[block:], part[:block])
+        part = gram[:width] * sign + pltpu.roll(gram[width:], width, 1) / SPEC
+        own_ref[k] = jnp.where(first, part[:block], part[block:])
+        other_ref[k] = jnp.where(first, part[block:], part[:block])
 
 
 def picks(orders, inputs, far, near, share):
@@ -179,7 +200,7 @@
     blocks = pick.shape[0]
     smem = pl.BlockSpec(memory_space=pltpu.SMEM)
     vmem = pl.BlockSpec(memory_space=pltpu.VMEM)
-    tile = jax.ShapeDtypeStruct((share, 2, block, blocks * block), jnp.float32)
+    tile = jax.ShapeDtypeStruct((share, block, 2 * blocks * block), jnp.float32)
     return pl.pallas_call(
         correlate_kernel,
         out_shape=(tile, tile),
@@ -193,26 +214,41 @@
     )(me.reshape(1), pick, arrived)
 
 
-def place_kernel(me_ref, own_ref, out_ref, sem):
-    share = own_ref.shape[0]
-    copy = pltpu.make_async_copy(own_ref, out_ref.at[pl.ds(me_ref[0] * share, share)], sem)
-    copy.start()
-    copy.wait()
-
-
-def place_own(own, me, blocks):
-    share = own.shape[0]
+def place_kernel(index_ref, packed_ref, *refs):
+    out_ref, parts, sems = refs[-3:]
+    share, _, _, width = parts.shape
+    copies = []
+    for k in range(share):
+        parts[k, 0] = packed_ref[k, :, :width]
+        parts[k, 1] = packed_ref[k, :, width:]
+        where = index_ref[0] * share + k
+        copies.append(pltpu.make_async_copy(parts.at[k], out_ref.at[where], sems.at[k]))
+        copies[-1].start()
+    for copy in copies:
+        copy.wait()
+
+
+def place(packed, index, blocks, base=None):
+    share, block, lanes = packed.shape
+    width = lanes // 2
+    anywhere = pl.BlockSpec(memory_space=pl.ANY)
     return pl.pallas_call(
         place_kernel,
-        out_shape=jax.ShapeDtypeStruct((blocks * share, *own.shape[1:]), own.dtype),
+        out_shape=jax.ShapeDtypeStruct((blocks * share, 2, block, width), packed.dtype),
         in_specs=[
             pl.BlockSpec(memory_space=pltpu.SMEM),
             pl.BlockSpec(memory_space=pltpu.VMEM),
+        ]
+        + ([] if base is None else [anywhere]),
+        out_specs=anywhere,
+        scratch_shapes=[
+            pltpu.VMEM((share, 2, block, width), packed.dtype),
+            pltpu.SemaphoreType.DMA((share,)),
         ],
-        out_specs=pl.BlockSpec(memory_space=pl.ANY),
-        scratch_shapes=[pltpu.SemaphoreType.DMA],
-        cost_estimate=pl.CostEstimate(flops=0, bytes_accessed=4 * own.size, transcendentals=0),
-    )(me.reshape(1), own)
+        input_output_aliases={} if base is None else {2: 0},
+        compiler_params=pltpu.CompilerParams(vmem_limit_bytes=VMEM_LIMIT),
+        cost_estimate=pl.CostEstimate(flops=0, bytes_accessed=8 * packed.size, transcendentals=0),
+    )(index.reshape(1), packed, *([] if base is None else [base]))
 
 
 def split_channels(far, near, blocks, samples, slot_order, flags):
@@ -231,8 +267,7 @@
     pick = picks(orders, inputs, far, near, share)
     own, other = correlate(arrived, pick, me, share, block)
     received = lax.ppermute(other, "blk", SWAP)
-    out = place_own(own, me, blocks)
-    return lax.dynamic_update_slice(out, received, ((1 - me) * share, 0, 0, 0))
+    return place(received, 1 - me, blocks, place(own, me, blocks))
 
 
 def gather_blocks(freq, samples, slot_order, flags):

time: 45 us -> 46.4 us (1.031)
  waiting for transfers between devices: 25.9 us -> 26.4 us
  Pallas kernels: 7.16 us -> 7.63 us
    unnamed x10, local copies, waits for them, and re-layouts: 0.71 us -> 3.69 us
    reshape x1 -> x0, local copies, waits for them, and re-layouts: 1.94 us -> none  [channelize(): frames = samples.reshape(inputs, SPEC + TAPS - 1, FRAME)]
    dynamic_update_slice x1 -> x0, local copies, waits for them, and re-layouts: 0.73 us -> none  [split_channels(): return lax.dynamic_update_slice(out, received, ((1 - me) * share, 0, 0, 0))]
    ppermute x1, waiting for transfers between devices: 0.01 us -> 0.49 us  [split_channels(): received = lax.ppermute(other, 'blk', SWAP)]
    pallas_call x1 -> x2, Pallas kernels: 1.66 us -> 1.66 us  [place(): pl.pallas_call(place_kernel, out_shape=jax.ShapeDtypeStruct((blocks * sha...]
  transfers between devices with their start and end apart: 3 -> 3, of which waited for: 2 -> 3; matrix products, arithmetic and copies ran while one was open for 1% -> 1% of each run, Pallas kernels for 4% -> 2%
where the time goes in v6:
time: 46.4 us; the launch traced here: 46 us
  waiting for transfers between devices  26.4 us (57%)
  starting transfers between devices  7.69 us (17%)
  Pallas kernels  7.63 us (16%)
  local copies, waits for them, and re-layouts  3.89 us (8%)
    all_to_all x1, waiting for transfers between devices, split_channels(): lax.all_to_all(sent, axes, split_axis=0, concat_axis=0, tiled=True)  25.1 us
    all_to_all x1, starting transfers between devices, split_channels(): lax.all_to_all(sent, axes, split_axis=0, concat_axis=0, tiled=True)  7.3 us
    pallas_call x1, Pallas kernels, channelize(): pl.pallas_call(channelize_kernel, out_shape=jax.ShapeDtypeStruct((FRAME,...  4.87 us
    unnamed x10, local copies, waits for them, and re-layouts  3.69 us
    pallas_call x2, Pallas kernels, place(): pl.pallas_call(place_kernel, out_shape=jax.ShapeDtypeStruct((blocks * sha...  1.66 us
    pallas_call x1, Pallas kernels, correlate(): pl.pallas_call(correlate_kernel, out_shape=(tile, tile), in_specs=[smem,...  1.09 us
  transfers between devices with their start and end apart: 3, of which 3 were waited for; matrix products, arithmetic and copies ran while one was open for 1% of the time, Pallas kernels for 2%

profile of v6, /device:TPU:0, one launch (start us, length us, event | category | flops | bytes accessed | tf_op | source)
XLA Modules:
  0.0 46.0 jit_solution(14388056004940669240)
XLA Ops:
  0.0 0.0 copy-start
  0.0 1.2 %copy-done = bf16[2,267776]{1,0:T(2,128)(2,1)S(1)} copy-done((bf16[2,267776]{1,0:T(2,128)(2,1)S(1)}, bf16[2,267776]{1,0:T(2,128)(2,1)}, u32[]{:S(2)}) %copy-start) | copy-done | bytes 1071128
  1.2 0.0 copy-start.1
  1.2 1.0 %copy-done.1 = bf16[512,512]{1,0:T(8,128)(2,1)S(1)} copy-done((bf16[512,512]{1,0:T(8,128)(2,1)S(1)}, bf16[512,512]{1,0:T(8,128)(2,1)}, u32[]{:S(2)}) %copy-start.1) | copy-done | bytes 524312
  2.3 0.0 copy-start.2
  2.3 0.8 %copy-done.2 = f32[12,512]{1,0:T(8,128)S(1)} copy-done((f32[12,512]{1,0:T(8,128)S(1)}, f32[12,512]{1,0:T(8,128)}, u32[]{:S(2)}) %copy-start.2) | copy-done | bytes 24600
  3.0 0.0 copy-start.3
  3.0 0.7 %copy-done.3 = s32[2]{0:T(128)S(1)} copy-done((s32[2]{0:T(128)S(1)}, s32[2]{0:T(128)}, u32[]{:S(2)}) %copy-start.3) | copy-done | bytes 32
  3.7 4.9 %shard_map.55 = bf16[512,1024]{1,0:T(8,128)(2,1)} custom-call(s32[2]{0:T(128)S(1)} %copy-done.3, bf16[2,267776]{1,0:T(2,128)(2,1)S(1)} %copy-done, f32[12,512]{1,0:T(8,128)S(1)} %copy-done.2, bf16[512,512]{1,0:T(8,128)(2,1)S(1)} %copy-done.1), custom_call_target="tpu_custom_call" | custom-call | flops 549453824 | bytes 2097152 | tf_op jit(solution)/shard_map/pallas_call | solution.py:127
  8.6 0.0 copy-start.4
  8.6 7.3 %all-to-all-start = ((bf16[32,16,1024]{2,1,0:T(8,128)(2,1)}), bf16[32,16,1024]{2,1,0:T(8,128)(2,1)S(1)}, u32[]{:S(2)}, u32[]{:S(2)}) async-start(bf16[32,16,1024]{2,1,0:T(8,128)(2,1)} %bitcast.2), calls=%async_computation | async-start | bytes 2097152 | tf_op jit(solution)/shard_map/all_to_all | solution.py:266
  15.9 0.0 copy-done.4
  15.9 0.3 collective-permute-start
  16.2 0.1 add.93
  16.3 0.8 %collective-permute-done = s32[1,32]{1,0:T(1,128)S(1)} collective-permute-done((s32[1,32]{1,0:T(1,128)S(1)}, s32[1,32]{1,0:T(1,128)S(1)}, u32[]{:S(2)}, u32[]{:S(2)}) %collective-permute-start) | collective-permute-done | bytes 160 | tf_op jit(solution)/shard_map/ppermute | solution.py:259
  17.1 0.1 broadcast_add_fusion.1
  17.2 0.1 add.91
  17.3 0.2 fusion.pick_ref
  17.6 25.1 %all-to-all-done = bf16[32,16,1024]{2,1,0:T(8,128)(2,1)S(1)} async-done(((bf16[32,16,1024]{2,1,0:T(8,128)(2,1)}), bf16[32,16,1024]{2,1,0:T(8,128)(2,1)S(1)}, u32[]{:S(2)}, u32[]{:S(2)}) %all-to-all-start) | async-done | bytes 1048608 | tf_op jit(solution)/shard_map/all_to_all | solution.py:266
  42.7 1.1 %shard_map.56 = (f32[8,32,128]{2,1,0:T(8,128)S(1)}, f32[8,32,128]{2,1,0:T(8,128)S(1)}) custom-call(s32[1]{0:T(128)} %bitcast.1.first_ref.index_ref, bf16[2,512,512]{2,1,0:T(8,128)(2,1)S(1)} %fusion.pick_ref, bf16[512,1024]{1,0:T(8,128)(2,1)S(1)} %bitcast.4), custom_call_target="tpu_custom_call" | custom-call | flops 536870912 | bytes 2097152 | tf_op jit(solution)/shard_map/pallas_call | solution.py:204
  43.8 0.1 collective-permute-start.1
  43.9 0.8 %shard_map.57.refs_0_ = f32[16,2,32,64]{3,2,1,0:T(8,128)} custom-call(s32[1]{0:T(128)} %bitcast.1.first_ref.index_ref, f32[8,32,128]{2,1,0:T(8,128)S(1)} %get-tuple-element.8.packed_ref), custom_call_target="tpu_custom_call" | custom-call | bytes 262144 | tf_op jit(solution)/shard_map/pallas_call | solution.py:235
  44.7 0.5 %collective-permute-done.1.packed_ref = f32[8,32,128]{2,1,0:T(8,128)S(1)} collective-permute-done((f32[8,32,128]{2,1,0:T(8,128)S(1)}, f32[8,32,128]{2,1,0:T(8,128)S(1)}, u32[]{:S(2)}, u32[]{:S(2)}) %collective-permute-start.1) | collective-permute-done | bytes 131104 | tf_op jit(solution)/shard_map/ppermute | solution.py:269
  45.2 0.8 %shard_map.58 = f32[16,2,32,64]{3,2,1,0:T(8,128)} custom-call(s32[1]{0:T(128)} %bitcast.index_ref, f32[8,32,128]{2,1,0:T(8,128)S(1)} %collective-permute-done.1.packed_ref, f32[16,2,32,64]{3,2,1,0:T(8,128)} %shard_map.57.refs_0_), custom_call_target="tpu_custom_call", output_to_operand_aliasing={{}: (2, {})} | custom-call | bytes 262144 | tf_op jit(solution)/shard_map/pallas_call | solution.py:235
  (5 shorter events, 0.1 us)
Async XLA Ops:
  0.0 1.2 %copy-start = (bf16[2,267776]{1,0:T(2,128)(2,1)S(1)}, bf16[2,267776]{1,0:T(2,128)(2,1)}, u32[]{:S(2)}) copy-start(bf16[2,267776]{1,0:T(2,128)(2,1)} %x_ref.1) | copy-start | bytes 3213316
  1.2 1.0 %copy-start.1 = (bf16[512,512]{1,0:T(8,128)(2,1)S(1)}, bf16[512,512]{1,0:T(8,128)(2,1)}, u32[]{:S(2)}) copy-start(bf16[512,512]{1,0:T(8,128)(2,1)} %constant.63.clone.table_ref) | copy-start | bytes 1572868
  2.3 0.8 %copy-start.2 = (f32[12,512]{1,0:T(8,128)S(1)}, f32[12,512]{1,0:T(8,128)}, u32[]{:S(2)}) copy-start(f32[12,512]{1,0:T(8,128)} %constant.64.clone.taps_ref) | copy-start | bytes 73732
  3.0 0.7 %copy-start.3 = (s32[2]{0:T(128)S(1)}, s32[2]{0:T(128)}, u32[]{:S(2)}) copy-start(s32[2]{0:T(128)} %flags_ref.1) | copy-start | bytes 28
  8.6 7.3 %copy-start.4 = (s32[1,32]{1,0:T(1,128)S(1)}, s32[1,32]{1,0:T(1,128)}, u32[]{:S(2)}) copy-start(s32[1,32]{1,0:T(1,128)} %param.6) | copy-start | bytes 388
  8.6 34.1 %all-to-all-start = ((bf16[32,16,1024]{2,1,0:T(8,128)(2,1)}), bf16[32,16,1024]{2,1,0:T(8,128)(2,1)S(1)}, u32[]{:S(2)}, u32[]{:S(2)}) async-start(bf16[32,16,1024]{2,1,0:T(8,128)(2,1)} %bitcast.2), calls=%async_computation | async-start | bytes 2097152 | tf_op jit(solution)/shard_map/all_to_all | solution.py:266
  15.9 1.2 %collective-permute-start = (s32[1,32]{1,0:T(1,128)S(1)}, s32[1,32]{1,0:T(1,128)S(1)}, u32[]{:S(2)}, u32[]{:S(2)}) collective-permute-start(s32[1,32]{1,0:T(1,128)S(1)} %copy-done.4), channel_id=1, source_target_pairs={{0,1},{1,0},{2,3},{3,2},{4,5},{5,4},{6,7},{7,6},{8,9},{9,8},{10,11... | collective-permute-start | bytes 392 | tf_op jit(solution)/shard_map/ppermute | solution.py:259
  43.8 1.4 %collective-permute-start.1 = (f32[8,32,128]{2,1,0:T(8,128)S(1)}, f32[8,32,128]{2,1,0:T(8,128)S(1)}, u32[]{:S(2)}, u32[]{:S(2)}) collective-permute-start(f32[8,32,128]{2,1,0:T(8,128)S(1)} %get-tuple-element.7), channel_id=1, source_target_pairs={{0,1},{1,0},{2,3},{3,2},{4,5},{5,4},{6,7},{7,6},{8,9},{9,8},{10,11... | collective-permute-start | bytes 393224 | tf_op jit(solution)/shard_map/ppermute | solution.py:269

commit v7 on v6

--- a/solution.py
+++ b/solution.py
@@ -16,7 +16,7 @@
 FRAME = 2 * CH
 LANES = 128
 SUB = 8
-GROUP = 128
+GROUP = 256
 STEP = GROUP // SUB
 STRIDE = STEP + 1
 FAR = 4
@@ -40,20 +40,42 @@
 
 
 def channelize_kernel(
-    flags_ref, x_ref, taps_ref, table_ref, out_ref, held, wide, fir, spectra, result, in_sems, sems
+    flags_hbm,
+    x_hbm,
+    taps_hbm,
+    table_hbm,
+    out_hbm,
+    flags,
+    taps_all,
+    table,
+    held,
+    wide,
+    fir,
+    spectra,
+    result,
+    load_sems,
+    sems,
 ):
     inputs = held.shape[0]
     frames = SPEC + TAPS - 1
+    groups = SPEC // GROUP
     pieces = sems.shape[1]
     rows = FRAME // pieces
     last = lax.broadcasted_iota(jnp.int32, (SUB, LANES), 0) == SUB - 1
-    edges = [0] + [g * GROUP + TAPS - 1 for g in range(1, SPEC // GROUP)] + [frames]
-    loads = []
-    for g, (begin, end) in enumerate(zip(edges, edges[1:])):
-        part = (slice(None), pl.ds(begin * FRAME, (end - begin) * FRAME))
-        load = pltpu.make_async_copy(x_ref.at[part], held.at[part], in_sems.at[g])
-        load.start()
-        loads.append(load)
+    edges = [0] + [g * GROUP + TAPS - 1 for g in range(1, groups)] + [frames]
+
+    def load(source, target, n):
+        copy = pltpu.make_async_copy(source, target, load_sems.at[n])
+        copy.start()
+        return copy
+
+    def span(g):
+        return slice(None), pl.ds(edges[g] * FRAME, (edges[g + 1] - edges[g]) * FRAME)
+
+    loads = [load(x_hbm.at[span(g)], held.at[span(g)], g) for g in range(groups)]
+    load_taps = load(taps_hbm, taps_all, groups)
+    load_table = load(table_hbm, table, groups + 1)
+    load_flags = load(flags_hbm, flags, groups + 2)
 
     def convert(g):
         for f in range(edges[g], edges[g + 1]):
@@ -63,7 +85,7 @@
 
     def filter_group(g, i, j):
         cols = pl.ds(j * LANES, LANES)
-        taps = [jnp.broadcast_to(taps_ref[pl.ds(t, 1), cols], (SUB, LANES)) for t in range(TAPS)]
+        taps = [jnp.broadcast_to(taps_all[pl.ds(t, 1), cols], (SUB, LANES)) for t in range(TAPS)]
 
         def take(b):
             first = inputs * (g * GROUP + b) + i
@@ -75,44 +97,67 @@
                 out = out + taps[t] * window[t]
             return out
 
-        window = [take(b) for b in range(STEP + TAPS)]
-        extra = total(window[STEP:])
-        for b in range(0, STEP, 2):
-            pair = []
-            for c in (b, b + 1):
-                row = total(window[c:])
-                past = c - (STEP - SUB + 1)
-                if past >= 0:
-                    row = jnp.where(last, pltpu.roll(extra, SUB - 1 - past, 0), row)
-                pair.append(row)
-            both = jnp.concatenate(pair, axis=0).astype(jnp.bfloat16)
-            fir[i, pl.ds(g * GROUP + b * SUB, 2 * SUB), cols] = both
-
-    for g in range(SPEC // GROUP):
+        extra = total([take(STEP + t) for t in range(TAPS)])
+        window = [take(b) for b in range(TAPS - 1)]
+        pair = []
+        for b in range(STEP):
+            window.append(take(b + TAPS - 1))
+            row = total(window[b:])
+            past = b - (STEP - SUB + 1)
+            if past >= 0:
+                row = jnp.where(last, pltpu.roll(extra, SUB - 1 - past, 0), row)
+            pair.append(row)
+            if len(pair) == 2:
+                both = jnp.concatenate(pair, axis=0).astype(jnp.bfloat16)
+                fir[i, pl.ds(g * GROUP + (b - 1) * SUB, 2 * SUB), cols] = both
+                pair = []
+
+    def transform(g, i):
+        part = pl.ds(g * GROUP, GROUP)
+        spectra[i, :, part] = lax.dot_general(
+            table[...],
+            fir[i, part, :],
+            (((1,), (1,)), ((), ())),
+            preferred_element_type=jnp.float32,
+        )
+
+    def normalise(i, piece):
+        good = (1 - flags[i]).astype(jnp.float32)
+        pairs = spectra[i, pl.ds(piece * rows, rows), :]
+        pairs = pairs.reshape(rows // (2 * SUB), 2, SUB, SPEC)
+        squares = jnp.sum(pairs * pairs, axis=1)
+        power = jnp.sum(squares, axis=2, keepdims=True) / SPEC
+        scale = good / jnp.sqrt(power + 1e-05)
+        scaled = (pairs * scale[:, None]).astype(jnp.bfloat16)
+        result[pl.ds(piece * rows, rows), pl.ds(i * SPEC, SPEC)] = scaled.reshape(rows, SPEC)
+
+    def store(i, piece):
+        place = (pl.ds(piece * rows, rows), pl.ds(i * SPEC, SPEC))
+        copy = pltpu.make_async_copy(result.at[place], out_hbm.at[place], sems.at[i, piece])
+        copy.start()
+        return copy
+
+    load_taps.wait()
+    for g in range(groups):
         loads[g].wait()
+        if g == 1:
+            load_table.wait()
+            load_flags.wait()
+        for i in range(inputs):
+            if g > 0:
+                transform(g - 1, i)
         convert(g)
         for i in range(inputs):
             for j in range(FRAME // LANES):
                 filter_group(g, i, j)
+    transform(groups - 1, 0)
     copies = []
     for i in range(inputs):
-        spectra[i] = lax.dot_general(
-            table_ref[...], fir[i], (((1,), (1,)), ((), ())), preferred_element_type=jnp.float32
-        )
-    for i in range(inputs):
-        good = (1 - flags_ref[i]).astype(jnp.float32)
+        if i + 1 < inputs:
+            transform(groups - 1, i + 1)
         for piece in range(pieces):
-            place = (pl.ds(piece * rows, rows), pl.ds(i * SPEC, SPEC))
-            pairs = spectra[i, pl.ds(piece * rows, rows), :]
-            pairs = pairs.reshape(rows // (2 * SUB), 2, SUB, SPEC)
-            squares = jnp.sum(pairs * pairs, axis=1)
-            power = jnp.sum(squares, axis=2, keepdims=True) / SPEC
-            scale = good / jnp.sqrt(power + 1e-05)
-            scaled = (pairs * scale[:, None]).astype(jnp.bfloat16)
-            result[place] = scaled.reshape(rows, SPEC)
-            copy = pltpu.make_async_copy(result.at[place], out_ref.at[place], sems.at[i, piece])
-            copy.start()
-            copies.append(copy)
+            normalise(i, piece)
+            copies.append(store(i, piece))
     for copy in copies:
         copy.wait()
 
@@ -122,23 +167,24 @@
     table = twiddle().reshape(far, near, blocks, SUB, 2, FRAME).transpose(2, 1, 0, 4, 3, 5)
     table = jnp.asarray(table.reshape(FRAME, FRAME), dtype=jnp.bfloat16)
     taps = jnp.asarray(prototype())
-    smem = pl.BlockSpec(memory_space=pltpu.SMEM)
-    vmem = pl.BlockSpec(memory_space=pltpu.VMEM)
+    hbm = pl.BlockSpec(memory_space=pltpu.HBM)
     return pl.pallas_call(
         channelize_kernel,
         out_shape=jax.ShapeDtypeStruct((FRAME, inputs * SPEC), jnp.bfloat16),
-        in_specs=[smem, pl.BlockSpec(memory_space=pltpu.HBM), vmem, vmem],
-        out_specs=pl.BlockSpec(memory_space=pl.ANY),
+        in_specs=[hbm] * 4,
+        out_specs=hbm,
         scratch_shapes=[
-            pltpu.VMEM(samples.shape, jnp.bfloat16),
+            pltpu.SMEM(flags.shape, flags.dtype),
+            pltpu.VMEM(taps.shape, taps.dtype),
+            pltpu.VMEM(table.shape, table.dtype),
+            pltpu.VMEM(samples.shape, samples.dtype),
             pltpu.VMEM((FRAME // LANES, inputs * (SPEC + 24), LANES), jnp.float32),
             pltpu.VMEM((inputs, SPEC, FRAME), jnp.bfloat16),
             pltpu.VMEM((inputs, FRAME, SPEC), jnp.float32),
             pltpu.VMEM((FRAME, inputs * SPEC), jnp.bfloat16),
-            pltpu.SemaphoreType.DMA((SPEC // GROUP,)),
+            pltpu.SemaphoreType.DMA((SPEC // GROUP + 3,)),
             pltpu.SemaphoreType.DMA((inputs, 8)),
         ],
-        compiler_params=pltpu.CompilerParams(vmem_limit_bytes=VMEM_LIMIT),
         cost_estimate=pl.CostEstimate(
             flops=2 * inputs * SPEC * FRAME * (FRAME + TAPS),
             bytes_accessed=4 * inputs * SPEC * FRAME,
@@ -147,12 +193,12 @@
     )(flags, samples, taps, table)
 
 
-def correlate_kernel(first_ref, pick_ref, arrived_ref, own_ref, other_ref, slots):
+def correlate_kernel(pick_ref, arrived_ref, own_ref, other_ref, slots):
     share, block, _ = own_ref.shape
     blocks = pick_ref.shape[0]
     width = blocks * block
     held = arrived_ref.shape[0] // blocks
-    first = first_ref[0] == 0
+    first = lax.axis_index("blk") == 0
     lane = lax.broadcasted_iota(jnp.int32, (width, 2 * width), 1)
     sign = jnp.where(lane < width, 1.0 / SPEC, -1.0 / SPEC)
     for n in range(blocks):
@@ -196,59 +242,55 @@
     return (column == target).astype(jnp.bfloat16)
 
 
-def correlate(arrived, pick, me, share, block):
+def correlate(arrived, pick, share, block):
     blocks = pick.shape[0]
-    smem = pl.BlockSpec(memory_space=pltpu.SMEM)
     vmem = pl.BlockSpec(memory_space=pltpu.VMEM)
     tile = jax.ShapeDtypeStruct((share, block, 2 * blocks * block), jnp.float32)
     return pl.pallas_call(
         correlate_kernel,
         out_shape=(tile, tile),
-        in_specs=[smem, vmem, vmem],
+        in_specs=[vmem, vmem],
         out_specs=(vmem, vmem),
         scratch_shapes=[pltpu.VMEM((blocks, share * 2 * block, SPEC), jnp.bfloat16)],
         compiler_params=pltpu.CompilerParams(vmem_limit_bytes=VMEM_LIMIT),
         cost_estimate=pl.CostEstimate(
             flops=2 * pick.size * SPEC, bytes_accessed=4 * arrived.size, transcendentals=0
         ),
-    )(me.reshape(1), pick, arrived)
-
-
-def place_kernel(index_ref, packed_ref, *refs):
+    )(pick, arrived)
+
+
+def place_kernel(packed_ref, *refs, own):
     out_ref, parts, sems = refs[-3:]
     share, _, _, width = parts.shape
+    me = lax.axis_index("blk")
+    start = (me if own else 1 - me) * share
     copies = []
     for k in range(share):
         parts[k, 0] = packed_ref[k, :, :width]
         parts[k, 1] = packed_ref[k, :, width:]
-        where = index_ref[0] * share + k
-        copies.append(pltpu.make_async_copy(parts.at[k], out_ref.at[where], sems.at[k]))
+        copies.append(pltpu.make_async_copy(parts.at[k], out_ref.at[start + k], sems.at[k]))
         copies[-1].start()
     for copy in copies:
         copy.wait()
 
 
-def place(packed, index, blocks, base=None):
+def place(packed, blocks, base=None):
     share, block, lanes = packed.shape
     width = lanes // 2
     anywhere = pl.BlockSpec(memory_space=pl.ANY)
     return pl.pallas_call(
-        place_kernel,
+        functools.partial(place_kernel, own=base is None),
         out_shape=jax.ShapeDtypeStruct((blocks * share, 2, block, width), packed.dtype),
-        in_specs=[
-            pl.BlockSpec(memory_space=pltpu.SMEM),
-            pl.BlockSpec(memory_space=pltpu.VMEM),
-        ]
-        + ([] if base is None else [anywhere]),
+        in_specs=[pl.BlockSpec(memory_space=pltpu.VMEM)] + ([] if base is None else [anywhere]),
         out_specs=anywhere,
         scratch_shapes=[
             pltpu.VMEM((share, 2, block, width), packed.dtype),
             pltpu.SemaphoreType.DMA((share,)),
         ],
-        input_output_aliases={} if base is None else {2: 0},
+        input_output_aliases={} if base is None else {1: 0},
         compiler_params=pltpu.CompilerParams(vmem_limit_bytes=VMEM_LIMIT),
         cost_estimate=pl.CostEstimate(flops=0, bytes_accessed=8 * packed.size, transcendentals=0),
-    )(index.reshape(1), packed, *([] if base is None else [base]))
+    )(packed, *([] if base is None else [base]))
 
 
 def split_channels(far, near, blocks, samples, slot_order, flags):
@@ -265,9 +307,9 @@
     sent = channelize(samples, flags, far, near, blocks)
     arrived = lax.all_to_all(sent, axes, split_axis=0, concat_axis=0, tiled=True)
     pick = picks(orders, inputs, far, near, share)
-    own, other = correlate(arrived, pick, me, share, block)
+    own, other = correlate(arrived, pick, share, block)
     received = lax.ppermute(other, "blk", SWAP)
-    return place(received, 1 - me, blocks, place(own, me, blocks))
+    return place(received, blocks, place(own, blocks))
 
 
 def gather_blocks(freq, samples, slot_order, flags):

time: 46.4 us -> 43.3 us (0.933)
  local copies, waits for them, and re-layouts: 3.89 us -> 0.2 us
  Pallas kernels: 7.63 us -> 8.37 us
    unnamed x10 -> x2, local copies, waits for them, and re-layouts: 3.69 us -> 0.01 us
    pallas_call x1, Pallas kernels: 4.87 us -> 5.62 us  [channelize(): pl.pallas_call(channelize_kernel, out_shape=jax.ShapeDtypeStruct((FRAME,...]
where the time goes in v7:
time: 43.3 us; the launch traced here: 43.1 us
  waiting for transfers between devices  26.4 us (61%)
  Pallas kernels  8.37 us (19%)
  starting transfers between devices  7.7 us (18%)
    all_to_all x1, waiting for transfers between devices, split_channels(): lax.all_to_all(sent, axes, split_axis=0, concat_axis=0, tiled=True)  25.1 us
    all_to_all x1, starting transfers between devices, split_channels(): lax.all_to_all(sent, axes, split_axis=0, concat_axis=0, tiled=True)  7.31 us
    pallas_call x1, Pallas kernels, channelize(): pl.pallas_call(channelize_kernel, out_shape=jax.ShapeDtypeStruct((FRAME,...  5.62 us
    pallas_call x2, Pallas kernels, place(): pl.pallas_call(functools.partial(place_kernel, own=base is None), out_sha...  1.66 us
    pallas_call x1, Pallas kernels, correlate(): pl.pallas_call(correlate_kernel, out_shape=(tile, tile), in_specs=[vmem,...  1.09 us
  transfers between devices with their start and end apart: 3, of which 3 were waited for; matrix products, arithmetic and copies ran while one was open for 1% of the time, Pallas kernels for 2%

profile of v7, /device:TPU:0, one launch (start us, length us, event | category | flops | bytes accessed | tf_op | source)
XLA Modules:
  0.0 43.1 jit_solution(11127111479245648675)
XLA Ops:
  0.0 5.6 %shard_map.55 = bf16[512,1024]{1,0:T(8,128)(2,1)} custom-call(s32[2]{0:T(128)} %flags_hbm.1, bf16[2,267776]{1,0:T(2,128)(2,1)} %x_hbm.1, f32[12,512]{1,0:T(8,128)} %constant.63.clone.taps_hbm, bf16[512,512]{1,0:T(8,128)(2,1)} %constant.62.clone.table_hbm), custom_call_target="tpu_custom_call" | custom-call | flops 549453824 | bytes 2097152 | tf_op jit(solution)/shard_map/pallas_call | solution.py:171
  5.6 0.0 copy-start
  5.6 7.3 %all-to-all-start = ((bf16[32,16,1024]{2,1,0:T(8,128)(2,1)}), bf16[32,16,1024]{2,1,0:T(8,128)(2,1)S(1)}, u32[]{:S(2)}, u32[]{:S(2)}) async-start(bf16[32,16,1024]{2,1,0:T(8,128)(2,1)} %bitcast.3), calls=%async_computation | async-start | bytes 2097152 | tf_op jit(solution)/shard_map/all_to_all | solution.py:308
  13.0 0.0 copy-done
  13.0 0.3 collective-permute-start
  13.3 0.1 add.93
  13.4 0.8 %collective-permute-done = s32[1,32]{1,0:T(1,128)S(1)} collective-permute-done((s32[1,32]{1,0:T(1,128)S(1)}, s32[1,32]{1,0:T(1,128)S(1)}, u32[]{:S(2)}, u32[]{:S(2)}) %collective-permute-start) | collective-permute-done | bytes 160 | tf_op jit(solution)/shard_map/ppermute | solution.py:301
  14.2 0.1 broadcast_add_fusion.1
  14.3 0.1 add.91
  14.4 0.2 fusion.pick_ref
  14.6 25.1 %all-to-all-done = bf16[32,16,1024]{2,1,0:T(8,128)(2,1)S(1)} async-done(((bf16[32,16,1024]{2,1,0:T(8,128)(2,1)}), bf16[32,16,1024]{2,1,0:T(8,128)(2,1)S(1)}, u32[]{:S(2)}, u32[]{:S(2)}) %all-to-all-start) | async-done | bytes 1048608 | tf_op jit(solution)/shard_map/all_to_all | solution.py:308
  39.7 1.1 %shard_map.56 = (f32[8,32,128]{2,1,0:T(8,128)S(1)}, f32[8,32,128]{2,1,0:T(8,128)S(1)}) custom-call(bf16[2,512,512]{2,1,0:T(8,128)(2,1)S(1)} %fusion.pick_ref, bf16[512,1024]{1,0:T(8,128)(2,1)S(1)} %bitcast.2), custom_call_target="tpu_custom_call" | custom-call | flops 536870912 | bytes 2097152 | tf_op jit(solution)/shard_map/pallas_call | solution.py:249
  40.8 0.1 collective-permute-start.1
  40.9 0.8 %shard_map.57.refs_0_ = f32[16,2,32,64]{3,2,1,0:T(8,128)} custom-call(f32[8,32,128]{2,1,0:T(8,128)S(1)} %get-tuple-element.8.packed_ref), custom_call_target="tpu_custom_call" | custom-call | bytes 262144 | tf_op jit(solution)/shard_map/pallas_call | solution.py:281
  41.8 0.5 %collective-permute-done.1.packed_ref = f32[8,32,128]{2,1,0:T(8,128)S(1)} collective-permute-done((f32[8,32,128]{2,1,0:T(8,128)S(1)}, f32[8,32,128]{2,1,0:T(8,128)S(1)}, u32[]{:S(2)}, u32[]{:S(2)}) %collective-permute-start.1) | collective-permute-done | bytes 131104 | tf_op jit(solution)/shard_map/ppermute | solution.py:311
  42.3 0.8 %shard_map.58 = f32[16,2,32,64]{3,2,1,0:T(8,128)} custom-call(f32[8,32,128]{2,1,0:T(8,128)S(1)} %collective-permute-done.1.packed_ref, f32[16,2,32,64]{3,2,1,0:T(8,128)} %shard_map.57.refs_0_), custom_call_target="tpu_custom_call", output_to_operand_aliasing={{}: (1, {})} | custom-call | bytes 262144 | tf_op jit(solution)/shard_map/pallas_call | solution.py:281
  (5 shorter events, 0.1 us)
Async XLA Ops:
  5.6 7.3 %copy-start = (s32[1,32]{1,0:T(1,128)S(1)}, s32[1,32]{1,0:T(1,128)}, u32[]{:S(2)}) copy-start(s32[1,32]{1,0:T(1,128)} %param.6) | copy-start | bytes 388
  5.6 34.1 %all-to-all-start = ((bf16[32,16,1024]{2,1,0:T(8,128)(2,1)}), bf16[32,16,1024]{2,1,0:T(8,128)(2,1)S(1)}, u32[]{:S(2)}, u32[]{:S(2)}) async-start(bf16[32,16,1024]{2,1,0:T(8,128)(2,1)} %bitcast.3), calls=%async_computation | async-start | bytes 2097152 | tf_op jit(solution)/shard_map/all_to_all | solution.py:308
  13.0 1.2 %collective-permute-start = (s32[1,32]{1,0:T(1,128)S(1)}, s32[1,32]{1,0:T(1,128)S(1)}, u32[]{:S(2)}, u32[]{:S(2)}) collective-permute-start(s32[1,32]{1,0:T(1,128)S(1)} %copy-done), channel_id=1, source_target_pairs={{0,1},{1,0},{2,3},{3,2},{4,5},{5,4},{6,7},{7,6},{8,9},{9,8},{10,11... | collective-permute-start | bytes 392 | tf_op jit(solution)/shard_map/ppermute | solution.py:301
  40.8 1.4 %collective-permute-start.1 = (f32[8,32,128]{2,1,0:T(8,128)S(1)}, f32[8,32,128]{2,1,0:T(8,128)S(1)}, u32[]{:S(2)}, u32[]{:S(2)}) collective-permute-start(f32[8,32,128]{2,1,0:T(8,128)S(1)} %get-tuple-element.7), channel_id=1, source_target_pairs={{0,1},{1,0},{2,3},{3,2},{4,5},{5,4},{6,7},{7,6},{8,9},{9,8},{10,11... | collective-permute-start | bytes 393224 | tf_op jit(solution)/shard_map/ppermute | solution.py:311

commit v8 on v7

--- a/solution.py
+++ b/solution.py
@@ -7,6 +7,7 @@
 from jax import lax
 from jax.experimental import pallas as pl
 from jax.experimental.pallas import tpu as pltpu
+from jax.experimental.layout import Layout, with_layout_constraint
 from jax.sharding import Mesh
 from jax.sharding import PartitionSpec as P
 
@@ -19,6 +20,7 @@
 GROUP = 256
 STEP = GROUP // SUB
 STRIDE = STEP + 1
+PITCH = SPEC + 25
 FAR = 4
 SWAP = [(0, 1), (1, 0)]
 VMEM_LIMIT = 40 * 1024 * 1024
@@ -56,40 +58,44 @@
     load_sems,
     sems,
 ):
-    inputs = held.shape[0]
+    inputs = fir.shape[0]
     frames = SPEC + TAPS - 1
+    spread = inputs * FRAME // LANES
     groups = SPEC // GROUP
     pieces = sems.shape[1]
     rows = FRAME // pieces
     last = lax.broadcasted_iota(jnp.int32, (SUB, LANES), 0) == SUB - 1
-    edges = [0] + [g * GROUP + TAPS - 1 for g in range(1, groups)] + [frames]
+    edges = [0, GROUP // 2] + [g * GROUP + TAPS for g in range(1, groups)] + [frames]
 
     def load(source, target, n):
         copy = pltpu.make_async_copy(source, target, load_sems.at[n])
         copy.start()
         return copy
 
-    def span(g):
-        return slice(None), pl.ds(edges[g] * FRAME, (edges[g + 1] - edges[g]) * FRAME)
-
-    loads = [load(x_hbm.at[span(g)], held.at[span(g)], g) for g in range(groups)]
-    load_taps = load(taps_hbm, taps_all, groups)
-    load_table = load(table_hbm, table, groups + 1)
-    load_flags = load(flags_hbm, flags, groups + 2)
-
-    def convert(g):
-        for f in range(edges[g], edges[g + 1]):
-            for j in range(FRAME // LANES):
-                tile = held[:, pl.ds(f * FRAME + j * LANES, LANES)]
-                wide[j, pl.ds(inputs * f, inputs), :] = tile.astype(jnp.float32)
+    def span(n):
+        return pl.ds(edges[n] * spread, (edges[n + 1] - edges[n]) * spread)
+
+    chunks = len(edges) - 1
+    loads = [load(x_hbm.at[span(n)], held.at[span(n)], n) for n in range(chunks)]
+    load_taps = load(taps_hbm, taps_all, chunks)
+    load_table = load(table_hbm, table, chunks + 1)
+    load_flags = load(flags_hbm, flags, chunks + 2)
+
+    def convert(n):
+        for f in range(edges[n], edges[n + 1], 2):
+            count = min(2, frames - f)
+            tile = held[pl.ds(f * spread, count * spread), :].astype(jnp.float32)
+            for c in range(count):
+                part = tile[c * spread : (c + 1) * spread]
+                wide[pl.ds(f + c, spread, stride=PITCH), :] = part
 
     def filter_group(g, i, j):
         cols = pl.ds(j * LANES, LANES)
         taps = [jnp.broadcast_to(taps_all[pl.ds(t, 1), cols], (SUB, LANES)) for t in range(TAPS)]
 
         def take(b):
-            first = inputs * (g * GROUP + b) + i
-            return wide[j, pl.ds(first, SUB, stride=inputs * STRIDE), :]
+            first = (inputs * j + i) * PITCH + g * GROUP + b
+            return wide[pl.ds(first, SUB, stride=STRIDE), :]
 
         def total(window):
             out = taps[0] * window[0]
@@ -137,16 +143,18 @@
         copy.start()
         return copy
 
+    loads[0].wait()
+    convert(0)
     load_taps.wait()
     for g in range(groups):
-        loads[g].wait()
+        loads[g + 1].wait()
         if g == 1:
             load_table.wait()
             load_flags.wait()
         for i in range(inputs):
             if g > 0:
                 transform(g - 1, i)
-        convert(g)
+        convert(g + 1)
         for i in range(inputs):
             for j in range(FRAME // LANES):
                 filter_group(g, i, j)
@@ -164,6 +172,10 @@
 
 def channelize(samples, flags, far, near, blocks):
     inputs = samples.shape[0]
+    tiles = samples.reshape(inputs, -1, LANES)
+    tiles = with_layout_constraint(tiles, Layout(major_to_minor=(1, 0, 2)))
+    tiles = tiles.transpose(1, 0, 2)
+    tiles = tiles.reshape(-1, LANES)
     table = twiddle().reshape(far, near, blocks, SUB, 2, FRAME).transpose(2, 1, 0, 4, 3, 5)
     table = jnp.asarray(table.reshape(FRAME, FRAME), dtype=jnp.bfloat16)
     taps = jnp.asarray(prototype())
@@ -177,12 +189,12 @@
             pltpu.SMEM(flags.shape, flags.dtype),
             pltpu.VMEM(taps.shape, taps.dtype),
             pltpu.VMEM(table.shape, table.dtype),
-            pltpu.VMEM(samples.shape, samples.dtype),
-            pltpu.VMEM((FRAME // LANES, inputs * (SPEC + 24), LANES), jnp.float32),
+            pltpu.VMEM(tiles.shape, tiles.dtype),
+            pltpu.VMEM((inputs * FRAME // LANES * PITCH, LANES), jnp.float32),
             pltpu.VMEM((inputs, SPEC, FRAME), jnp.bfloat16),
             pltpu.VMEM((inputs, FRAME, SPEC), jnp.float32),
             pltpu.VMEM((FRAME, inputs * SPEC), jnp.bfloat16),
-            pltpu.SemaphoreType.DMA((SPEC // GROUP + 3,)),
+            pltpu.SemaphoreType.DMA((SPEC // GROUP + 4,)),
             pltpu.SemaphoreType.DMA((inputs, 8)),
         ],
         cost_estimate=pl.CostEstimate(
@@ -190,7 +202,7 @@
             bytes_accessed=4 * inputs * SPEC * FRAME,
             transcendentals=0,
         ),
-    )(flags, samples, taps, table)
+    )(flags, tiles, taps, table)
 
 
 def correlate_kernel(pick_ref, arrived_ref, own_ref, other_ref, slots):
@@ -265,10 +277,13 @@
     me = lax.axis_index("blk")
     start = (me if own else 1 - me) * share
     copies = []
-    for k in range(share):
-        parts[k, 0] = packed_ref[k, :, :width]
-        parts[k, 1] = packed_ref[k, :, width:]
-        copies.append(pltpu.make_async_copy(parts.at[k], out_ref.at[start + k], sems.at[k]))
+    count = share // sems.shape[0]
+    for n in range(sems.shape[0]):
+        for k in range(n * count, (n + 1) * count):
+            parts[k, 0] = packed_ref[k, :, :width]
+            parts[k, 1] = packed_ref[k, :, width:]
+        target = out_ref.at[pl.ds(start + n * count, count)]
+        copies.append(pltpu.make_async_copy(parts.at[pl.ds(n * count, count)], target, sems.at[n]))
         copies[-1].start()
     for copy in copies:
         copy.wait()
@@ -285,7 +300,7 @@
         out_specs=anywhere,
         scratch_shapes=[
             pltpu.VMEM((share, 2, block, width), packed.dtype),
-            pltpu.SemaphoreType.DMA((share,)),
+            pltpu.SemaphoreType.DMA((2,)),
         ],
         input_output_aliases={} if base is None else {1: 0},
         compiler_params=pltpu.CompilerParams(vmem_limit_bytes=VMEM_LIMIT),

time: 43.3 us -> 42.8 us (0.988)
  Pallas kernels: 8.37 us -> 7.82 us
    pallas_call x1, Pallas kernels: 5.62 us -> 5.13 us  [channelize(): pl.pallas_call(channelize_kernel, out_shape=jax.ShapeDtypeStruct((FRAME,...]
where the time goes in v8:
time: 42.8 us; the launch traced here: 42.6 us
  waiting for transfers between devices  26.4 us (62%)
  Pallas kernels  7.82 us (18%)
  starting transfers between devices  7.69 us (18%)
    all_to_all x1, waiting for transfers between devices, split_channels(): lax.all_to_all(sent, axes, split_axis=0, concat_axis=0, tiled=True)  25.1 us
    all_to_all x1, starting transfers between devices, split_channels(): lax.all_to_all(sent, axes, split_axis=0, concat_axis=0, tiled=True)  7.31 us
    pallas_call x1, Pallas kernels, channelize(): pl.pallas_call(channelize_kernel, out_shape=jax.ShapeDtypeStruct((FRAME,...  5.13 us
    pallas_call x2, Pallas kernels, place(): pl.pallas_call(functools.partial(place_kernel, own=base is None), out_sha...  1.6 us
    pallas_call x1, Pallas kernels, correlate(): pl.pallas_call(correlate_kernel, out_shape=(tile, tile), in_specs=[vmem,...  1.1 us
  transfers between devices with their start and end apart: 3, of which 3 were waited for; matrix products, arithmetic and copies ran while one was open for 1% of the time, Pallas kernels for 2%

profile of v8, /device:TPU:0, one launch (start us, length us, event | category | flops | bytes accessed | tf_op | source)
XLA Modules:
  0.0 42.6 jit_solution(585026542090422956)
XLA Ops:
  0.0 5.1 %shard_map.55 = bf16[512,1024]{1,0:T(8,128)(2,1)} custom-call(s32[2]{0:T(128)} %flags_hbm.1, bf16[4184,128]{1,0:T(8,128)(2,1)} %bitcast.9, f32[12,512]{1,0:T(8,128)} %constant.63.clone.taps_hbm, bf16[512,512]{1,0:T(8,128)(2,1)} %constant.62.clone.table_hbm), custom_call_target="tpu_custom_call" | custom-call | flops 549453824 | bytes 2097152 | tf_op jit(solution)/shard_map/pallas_call | solution.py:183
  5.1 0.0 copy-start
  5.1 7.3 %all-to-all-start = ((bf16[32,16,1024]{2,1,0:T(8,128)(2,1)}), bf16[32,16,1024]{2,1,0:T(8,128)(2,1)S(1)}, u32[]{:S(2)}, u32[]{:S(2)}) async-start(bf16[32,16,1024]{2,1,0:T(8,128)(2,1)} %bitcast.8), calls=%async_computation | async-start | bytes 2097152 | tf_op jit(solution)/shard_map/all_to_all | solution.py:323
  12.5 0.0 copy-done
  12.5 0.3 collective-permute-start
  12.8 0.1 add.93
  12.9 0.8 %collective-permute-done = s32[1,32]{1,0:T(1,128)S(1)} collective-permute-done((s32[1,32]{1,0:T(1,128)S(1)}, s32[1,32]{1,0:T(1,128)S(1)}, u32[]{:S(2)}, u32[]{:S(2)}) %collective-permute-start) | collective-permute-done | bytes 160 | tf_op jit(solution)/shard_map/ppermute | solution.py:316
  13.7 0.1 broadcast_add_fusion.1
  13.8 0.1 add.91
  13.9 0.2 fusion.pick_ref
  14.1 25.1 %all-to-all-done = bf16[32,16,1024]{2,1,0:T(8,128)(2,1)S(1)} async-done(((bf16[32,16,1024]{2,1,0:T(8,128)(2,1)}), bf16[32,16,1024]{2,1,0:T(8,128)(2,1)S(1)}, u32[]{:S(2)}, u32[]{:S(2)}) %all-to-all-start) | async-done | bytes 1048608 | tf_op jit(solution)/shard_map/all_to_all | solution.py:323
  39.2 1.1 %shard_map.56 = (f32[8,32,128]{2,1,0:T(8,128)S(1)}, f32[8,32,128]{2,1,0:T(8,128)S(1)}) custom-call(bf16[2,512,512]{2,1,0:T(8,128)(2,1)S(1)} %fusion.pick_ref, bf16[512,1024]{1,0:T(8,128)(2,1)S(1)} %bitcast.7), custom_call_target="tpu_custom_call" | custom-call | flops 536870912 | bytes 2097152 | tf_op jit(solution)/shard_map/pallas_call | solution.py:261
  40.4 0.1 collective-permute-start.1
  40.4 0.8 %shard_map.57.refs_0_ = f32[16,2,32,64]{3,2,1,0:T(8,128)} custom-call(f32[8,32,128]{2,1,0:T(8,128)S(1)} %get-tuple-element.8.packed_ref), custom_call_target="tpu_custom_call" | custom-call | bytes 262144 | tf_op jit(solution)/shard_map/pallas_call | solution.py:296
  41.2 0.5 %collective-permute-done.1.packed_ref = f32[8,32,128]{2,1,0:T(8,128)S(1)} collective-permute-done((f32[8,32,128]{2,1,0:T(8,128)S(1)}, f32[8,32,128]{2,1,0:T(8,128)S(1)}, u32[]{:S(2)}, u32[]{:S(2)}) %collective-permute-start.1) | collective-permute-done | bytes 131104 | tf_op jit(solution)/shard_map/ppermute | solution.py:326
  41.8 0.8 %shard_map.58 = f32[16,2,32,64]{3,2,1,0:T(8,128)} custom-call(f32[8,32,128]{2,1,0:T(8,128)S(1)} %collective-permute-done.1.packed_ref, f32[16,2,32,64]{3,2,1,0:T(8,128)} %shard_map.57.refs_0_), custom_call_target="tpu_custom_call", output_to_operand_aliasing={{}: (1, {})} | custom-call | bytes 262144 | tf_op jit(solution)/shard_map/pallas_call | solution.py:296
  (5 shorter events, 0.1 us)
Async XLA Ops:
  5.1 7.3 %copy-start = (s32[1,32]{1,0:T(1,128)S(1)}, s32[1,32]{1,0:T(1,128)}, u32[]{:S(2)}) copy-start(s32[1,32]{1,0:T(1,128)} %param.6) | copy-start | bytes 388
  5.1 34.1 %all-to-all-start = ((bf16[32,16,1024]{2,1,0:T(8,128)(2,1)}), bf16[32,16,1024]{2,1,0:T(8,128)(2,1)S(1)}, u32[]{:S(2)}, u32[]{:S(2)}) async-start(bf16[32,16,1024]{2,1,0:T(8,128)(2,1)} %bitcast.8), calls=%async_computation | async-start | bytes 2097152 | tf_op jit(solution)/shard_map/all_to_all | solution.py:323
  12.5 1.2 %collective-permute-start = (s32[1,32]{1,0:T(1,128)S(1)}, s32[1,32]{1,0:T(1,128)S(1)}, u32[]{:S(2)}, u32[]{:S(2)}) collective-permute-start(s32[1,32]{1,0:T(1,128)S(1)} %copy-done), channel_id=1, source_target_pairs={{0,1},{1,0},{2,3},{3,2},{4,5},{5,4},{6,7},{7,6},{8,9},{9,8},{10,11... | collective-permute-start | bytes 392 | tf_op jit(solution)/shard_map/ppermute | solution.py:316
  40.4 1.4 %collective-permute-start.1 = (f32[8,32,128]{2,1,0:T(8,128)S(1)}, f32[8,32,128]{2,1,0:T(8,128)S(1)}, u32[]{:S(2)}, u32[]{:S(2)}) collective-permute-start(f32[8,32,128]{2,1,0:T(8,128)S(1)} %get-tuple-element.7), channel_id=1, source_target_pairs={{0,1},{1,0},{2,3},{3,2},{4,5},{5,4},{6,7},{7,6},{8,9},{9,8},{10,11... | collective-permute-start | bytes 393224 | tf_op jit(solution)/shard_map/ppermute | solution.py:326

commit v9 on v8

--- a/solution.py
+++ b/solution.py
@@ -62,7 +62,7 @@
     frames = SPEC + TAPS - 1
     spread = inputs * FRAME // LANES
     groups = SPEC // GROUP
-    pieces = sems.shape[1]
+    pieces = sems.shape[0]
     rows = FRAME // pieces
     last = lax.broadcasted_iota(jnp.int32, (SUB, LANES), 0) == SUB - 1
     edges = [0, GROUP // 2] + [g * GROUP + TAPS for g in range(1, groups)] + [frames]
@@ -78,7 +78,6 @@
     chunks = len(edges) - 1
     loads = [load(x_hbm.at[span(n)], held.at[span(n)], n) for n in range(chunks)]
     load_taps = load(taps_hbm, taps_all, chunks)
-    load_table = load(table_hbm, table, chunks + 1)
     load_flags = load(flags_hbm, flags, chunks + 2)
 
     def convert(n):
@@ -127,45 +126,53 @@
             preferred_element_type=jnp.float32,
         )
 
-    def normalise(i, piece):
+    def scaled(i, piece):
         good = (1 - flags[i]).astype(jnp.float32)
         pairs = spectra[i, pl.ds(piece * rows, rows), :]
         pairs = pairs.reshape(rows // (2 * SUB), 2, SUB, SPEC)
         squares = jnp.sum(pairs * pairs, axis=1)
         power = jnp.sum(squares, axis=2, keepdims=True) / SPEC
         scale = good / jnp.sqrt(power + 1e-05)
-        scaled = (pairs * scale[:, None]).astype(jnp.bfloat16)
-        result[pl.ds(piece * rows, rows), pl.ds(i * SPEC, SPEC)] = scaled.reshape(rows, SPEC)
-
-    def store(i, piece):
-        place = (pl.ds(piece * rows, rows), pl.ds(i * SPEC, SPEC))
-        copy = pltpu.make_async_copy(result.at[place], out_hbm.at[place], sems.at[i, piece])
+        return pairs * scale[:, None]
+
+    def pack(piece, parts):
+        place = pl.ds(piece * rows, rows)
+        for p in range(2):
+            both = jnp.concatenate([part[:, p] for part in parts], axis=1)
+            result[place, pl.ds(p * SPEC, SPEC)] = both.astype(jnp.bfloat16).reshape(rows, SPEC)
+        copy = pltpu.make_async_copy(result.at[place], out_hbm.at[place], sems.at[piece])
         copy.start()
         return copy
 
     loads[0].wait()
     convert(0)
     load_taps.wait()
-    for g in range(groups):
-        loads[g + 1].wait()
-        if g == 1:
-            load_table.wait()
-            load_flags.wait()
-        for i in range(inputs):
-            if g > 0:
-                transform(g - 1, i)
-        convert(g + 1)
-        for i in range(inputs):
-            for j in range(FRAME // LANES):
-                filter_group(g, i, j)
-    transform(groups - 1, 0)
+    loads[1].wait()
+    load_table = load(table_hbm, table, chunks + 1)
+    convert(1)
+    for i in range(inputs):
+        for j in range(FRAME // LANES):
+            filter_group(0, i, j)
+    loads[2].wait()
+    load_table.wait()
+    load_flags.wait()
+    for i in range(inputs):
+        transform(0, i)
+    convert(2)
+    for i in range(inputs):
+        if i > 0:
+            transform(1, i - 1)
+        for j in range(FRAME // LANES):
+            filter_group(1, i, j)
+    transform(1, inputs - 1)
+    for piece in range(pieces):
+        part = scaled(0, piece)
+        spectra[0, pl.ds(piece * rows, rows), :] = part.reshape(rows, SPEC)
     copies = []
-    for i in range(inputs):
-        if i + 1 < inputs:
-            transform(groups - 1, i + 1)
-        for piece in range(pieces):
-            normalise(i, piece)
-            copies.append(store(i, piece))
+    for piece in range(pieces):
+        held_part = spectra[0, pl.ds(piece * rows, rows), :]
+        held_part = held_part.reshape(rows // (2 * SUB), 2, SUB, SPEC)
+        copies.append(pack(piece, [held_part, scaled(1, piece)]))
     for copy in copies:
         copy.wait()
 
@@ -195,7 +202,7 @@
             pltpu.VMEM((inputs, FRAME, SPEC), jnp.float32),
             pltpu.VMEM((FRAME, inputs * SPEC), jnp.bfloat16),
             pltpu.SemaphoreType.DMA((SPEC // GROUP + 4,)),
-            pltpu.SemaphoreType.DMA((inputs, 8)),
+            pltpu.SemaphoreType.DMA((8,)),
         ],
         cost_estimate=pl.CostEstimate(
             flops=2 * inputs * SPEC * FRAME * (FRAME + TAPS),
@@ -215,20 +222,13 @@
     sign = jnp.where(lane < width, 1.0 / SPEC, -1.0 / SPEC)
     for n in range(blocks):
         rows = pl.ds(n * held, held)
-        stacked = jnp.concatenate(
-            [
-                arrived_ref[rows, pl.ds(i * SPEC, SPEC)]
-                for i in range(arrived_ref.shape[1] // SPEC)
-            ],
-            axis=0,
-        )
         slots[n] = jnp.dot(
-            pick_ref[n], stacked, preferred_element_type=jnp.float32
+            pick_ref[n], arrived_ref[rows, :], preferred_element_type=jnp.float32
         ).astype(jnp.bfloat16)
     for k in range(share):
         pair = jnp.concatenate(
             [
-                slots[n, pl.ds((2 * k + p) * block, block), :]
+                slots[n, pl.ds(k * block, block), pl.ds(p * SPEC, SPEC)]
                 for p in range(2)
                 for n in range(blocks)
             ],
@@ -246,11 +246,10 @@
     blocks, block = orders.shape
     device, held = orders // inputs, orders % inputs
     place = (device % near) * far + device // near
-    start = ((held * far * near + place) * 2 * share)[:, None, None, :]
-    chan = jnp.arange(share, dtype=jnp.int32)[:, None, None]
-    part = jnp.arange(2, dtype=jnp.int32)[:, None]
-    target = (start + part * share + chan).reshape(blocks, share * 2 * block, 1)
-    column = lax.broadcasted_iota(jnp.int32, (1, 1, inputs * far * near * 2 * share), 2)
+    start = ((place * inputs + held) * share)[:, None, :]
+    chan = jnp.arange(share, dtype=jnp.int32)[:, None]
+    target = (start + chan).reshape(blocks, share * block, 1)
+    column = lax.broadcasted_iota(jnp.int32, (1, 1, far * near * inputs * share), 2)
     return (column == target).astype(jnp.bfloat16)
 
 
@@ -263,10 +262,10 @@
         out_shape=(tile, tile),
         in_specs=[vmem, vmem],
         out_specs=(vmem, vmem),
-        scratch_shapes=[pltpu.VMEM((blocks, share * 2 * block, SPEC), jnp.bfloat16)],
+        scratch_shapes=[pltpu.VMEM((blocks, share * block, 2 * SPEC), jnp.bfloat16)],
         compiler_params=pltpu.CompilerParams(vmem_limit_bytes=VMEM_LIMIT),
         cost_estimate=pl.CostEstimate(
-            flops=2 * pick.size * SPEC, bytes_accessed=4 * arrived.size, transcendentals=0
+            flops=4 * pick.size * SPEC, bytes_accessed=4 * arrived.size, transcendentals=0
         ),
     )(pick, arrived)
 

time: 42.8 us -> 42.6 us (level)
  no operation moved by 1% of the time
where the time goes in v9:
time: 42.6 us; the launch traced here: 42.4 us
  waiting for transfers between devices  26.6 us (62%)
  starting transfers between devices  7.69 us (18%)
  Pallas kernels  7.64 us (18%)
    all_to_all x1, waiting for transfers between devices, split_channels(): lax.all_to_all(sent, axes, split_axis=0, concat_axis=0, tiled=True)  25.3 us
    all_to_all x1, starting transfers between devices, split_channels(): lax.all_to_all(sent, axes, split_axis=0, concat_axis=0, tiled=True)  7.31 us
    pallas_call x1, Pallas kernels, channelize(): pl.pallas_call(channelize_kernel, out_shape=jax.ShapeDtypeStruct((FRAME,...  5.17 us
    pallas_call x2, Pallas kernels, place(): pl.pallas_call(functools.partial(place_kernel, own=base is None), out_sha...  1.6 us
    pallas_call x1, Pallas kernels, correlate(): pl.pallas_call(correlate_kernel, out_shape=(tile, tile), in_specs=[vmem,...  0.87 us
  transfers between devices with their start and end apart: 3, of which 3 were waited for; matrix products, arithmetic and copies ran while one was open for 1% of the time, Pallas kernels for 2%

profile of v9, /device:TPU:0, one launch (start us, length us, event | category | flops | bytes accessed | tf_op | source)
XLA Modules:
  0.0 42.4 jit_solution(13192444663664820881)
XLA Ops:
  0.0 5.2 %shard_map.55 = bf16[512,1024]{1,0:T(8,128)(2,1)} custom-call(s32[2]{0:T(128)} %flags_hbm.1, bf16[4184,128]{1,0:T(8,128)(2,1)} %bitcast.9, f32[12,512]{1,0:T(8,128)} %constant.59.clone.taps_hbm, bf16[512,512]{1,0:T(8,128)(2,1)} %constant.58.clone.table_hbm), custom_call_target="tpu_custom_call" | custom-call | flops 549453824 | bytes 2097152 | tf_op jit(solution)/shard_map/pallas_call | solution.py:190
  5.2 0.0 copy-start
  5.2 7.3 %all-to-all-start = ((bf16[32,16,1024]{2,1,0:T(8,128)(2,1)}), bf16[32,16,1024]{2,1,0:T(8,128)(2,1)S(1)}, u32[]{:S(2)}, u32[]{:S(2)}) async-start(bf16[32,16,1024]{2,1,0:T(8,128)(2,1)} %bitcast.8), calls=%async_computation | async-start | bytes 2097152 | tf_op jit(solution)/shard_map/all_to_all | solution.py:322
  12.5 0.0 copy-done
  12.5 0.3 collective-permute-start
  12.8 0.1 add.72
  12.9 0.8 %collective-permute-done = s32[1,32]{1,0:T(1,128)S(1)} collective-permute-done((s32[1,32]{1,0:T(1,128)S(1)}, s32[1,32]{1,0:T(1,128)S(1)}, u32[]{:S(2)}, u32[]{:S(2)}) %collective-permute-start) | collective-permute-done | bytes 160 | tf_op jit(solution)/shard_map/ppermute | solution.py:315
  13.7 0.1 add.70
  13.8 0.1 fusion.pick_ref
  14.0 25.3 %all-to-all-done = bf16[32,16,1024]{2,1,0:T(8,128)(2,1)S(1)} async-done(((bf16[32,16,1024]{2,1,0:T(8,128)(2,1)}), bf16[32,16,1024]{2,1,0:T(8,128)(2,1)S(1)}, u32[]{:S(2)}, u32[]{:S(2)}) %all-to-all-start) | async-done | bytes 1048608 | tf_op jit(solution)/shard_map/all_to_all | solution.py:322
  39.3 0.9 %shard_map.56 = (f32[8,32,128]{2,1,0:T(8,128)S(1)}, f32[8,32,128]{2,1,0:T(8,128)S(1)}) custom-call(bf16[2,256,256]{2,1,0:T(8,128)(2,1)S(1)} %fusion.pick_ref, bf16[512,1024]{1,0:T(8,128)(2,1)S(1)} %bitcast.7), custom_call_target="tpu_custom_call" | custom-call | flops 268435456 | bytes 2097152 | tf_op jit(solution)/shard_map/pallas_call | solution.py:260
  40.2 0.1 collective-permute-start.1
  40.3 0.8 %shard_map.57.refs_0_ = f32[16,2,32,64]{3,2,1,0:T(8,128)} custom-call(f32[8,32,128]{2,1,0:T(8,128)S(1)} %get-tuple-element.8.packed_ref), custom_call_target="tpu_custom_call" | custom-call | bytes 262144 | tf_op jit(solution)/shard_map/pallas_call | solution.py:295
  41.1 0.5 %collective-permute-done.1.packed_ref = f32[8,32,128]{2,1,0:T(8,128)S(1)} collective-permute-done((f32[8,32,128]{2,1,0:T(8,128)S(1)}, f32[8,32,128]{2,1,0:T(8,128)S(1)}, u32[]{:S(2)}, u32[]{:S(2)}) %collective-permute-start.1) | collective-permute-done | bytes 131104 | tf_op jit(solution)/shard_map/ppermute | solution.py:325
  41.6 0.8 %shard_map.58 = f32[16,2,32,64]{3,2,1,0:T(8,128)} custom-call(f32[8,32,128]{2,1,0:T(8,128)S(1)} %collective-permute-done.1.packed_ref, f32[16,2,32,64]{3,2,1,0:T(8,128)} %shard_map.57.refs_0_), custom_call_target="tpu_custom_call", output_to_operand_aliasing={{}: (1, {})} | custom-call | bytes 262144 | tf_op jit(solution)/shard_map/pallas_call | solution.py:295
  (4 shorter events, 0.0 us)
Async XLA Ops:
  5.2 7.3 %copy-start = (s32[1,32]{1,0:T(1,128)S(1)}, s32[1,32]{1,0:T(1,128)}, u32[]{:S(2)}) copy-start(s32[1,32]{1,0:T(1,128)} %param.6) | copy-start | bytes 388
  5.2 34.1 %all-to-all-start = ((bf16[32,16,1024]{2,1,0:T(8,128)(2,1)}), bf16[32,16,1024]{2,1,0:T(8,128)(2,1)S(1)}, u32[]{:S(2)}, u32[]{:S(2)}) async-start(bf16[32,16,1024]{2,1,0:T(8,128)(2,1)} %bitcast.8), calls=%async_computation | async-start | bytes 2097152 | tf_op jit(solution)/shard_map/all_to_all | solution.py:322
  12.5 1.2 %collective-permute-start = (s32[1,32]{1,0:T(1,128)S(1)}, s32[1,32]{1,0:T(1,128)S(1)}, u32[]{:S(2)}, u32[]{:S(2)}) collective-permute-start(s32[1,32]{1,0:T(1,128)S(1)} %copy-done), channel_id=1, source_target_pairs={{0,1},{1,0},{2,3},{3,2},{4,5},{5,4},{6,7},{7,6},{8,9},{9,8},{10,11... | collective-permute-start | bytes 392 | tf_op jit(solution)/shard_map/ppermute | solution.py:315
  40.2 1.4 %collective-permute-start.1 = (f32[8,32,128]{2,1,0:T(8,128)S(1)}, f32[8,32,128]{2,1,0:T(8,128)S(1)}, u32[]{:S(2)}, u32[]{:S(2)}) collective-permute-start(f32[8,32,128]{2,1,0:T(8,128)S(1)} %get-tuple-element.7), channel_id=1, source_target_pairs={{0,1},{1,0},{2,3},{3,2},{4,5},{5,4},{6,7},{7,6},{8,9},{9,8},{10,11... | collective-permute-start | bytes 393224 | tf_op jit(solution)/shard_map/ppermute | solution.py:325

commit v10 on v9

--- a/solution.py
+++ b/solution.py
@@ -96,26 +96,23 @@
             first = (inputs * j + i) * PITCH + g * GROUP + b
             return wide[pl.ds(first, SUB, stride=STRIDE), :]
 
-        def total(window):
-            out = taps[0] * window[0]
+        def total(first, count):
+            window = [take(first + b) for b in range(count + TAPS - 1)]
+            out = [taps[0] * window[b] for b in range(count)]
             for t in range(1, TAPS):
-                out = out + taps[t] * window[t]
+                out = [out[b] + taps[t] * window[b + t] for b in range(count)]
             return out
 
-        extra = total([take(STEP + t) for t in range(TAPS)])
-        window = [take(b) for b in range(TAPS - 1)]
-        pair = []
-        for b in range(STEP):
-            window.append(take(b + TAPS - 1))
-            row = total(window[b:])
-            past = b - (STEP - SUB + 1)
-            if past >= 0:
-                row = jnp.where(last, pltpu.roll(extra, SUB - 1 - past, 0), row)
-            pair.append(row)
-            if len(pair) == 2:
-                both = jnp.concatenate(pair, axis=0).astype(jnp.bfloat16)
-                fir[i, pl.ds(g * GROUP + (b - 1) * SUB, 2 * SUB), cols] = both
-                pair = []
+        extra = total(STEP, 1)[0]
+        for first in range(0, STEP, SUB):
+            out = total(first, SUB)
+            for b in range(SUB):
+                past = first + b - (STEP - SUB + 1)
+                if past >= 0:
+                    out[b] = jnp.where(last, pltpu.roll(extra, SUB - 1 - past, 0), out[b])
+            for b in range(0, SUB, 2):
+                both = jnp.concatenate(out[b : b + 2], axis=0).astype(jnp.bfloat16)
+                fir[i, pl.ds(g * GROUP + (first + b) * SUB, 2 * SUB), cols] = both
 
     def transform(g, i):
         part = pl.ds(g * GROUP, GROUP)

time: 42.6 us -> 42.5 us (level)
  no operation moved by 1% of the time
where the time goes in v10:
time: 42.5 us; the launch traced here: 42.3 us
  waiting for transfers between devices  26.6 us (63%)
  starting transfers between devices  7.69 us (18%)
  Pallas kernels  7.57 us (18%)
    all_to_all x1, waiting for transfers between devices, split_channels(): lax.all_to_all(sent, axes, split_axis=0, concat_axis=0, tiled=True)  25.3 us
    all_to_all x1, starting transfers between devices, split_channels(): lax.all_to_all(sent, axes, split_axis=0, concat_axis=0, tiled=True)  7.3 us
    pallas_call x1, Pallas kernels, channelize(): pl.pallas_call(channelize_kernel, out_shape=jax.ShapeDtypeStruct((FRAME,...  5.1 us
    pallas_call x2, Pallas kernels, place(): pl.pallas_call(functools.partial(place_kernel, own=base is None), out_sha...  1.6 us
    pallas_call x1, Pallas kernels, correlate(): pl.pallas_call(correlate_kernel, out_shape=(tile, tile), in_specs=[vmem,...  0.87 us
  transfers between devices with their start and end apart: 3, of which 3 were waited for; matrix products, arithmetic and copies ran while one was open for 1% of the time, Pallas kernels for 2%

profile of v10, /device:TPU:0, one launch (start us, length us, event | category | flops | bytes accessed | tf_op | source)
XLA Modules:
  0.0 42.3 jit_solution(14952507940513949126)
XLA Ops:
  0.0 5.1 %shard_map.55 = bf16[512,1024]{1,0:T(8,128)(2,1)} custom-call(s32[2]{0:T(128)} %flags_hbm.1, bf16[4184,128]{1,0:T(8,128)(2,1)} %bitcast.9, f32[12,512]{1,0:T(8,128)} %constant.59.clone.taps_hbm, bf16[512,512]{1,0:T(8,128)(2,1)} %constant.58.clone.table_hbm), custom_call_target="tpu_custom_call" | custom-call | flops 549453824 | bytes 2097152 | tf_op jit(solution)/shard_map/pallas_call | solution.py:187
  5.1 0.0 copy-start
  5.1 7.3 %all-to-all-start = ((bf16[32,16,1024]{2,1,0:T(8,128)(2,1)}), bf16[32,16,1024]{2,1,0:T(8,128)(2,1)S(1)}, u32[]{:S(2)}, u32[]{:S(2)}) async-start(bf16[32,16,1024]{2,1,0:T(8,128)(2,1)} %bitcast.8), calls=%async_computation | async-start | bytes 2097152 | tf_op jit(solution)/shard_map/all_to_all | solution.py:319
  12.4 0.0 copy-done
  12.4 0.3 collective-permute-start
  12.8 0.1 add.72
  12.8 0.8 %collective-permute-done = s32[1,32]{1,0:T(1,128)S(1)} collective-permute-done((s32[1,32]{1,0:T(1,128)S(1)}, s32[1,32]{1,0:T(1,128)S(1)}, u32[]{:S(2)}, u32[]{:S(2)}) %collective-permute-start) | collective-permute-done | bytes 160 | tf_op jit(solution)/shard_map/ppermute | solution.py:312
  13.7 0.1 add.70
  13.8 0.1 fusion.pick_ref
  13.9 25.3 %all-to-all-done = bf16[32,16,1024]{2,1,0:T(8,128)(2,1)S(1)} async-done(((bf16[32,16,1024]{2,1,0:T(8,128)(2,1)}), bf16[32,16,1024]{2,1,0:T(8,128)(2,1)S(1)}, u32[]{:S(2)}, u32[]{:S(2)}) %all-to-all-start) | async-done | bytes 1048608 | tf_op jit(solution)/shard_map/all_to_all | solution.py:319
  39.2 0.9 %shard_map.56 = (f32[8,32,128]{2,1,0:T(8,128)S(1)}, f32[8,32,128]{2,1,0:T(8,128)S(1)}) custom-call(bf16[2,256,256]{2,1,0:T(8,128)(2,1)S(1)} %fusion.pick_ref, bf16[512,1024]{1,0:T(8,128)(2,1)S(1)} %bitcast.7), custom_call_target="tpu_custom_call" | custom-call | flops 268435456 | bytes 2097152 | tf_op jit(solution)/shard_map/pallas_call | solution.py:257
  40.1 0.1 collective-permute-start.1
  40.2 0.8 %shard_map.57.refs_0_ = f32[16,2,32,64]{3,2,1,0:T(8,128)} custom-call(f32[8,32,128]{2,1,0:T(8,128)S(1)} %get-tuple-element.8.packed_ref), custom_call_target="tpu_custom_call" | custom-call | bytes 262144 | tf_op jit(solution)/shard_map/pallas_call | solution.py:292
  41.0 0.5 %collective-permute-done.1.packed_ref = f32[8,32,128]{2,1,0:T(8,128)S(1)} collective-permute-done((f32[8,32,128]{2,1,0:T(8,128)S(1)}, f32[8,32,128]{2,1,0:T(8,128)S(1)}, u32[]{:S(2)}, u32[]{:S(2)}) %collective-permute-start.1) | collective-permute-done | bytes 131104 | tf_op jit(solution)/shard_map/ppermute | solution.py:322
  41.5 0.8 %shard_map.58 = f32[16,2,32,64]{3,2,1,0:T(8,128)} custom-call(f32[8,32,128]{2,1,0:T(8,128)S(1)} %collective-permute-done.1.packed_ref, f32[16,2,32,64]{3,2,1,0:T(8,128)} %shard_map.57.refs_0_), custom_call_target="tpu_custom_call", output_to_operand_aliasing={{}: (1, {})} | custom-call | bytes 262144 | tf_op jit(solution)/shard_map/pallas_call | solution.py:292
  (4 shorter events, 0.0 us)
Async XLA Ops:
  5.1 7.3 %copy-start = (s32[1,32]{1,0:T(1,128)S(1)}, s32[1,32]{1,0:T(1,128)}, u32[]{:S(2)}) copy-start(s32[1,32]{1,0:T(1,128)} %param.6) | copy-start | bytes 388
  5.1 34.1 %all-to-all-start = ((bf16[32,16,1024]{2,1,0:T(8,128)(2,1)}), bf16[32,16,1024]{2,1,0:T(8,128)(2,1)S(1)}, u32[]{:S(2)}, u32[]{:S(2)}) async-start(bf16[32,16,1024]{2,1,0:T(8,128)(2,1)} %bitcast.8), calls=%async_computation | async-start | bytes 2097152 | tf_op jit(solution)/shard_map/all_to_all | solution.py:319
  12.4 1.2 %collective-permute-start = (s32[1,32]{1,0:T(1,128)S(1)}, s32[1,32]{1,0:T(1,128)S(1)}, u32[]{:S(2)}, u32[]{:S(2)}) collective-permute-start(s32[1,32]{1,0:T(1,128)S(1)} %copy-done), channel_id=1, source_target_pairs={{0,1},{1,0},{2,3},{3,2},{4,5},{5,4},{6,7},{7,6},{8,9},{9,8},{10,11... | collective-permute-start | bytes 392 | tf_op jit(solution)/shard_map/ppermute | solution.py:312
  40.1 1.4 %collective-permute-start.1 = (f32[8,32,128]{2,1,0:T(8,128)S(1)}, f32[8,32,128]{2,1,0:T(8,128)S(1)}, u32[]{:S(2)}, u32[]{:S(2)}) collective-permute-start(f32[8,32,128]{2,1,0:T(8,128)S(1)} %get-tuple-element.7), channel_id=1, source_target_pairs={{0,1},{1,0},{2,3},{3,2},{4,5},{5,4},{6,7},{7,6},{8,9},{9,8},{10,11... | collective-permute-start | bytes 393224 | tf_op jit(solution)/shard_map/ppermute | solution.py:322

commit v11 on v10

--- a/solution.py
+++ b/solution.py
@@ -89,11 +89,11 @@
                 wide[pl.ds(f + c, spread, stride=PITCH), :] = part
 
     def filter_group(g, i, j):
-        cols = pl.ds(j * LANES, LANES)
+        cols = pl.ds(pl.multiple_of(j * LANES, LANES), LANES)
         taps = [jnp.broadcast_to(taps_all[pl.ds(t, 1), cols], (SUB, LANES)) for t in range(TAPS)]
 
         def take(b):
-            first = (inputs * j + i) * PITCH + g * GROUP + b
+            first = (inputs * j + i) * PITCH + (g * GROUP + b)
             return wide[pl.ds(first, SUB, stride=STRIDE), :]
 
         def total(first, count):
@@ -114,10 +114,11 @@
                 both = jnp.concatenate(out[b : b + 2], axis=0).astype(jnp.bfloat16)
                 fir[i, pl.ds(g * GROUP + (first + b) * SUB, 2 * SUB), cols] = both
 
-    def transform(g, i):
+    def transform(g, i, start=0, count=FRAME):
         part = pl.ds(g * GROUP, GROUP)
-        spectra[i, :, part] = lax.dot_general(
-            table[...],
+        out = pl.ds(start, count)
+        spectra[i, out, part] = lax.dot_general(
+            table[out, :],
             fir[i, part, :],
             (((1,), (1,)), ((), ())),
             preferred_element_type=jnp.float32,
@@ -147,21 +148,27 @@
     loads[1].wait()
     load_table = load(table_hbm, table, chunks + 1)
     convert(1)
-    for i in range(inputs):
-        for j in range(FRAME // LANES):
+    columns = FRAME // LANES
+
+    @pl.loop(0, columns)
+    def _(j):
+        for i in range(inputs):
             filter_group(0, i, j)
+
     loads[2].wait()
     load_table.wait()
     load_flags.wait()
+    convert(2)
+    count = FRAME // columns
+
+    @pl.loop(0, columns)
+    def _(j):
+        for i in range(inputs):
+            transform(0, i, pl.multiple_of(j * count, count), count)
+            filter_group(1, i, j)
+
     for i in range(inputs):
-        transform(0, i)
-    convert(2)
-    for i in range(inputs):
-        if i > 0:
-            transform(1, i - 1)
-        for j in range(FRAME // LANES):
-            filter_group(1, i, j)
-    transform(1, inputs - 1)
+        transform(1, i)
     for piece in range(pieces):
         part = scaled(0, piece)
         spectra[0, pl.ds(piece * rows, rows), :] = part.reshape(rows, SPEC)

time: 42.5 us -> 42.9 us (level)
  no operation moved by 1% of the time
where the time goes in v11:
time: 42.9 us; the launch traced here: 42.7 us
  waiting for transfers between devices  26.6 us (62%)
  Pallas kernels  7.92 us (18%)
  starting transfers between devices  7.69 us (18%)
    all_to_all x1, waiting for transfers between devices, split_channels(): lax.all_to_all(sent, axes, split_axis=0, concat_axis=0, tiled=True)  25.3 us
    all_to_all x1, starting transfers between devices, split_channels(): lax.all_to_all(sent, axes, split_axis=0, concat_axis=0, tiled=True)  7.3 us
    pallas_call x1, Pallas kernels, channelize(): pl.pallas_call(channelize_kernel, out_shape=jax.ShapeDtypeStruct((FRAME,...  5.45 us
    pallas_call x2, Pallas kernels, place(): pl.pallas_call(functools.partial(place_kernel, own=base is None), out_sha...  1.6 us
    pallas_call x1, Pallas kernels, correlate(): pl.pallas_call(correlate_kernel, out_shape=(tile, tile), in_specs=[vmem,...  0.87 us
  transfers between devices with their start and end apart: 3, of which 3 were waited for; matrix products, arithmetic and copies ran while one was open for 1% of the time, Pallas kernels for 2%

profile of v11, /device:TPU:0, one launch (start us, length us, event | category | flops | bytes accessed | tf_op | source)
XLA Modules:
  0.0 42.7 jit_solution(9803680560013385023)
XLA Ops:
  0.0 5.4 %shard_map.55 = bf16[512,1024]{1,0:T(8,128)(2,1)} custom-call(s32[2]{0:T(128)} %flags_hbm.1, bf16[4184,128]{1,0:T(8,128)(2,1)} %bitcast.9, f32[12,512]{1,0:T(8,128)} %constant.59.clone.taps_hbm, bf16[512,512]{1,0:T(8,128)(2,1)} %constant.58.clone.table_hbm), custom_call_target="tpu_custom_call" | custom-call | flops 549453824 | bytes 2097152 | tf_op jit(solution)/shard_map/pallas_call | solution.py:194
  5.5 0.0 copy-start
  5.5 7.3 %all-to-all-start = ((bf16[32,16,1024]{2,1,0:T(8,128)(2,1)}), bf16[32,16,1024]{2,1,0:T(8,128)(2,1)S(1)}, u32[]{:S(2)}, u32[]{:S(2)}) async-start(bf16[32,16,1024]{2,1,0:T(8,128)(2,1)} %bitcast.8), calls=%async_computation | async-start | bytes 2097152 | tf_op jit(solution)/shard_map/all_to_all | solution.py:326
  12.8 0.0 copy-done
  12.8 0.3 collective-permute-start
  13.1 0.1 add.72
  13.2 0.8 %collective-permute-done = s32[1,32]{1,0:T(1,128)S(1)} collective-permute-done((s32[1,32]{1,0:T(1,128)S(1)}, s32[1,32]{1,0:T(1,128)S(1)}, u32[]{:S(2)}, u32[]{:S(2)}) %collective-permute-start) | collective-permute-done | bytes 160 | tf_op jit(solution)/shard_map/ppermute | solution.py:319
  14.0 0.1 add.70
  14.1 0.1 fusion.pick_ref
  14.2 25.3 %all-to-all-done = bf16[32,16,1024]{2,1,0:T(8,128)(2,1)S(1)} async-done(((bf16[32,16,1024]{2,1,0:T(8,128)(2,1)}), bf16[32,16,1024]{2,1,0:T(8,128)(2,1)S(1)}, u32[]{:S(2)}, u32[]{:S(2)}) %all-to-all-start) | async-done | bytes 1048608 | tf_op jit(solution)/shard_map/all_to_all | solution.py:326
  39.6 0.9 %shard_map.56 = (f32[8,32,128]{2,1,0:T(8,128)S(1)}, f32[8,32,128]{2,1,0:T(8,128)S(1)}) custom-call(bf16[2,256,256]{2,1,0:T(8,128)(2,1)S(1)} %fusion.pick_ref, bf16[512,1024]{1,0:T(8,128)(2,1)S(1)} %bitcast.7), custom_call_target="tpu_custom_call" | custom-call | flops 268435456 | bytes 2097152 | tf_op jit(solution)/shard_map/pallas_call | solution.py:264
  40.4 0.1 collective-permute-start.1
  40.5 0.8 %shard_map.57.refs_0_ = f32[16,2,32,64]{3,2,1,0:T(8,128)} custom-call(f32[8,32,128]{2,1,0:T(8,128)S(1)} %get-tuple-element.8.packed_ref), custom_call_target="tpu_custom_call" | custom-call | bytes 262144 | tf_op jit(solution)/shard_map/pallas_call | solution.py:299
  41.3 0.5 %collective-permute-done.1.packed_ref = f32[8,32,128]{2,1,0:T(8,128)S(1)} collective-permute-done((f32[8,32,128]{2,1,0:T(8,128)S(1)}, f32[8,32,128]{2,1,0:T(8,128)S(1)}, u32[]{:S(2)}, u32[]{:S(2)}) %collective-permute-start.1) | collective-permute-done | bytes 131104 | tf_op jit(solution)/shard_map/ppermute | solution.py:329
  41.9 0.8 %shard_map.58 = f32[16,2,32,64]{3,2,1,0:T(8,128)} custom-call(f32[8,32,128]{2,1,0:T(8,128)S(1)} %collective-permute-done.1.packed_ref, f32[16,2,32,64]{3,2,1,0:T(8,128)} %shard_map.57.refs_0_), custom_call_target="tpu_custom_call", output_to_operand_aliasing={{}: (1, {})} | custom-call | bytes 262144 | tf_op jit(solution)/shard_map/pallas_call | solution.py:299
  (4 shorter events, 0.0 us)
Async XLA Ops:
  5.5 7.3 %copy-start = (s32[1,32]{1,0:T(1,128)S(1)}, s32[1,32]{1,0:T(1,128)}, u32[]{:S(2)}) copy-start(s32[1,32]{1,0:T(1,128)} %param.6) | copy-start | bytes 388
  5.5 34.1 %all-to-all-start = ((bf16[32,16,1024]{2,1,0:T(8,128)(2,1)}), bf16[32,16,1024]{2,1,0:T(8,128)(2,1)S(1)}, u32[]{:S(2)}, u32[]{:S(2)}) async-start(bf16[32,16,1024]{2,1,0:T(8,128)(2,1)} %bitcast.8), calls=%async_computation | async-start | bytes 2097152 | tf_op jit(solution)/shard_map/all_to_all | solution.py:326
  12.8 1.2 %collective-permute-start = (s32[1,32]{1,0:T(1,128)S(1)}, s32[1,32]{1,0:T(1,128)S(1)}, u32[]{:S(2)}, u32[]{:S(2)}) collective-permute-start(s32[1,32]{1,0:T(1,128)S(1)} %copy-done), channel_id=1, source_target_pairs={{0,1},{1,0},{2,3},{3,2},{4,5},{5,4},{6,7},{7,6},{8,9},{9,8},{10,11... | collective-permute-start | bytes 392 | tf_op jit(solution)/shard_map/ppermute | solution.py:319
  40.4 1.4 %collective-permute-start.1 = (f32[8,32,128]{2,1,0:T(8,128)S(1)}, f32[8,32,128]{2,1,0:T(8,128)S(1)}, u32[]{:S(2)}, u32[]{:S(2)}) collective-permute-start(f32[8,32,128]{2,1,0:T(8,128)S(1)} %get-tuple-element.7), channel_id=1, source_target_pairs={{0,1},{1,0},{2,3},{3,2},{4,5},{5,4},{6,7},{7,6},{8,9},{9,8},{10,11... | collective-permute-start | bytes 393224 | tf_op jit(solution)/shard_map/ppermute | solution.py:329

commit v12 on v10

--- a/solution.py
+++ b/solution.py
@@ -54,6 +54,7 @@
     wide,
     fir,
     spectra,
+    scales,
     result,
     load_sems,
     sems,
@@ -123,17 +124,27 @@
             preferred_element_type=jnp.float32,
         )
 
+    def rate(i):
+        good = (1 - flags[i]).astype(jnp.float32)
+        for piece in range(pieces):
+            pairs = spectra[i, pl.ds(piece * rows, rows), :]
+            pairs = pairs.reshape(rows // (2 * SUB), 2, SUB, SPEC)
+            squares = jnp.sum(pairs * pairs, axis=1)
+            power = jnp.sum(squares, axis=2, keepdims=True) / SPEC
+            scale = good / jnp.sqrt(power + 1e-05)
+            place = pl.ds(piece * rows // 2, rows // 2)
+            scales[i, place, :] = jnp.broadcast_to(scale.reshape(rows // 2, 1), (rows // 2, LANES))
+
     def scaled(i, piece):
-        good = (1 - flags[i]).astype(jnp.float32)
         pairs = spectra[i, pl.ds(piece * rows, rows), :]
         pairs = pairs.reshape(rows // (2 * SUB), 2, SUB, SPEC)
-        squares = jnp.sum(pairs * pairs, axis=1)
-        power = jnp.sum(squares, axis=2, keepdims=True) / SPEC
-        scale = good / jnp.sqrt(power + 1e-05)
-        return pairs * scale[:, None]
-
-    def pack(piece, parts):
+        scale = scales[i, pl.ds(piece * rows // 2, rows // 2), :]
+        scale = jnp.concatenate([scale] * (SPEC // LANES), axis=1)
+        return pairs * scale.reshape(rows // (2 * SUB), 1, SUB, SPEC)
+
+    def pack(piece):
         place = pl.ds(piece * rows, rows)
+        parts = [scaled(i, piece) for i in range(inputs)]
         for p in range(2):
             both = jnp.concatenate([part[:, p] for part in parts], axis=1)
             result[place, pl.ds(p * SPEC, SPEC)] = both.astype(jnp.bfloat16).reshape(rows, SPEC)
@@ -162,14 +173,9 @@
         for j in range(FRAME // LANES):
             filter_group(1, i, j)
     transform(1, inputs - 1)
-    for piece in range(pieces):
-        part = scaled(0, piece)
-        spectra[0, pl.ds(piece * rows, rows), :] = part.reshape(rows, SPEC)
-    copies = []
-    for piece in range(pieces):
-        held_part = spectra[0, pl.ds(piece * rows, rows), :]
-        held_part = held_part.reshape(rows // (2 * SUB), 2, SUB, SPEC)
-        copies.append(pack(piece, [held_part, scaled(1, piece)]))
+    for i in range(inputs):
+        rate(i)
+    copies = [pack(piece) for piece in range(pieces)]
     for copy in copies:
         copy.wait()
 
@@ -197,6 +203,7 @@
             pltpu.VMEM((inputs * FRAME // LANES * PITCH, LANES), jnp.float32),
             pltpu.VMEM((inputs, SPEC, FRAME), jnp.bfloat16),
             pltpu.VMEM((inputs, FRAME, SPEC), jnp.float32),
+            pltpu.VMEM((inputs, CH, LANES), jnp.float32),
             pltpu.VMEM((FRAME, inputs * SPEC), jnp.bfloat16),
             pltpu.SemaphoreType.DMA((SPEC // GROUP + 4,)),
             pltpu.SemaphoreType.DMA((8,)),

time: 42.5 us -> 42.5 us (level)
  no operation moved by 1% of the time
where the time goes in v12:
time: 42.5 us; the launch traced here: 42.3 us
  waiting for transfers between devices  26.6 us (63%)
  starting transfers between devices  7.69 us (18%)
  Pallas kernels  7.57 us (18%)
    all_to_all x1, waiting for transfers between devices, split_channels(): lax.all_to_all(sent, axes, split_axis=0, concat_axis=0, tiled=True)  25.3 us
    all_to_all x1, starting transfers between devices, split_channels(): lax.all_to_all(sent, axes, split_axis=0, concat_axis=0, tiled=True)  7.3 us
    pallas_call x1, Pallas kernels, channelize(): pl.pallas_call(channelize_kernel, out_shape=jax.ShapeDtypeStruct((FRAME,...  5.1 us
    pallas_call x2, Pallas kernels, place(): pl.pallas_call(functools.partial(place_kernel, own=base is None), out_sha...  1.6 us
    pallas_call x1, Pallas kernels, correlate(): pl.pallas_call(correlate_kernel, out_shape=(tile, tile), in_specs=[vmem,...  0.87 us
  transfers between devices with their start and end apart: 3, of which 3 were waited for; matrix products, arithmetic and copies ran while one was open for 1% of the time, Pallas kernels for 2%

profile of v12, /device:TPU:0, one launch (start us, length us, event | category | flops | bytes accessed | tf_op | source)
XLA Modules:
  0.0 42.3 jit_solution(5992133419133535855)
XLA Ops:
  0.0 5.1 %shard_map.55 = bf16[512,1024]{1,0:T(8,128)(2,1)} custom-call(s32[2]{0:T(128)} %flags_hbm.1, bf16[4184,128]{1,0:T(8,128)(2,1)} %bitcast.9, f32[12,512]{1,0:T(8,128)} %constant.59.clone.taps_hbm, bf16[512,512]{1,0:T(8,128)(2,1)} %constant.58.clone.table_hbm), custom_call_target="tpu_custom_call" | custom-call | flops 549453824 | bytes 2097152 | tf_op jit(solution)/shard_map/pallas_call | solution.py:193
  5.1 0.0 copy-start
  5.1 7.3 %all-to-all-start = ((bf16[32,16,1024]{2,1,0:T(8,128)(2,1)}), bf16[32,16,1024]{2,1,0:T(8,128)(2,1)S(1)}, u32[]{:S(2)}, u32[]{:S(2)}) async-start(bf16[32,16,1024]{2,1,0:T(8,128)(2,1)} %bitcast.8), calls=%async_computation | async-start | bytes 2097152 | tf_op jit(solution)/shard_map/all_to_all | solution.py:326
  12.4 0.0 copy-done
  12.4 0.3 collective-permute-start
  12.8 0.1 add.72
  12.8 0.8 %collective-permute-done = s32[1,32]{1,0:T(1,128)S(1)} collective-permute-done((s32[1,32]{1,0:T(1,128)S(1)}, s32[1,32]{1,0:T(1,128)S(1)}, u32[]{:S(2)}, u32[]{:S(2)}) %collective-permute-start) | collective-permute-done | bytes 160 | tf_op jit(solution)/shard_map/ppermute | solution.py:319
  13.7 0.1 add.70
  13.8 0.1 fusion.pick_ref
  13.9 25.3 %all-to-all-done = bf16[32,16,1024]{2,1,0:T(8,128)(2,1)S(1)} async-done(((bf16[32,16,1024]{2,1,0:T(8,128)(2,1)}), bf16[32,16,1024]{2,1,0:T(8,128)(2,1)S(1)}, u32[]{:S(2)}, u32[]{:S(2)}) %all-to-all-start) | async-done | bytes 1048608 | tf_op jit(solution)/shard_map/all_to_all | solution.py:326
  39.2 0.9 %shard_map.56 = (f32[8,32,128]{2,1,0:T(8,128)S(1)}, f32[8,32,128]{2,1,0:T(8,128)S(1)}) custom-call(bf16[2,256,256]{2,1,0:T(8,128)(2,1)S(1)} %fusion.pick_ref, bf16[512,1024]{1,0:T(8,128)(2,1)S(1)} %bitcast.7), custom_call_target="tpu_custom_call" | custom-call | flops 268435456 | bytes 2097152 | tf_op jit(solution)/shard_map/pallas_call | solution.py:264
  40.1 0.1 collective-permute-start.1
  40.2 0.8 %shard_map.57.refs_0_ = f32[16,2,32,64]{3,2,1,0:T(8,128)} custom-call(f32[8,32,128]{2,1,0:T(8,128)S(1)} %get-tuple-element.8.packed_ref), custom_call_target="tpu_custom_call" | custom-call | bytes 262144 | tf_op jit(solution)/shard_map/pallas_call | solution.py:299
  41.0 0.5 %collective-permute-done.1.packed_ref = f32[8,32,128]{2,1,0:T(8,128)S(1)} collective-permute-done((f32[8,32,128]{2,1,0:T(8,128)S(1)}, f32[8,32,128]{2,1,0:T(8,128)S(1)}, u32[]{:S(2)}, u32[]{:S(2)}) %collective-permute-start.1) | collective-permute-done | bytes 131104 | tf_op jit(solution)/shard_map/ppermute | solution.py:329
  41.5 0.8 %shard_map.58 = f32[16,2,32,64]{3,2,1,0:T(8,128)} custom-call(f32[8,32,128]{2,1,0:T(8,128)S(1)} %collective-permute-done.1.packed_ref, f32[16,2,32,64]{3,2,1,0:T(8,128)} %shard_map.57.refs_0_), custom_call_target="tpu_custom_call", output_to_operand_aliasing={{}: (1, {})} | custom-call | bytes 262144 | tf_op jit(solution)/shard_map/pallas_call | solution.py:299
  (4 shorter events, 0.0 us)
Async XLA Ops:
  5.1 7.3 %copy-start = (s32[1,32]{1,0:T(1,128)S(1)}, s32[1,32]{1,0:T(1,128)}, u32[]{:S(2)}) copy-start(s32[1,32]{1,0:T(1,128)} %param.6) | copy-start | bytes 388
  5.1 34.1 %all-to-all-start = ((bf16[32,16,1024]{2,1,0:T(8,128)(2,1)}), bf16[32,16,1024]{2,1,0:T(8,128)(2,1)S(1)}, u32[]{:S(2)}, u32[]{:S(2)}) async-start(bf16[32,16,1024]{2,1,0:T(8,128)(2,1)} %bitcast.8), calls=%async_computation | async-start | bytes 2097152 | tf_op jit(solution)/shard_map/all_to_all | solution.py:326
  12.4 1.2 %collective-permute-start = (s32[1,32]{1,0:T(1,128)S(1)}, s32[1,32]{1,0:T(1,128)S(1)}, u32[]{:S(2)}, u32[]{:S(2)}) collective-permute-start(s32[1,32]{1,0:T(1,128)S(1)} %copy-done), channel_id=1, source_target_pairs={{0,1},{1,0},{2,3},{3,2},{4,5},{5,4},{6,7},{7,6},{8,9},{9,8},{10,11... | collective-permute-start | bytes 392 | tf_op jit(solution)/shard_map/ppermute | solution.py:319
  40.1 1.4 %collective-permute-start.1 = (f32[8,32,128]{2,1,0:T(8,128)S(1)}, f32[8,32,128]{2,1,0:T(8,128)S(1)}, u32[]{:S(2)}, u32[]{:S(2)}) collective-permute-start(f32[8,32,128]{2,1,0:T(8,128)S(1)} %get-tuple-element.7), channel_id=1, source_target_pairs={{0,1},{1,0},{2,3},{3,2},{4,5},{5,4},{6,7},{7,6},{8,9},{9,8},{10,11... | collective-permute-start | bytes 393224 | tf_op jit(solution)/shard_map/ppermute | solution.py:329

commit v13 on v10

--- a/solution.py
+++ b/solution.py
@@ -62,7 +62,7 @@
     frames = SPEC + TAPS - 1
     spread = inputs * FRAME // LANES
     groups = SPEC // GROUP
-    pieces = sems.shape[0]
+    pieces = sems.shape[1]
     rows = FRAME // pieces
     last = lax.broadcasted_iota(jnp.int32, (SUB, LANES), 0) == SUB - 1
     edges = [0, GROUP // 2] + [g * GROUP + TAPS for g in range(1, groups)] + [frames]
@@ -90,7 +90,10 @@
 
     def filter_group(g, i, j):
         cols = pl.ds(j * LANES, LANES)
-        taps = [jnp.broadcast_to(taps_all[pl.ds(t, 1), cols], (SUB, LANES)) for t in range(TAPS)]
+        good = (1 - flags[i]).astype(jnp.float32)
+        taps = [
+            jnp.broadcast_to(taps_all[pl.ds(t, 1), cols] * good, (SUB, LANES)) for t in range(TAPS)
+        ]
 
         def take(b):
             first = (inputs * j + i) * PITCH + g * GROUP + b
@@ -116,34 +119,35 @@
 
     def transform(g, i):
         part = pl.ds(g * GROUP, GROUP)
-        spectra[i, :, part] = lax.dot_general(
+        spectra[g, i] = lax.dot_general(
             table[...],
             fir[i, part, :],
             (((1,), (1,)), ((), ())),
             preferred_element_type=jnp.float32,
         )
 
-    def scaled(i, piece):
-        good = (1 - flags[i]).astype(jnp.float32)
-        pairs = spectra[i, pl.ds(piece * rows, rows), :]
-        pairs = pairs.reshape(rows // (2 * SUB), 2, SUB, SPEC)
-        squares = jnp.sum(pairs * pairs, axis=1)
-        power = jnp.sum(squares, axis=2, keepdims=True) / SPEC
-        scale = good / jnp.sqrt(power + 1e-05)
-        return pairs * scale[:, None]
-
-    def pack(piece, parts):
+    def pack(g, piece):
         place = pl.ds(piece * rows, rows)
+        shape = (rows // (2 * SUB), 2, SUB, GROUP)
+        parts = [spectra[g, i, place, :].reshape(shape) for i in range(inputs)]
         for p in range(2):
             both = jnp.concatenate([part[:, p] for part in parts], axis=1)
-            result[place, pl.ds(p * SPEC, SPEC)] = both.astype(jnp.bfloat16).reshape(rows, SPEC)
-        copy = pltpu.make_async_copy(result.at[place], out_hbm.at[place], sems.at[piece])
-        copy.start()
-        return copy
+            cols = pl.ds(p * SPEC + g * GROUP, GROUP)
+            result[place, cols] = both.astype(jnp.bfloat16).reshape(rows, GROUP)
+
+    def store(g, piece):
+        copies = []
+        for p in range(2):
+            place = (pl.ds(piece * rows, rows), pl.ds(p * SPEC + g * GROUP, GROUP))
+            sem = sems.at[g, piece, p]
+            copies.append(pltpu.make_async_copy(result.at[place], out_hbm.at[place], sem))
+            copies[-1].start()
+        return copies
 
     loads[0].wait()
     convert(0)
     load_taps.wait()
+    load_flags.wait()
     loads[1].wait()
     load_table = load(table_hbm, table, chunks + 1)
     convert(1)
@@ -152,7 +156,6 @@
             filter_group(0, i, j)
     loads[2].wait()
     load_table.wait()
-    load_flags.wait()
     for i in range(inputs):
         transform(0, i)
     convert(2)
@@ -161,15 +164,16 @@
             transform(1, i - 1)
         for j in range(FRAME // LANES):
             filter_group(1, i, j)
+        if i == 0:
+            for piece in range(pieces):
+                pack(0, piece)
+    copies = []
+    for piece in range(pieces):
+        copies += store(0, piece)
     transform(1, inputs - 1)
     for piece in range(pieces):
-        part = scaled(0, piece)
-        spectra[0, pl.ds(piece * rows, rows), :] = part.reshape(rows, SPEC)
-    copies = []
-    for piece in range(pieces):
-        held_part = spectra[0, pl.ds(piece * rows, rows), :]
-        held_part = held_part.reshape(rows // (2 * SUB), 2, SUB, SPEC)
-        copies.append(pack(piece, [held_part, scaled(1, piece)]))
+        pack(1, piece)
+        copies += store(1, piece)
     for copy in copies:
         copy.wait()
 
@@ -196,10 +200,10 @@
             pltpu.VMEM(tiles.shape, tiles.dtype),
             pltpu.VMEM((inputs * FRAME // LANES * PITCH, LANES), jnp.float32),
             pltpu.VMEM((inputs, SPEC, FRAME), jnp.bfloat16),
-            pltpu.VMEM((inputs, FRAME, SPEC), jnp.float32),
+            pltpu.VMEM((SPEC // GROUP, inputs, FRAME, GROUP), jnp.float32),
             pltpu.VMEM((FRAME, inputs * SPEC), jnp.bfloat16),
             pltpu.SemaphoreType.DMA((SPEC // GROUP + 4,)),
-            pltpu.SemaphoreType.DMA((8,)),
+            pltpu.SemaphoreType.DMA((SPEC // GROUP, 4, 2)),
         ],
         cost_estimate=pl.CostEstimate(
             flops=2 * inputs * SPEC * FRAME * (FRAME + TAPS),
@@ -216,7 +220,8 @@
     held = arrived_ref.shape[0] // blocks
     first = lax.axis_index("blk") == 0
     lane = lax.broadcasted_iota(jnp.int32, (width, 2 * width), 1)
-    sign = jnp.where(lane < width, 1.0 / SPEC, -1.0 / SPEC)
+    sign = jnp.where(lane < width, 1.0, -1.0)
+    diagonal = lane == lax.broadcasted_iota(jnp.int32, (width, 2 * width), 0)
     for n in range(blocks):
         rows = pl.ds(n * held, held)
         slots[n] = jnp.dot(
@@ -234,7 +239,13 @@
         gram = lax.dot_general(
             pair, pair, (((1,), (1,)), ((), ())), preferred_element_type=jnp.float32
         )
-        part = gram[:width] * sign + pltpu.roll(gram[width:], width, 1) / SPEC
+        part = gram[:width] * sign + pltpu.roll(gram[width:], width, 1)
+        square = jnp.where(diagonal, part, 0.0)
+        across = jnp.sum(square, axis=0, keepdims=True)
+        across = across + pltpu.roll(across, width, 1)
+        down = jnp.sum(square, axis=1, keepdims=True)
+        part = part * (1.0 / jnp.sqrt(across / SPEC + 1e-05) / SPEC)
+        part = part * (1.0 / jnp.sqrt(down / SPEC + 1e-05))
         own_ref[k] = jnp.where(first, part[:block], part[block:])
         other_ref[k] = jnp.where(first, part[block:], part[:block])
 

time: 42.5 us -> 42.7 us (level)
  no operation moved by 1% of the time
where the time goes in v13:
time: 42.7 us; the launch traced here: 42.4 us
  waiting for transfers between devices  26.6 us (62%)
  Pallas kernels  7.71 us (18%)
  starting transfers between devices  7.69 us (18%)
    all_to_all x1, waiting for transfers between devices, split_channels(): lax.all_to_all(sent, axes, split_axis=0, concat_axis=0, tiled=True)  25.3 us
    all_to_all x1, starting transfers between devices, split_channels(): lax.all_to_all(sent, axes, split_axis=0, concat_axis=0, tiled=True)  7.3 us
    pallas_call x1, Pallas kernels, channelize(): pl.pallas_call(channelize_kernel, out_shape=jax.ShapeDtypeStruct((FRAME,...  4.84 us
    pallas_call x2, Pallas kernels, place(): pl.pallas_call(functools.partial(place_kernel, own=base is None), out_sha...  1.6 us
    pallas_call x1, Pallas kernels, correlate(): pl.pallas_call(correlate_kernel, out_shape=(tile, tile), in_specs=[vmem,...  1.27 us
  transfers between devices with their start and end apart: 3, of which 3 were waited for; matrix products, arithmetic and copies ran while one was open for 1% of the time, Pallas kernels for 2%

profile of v13, /device:TPU:0, one launch (start us, length us, event | category | flops | bytes accessed | tf_op | source)
XLA Modules:
  0.0 42.4 jit_solution(2193732029610177562)
XLA Ops:
  0.0 4.8 %shard_map.55 = bf16[512,1024]{1,0:T(8,128)(2,1)} custom-call(s32[2]{0:T(128)} %flags_hbm.1, bf16[4184,128]{1,0:T(8,128)(2,1)} %bitcast.9, f32[12,512]{1,0:T(8,128)} %constant.59.clone.taps_hbm, bf16[512,512]{1,0:T(8,128)(2,1)} %constant.58.clone.table_hbm), custom_call_target="tpu_custom_call" | custom-call | flops 549453824 | bytes 2097152 | tf_op jit(solution)/shard_map/pallas_call | solution.py:191
  4.8 0.0 copy-start
  4.9 7.3 %all-to-all-start = ((bf16[32,16,1024]{2,1,0:T(8,128)(2,1)}), bf16[32,16,1024]{2,1,0:T(8,128)(2,1)S(1)}, u32[]{:S(2)}, u32[]{:S(2)}) async-start(bf16[32,16,1024]{2,1,0:T(8,128)(2,1)} %bitcast.8), calls=%async_computation | async-start | bytes 2097152 | tf_op jit(solution)/shard_map/all_to_all | solution.py:330
  12.2 0.0 copy-done
  12.2 0.3 collective-permute-start
  12.5 0.1 add.72
  12.6 0.8 %collective-permute-done = s32[1,32]{1,0:T(1,128)S(1)} collective-permute-done((s32[1,32]{1,0:T(1,128)S(1)}, s32[1,32]{1,0:T(1,128)S(1)}, u32[]{:S(2)}, u32[]{:S(2)}) %collective-permute-start) | collective-permute-done | bytes 160 | tf_op jit(solution)/shard_map/ppermute | solution.py:323
  13.4 0.1 add.70
  13.5 0.1 fusion.pick_ref
  13.6 25.3 %all-to-all-done = bf16[32,16,1024]{2,1,0:T(8,128)(2,1)S(1)} async-done(((bf16[32,16,1024]{2,1,0:T(8,128)(2,1)}), bf16[32,16,1024]{2,1,0:T(8,128)(2,1)S(1)}, u32[]{:S(2)}, u32[]{:S(2)}) %all-to-all-start) | async-done | bytes 1048608 | tf_op jit(solution)/shard_map/all_to_all | solution.py:330
  39.0 1.3 %shard_map.56 = (f32[8,32,128]{2,1,0:T(8,128)S(1)}, f32[8,32,128]{2,1,0:T(8,128)S(1)}) custom-call(bf16[2,256,256]{2,1,0:T(8,128)(2,1)S(1)} %fusion.pick_ref, bf16[512,1024]{1,0:T(8,128)(2,1)S(1)} %bitcast.7), custom_call_target="tpu_custom_call" | custom-call | flops 268435456 | bytes 2097152 | tf_op jit(solution)/shard_map/pallas_call | solution.py:268
  40.2 0.1 collective-permute-start.1
  40.3 0.8 %shard_map.57.refs_0_ = f32[16,2,32,64]{3,2,1,0:T(8,128)} custom-call(f32[8,32,128]{2,1,0:T(8,128)S(1)} %get-tuple-element.8.packed_ref), custom_call_target="tpu_custom_call" | custom-call | bytes 262144 | tf_op jit(solution)/shard_map/pallas_call | solution.py:303
  41.1 0.5 %collective-permute-done.1.packed_ref = f32[8,32,128]{2,1,0:T(8,128)S(1)} collective-permute-done((f32[8,32,128]{2,1,0:T(8,128)S(1)}, f32[8,32,128]{2,1,0:T(8,128)S(1)}, u32[]{:S(2)}, u32[]{:S(2)}) %collective-permute-start.1) | collective-permute-done | bytes 131104 | tf_op jit(solution)/shard_map/ppermute | solution.py:333
  41.6 0.8 %shard_map.58 = f32[16,2,32,64]{3,2,1,0:T(8,128)} custom-call(f32[8,32,128]{2,1,0:T(8,128)S(1)} %collective-permute-done.1.packed_ref, f32[16,2,32,64]{3,2,1,0:T(8,128)} %shard_map.57.refs_0_), custom_call_target="tpu_custom_call", output_to_operand_aliasing={{}: (1, {})} | custom-call | bytes 262144 | tf_op jit(solution)/shard_map/pallas_call | solution.py:303
  (4 shorter events, 0.0 us)
Async XLA Ops:
  4.8 7.3 %copy-start = (s32[1,32]{1,0:T(1,128)S(1)}, s32[1,32]{1,0:T(1,128)}, u32[]{:S(2)}) copy-start(s32[1,32]{1,0:T(1,128)} %param.6) | copy-start | bytes 388
  4.9 34.1 %all-to-all-start = ((bf16[32,16,1024]{2,1,0:T(8,128)(2,1)}), bf16[32,16,1024]{2,1,0:T(8,128)(2,1)S(1)}, u32[]{:S(2)}, u32[]{:S(2)}) async-start(bf16[32,16,1024]{2,1,0:T(8,128)(2,1)} %bitcast.8), calls=%async_computation | async-start | bytes 2097152 | tf_op jit(solution)/shard_map/all_to_all | solution.py:330
  12.2 1.2 %collective-permute-start = (s32[1,32]{1,0:T(1,128)S(1)}, s32[1,32]{1,0:T(1,128)S(1)}, u32[]{:S(2)}, u32[]{:S(2)}) collective-permute-start(s32[1,32]{1,0:T(1,128)S(1)} %copy-done), channel_id=1, source_target_pairs={{0,1},{1,0},{2,3},{3,2},{4,5},{5,4},{6,7},{7,6},{8,9},{9,8},{10,11... | collective-permute-start | bytes 392 | tf_op jit(solution)/shard_map/ppermute | solution.py:323
  40.2 1.4 %collective-permute-start.1 = (f32[8,32,128]{2,1,0:T(8,128)S(1)}, f32[8,32,128]{2,1,0:T(8,128)S(1)}, u32[]{:S(2)}, u32[]{:S(2)}) collective-permute-start(f32[8,32,128]{2,1,0:T(8,128)S(1)} %get-tuple-element.7), channel_id=1, source_target_pairs={{0,1},{1,0},{2,3},{3,2},{4,5},{5,4},{6,7},{7,6},{8,9},{9,8},{10,11... | collective-permute-start | bytes 393224 | tf_op jit(solution)/shard_map/ppermute | solution.py:333

commit v14 on v12

--- a/solution.py
+++ b/solution.py
@@ -187,6 +187,7 @@
     tiles = tiles.transpose(1, 0, 2)
     tiles = tiles.reshape(-1, LANES)
     table = twiddle().reshape(far, near, blocks, SUB, 2, FRAME).transpose(2, 1, 0, 4, 3, 5)
+    table = table.reshape(far * near * blocks, 2 * SUB, FRAME)[::-1]
     table = jnp.asarray(table.reshape(FRAME, FRAME), dtype=jnp.bfloat16)
     taps = jnp.asarray(prototype())
     hbm = pl.BlockSpec(memory_space=pltpu.HBM)
@@ -225,7 +226,7 @@
     lane = lax.broadcasted_iota(jnp.int32, (width, 2 * width), 1)
     sign = jnp.where(lane < width, 1.0 / SPEC, -1.0 / SPEC)
     for n in range(blocks):
-        rows = pl.ds(n * held, held)
+        rows = pl.ds((blocks - 1 - n) * held, held)
         slots[n] = jnp.dot(
             pick_ref[n], arrived_ref[rows, :], preferred_element_type=jnp.float32
         ).astype(jnp.bfloat16)
@@ -249,7 +250,7 @@
 def picks(orders, inputs, far, near, share):
     blocks, block = orders.shape
     device, held = orders // inputs, orders % inputs
-    place = (device % near) * far + device // near
+    place = far * near - 1 - ((device % near) * far + device // near)
     start = ((place * inputs + held) * share)[:, None, :]
     chan = jnp.arange(share, dtype=jnp.int32)[:, None]
     target = (start + chan).reshape(blocks, share * block, 1)
@@ -323,7 +324,10 @@
         jnp.concatenate([partner, slot_order]),
     )
     sent = channelize(samples, flags, far, near, blocks)
-    arrived = lax.all_to_all(sent, axes, split_axis=0, concat_axis=0, tiled=True)
+    order = list(reversed(range(blocks * near * far)))
+    arrived = lax.all_to_all(
+        sent, axes, split_axis=0, concat_axis=0, axis_index_groups=[order], tiled=True
+    )
     pick = picks(orders, inputs, far, near, share)
     own, other = correlate(arrived, pick, share, block)
     received = lax.ppermute(other, "blk", SWAP)

time: 42.5 us -> 42 us (0.988)
  waiting for transfers between devices: 26.6 us -> 25.5 us
  starting transfers between devices: 7.69 us -> 8.33 us
    all_to_all x1, waiting for transfers between devices: 25.3 us -> 24.5 us  [split_channels(): lax.all_to_all(sent, axes, split_axis=0, concat_axis=0, axis_index_groups...]
    ppermute x1, starting transfers between devices: 0.07 us -> 0.71 us  [split_channels(): received = lax.ppermute(other, 'blk', SWAP)]
where the time goes in v14:
time: 42 us; the launch traced here: 41.8 us
  waiting for transfers between devices  25.5 us (61%)
  starting transfers between devices  8.33 us (20%)
  Pallas kernels  7.57 us (18%)
    all_to_all x1, waiting for transfers between devices, split_channels(): lax.all_to_all(sent, axes, split_axis=0, concat_axis=0, axis_index_groups...  24.5 us
    all_to_all x1, starting transfers between devices, split_channels(): lax.all_to_all(sent, axes, split_axis=0, concat_axis=0, axis_index_groups...  7.3 us
    pallas_call x1, Pallas kernels, channelize(): pl.pallas_call(channelize_kernel, out_shape=jax.ShapeDtypeStruct((FRAME,...  5.1 us
    pallas_call x2, Pallas kernels, place(): pl.pallas_call(functools.partial(place_kernel, own=base is None), out_sha...  1.59 us
    pallas_call x1, Pallas kernels, correlate(): pl.pallas_call(correlate_kernel, out_shape=(tile, tile), in_specs=[vmem,...  0.87 us
  transfers between devices with their start and end apart: 3, of which 3 were waited for; matrix products, arithmetic and copies ran while one was open for 1% of the time, Pallas kernels for 2%

profile of v14, /device:TPU:0, one launch (start us, length us, event | category | flops | bytes accessed | tf_op | source)
XLA Modules:
  0.0 41.8 jit_solution(4949814999990805998)
XLA Ops:
  0.0 5.1 %shard_map.55 = bf16[512,1024]{1,0:T(8,128)(2,1)} custom-call(s32[2]{0:T(128)} %flags_hbm.1, bf16[4184,128]{1,0:T(8,128)(2,1)} %bitcast.9, f32[12,512]{1,0:T(8,128)} %constant.61.clone.taps_hbm, bf16[512,512]{1,0:T(8,128)(2,1)} %constant.60.clone.table_hbm), custom_call_target="tpu_custom_call" | custom-call | flops 549453824 | bytes 2097152 | tf_op jit(solution)/shard_map/pallas_call | solution.py:194
  5.1 0.0 copy-start
  5.1 7.3 %all-to-all-start = ((bf16[32,16,1024]{2,1,0:T(8,128)(2,1)}), bf16[32,16,1024]{2,1,0:T(8,128)(2,1)S(1)}, u32[]{:S(2)}, u32[]{:S(2)}) async-start(bf16[32,16,1024]{2,1,0:T(8,128)(2,1)} %bitcast.8), calls=%async_computation | async-start | bytes 2097152 | tf_op jit(solution)/shard_map/all_to_all | solution.py:328
  12.4 0.0 copy-done
  12.4 0.3 collective-permute-start
  12.8 0.1 add.72
  12.8 0.8 %collective-permute-done = s32[1,32]{1,0:T(1,128)S(1)} collective-permute-done((s32[1,32]{1,0:T(1,128)S(1)}, s32[1,32]{1,0:T(1,128)S(1)}, u32[]{:S(2)}, u32[]{:S(2)}) %collective-permute-start) | collective-permute-done | bytes 160 | tf_op jit(solution)/shard_map/ppermute | solution.py:320
  13.7 0.1 add.70
  13.8 0.1 fusion.pick_ref
  13.9 24.5 %all-to-all-done = bf16[32,16,1024]{2,1,0:T(8,128)(2,1)S(1)} async-done(((bf16[32,16,1024]{2,1,0:T(8,128)(2,1)}), bf16[32,16,1024]{2,1,0:T(8,128)(2,1)S(1)}, u32[]{:S(2)}, u32[]{:S(2)}) %all-to-all-start) | async-done | bytes 1048608 | tf_op jit(solution)/shard_map/all_to_all | solution.py:328
  38.4 0.9 %shard_map.56 = (f32[8,32,128]{2,1,0:T(8,128)S(1)}, f32[8,32,128]{2,1,0:T(8,128)S(1)}) custom-call(bf16[2,256,256]{2,1,0:T(8,128)(2,1)S(1)} %fusion.pick_ref, bf16[512,1024]{1,0:T(8,128)(2,1)S(1)} %bitcast.7), custom_call_target="tpu_custom_call" | custom-call | flops 268435456 | bytes 2097152 | tf_op jit(solution)/shard_map/pallas_call | solution.py:265
  39.3 0.7 %collective-permute-start.1 = (f32[8,32,128]{2,1,0:T(8,128)S(1)}, f32[8,32,128]{2,1,0:T(8,128)S(1)}, u32[]{:S(2)}, u32[]{:S(2)}) collective-permute-start(f32[8,32,128]{2,1,0:T(8,128)S(1)} %get-tuple-element.7), channel_id=1, source_target_pairs={{0,1},{1,0},{2,3},{3,2},{4,5},{5,4},{6,7},{7,6},{8,9},{9,8},{10,11... | collective-permute-start | bytes 393224 | tf_op jit(solution)/shard_map/ppermute | solution.py:333
  40.0 0.8 %shard_map.57.refs_0_ = f32[16,2,32,64]{3,2,1,0:T(8,128)} custom-call(f32[8,32,128]{2,1,0:T(8,128)S(1)} %get-tuple-element.8.packed_ref), custom_call_target="tpu_custom_call" | custom-call | bytes 262144 | tf_op jit(solution)/shard_map/pallas_call | solution.py:300
  40.8 0.2 collective-permute-done.1.packed_ref
  41.0 0.8 %shard_map.58 = f32[16,2,32,64]{3,2,1,0:T(8,128)} custom-call(f32[8,32,128]{2,1,0:T(8,128)S(1)} %collective-permute-done.1.packed_ref, f32[16,2,32,64]{3,2,1,0:T(8,128)} %shard_map.57.refs_0_), custom_call_target="tpu_custom_call", output_to_operand_aliasing={{}: (1, {})} | custom-call | bytes 262144 | tf_op jit(solution)/shard_map/pallas_call | solution.py:300
  (4 shorter events, 0.0 us)
Async XLA Ops:
  5.1 7.3 %copy-start = (s32[1,32]{1,0:T(1,128)S(1)}, s32[1,32]{1,0:T(1,128)}, u32[]{:S(2)}) copy-start(s32[1,32]{1,0:T(1,128)} %param.6) | copy-start | bytes 388
  5.1 33.3 %all-to-all-start = ((bf16[32,16,1024]{2,1,0:T(8,128)(2,1)}), bf16[32,16,1024]{2,1,0:T(8,128)(2,1)S(1)}, u32[]{:S(2)}, u32[]{:S(2)}) async-start(bf16[32,16,1024]{2,1,0:T(8,128)(2,1)} %bitcast.8), calls=%async_computation | async-start | bytes 2097152 | tf_op jit(solution)/shard_map/all_to_all | solution.py:328
  12.4 1.2 %collective-permute-start = (s32[1,32]{1,0:T(1,128)S(1)}, s32[1,32]{1,0:T(1,128)S(1)}, u32[]{:S(2)}, u32[]{:S(2)}) collective-permute-start(s32[1,32]{1,0:T(1,128)S(1)} %copy-done), channel_id=1, source_target_pairs={{0,1},{1,0},{2,3},{3,2},{4,5},{5,4},{6,7},{7,6},{8,9},{9,8},{10,11... | collective-permute-start | bytes 392 | tf_op jit(solution)/shard_map/ppermute | solution.py:320
  39.3 1.7 %collective-permute-start.1 = (f32[8,32,128]{2,1,0:T(8,128)S(1)}, f32[8,32,128]{2,1,0:T(8,128)S(1)}, u32[]{:S(2)}, u32[]{:S(2)}) collective-permute-start(f32[8,32,128]{2,1,0:T(8,128)S(1)} %get-tuple-element.7), channel_id=1, source_target_pairs={{0,1},{1,0},{2,3},{3,2},{4,5},{5,4},{6,7},{7,6},{8,9},{9,8},{10,11... | collective-permute-start | bytes 393224 | tf_op jit(solution)/shard_map/ppermute | solution.py:333

commit v15 on v14

--- a/solution.py
+++ b/solution.py
@@ -8,7 +8,6 @@
 from jax.experimental import pallas as pl
 from jax.experimental.pallas import tpu as pltpu
 from jax.experimental.layout import Layout, with_layout_constraint
-from jax.sharding import Mesh
 from jax.sharding import PartitionSpec as P
 
 CH = 256
@@ -21,7 +20,6 @@
 STEP = GROUP // SUB
 STRIDE = STEP + 1
 PITCH = SPEC + 25
-FAR = 4
 SWAP = [(0, 1), (1, 0)]
 VMEM_LIMIT = 40 * 1024 * 1024
 
@@ -180,14 +178,13 @@
         copy.wait()
 
 
-def channelize(samples, flags, far, near, blocks):
+def channelize(samples, flags, order):
     inputs = samples.shape[0]
     tiles = samples.reshape(inputs, -1, LANES)
     tiles = with_layout_constraint(tiles, Layout(major_to_minor=(1, 0, 2)))
     tiles = tiles.transpose(1, 0, 2)
     tiles = tiles.reshape(-1, LANES)
-    table = twiddle().reshape(far, near, blocks, SUB, 2, FRAME).transpose(2, 1, 0, 4, 3, 5)
-    table = table.reshape(far * near * blocks, 2 * SUB, FRAME)[::-1]
+    table = twiddle().reshape(len(order), SUB, 2, FRAME)[np.asarray(order)].transpose(0, 2, 1, 3)
     table = jnp.asarray(table.reshape(FRAME, FRAME), dtype=jnp.bfloat16)
     taps = jnp.asarray(prototype())
     hbm = pl.BlockSpec(memory_space=pltpu.HBM)
@@ -217,18 +214,19 @@
     )(flags, tiles, taps, table)
 
 
-def correlate_kernel(pick_ref, arrived_ref, own_ref, other_ref, slots):
+def correlate_kernel(pick_ref, arrived_ref, own_ref, other_ref, slots, *, order):
     share, block, _ = own_ref.shape
     blocks = pick_ref.shape[0]
     width = blocks * block
-    held = arrived_ref.shape[0] // blocks
+    held = arrived_ref.shape[0] // len(order)
     first = lax.axis_index("blk") == 0
     lane = lax.broadcasted_iota(jnp.int32, (width, 2 * width), 1)
     sign = jnp.where(lane < width, 1.0 / SPEC, -1.0 / SPEC)
     for n in range(blocks):
-        rows = pl.ds((blocks - 1 - n) * held, held)
+        places = [place for place, device in enumerate(order) if device % blocks == n]
+        rows = [arrived_ref[pl.ds(place * held, held), :] for place in places]
         slots[n] = jnp.dot(
-            pick_ref[n], arrived_ref[rows, :], preferred_element_type=jnp.float32
+            pick_ref[n], jnp.concatenate(rows, axis=0), preferred_element_type=jnp.float32
         ).astype(jnp.bfloat16)
     for k in range(share):
         pair = jnp.concatenate(
@@ -247,23 +245,26 @@
         other_ref[k] = jnp.where(first, part[block:], part[:block])
 
 
-def picks(orders, inputs, far, near, share):
+def picks(orders, inputs, order, share):
     blocks, block = orders.shape
     device, held = orders // inputs, orders % inputs
-    place = far * near - 1 - ((device % near) * far + device // near)
+    rank = [np.argsort([d for d in order if d % blocks == n]) for n in range(blocks)]
+    known = jnp.asarray(np.stack(rank), dtype=jnp.int32)
+    match = device[:, :, None] == jnp.arange(known.shape[1], dtype=jnp.int32)
+    place = jnp.sum(jnp.where(match, known[:, None, :], 0), axis=2)
     start = ((place * inputs + held) * share)[:, None, :]
     chan = jnp.arange(share, dtype=jnp.int32)[:, None]
     target = (start + chan).reshape(blocks, share * block, 1)
-    column = lax.broadcasted_iota(jnp.int32, (1, 1, far * near * inputs * share), 2)
+    column = lax.broadcasted_iota(jnp.int32, (1, 1, known.shape[1] * inputs * share), 2)
     return (column == target).astype(jnp.bfloat16)
 
 
-def correlate(arrived, pick, share, block):
+def correlate(arrived, pick, order, share, block):
     blocks = pick.shape[0]
     vmem = pl.BlockSpec(memory_space=pltpu.VMEM)
     tile = jax.ShapeDtypeStruct((share, block, 2 * blocks * block), jnp.float32)
     return pl.pallas_call(
-        correlate_kernel,
+        functools.partial(correlate_kernel, order=order),
         out_shape=(tile, tile),
         in_specs=[vmem, vmem],
         out_specs=(vmem, vmem),
@@ -312,10 +313,11 @@
     )(packed, *([] if base is None else [base]))
 
 
-def split_channels(far, near, blocks, samples, slot_order, flags):
-    share = CH // (far * near * blocks)
+def split_channels(freq, blocks, samples, slot_order, flags):
+    share = CH // (freq * blocks)
     inputs, block = samples.shape[0], slot_order.shape[1]
-    axes = ("blk", "near", "far")
+    axes = ("freq", "blk")
+    order = list(reversed(range(freq * blocks)))
     me = lax.axis_index("blk").astype(jnp.int32)
     partner = lax.ppermute(slot_order, "blk", SWAP)
     orders = jnp.where(
@@ -323,13 +325,12 @@
         jnp.concatenate([slot_order, partner]),
         jnp.concatenate([partner, slot_order]),
     )
-    sent = channelize(samples, flags, far, near, blocks)
-    order = list(reversed(range(blocks * near * far)))
+    sent = channelize(samples, flags, order)
     arrived = lax.all_to_all(
         sent, axes, split_axis=0, concat_axis=0, axis_index_groups=[order], tiled=True
     )
-    pick = picks(orders, inputs, far, near, share)
-    own, other = correlate(arrived, pick, share, block)
+    pick = picks(orders, inputs, order, share)
+    own, other = correlate(arrived, pick, order, share, block)
     received = lax.ppermute(other, "blk", SWAP)
     return place(received, blocks, place(own, blocks))
 
@@ -350,7 +351,7 @@
     power = jnp.sum(squares.reshape(CH, 2, inputs), axis=1) / SPEC
     scale = good[None, :] / jnp.sqrt(power + 1e-05)
     quantized = (spectra * jnp.repeat(scale, 2, axis=0)[:, :, None]).astype(jnp.bfloat16)
-    arrived = lax.all_to_all(quantized, ("far", "near"), split_axis=0, concat_axis=1, tiled=True)
+    arrived = lax.all_to_all(quantized, "freq", split_axis=0, concat_axis=1, tiled=True)
     share = CH // freq
     block = slot_order.shape[1]
     own = jnp.take(arrived.reshape(share, 2, block, SPEC), slot_order[0], axis=2)
@@ -363,16 +364,12 @@
 
 def solution(mesh):
     freq, blocks = mesh.shape["freq"], mesh.shape["blk"]
-    far = math.gcd(freq, FAR)
-    near = freq // far
-    split = Mesh(mesh.devices.reshape(far, near, blocks), ("far", "near", "blk"))
 
     def body(samples, slot_order, flags):
         if blocks == 2 and CH == SUB * freq * blocks:
-            return split_channels(far, near, blocks, samples, slot_order, flags)
+            return split_channels(freq, blocks, samples, slot_order, flags)
         return gather_blocks(freq, samples, slot_order, flags)
 
-    held = ("blk", "far", "near")
-    in_specs = (P(held, None), P("blk", None), P(held))
-    out_specs = P(("far", "near"), None, "blk", None)
-    return jax.shard_map(body, mesh=split, in_specs=in_specs, out_specs=out_specs, check_vma=False)
+    in_specs = (P(("blk", "freq"), None), P("blk", None), P(("blk", "freq")))
+    out_specs = P("freq", None, "blk", None)
+    return jax.shard_map(body, mesh=mesh, in_specs=in_specs, out_specs=out_specs, check_vma=False)

time: 42 us -> 43 us (1.024)
  starting transfers between devices: 8.33 us -> 8.99 us
    ppermute x1, starting transfers between devices: 0.71 us -> 1.37 us  [split_channels(): received = lax.ppermute(other, 'blk', SWAP)]
where the time goes in v15:
time: 43 us; the launch traced here: 42.7 us
  waiting for transfers between devices  25.6 us (60%)
  starting transfers between devices  8.99 us (21%)
  Pallas kernels  7.56 us (18%)
    all_to_all x1, waiting for transfers between devices, split_channels(): lax.all_to_all(sent, axes, split_axis=0, concat_axis=0, axis_index_groups...  24.7 us
    all_to_all x1, starting transfers between devices, split_channels(): lax.all_to_all(sent, axes, split_axis=0, concat_axis=0, axis_index_groups...  7.3 us
    pallas_call x1, Pallas kernels, channelize(): pl.pallas_call(channelize_kernel, out_shape=jax.ShapeDtypeStruct((FRAME,...  5.09 us
    pallas_call x2, Pallas kernels, place(): pl.pallas_call(functools.partial(place_kernel, own=base is None), out_sha...  1.59 us
    ppermute x1, starting transfers between devices, split_channels(): received = lax.ppermute(other, 'blk', SWAP)  1.37 us
    pallas_call x1, Pallas kernels, correlate(): pl.pallas_call(functools.partial(correlate_kernel, order=order), out_shap...  0.87 us
  transfers between devices with their start and end apart: 3, of which 3 were waited for; matrix products, arithmetic and copies ran while one was open for 1% of the time, Pallas kernels for 2%

profile of v15, /device:TPU:0, one launch (start us, length us, event | category | flops | bytes accessed | tf_op | source)
XLA Modules:
  0.0 42.7 jit_solution(7242881278177374788)
XLA Ops:
  0.0 5.1 %shard_map.64 = bf16[512,1024]{1,0:T(8,128)(2,1)} custom-call(s32[2]{0:T(128)} %flags_hbm.1, bf16[4184,128]{1,0:T(8,128)(2,1)} %bitcast.9, f32[12,512]{1,0:T(8,128)} %constant.41.clone.taps_hbm, bf16[512,512]{1,0:T(8,128)(2,1)} %constant.40.clone.table_hbm), custom_call_target="tpu_custom_call" | custom-call | flops 549453824 | bytes 2097152 | tf_op jit(solution)/shard_map/pallas_call | solution.py:191
  5.1 0.0 copy-start
  5.1 0.0 copy-start.1
  5.1 7.3 %all-to-all-start = ((bf16[32,16,1024]{2,1,0:T(8,128)(2,1)}), bf16[32,16,1024]{2,1,0:T(8,128)(2,1)S(1)}, u32[]{:S(2)}, u32[]{:S(2)}) async-start(bf16[32,16,1024]{2,1,0:T(8,128)(2,1)} %bitcast.8), calls=%async_computation | async-start | bytes 2097152 | tf_op jit(solution)/shard_map/all_to_all | solution.py:329
  12.4 0.0 copy-done
  12.4 0.3 collective-permute-start
  12.8 0.1 add.50
  12.8 0.8 %collective-permute-done = s32[1,32]{1,0:T(1,128)S(1)} collective-permute-done((s32[1,32]{1,0:T(1,128)S(1)}, s32[1,32]{1,0:T(1,128)S(1)}, u32[]{:S(2)}, u32[]{:S(2)}) %collective-permute-start) | collective-permute-done | bytes 160 | tf_op jit(solution)/shard_map/ppermute | solution.py:322
  13.6 0.0 copy-done.1
  13.7 0.1 select_reduce_fusion
  13.8 0.1 add.48
  13.9 0.1 fusion.pick_ref
  14.0 24.7 %all-to-all-done = bf16[32,16,1024]{2,1,0:T(8,128)(2,1)S(1)} async-done(((bf16[32,16,1024]{2,1,0:T(8,128)(2,1)}), bf16[32,16,1024]{2,1,0:T(8,128)(2,1)S(1)}, u32[]{:S(2)}, u32[]{:S(2)}) %all-to-all-start) | async-done | bytes 1048608 | tf_op jit(solution)/shard_map/all_to_all | solution.py:329
  38.7 0.9 %shard_map.65 = (f32[8,32,128]{2,1,0:T(8,128)S(1)}, f32[8,32,128]{2,1,0:T(8,128)S(1)}) custom-call(bf16[2,256,256]{2,1,0:T(8,128)(2,1)S(1)} %fusion.pick_ref, bf16[512,1024]{1,0:T(8,128)(2,1)S(1)} %bitcast.7), custom_call_target="tpu_custom_call" | custom-call | flops 268435456 | bytes 2097152 | tf_op jit(solution)/shard_map/pallas_call | solution.py:266
  39.6 1.4 %collective-permute-start.1 = (f32[8,32,128]{2,1,0:T(8,128)S(1)}, f32[8,32,128]{2,1,0:T(8,128)S(1)}, u32[]{:S(2)}, u32[]{:S(2)}) collective-permute-start(f32[8,32,128]{2,1,0:T(8,128)S(1)} %get-tuple-element.7), channel_id=1, source_target_pairs={{0,1},{1,0},{2,3},{3,2},{4,5},{5,4},{6,7},{7,6},{8,9},{9,8},{10,11... | collective-permute-start | bytes 393224 | tf_op jit(solution)/shard_map/ppermute | solution.py:334
  40.9 0.8 %shard_map.66.refs_0_ = f32[16,2,32,64]{3,2,1,0:T(8,128)} custom-call(f32[8,32,128]{2,1,0:T(8,128)S(1)} %get-tuple-element.8.packed_ref), custom_call_target="tpu_custom_call" | custom-call | bytes 262144 | tf_op jit(solution)/shard_map/pallas_call | solution.py:301
  41.7 0.2 collective-permute-done.1.packed_ref
  41.9 0.8 %shard_map.67 = f32[16,2,32,64]{3,2,1,0:T(8,128)} custom-call(f32[8,32,128]{2,1,0:T(8,128)S(1)} %collective-permute-done.1.packed_ref, f32[16,2,32,64]{3,2,1,0:T(8,128)} %shard_map.66.refs_0_), custom_call_target="tpu_custom_call", output_to_operand_aliasing={{}: (1, {})} | custom-call | bytes 262144 | tf_op jit(solution)/shard_map/pallas_call | solution.py:301
  (5 shorter events, 0.1 us)
Async XLA Ops:
  5.1 7.3 %copy-start = (s32[1,32]{1,0:T(1,128)S(1)}, s32[1,32]{1,0:T(1,128)}, u32[]{:S(2)}) copy-start(s32[1,32]{1,0:T(1,128)} %param.7) | copy-start | bytes 388
  5.1 8.5 %copy-start.1 = (s32[2,16]{1,0:T(2,128)S(1)}, s32[2,16]{1,0:T(2,128)}, u32[]{:S(2)}) copy-start(s32[2,16]{1,0:T(2,128)} %constant.42.clone) | copy-start | bytes 388
  5.1 33.5 %all-to-all-start = ((bf16[32,16,1024]{2,1,0:T(8,128)(2,1)}), bf16[32,16,1024]{2,1,0:T(8,128)(2,1)S(1)}, u32[]{:S(2)}, u32[]{:S(2)}) async-start(bf16[32,16,1024]{2,1,0:T(8,128)(2,1)} %bitcast.8), calls=%async_computation | async-start | bytes 2097152 | tf_op jit(solution)/shard_map/all_to_all | solution.py:329
  12.4 1.2 %collective-permute-start = (s32[1,32]{1,0:T(1,128)S(1)}, s32[1,32]{1,0:T(1,128)S(1)}, u32[]{:S(2)}, u32[]{:S(2)}) collective-permute-start(s32[1,32]{1,0:T(1,128)S(1)} %copy-done), channel_id=1, source_target_pairs={{0,1},{1,0},{2,3},{3,2},{4,5},{5,4},{6,7},{7,6},{8,9},{9,8},{10,11... | collective-permute-start | bytes 392 | tf_op jit(solution)/shard_map/ppermute | solution.py:322
  39.6 2.4 %collective-permute-start.1 = (f32[8,32,128]{2,1,0:T(8,128)S(1)}, f32[8,32,128]{2,1,0:T(8,128)S(1)}, u32[]{:S(2)}, u32[]{:S(2)}) collective-permute-start(f32[8,32,128]{2,1,0:T(8,128)S(1)} %get-tuple-element.7), channel_id=1, source_target_pairs={{0,1},{1,0},{2,3},{3,2},{4,5},{5,4},{6,7},{7,6},{8,9},{9,8},{10,11... | collective-permute-start | bytes 393224 | tf_op jit(solution)/shard_map/ppermute | solution.py:334

commit v16 on v15

--- a/solution.py
+++ b/solution.py
@@ -317,7 +317,8 @@
     share = CH // (freq * blocks)
     inputs, block = samples.shape[0], slot_order.shape[1]
     axes = ("freq", "blk")
-    order = list(reversed(range(freq * blocks)))
+    plane = freq * blocks // 4
+    order = [*reversed(range(plane, freq * blocks)), *range(plane)]
     me = lax.axis_index("blk").astype(jnp.int32)
     partner = lax.ppermute(slot_order, "blk", SWAP)
     orders = jnp.where(

time: 43 us -> 43.4 us (level)
  waiting for transfers between devices: 25.6 us -> 27.1 us
  starting transfers between devices: 8.99 us -> 7.98 us
    all_to_all x1, waiting for transfers between devices: 24.7 us -> 26 us  [split_channels(): lax.all_to_all(sent, axes, split_axis=0, concat_axis=0, axis_index_groups...]
    ppermute x1, starting transfers between devices: 1.37 us -> 0.36 us  [split_channels(): received = lax.ppermute(other, 'blk', SWAP)]
where the time goes in v16:
time: 43.4 us; the launch traced here: 43.1 us
  waiting for transfers between devices  27.1 us (62%)
  starting transfers between devices  7.98 us (18%)
  Pallas kernels  7.56 us (17%)
    all_to_all x1, waiting for transfers between devices, split_channels(): lax.all_to_all(sent, axes, split_axis=0, concat_axis=0, axis_index_groups...  26 us
    all_to_all x1, starting transfers between devices, split_channels(): lax.all_to_all(sent, axes, split_axis=0, concat_axis=0, axis_index_groups...  7.3 us
    pallas_call x1, Pallas kernels, channelize(): pl.pallas_call(channelize_kernel, out_shape=jax.ShapeDtypeStruct((FRAME,...  5.09 us
    pallas_call x2, Pallas kernels, place(): pl.pallas_call(functools.partial(place_kernel, own=base is None), out_sha...  1.6 us
    pallas_call x1, Pallas kernels, correlate(): pl.pallas_call(functools.partial(correlate_kernel, order=order), out_shap...  0.87 us
  transfers between devices with their start and end apart: 3, of which 3 were waited for; matrix products, arithmetic and copies ran while one was open for 1% of the time, Pallas kernels for 2%

profile of v16, /device:TPU:0, one launch (start us, length us, event | category | flops | bytes accessed | tf_op | source)
XLA Modules:
  0.0 43.1 jit_solution(6113388578644432174)
XLA Ops:
  0.0 5.1 %shard_map.64 = bf16[512,1024]{1,0:T(8,128)(2,1)} custom-call(s32[2]{0:T(128)} %flags_hbm.1, bf16[4184,128]{1,0:T(8,128)(2,1)} %bitcast.9, f32[12,512]{1,0:T(8,128)} %constant.41.clone.taps_hbm, bf16[512,512]{1,0:T(8,128)(2,1)} %constant.40.clone.table_hbm), custom_call_target="tpu_custom_call" | custom-call | flops 549453824 | bytes 2097152 | tf_op jit(solution)/shard_map/pallas_call | solution.py:191
  5.1 0.0 copy-start
  5.1 0.0 copy-start.1
  5.1 7.3 %all-to-all-start = ((bf16[32,16,1024]{2,1,0:T(8,128)(2,1)}), bf16[32,16,1024]{2,1,0:T(8,128)(2,1)S(1)}, u32[]{:S(2)}, u32[]{:S(2)}) async-start(bf16[32,16,1024]{2,1,0:T(8,128)(2,1)} %bitcast.8), calls=%async_computation | async-start | bytes 2097152 | tf_op jit(solution)/shard_map/all_to_all | solution.py:330
  12.4 0.0 copy-done
  12.4 0.3 collective-permute-start
  12.8 0.1 add.50
  12.8 0.8 %collective-permute-done = s32[1,32]{1,0:T(1,128)S(1)} collective-permute-done((s32[1,32]{1,0:T(1,128)S(1)}, s32[1,32]{1,0:T(1,128)S(1)}, u32[]{:S(2)}, u32[]{:S(2)}) %collective-permute-start) | collective-permute-done | bytes 160 | tf_op jit(solution)/shard_map/ppermute | solution.py:323
  13.6 0.0 copy-done.1
  13.7 0.1 select_reduce_fusion
  13.8 0.1 add.48
  13.9 0.1 fusion.pick_ref
  14.0 26.0 %all-to-all-done = bf16[32,16,1024]{2,1,0:T(8,128)(2,1)S(1)} async-done(((bf16[32,16,1024]{2,1,0:T(8,128)(2,1)}), bf16[32,16,1024]{2,1,0:T(8,128)(2,1)S(1)}, u32[]{:S(2)}, u32[]{:S(2)}) %all-to-all-start) | async-done | bytes 1048608 | tf_op jit(solution)/shard_map/all_to_all | solution.py:330
  40.0 0.9 %shard_map.65 = (f32[8,32,128]{2,1,0:T(8,128)S(1)}, f32[8,32,128]{2,1,0:T(8,128)S(1)}) custom-call(bf16[2,256,256]{2,1,0:T(8,128)(2,1)S(1)} %fusion.pick_ref, bf16[512,1024]{1,0:T(8,128)(2,1)S(1)} %bitcast.7), custom_call_target="tpu_custom_call" | custom-call | flops 268435456 | bytes 2097152 | tf_op jit(solution)/shard_map/pallas_call | solution.py:266
  40.9 0.4 collective-permute-start.1
  41.3 0.8 %shard_map.66.refs_0_ = f32[16,2,32,64]{3,2,1,0:T(8,128)} custom-call(f32[8,32,128]{2,1,0:T(8,128)S(1)} %get-tuple-element.8.packed_ref), custom_call_target="tpu_custom_call" | custom-call | bytes 262144 | tf_op jit(solution)/shard_map/pallas_call | solution.py:301
  42.1 0.2 collective-permute-done.1.packed_ref
  42.3 0.8 %shard_map.67 = f32[16,2,32,64]{3,2,1,0:T(8,128)} custom-call(f32[8,32,128]{2,1,0:T(8,128)S(1)} %collective-permute-done.1.packed_ref, f32[16,2,32,64]{3,2,1,0:T(8,128)} %shard_map.66.refs_0_), custom_call_target="tpu_custom_call", output_to_operand_aliasing={{}: (1, {})} | custom-call | bytes 262144 | tf_op jit(solution)/shard_map/pallas_call | solution.py:301
  (5 shorter events, 0.1 us)
Async XLA Ops:
  5.1 7.3 %copy-start = (s32[1,32]{1,0:T(1,128)S(1)}, s32[1,32]{1,0:T(1,128)}, u32[]{:S(2)}) copy-start(s32[1,32]{1,0:T(1,128)} %param.7) | copy-start | bytes 388
  5.1 8.5 %copy-start.1 = (s32[2,16]{1,0:T(2,128)S(1)}, s32[2,16]{1,0:T(2,128)}, u32[]{:S(2)}) copy-start(s32[2,16]{1,0:T(2,128)} %constant.42.clone) | copy-start | bytes 388
  5.1 34.9 %all-to-all-start = ((bf16[32,16,1024]{2,1,0:T(8,128)(2,1)}), bf16[32,16,1024]{2,1,0:T(8,128)(2,1)S(1)}, u32[]{:S(2)}, u32[]{:S(2)}) async-start(bf16[32,16,1024]{2,1,0:T(8,128)(2,1)} %bitcast.8), calls=%async_computation | async-start | bytes 2097152 | tf_op jit(solution)/shard_map/all_to_all | solution.py:330
  12.4 1.2 %collective-permute-start = (s32[1,32]{1,0:T(1,128)S(1)}, s32[1,32]{1,0:T(1,128)S(1)}, u32[]{:S(2)}, u32[]{:S(2)}) collective-permute-start(s32[1,32]{1,0:T(1,128)S(1)} %copy-done), channel_id=1, source_target_pairs={{0,1},{1,0},{2,3},{3,2},{4,5},{5,4},{6,7},{7,6},{8,9},{9,8},{10,11... | collective-permute-start | bytes 392 | tf_op jit(solution)/shard_map/ppermute | solution.py:323
  40.9 1.4 %collective-permute-start.1 = (f32[8,32,128]{2,1,0:T(8,128)S(1)}, f32[8,32,128]{2,1,0:T(8,128)S(1)}, u32[]{:S(2)}, u32[]{:S(2)}) collective-permute-start(f32[8,32,128]{2,1,0:T(8,128)S(1)} %get-tuple-element.7), channel_id=1, source_target_pairs={{0,1},{1,0},{2,3},{3,2},{4,5},{5,4},{6,7},{7,6},{8,9},{9,8},{10,11... | collective-permute-start | bytes 393224 | tf_op jit(solution)/shard_map/ppermute | solution.py:335

commit v17 on v16

--- a/solution.py
+++ b/solution.py
@@ -318,7 +318,7 @@
     inputs, block = samples.shape[0], slot_order.shape[1]
     axes = ("freq", "blk")
     plane = freq * blocks // 4
-    order = [*reversed(range(plane, freq * blocks)), *range(plane)]
+    order = [d for z in (3, 2, 0, 1) for d in reversed(range(z * plane, (z + 1) * plane))]
     me = lax.axis_index("blk").astype(jnp.int32)
     partner = lax.ppermute(slot_order, "blk", SWAP)
     orders = jnp.where(

time: 43.4 us -> 41.7 us (0.961)
  waiting for transfers between devices: 27.1 us -> 24.7 us
  starting transfers between devices: 7.98 us -> 8.63 us
    all_to_all x1, waiting for transfers between devices: 26 us -> 23.7 us  [split_channels(): lax.all_to_all(sent, axes, split_axis=0, concat_axis=0, axis_index_groups...]
    ppermute x1, starting transfers between devices: 0.36 us -> 1.01 us  [split_channels(): received = lax.ppermute(other, 'blk', SWAP)]
where the time goes in v17:
time: 41.7 us; the launch traced here: 41.4 us
  waiting for transfers between devices  24.7 us (59%)
  starting transfers between devices  8.63 us (21%)
  Pallas kernels  7.56 us (18%)
    all_to_all x1, waiting for transfers between devices, split_channels(): lax.all_to_all(sent, axes, split_axis=0, concat_axis=0, axis_index_groups...  23.7 us
    all_to_all x1, starting transfers between devices, split_channels(): lax.all_to_all(sent, axes, split_axis=0, concat_axis=0, axis_index_groups...  7.3 us
    pallas_call x1, Pallas kernels, channelize(): pl.pallas_call(channelize_kernel, out_shape=jax.ShapeDtypeStruct((FRAME,...  5.09 us
    pallas_call x2, Pallas kernels, place(): pl.pallas_call(functools.partial(place_kernel, own=base is None), out_sha...  1.59 us
    ppermute x1, starting transfers between devices, split_channels(): received = lax.ppermute(other, 'blk', SWAP)  1.01 us
    pallas_call x1, Pallas kernels, correlate(): pl.pallas_call(functools.partial(correlate_kernel, order=order), out_shap...  0.87 us
  transfers between devices with their start and end apart: 3, of which 3 were waited for; matrix products, arithmetic and copies ran while one was open for 1% of the time, Pallas kernels for 2%

profile of v17, /device:TPU:0, one launch (start us, length us, event | category | flops | bytes accessed | tf_op | source)
XLA Modules:
  0.0 41.4 jit_solution(371365821775967953)
XLA Ops:
  0.0 5.1 %shard_map.64 = bf16[512,1024]{1,0:T(8,128)(2,1)} custom-call(s32[2]{0:T(128)} %flags_hbm.1, bf16[4184,128]{1,0:T(8,128)(2,1)} %bitcast.9, f32[12,512]{1,0:T(8,128)} %constant.41.clone.taps_hbm, bf16[512,512]{1,0:T(8,128)(2,1)} %constant.40.clone.table_hbm), custom_call_target="tpu_custom_call" | custom-call | flops 549453824 | bytes 2097152 | tf_op jit(solution)/shard_map/pallas_call | solution.py:191
  5.1 0.0 copy-start
  5.1 0.0 copy-start.1
  5.1 7.3 %all-to-all-start = ((bf16[32,16,1024]{2,1,0:T(8,128)(2,1)}), bf16[32,16,1024]{2,1,0:T(8,128)(2,1)S(1)}, u32[]{:S(2)}, u32[]{:S(2)}) async-start(bf16[32,16,1024]{2,1,0:T(8,128)(2,1)} %bitcast.8), calls=%async_computation | async-start | bytes 2097152 | tf_op jit(solution)/shard_map/all_to_all | solution.py:330
  12.4 0.0 copy-done
  12.4 0.3 collective-permute-start
  12.8 0.1 add.50
  12.8 0.8 %collective-permute-done = s32[1,32]{1,0:T(1,128)S(1)} collective-permute-done((s32[1,32]{1,0:T(1,128)S(1)}, s32[1,32]{1,0:T(1,128)S(1)}, u32[]{:S(2)}, u32[]{:S(2)}) %collective-permute-start) | collective-permute-done | bytes 160 | tf_op jit(solution)/shard_map/ppermute | solution.py:323
  13.6 0.0 copy-done.1
  13.7 0.1 select_reduce_fusion
  13.8 0.1 add.48
  13.9 0.1 fusion.pick_ref
  14.0 23.7 %all-to-all-done = bf16[32,16,1024]{2,1,0:T(8,128)(2,1)S(1)} async-done(((bf16[32,16,1024]{2,1,0:T(8,128)(2,1)}), bf16[32,16,1024]{2,1,0:T(8,128)(2,1)S(1)}, u32[]{:S(2)}, u32[]{:S(2)}) %all-to-all-start) | async-done | bytes 1048608 | tf_op jit(solution)/shard_map/all_to_all | solution.py:330
  37.7 0.9 %shard_map.65 = (f32[8,32,128]{2,1,0:T(8,128)S(1)}, f32[8,32,128]{2,1,0:T(8,128)S(1)}) custom-call(bf16[2,256,256]{2,1,0:T(8,128)(2,1)S(1)} %fusion.pick_ref, bf16[512,1024]{1,0:T(8,128)(2,1)S(1)} %bitcast.7), custom_call_target="tpu_custom_call" | custom-call | flops 268435456 | bytes 2097152 | tf_op jit(solution)/shard_map/pallas_call | solution.py:266
  38.6 1.0 %collective-permute-start.1 = (f32[8,32,128]{2,1,0:T(8,128)S(1)}, f32[8,32,128]{2,1,0:T(8,128)S(1)}, u32[]{:S(2)}, u32[]{:S(2)}) collective-permute-start(f32[8,32,128]{2,1,0:T(8,128)S(1)} %get-tuple-element.7), channel_id=1, source_target_pairs={{0,1},{1,0},{2,3},{3,2},{4,5},{5,4},{6,7},{7,6},{8,9},{9,8},{10,11... | collective-permute-start | bytes 393224 | tf_op jit(solution)/shard_map/ppermute | solution.py:335
  39.6 0.8 %shard_map.66.refs_0_ = f32[16,2,32,64]{3,2,1,0:T(8,128)} custom-call(f32[8,32,128]{2,1,0:T(8,128)S(1)} %get-tuple-element.8.packed_ref), custom_call_target="tpu_custom_call" | custom-call | bytes 262144 | tf_op jit(solution)/shard_map/pallas_call | solution.py:301
  40.4 0.2 collective-permute-done.1.packed_ref
  40.6 0.8 %shard_map.67 = f32[16,2,32,64]{3,2,1,0:T(8,128)} custom-call(f32[8,32,128]{2,1,0:T(8,128)S(1)} %collective-permute-done.1.packed_ref, f32[16,2,32,64]{3,2,1,0:T(8,128)} %shard_map.66.refs_0_), custom_call_target="tpu_custom_call", output_to_operand_aliasing={{}: (1, {})} | custom-call | bytes 262144 | tf_op jit(solution)/shard_map/pallas_call | solution.py:301
  (5 shorter events, 0.1 us)
Async XLA Ops:
  5.1 7.3 %copy-start = (s32[1,32]{1,0:T(1,128)S(1)}, s32[1,32]{1,0:T(1,128)}, u32[]{:S(2)}) copy-start(s32[1,32]{1,0:T(1,128)} %param.7) | copy-start | bytes 388
  5.1 8.5 %copy-start.1 = (s32[2,16]{1,0:T(2,128)S(1)}, s32[2,16]{1,0:T(2,128)}, u32[]{:S(2)}) copy-start(s32[2,16]{1,0:T(2,128)} %constant.42.clone) | copy-start | bytes 388
  5.1 32.6 %all-to-all-start = ((bf16[32,16,1024]{2,1,0:T(8,128)(2,1)}), bf16[32,16,1024]{2,1,0:T(8,128)(2,1)S(1)}, u32[]{:S(2)}, u32[]{:S(2)}) async-start(bf16[32,16,1024]{2,1,0:T(8,128)(2,1)} %bitcast.8), calls=%async_computation | async-start | bytes 2097152 | tf_op jit(solution)/shard_map/all_to_all | solution.py:330
  12.4 1.2 %collective-permute-start = (s32[1,32]{1,0:T(1,128)S(1)}, s32[1,32]{1,0:T(1,128)S(1)}, u32[]{:S(2)}, u32[]{:S(2)}) collective-permute-start(s32[1,32]{1,0:T(1,128)S(1)} %copy-done), channel_id=1, source_target_pairs={{0,1},{1,0},{2,3},{3,2},{4,5},{5,4},{6,7},{7,6},{8,9},{9,8},{10,11... | collective-permute-start | bytes 392 | tf_op jit(solution)/shard_map/ppermute | solution.py:323
  38.6 2.0 %collective-permute-start.1 = (f32[8,32,128]{2,1,0:T(8,128)S(1)}, f32[8,32,128]{2,1,0:T(8,128)S(1)}, u32[]{:S(2)}, u32[]{:S(2)}) collective-permute-start(f32[8,32,128]{2,1,0:T(8,128)S(1)} %get-tuple-element.7), channel_id=1, source_target_pairs={{0,1},{1,0},{2,3},{3,2},{4,5},{5,4},{6,7},{7,6},{8,9},{9,8},{10,11... | collective-permute-start | bytes 393224 | tf_op jit(solution)/shard_map/ppermute | solution.py:335

commit v18 on v13

--- a/solution.py
+++ b/solution.py
@@ -8,7 +8,6 @@
 from jax.experimental import pallas as pl
 from jax.experimental.pallas import tpu as pltpu
 from jax.experimental.layout import Layout, with_layout_constraint
-from jax.sharding import Mesh
 from jax.sharding import PartitionSpec as P
 
 CH = 256
@@ -18,10 +17,10 @@
 LANES = 128
 SUB = 8
 GROUP = 256
-STEP = GROUP // SUB
+PART = 128
+STEP = PART // SUB
 STRIDE = STEP + 1
 PITCH = SPEC + 25
-FAR = 4
 SWAP = [(0, 1), (1, 0)]
 VMEM_LIMIT = 40 * 1024 * 1024
 
@@ -62,10 +61,11 @@
     frames = SPEC + TAPS - 1
     spread = inputs * FRAME // LANES
     groups = SPEC // GROUP
+    parts = SPEC // PART
     pieces = sems.shape[1]
     rows = FRAME // pieces
     last = lax.broadcasted_iota(jnp.int32, (SUB, LANES), 0) == SUB - 1
-    edges = [0, GROUP // 2] + [g * GROUP + TAPS for g in range(1, groups)] + [frames]
+    edges = [0] + [n * PART + TAPS for n in range(1, parts)] + [frames]
 
     def load(source, target, n):
         copy = pltpu.make_async_copy(source, target, load_sems.at[n])
@@ -88,7 +88,7 @@
                 part = tile[c * spread : (c + 1) * spread]
                 wide[pl.ds(f + c, spread, stride=PITCH), :] = part
 
-    def filter_group(g, i, j):
+    def filter_part(n, i, j):
         cols = pl.ds(j * LANES, LANES)
         good = (1 - flags[i]).astype(jnp.float32)
         taps = [
@@ -96,7 +96,7 @@
         ]
 
         def take(b):
-            first = (inputs * j + i) * PITCH + g * GROUP + b
+            first = (inputs * j + i) * PITCH + n * PART + b
             return wide[pl.ds(first, SUB, stride=STRIDE), :]
 
         def total(first, count):
@@ -115,7 +115,7 @@
                     out[b] = jnp.where(last, pltpu.roll(extra, SUB - 1 - past, 0), out[b])
             for b in range(0, SUB, 2):
                 both = jnp.concatenate(out[b : b + 2], axis=0).astype(jnp.bfloat16)
-                fir[i, pl.ds(g * GROUP + (first + b) * SUB, 2 * SUB), cols] = both
+                fir[i, pl.ds(n * PART + (first + b) * SUB, 2 * SUB), cols] = both
 
     def transform(g, i):
         part = pl.ds(g * GROUP, GROUP)
@@ -144,26 +144,33 @@
             copies[-1].start()
         return copies
 
+    def filter_input(n, i):
+        for j in range(FRAME // LANES):
+            filter_part(n, i, j)
+
+    load_taps.wait()
+    load_flags.wait()
     loads[0].wait()
     convert(0)
-    load_taps.wait()
-    load_flags.wait()
+    for i in range(inputs):
+        filter_input(0, i)
     loads[1].wait()
     load_table = load(table_hbm, table, chunks + 1)
     convert(1)
     for i in range(inputs):
-        for j in range(FRAME // LANES):
-            filter_group(0, i, j)
+        filter_input(1, i)
     loads[2].wait()
+    loads[3].wait()
     load_table.wait()
     for i in range(inputs):
         transform(0, i)
     convert(2)
+    convert(3)
     for i in range(inputs):
         if i > 0:
             transform(1, i - 1)
-        for j in range(FRAME // LANES):
-            filter_group(1, i, j)
+        filter_input(2, i)
+        filter_input(3, i)
         if i == 0:
             for piece in range(pieces):
                 pack(0, piece)
@@ -178,13 +185,13 @@
         copy.wait()
 
 
-def channelize(samples, flags, far, near, blocks):
+def channelize(samples, flags, order):
     inputs = samples.shape[0]
     tiles = samples.reshape(inputs, -1, LANES)
     tiles = with_layout_constraint(tiles, Layout(major_to_minor=(1, 0, 2)))
     tiles = tiles.transpose(1, 0, 2)
     tiles = tiles.reshape(-1, LANES)
-    table = twiddle().reshape(far, near, blocks, SUB, 2, FRAME).transpose(2, 1, 0, 4, 3, 5)
+    table = twiddle().reshape(len(order), SUB, 2, FRAME)[np.asarray(order)].transpose(0, 2, 1, 3)
     table = jnp.asarray(table.reshape(FRAME, FRAME), dtype=jnp.bfloat16)
     taps = jnp.asarray(prototype())
     hbm = pl.BlockSpec(memory_space=pltpu.HBM)
@@ -202,7 +209,7 @@
             pltpu.VMEM((inputs, SPEC, FRAME), jnp.bfloat16),
             pltpu.VMEM((SPEC // GROUP, inputs, FRAME, GROUP), jnp.float32),
             pltpu.VMEM((FRAME, inputs * SPEC), jnp.bfloat16),
-            pltpu.SemaphoreType.DMA((SPEC // GROUP + 4,)),
+            pltpu.SemaphoreType.DMA((SPEC // PART + 3,)),
             pltpu.SemaphoreType.DMA((SPEC // GROUP, 4, 2)),
         ],
         cost_estimate=pl.CostEstimate(
@@ -213,19 +220,20 @@
     )(flags, tiles, taps, table)
 
 
-def correlate_kernel(pick_ref, arrived_ref, own_ref, other_ref, slots):
+def correlate_kernel(pick_ref, arrived_ref, own_ref, other_ref, slots, grams, *, order):
     share, block, _ = own_ref.shape
     blocks = pick_ref.shape[0]
     width = blocks * block
-    held = arrived_ref.shape[0] // blocks
+    held = arrived_ref.shape[0] // len(order)
     first = lax.axis_index("blk") == 0
     lane = lax.broadcasted_iota(jnp.int32, (width, 2 * width), 1)
     sign = jnp.where(lane < width, 1.0, -1.0)
     diagonal = lane == lax.broadcasted_iota(jnp.int32, (width, 2 * width), 0)
     for n in range(blocks):
-        rows = pl.ds(n * held, held)
+        places = [place for place, device in enumerate(order) if device % blocks == n]
+        rows = [arrived_ref[pl.ds(place * held, held), :] for place in places]
         slots[n] = jnp.dot(
-            pick_ref[n], arrived_ref[rows, :], preferred_element_type=jnp.float32
+            pick_ref[n], jnp.concatenate(rows, axis=0), preferred_element_type=jnp.float32
         ).astype(jnp.bfloat16)
     for k in range(share):
         pair = jnp.concatenate(
@@ -239,38 +247,45 @@
         gram = lax.dot_general(
             pair, pair, (((1,), (1,)), ((), ())), preferred_element_type=jnp.float32
         )
-        part = gram[:width] * sign + pltpu.roll(gram[width:], width, 1)
-        square = jnp.where(diagonal, part, 0.0)
-        across = jnp.sum(square, axis=0, keepdims=True)
-        across = across + pltpu.roll(across, width, 1)
-        down = jnp.sum(square, axis=1, keepdims=True)
-        part = part * (1.0 / jnp.sqrt(across / SPEC + 1e-05) / SPEC)
-        part = part * (1.0 / jnp.sqrt(down / SPEC + 1e-05))
-        own_ref[k] = jnp.where(first, part[:block], part[block:])
-        other_ref[k] = jnp.where(first, part[block:], part[:block])
-
-
-def picks(orders, inputs, far, near, share):
+        grams[k] = gram[:width] * sign + pltpu.roll(gram[width:], width, 1)
+    part = grams[...]
+    square = jnp.where(diagonal[None], part, 0.0)
+    across = jnp.sum(square, axis=1, keepdims=True)
+    across = jnp.concatenate([across[:, :, :width], across[:, :, :width]], axis=2)
+    down = jnp.sum(square, axis=2, keepdims=True)
+    part = part * (lax.rsqrt(across / SPEC + 1e-05) / SPEC)
+    part = part * lax.rsqrt(down / SPEC + 1e-05)
+    own_ref[...] = jnp.where(first, part[:, :block], part[:, block:])
+    other_ref[...] = jnp.where(first, part[:, block:], part[:, :block])
+
+
+def picks(orders, inputs, order, share):
     blocks, block = orders.shape
     device, held = orders // inputs, orders % inputs
-    place = (device % near) * far + device // near
+    rank = [np.argsort([d for d in order if d % blocks == n]) for n in range(blocks)]
+    known = jnp.asarray(np.stack(rank), dtype=jnp.int32)
+    match = device[:, :, None] == jnp.arange(known.shape[1], dtype=jnp.int32)
+    place = jnp.sum(jnp.where(match, known[:, None, :], 0), axis=2)
     start = ((place * inputs + held) * share)[:, None, :]
     chan = jnp.arange(share, dtype=jnp.int32)[:, None]
     target = (start + chan).reshape(blocks, share * block, 1)
-    column = lax.broadcasted_iota(jnp.int32, (1, 1, far * near * inputs * share), 2)
+    column = lax.broadcasted_iota(jnp.int32, (1, 1, known.shape[1] * inputs * share), 2)
     return (column == target).astype(jnp.bfloat16)
 
 
-def correlate(arrived, pick, share, block):
+def correlate(arrived, pick, order, share, block):
     blocks = pick.shape[0]
     vmem = pl.BlockSpec(memory_space=pltpu.VMEM)
     tile = jax.ShapeDtypeStruct((share, block, 2 * blocks * block), jnp.float32)
     return pl.pallas_call(
-        correlate_kernel,
+        functools.partial(correlate_kernel, order=order),
         out_shape=(tile, tile),
         in_specs=[vmem, vmem],
         out_specs=(vmem, vmem),
-        scratch_shapes=[pltpu.VMEM((blocks, share * block, 2 * SPEC), jnp.bfloat16)],
+        scratch_shapes=[
+            pltpu.VMEM((blocks, share * block, 2 * SPEC), jnp.bfloat16),
+            pltpu.VMEM((share, blocks * block, 2 * blocks * block), jnp.float32),
+        ],
         compiler_params=pltpu.CompilerParams(vmem_limit_bytes=VMEM_LIMIT),
         cost_estimate=pl.CostEstimate(
             flops=4 * pick.size * SPEC, bytes_accessed=4 * arrived.size, transcendentals=0
@@ -315,10 +330,12 @@
     )(packed, *([] if base is None else [base]))
 
 
-def split_channels(far, near, blocks, samples, slot_order, flags):
-    share = CH // (far * near * blocks)
+def split_channels(freq, blocks, samples, slot_order, flags):
+    share = CH // (freq * blocks)
     inputs, block = samples.shape[0], slot_order.shape[1]
-    axes = ("blk", "near", "far")
+    axes = ("freq", "blk")
+    plane = freq * blocks // 4
+    order = [d for z in (3, 2, 0, 1) for d in reversed(range(z * plane, (z + 1) * plane))]
     me = lax.axis_index("blk").astype(jnp.int32)
     partner = lax.ppermute(slot_order, "blk", SWAP)
     orders = jnp.where(
@@ -326,10 +343,12 @@
         jnp.concatenate([slot_order, partner]),
         jnp.concatenate([partner, slot_order]),
     )
-    sent = channelize(samples, flags, far, near, blocks)
-    arrived = lax.all_to_all(sent, axes, split_axis=0, concat_axis=0, tiled=True)
-    pick = picks(orders, inputs, far, near, share)
-    own, other = correlate(arrived, pick, share, block)
+    sent = channelize(samples, flags, order)
+    arrived = lax.all_to_all(
+        sent, axes, split_axis=0, concat_axis=0, axis_index_groups=[order], tiled=True
+    )
+    pick = picks(orders, inputs, order, share)
+    own, other = correlate(arrived, pick, order, share, block)
     received = lax.ppermute(other, "blk", SWAP)
     return place(received, blocks, place(own, blocks))
 
@@ -350,7 +369,7 @@
     power = jnp.sum(squares.reshape(CH, 2, inputs), axis=1) / SPEC
     scale = good[None, :] / jnp.sqrt(power + 1e-05)
     quantized = (spectra * jnp.repeat(scale, 2, axis=0)[:, :, None]).astype(jnp.bfloat16)
-    arrived = lax.all_to_all(quantized, ("far", "near"), split_axis=0, concat_axis=1, tiled=True)
+    arrived = lax.all_to_all(quantized, "freq", split_axis=0, concat_axis=1, tiled=True)
     share = CH // freq
     block = slot_order.shape[1]
     own = jnp.take(arrived.reshape(share, 2, block, SPEC), slot_order[0], axis=2)
@@ -363,16 +382,12 @@
 
 def solution(mesh):
     freq, blocks = mesh.shape["freq"], mesh.shape["blk"]
-    far = math.gcd(freq, FAR)
-    near = freq // far
-    split = Mesh(mesh.devices.reshape(far, near, blocks), ("far", "near", "blk"))
 
     def body(samples, slot_order, flags):
         if blocks == 2 and CH == SUB * freq * blocks:
-            return split_channels(far, near, blocks, samples, slot_order, flags)
+            return split_channels(freq, blocks, samples, slot_order, flags)
         return gather_blocks(freq, samples, slot_order, flags)
 
-    held = ("blk", "far", "near")
-    in_specs = (P(held, None), P("blk", None), P(held))
-    out_specs = P(("far", "near"), None, "blk", None)
-    return jax.shard_map(body, mesh=split, in_specs=in_specs, out_specs=out_specs, check_vma=False)
+    in_specs = (P(("blk", "freq"), None), P("blk", None), P(("blk", "freq")))
+    out_specs = P("freq", None, "blk", None)
+    return jax.shard_map(body, mesh=mesh, in_specs=in_specs, out_specs=out_specs, check_vma=False)

time: 42.7 us -> 42.4 us (level)
  waiting for transfers between devices: 26.6 us -> 24.7 us
  starting transfers between devices: 7.69 us -> 8.63 us
  Pallas kernels: 7.71 us -> 8.27 us
    all_to_all x1, waiting for transfers between devices: 25.3 us -> 23.7 us  [split_channels(): lax.all_to_all(sent, axes, split_axis=0, concat_axis=0, axis_index_groups...]
    ppermute x1, starting transfers between devices: 0.07 us -> 1.01 us  [split_channels(): received = lax.ppermute(other, 'blk', SWAP)]
    pallas_call x1, Pallas kernels: 4.84 us -> 5.4 us  [channelize(): pl.pallas_call(channelize_kernel, out_shape=jax.ShapeDtypeStruct((FRAME,...]
where the time goes in v18:
time: 42.4 us; the launch traced here: 42.1 us
  waiting for transfers between devices  24.7 us (58%)
  starting transfers between devices  8.63 us (20%)
  Pallas kernels  8.27 us (20%)
    all_to_all x1, waiting for transfers between devices, split_channels(): lax.all_to_all(sent, axes, split_axis=0, concat_axis=0, axis_index_groups...  23.7 us
    all_to_all x1, starting transfers between devices, split_channels(): lax.all_to_all(sent, axes, split_axis=0, concat_axis=0, axis_index_groups...  7.3 us
    pallas_call x1, Pallas kernels, channelize(): pl.pallas_call(channelize_kernel, out_shape=jax.ShapeDtypeStruct((FRAME,...  5.4 us
    pallas_call x2, Pallas kernels, place(): pl.pallas_call(functools.partial(place_kernel, own=base is None), out_sha...  1.59 us
    pallas_call x1, Pallas kernels, correlate(): pl.pallas_call(functools.partial(correlate_kernel, order=order), out_shap...  1.28 us
    ppermute x1, starting transfers between devices, split_channels(): received = lax.ppermute(other, 'blk', SWAP)  1.01 us
  transfers between devices with their start and end apart: 3, of which 3 were waited for; matrix products, arithmetic and copies ran while one was open for 1% of the time, Pallas kernels for 2%

profile of v18, /device:TPU:0, one launch (start us, length us, event | category | flops | bytes accessed | tf_op | source)
XLA Modules:
  0.0 42.1 jit_solution(4094761765675632175)
XLA Ops:
  0.0 5.4 %shard_map.64 = bf16[512,1024]{1,0:T(8,128)(2,1)} custom-call(s32[2]{0:T(128)} %flags_hbm.1, bf16[4184,128]{1,0:T(8,128)(2,1)} %bitcast.9, f32[12,512]{1,0:T(8,128)} %constant.41.clone.taps_hbm, bf16[512,512]{1,0:T(8,128)(2,1)} %constant.40.clone.table_hbm), custom_call_target="tpu_custom_call" | custom-call | flops 549453824 | bytes 2097152 | tf_op jit(solution)/shard_map/pallas_call | solution.py:198
  5.4 0.0 copy-start
  5.4 0.0 copy-start.1
  5.4 7.3 %all-to-all-start = ((bf16[32,16,1024]{2,1,0:T(8,128)(2,1)}), bf16[32,16,1024]{2,1,0:T(8,128)(2,1)S(1)}, u32[]{:S(2)}, u32[]{:S(2)}) async-start(bf16[32,16,1024]{2,1,0:T(8,128)(2,1)} %bitcast.8), calls=%async_computation | async-start | bytes 2097152 | tf_op jit(solution)/shard_map/all_to_all | solution.py:347
  12.7 0.0 copy-done
  12.8 0.3 collective-permute-start
  13.1 0.1 add.50
  13.2 0.8 %collective-permute-done = s32[1,32]{1,0:T(1,128)S(1)} collective-permute-done((s32[1,32]{1,0:T(1,128)S(1)}, s32[1,32]{1,0:T(1,128)S(1)}, u32[]{:S(2)}, u32[]{:S(2)}) %collective-permute-start) | collective-permute-done | bytes 160 | tf_op jit(solution)/shard_map/ppermute | solution.py:340
  14.0 0.0 copy-done.1
  14.0 0.1 select_reduce_fusion
  14.1 0.1 add.48
  14.2 0.1 fusion.pick_ref
  14.3 23.7 %all-to-all-done = bf16[32,16,1024]{2,1,0:T(8,128)(2,1)S(1)} async-done(((bf16[32,16,1024]{2,1,0:T(8,128)(2,1)}), bf16[32,16,1024]{2,1,0:T(8,128)(2,1)S(1)}, u32[]{:S(2)}, u32[]{:S(2)}) %all-to-all-start) | async-done | bytes 1048608 | tf_op jit(solution)/shard_map/all_to_all | solution.py:347
  38.1 1.3 %shard_map.65 = (f32[8,32,128]{2,1,0:T(8,128)S(1)}, f32[8,32,128]{2,1,0:T(8,128)S(1)}) custom-call(bf16[2,256,256]{2,1,0:T(8,128)(2,1)S(1)} %fusion.pick_ref, bf16[512,1024]{1,0:T(8,128)(2,1)S(1)} %bitcast.7), custom_call_target="tpu_custom_call" | custom-call | flops 268435456 | bytes 2097152 | tf_op jit(solution)/shard_map/pallas_call | solution.py:280
  39.3 1.0 %collective-permute-start.1 = (f32[8,32,128]{2,1,0:T(8,128)S(1)}, f32[8,32,128]{2,1,0:T(8,128)S(1)}, u32[]{:S(2)}, u32[]{:S(2)}) collective-permute-start(f32[8,32,128]{2,1,0:T(8,128)S(1)} %get-tuple-element.7), channel_id=1, source_target_pairs={{0,1},{1,0},{2,3},{3,2},{4,5},{5,4},{6,7},{7,6},{8,9},{9,8},{10,11... | collective-permute-start | bytes 393224 | tf_op jit(solution)/shard_map/ppermute | solution.py:352
  40.3 0.8 %shard_map.66.refs_0_ = f32[16,2,32,64]{3,2,1,0:T(8,128)} custom-call(f32[8,32,128]{2,1,0:T(8,128)S(1)} %get-tuple-element.8.packed_ref), custom_call_target="tpu_custom_call" | custom-call | bytes 262144 | tf_op jit(solution)/shard_map/pallas_call | solution.py:318
  41.1 0.2 collective-permute-done.1.packed_ref
  41.3 0.8 %shard_map.67 = f32[16,2,32,64]{3,2,1,0:T(8,128)} custom-call(f32[8,32,128]{2,1,0:T(8,128)S(1)} %collective-permute-done.1.packed_ref, f32[16,2,32,64]{3,2,1,0:T(8,128)} %shard_map.66.refs_0_), custom_call_target="tpu_custom_call", output_to_operand_aliasing={{}: (1, {})} | custom-call | bytes 262144 | tf_op jit(solution)/shard_map/pallas_call | solution.py:318
  (5 shorter events, 0.1 us)
Async XLA Ops:
  5.4 7.3 %copy-start = (s32[1,32]{1,0:T(1,128)S(1)}, s32[1,32]{1,0:T(1,128)}, u32[]{:S(2)}) copy-start(s32[1,32]{1,0:T(1,128)} %param.7) | copy-start | bytes 388
  5.4 8.5 %copy-start.1 = (s32[2,16]{1,0:T(2,128)S(1)}, s32[2,16]{1,0:T(2,128)}, u32[]{:S(2)}) copy-start(s32[2,16]{1,0:T(2,128)} %constant.42.clone) | copy-start | bytes 388
  5.4 32.6 %all-to-all-start = ((bf16[32,16,1024]{2,1,0:T(8,128)(2,1)}), bf16[32,16,1024]{2,1,0:T(8,128)(2,1)S(1)}, u32[]{:S(2)}, u32[]{:S(2)}) async-start(bf16[32,16,1024]{2,1,0:T(8,128)(2,1)} %bitcast.8), calls=%async_computation | async-start | bytes 2097152 | tf_op jit(solution)/shard_map/all_to_all | solution.py:347
  12.8 1.2 %collective-permute-start = (s32[1,32]{1,0:T(1,128)S(1)}, s32[1,32]{1,0:T(1,128)S(1)}, u32[]{:S(2)}, u32[]{:S(2)}) collective-permute-start(s32[1,32]{1,0:T(1,128)S(1)} %copy-done), channel_id=1, source_target_pairs={{0,1},{1,0},{2,3},{3,2},{4,5},{5,4},{6,7},{7,6},{8,9},{9,8},{10,11... | collective-permute-start | bytes 392 | tf_op jit(solution)/shard_map/ppermute | solution.py:340
  39.3 2.0 %collective-permute-start.1 = (f32[8,32,128]{2,1,0:T(8,128)S(1)}, f32[8,32,128]{2,1,0:T(8,128)S(1)}, u32[]{:S(2)}, u32[]{:S(2)}) collective-permute-start(f32[8,32,128]{2,1,0:T(8,128)S(1)} %get-tuple-element.7), channel_id=1, source_target_pairs={{0,1},{1,0},{2,3},{3,2},{4,5},{5,4},{6,7},{7,6},{8,9},{9,8},{10,11... | collective-permute-start | bytes 393224 | tf_op jit(solution)/shard_map/ppermute | solution.py:352

commit v19 on v17

--- a/solution.py
+++ b/solution.py
@@ -318,7 +318,12 @@
     inputs, block = samples.shape[0], slot_order.shape[1]
     axes = ("freq", "blk")
     plane = freq * blocks // 4
-    order = [d for z in (3, 2, 0, 1) for d in reversed(range(z * plane, (z + 1) * plane))]
+    order = [
+        z * plane + d
+        for z in (3, 2, 0, 1)
+        for core in reversed(range(blocks))
+        for d in reversed(range(core, plane, blocks))
+    ]
     me = lax.axis_index("blk").astype(jnp.int32)
     partner = lax.ppermute(slot_order, "blk", SWAP)
     orders = jnp.where(

time: 41.7 us -> 41.1 us (0.986)
  starting transfers between devices: 8.63 us -> 7.69 us
    ppermute x1, starting transfers between devices: 1.01 us -> 0.07 us  [split_channels(): received = lax.ppermute(other, 'blk', SWAP)]
where the time goes in v19:
time: 41.1 us; the launch traced here: 40.8 us
  waiting for transfers between devices  25 us (61%)
  starting transfers between devices  7.69 us (19%)
  Pallas kernels  7.56 us (18%)
    all_to_all x1, waiting for transfers between devices, split_channels(): lax.all_to_all(sent, axes, split_axis=0, concat_axis=0, axis_index_groups...  23.7 us
    all_to_all x1, starting transfers between devices, split_channels(): lax.all_to_all(sent, axes, split_axis=0, concat_axis=0, axis_index_groups...  7.3 us
    pallas_call x1, Pallas kernels, channelize(): pl.pallas_call(channelize_kernel, out_shape=jax.ShapeDtypeStruct((FRAME,...  5.09 us
    pallas_call x2, Pallas kernels, place(): pl.pallas_call(functools.partial(place_kernel, own=base is None), out_sha...  1.6 us
    pallas_call x1, Pallas kernels, correlate(): pl.pallas_call(functools.partial(correlate_kernel, order=order), out_shap...  0.87 us
  transfers between devices with their start and end apart: 3, of which 3 were waited for; matrix products, arithmetic and copies ran while one was open for 1% of the time, Pallas kernels for 2%

profile of v19, /device:TPU:0, one launch (start us, length us, event | category | flops | bytes accessed | tf_op | source)
XLA Modules:
  0.0 40.8 jit_solution(7235225876901005590)
XLA Ops:
  0.0 5.1 %shard_map.64 = bf16[512,1024]{1,0:T(8,128)(2,1)} custom-call(s32[2]{0:T(128)} %flags_hbm.1, bf16[4184,128]{1,0:T(8,128)(2,1)} %bitcast.9, f32[12,512]{1,0:T(8,128)} %constant.41.clone.taps_hbm, bf16[512,512]{1,0:T(8,128)(2,1)} %constant.40.clone.table_hbm), custom_call_target="tpu_custom_call" | custom-call | flops 549453824 | bytes 2097152 | tf_op jit(solution)/shard_map/pallas_call | solution.py:191
  5.1 0.0 copy-start
  5.1 0.0 copy-start.1
  5.1 7.3 %all-to-all-start = ((bf16[32,16,1024]{2,1,0:T(8,128)(2,1)}), bf16[32,16,1024]{2,1,0:T(8,128)(2,1)S(1)}, u32[]{:S(2)}, u32[]{:S(2)}) async-start(bf16[32,16,1024]{2,1,0:T(8,128)(2,1)} %bitcast.8), calls=%async_computation | async-start | bytes 2097152 | tf_op jit(solution)/shard_map/all_to_all | solution.py:335
  12.4 0.0 copy-done
  12.4 0.3 collective-permute-start
  12.8 0.1 add.50
  12.8 0.8 %collective-permute-done = s32[1,32]{1,0:T(1,128)S(1)} collective-permute-done((s32[1,32]{1,0:T(1,128)S(1)}, s32[1,32]{1,0:T(1,128)S(1)}, u32[]{:S(2)}, u32[]{:S(2)}) %collective-permute-start) | collective-permute-done | bytes 160 | tf_op jit(solution)/shard_map/ppermute | solution.py:328
  13.6 0.0 copy-done.1
  13.7 0.1 select_reduce_fusion
  13.8 0.1 add.48
  13.9 0.1 fusion.pick_ref
  14.0 23.7 %all-to-all-done = bf16[32,16,1024]{2,1,0:T(8,128)(2,1)S(1)} async-done(((bf16[32,16,1024]{2,1,0:T(8,128)(2,1)}), bf16[32,16,1024]{2,1,0:T(8,128)(2,1)S(1)}, u32[]{:S(2)}, u32[]{:S(2)}) %all-to-all-start) | async-done | bytes 1048608 | tf_op jit(solution)/shard_map/all_to_all | solution.py:335
  37.7 0.9 %shard_map.65 = (f32[8,32,128]{2,1,0:T(8,128)S(1)}, f32[8,32,128]{2,1,0:T(8,128)S(1)}) custom-call(bf16[2,256,256]{2,1,0:T(8,128)(2,1)S(1)} %fusion.pick_ref, bf16[512,1024]{1,0:T(8,128)(2,1)S(1)} %bitcast.7), custom_call_target="tpu_custom_call" | custom-call | flops 268435456 | bytes 2097152 | tf_op jit(solution)/shard_map/pallas_call | solution.py:266
  38.6 0.1 collective-permute-start.1
  38.7 0.8 %shard_map.66.refs_0_ = f32[16,2,32,64]{3,2,1,0:T(8,128)} custom-call(f32[8,32,128]{2,1,0:T(8,128)S(1)} %get-tuple-element.8.packed_ref), custom_call_target="tpu_custom_call" | custom-call | bytes 262144 | tf_op jit(solution)/shard_map/pallas_call | solution.py:301
  39.5 0.5 %collective-permute-done.1.packed_ref = f32[8,32,128]{2,1,0:T(8,128)S(1)} collective-permute-done((f32[8,32,128]{2,1,0:T(8,128)S(1)}, f32[8,32,128]{2,1,0:T(8,128)S(1)}, u32[]{:S(2)}, u32[]{:S(2)}) %collective-permute-start.1) | collective-permute-done | bytes 131104 | tf_op jit(solution)/shard_map/ppermute | solution.py:340
  40.0 0.8 %shard_map.67 = f32[16,2,32,64]{3,2,1,0:T(8,128)} custom-call(f32[8,32,128]{2,1,0:T(8,128)S(1)} %collective-permute-done.1.packed_ref, f32[16,2,32,64]{3,2,1,0:T(8,128)} %shard_map.66.refs_0_), custom_call_target="tpu_custom_call", output_to_operand_aliasing={{}: (1, {})} | custom-call | bytes 262144 | tf_op jit(solution)/shard_map/pallas_call | solution.py:301
  (5 shorter events, 0.1 us)
Async XLA Ops:
  5.1 7.3 %copy-start = (s32[1,32]{1,0:T(1,128)S(1)}, s32[1,32]{1,0:T(1,128)}, u32[]{:S(2)}) copy-start(s32[1,32]{1,0:T(1,128)} %param.7) | copy-start | bytes 388
  5.1 8.5 %copy-start.1 = (s32[2,16]{1,0:T(2,128)S(1)}, s32[2,16]{1,0:T(2,128)}, u32[]{:S(2)}) copy-start(s32[2,16]{1,0:T(2,128)} %constant.42.clone) | copy-start | bytes 388
  5.1 32.6 %all-to-all-start = ((bf16[32,16,1024]{2,1,0:T(8,128)(2,1)}), bf16[32,16,1024]{2,1,0:T(8,128)(2,1)S(1)}, u32[]{:S(2)}, u32[]{:S(2)}) async-start(bf16[32,16,1024]{2,1,0:T(8,128)(2,1)} %bitcast.8), calls=%async_computation | async-start | bytes 2097152 | tf_op jit(solution)/shard_map/all_to_all | solution.py:335
  12.4 1.2 %collective-permute-start = (s32[1,32]{1,0:T(1,128)S(1)}, s32[1,32]{1,0:T(1,128)S(1)}, u32[]{:S(2)}, u32[]{:S(2)}) collective-permute-start(s32[1,32]{1,0:T(1,128)S(1)} %copy-done), channel_id=1, source_target_pairs={{0,1},{1,0},{2,3},{3,2},{4,5},{5,4},{6,7},{7,6},{8,9},{9,8},{10,11... | collective-permute-start | bytes 392 | tf_op jit(solution)/shard_map/ppermute | solution.py:328
  38.6 1.4 %collective-permute-start.1 = (f32[8,32,128]{2,1,0:T(8,128)S(1)}, f32[8,32,128]{2,1,0:T(8,128)S(1)}, u32[]{:S(2)}, u32[]{:S(2)}) collective-permute-start(f32[8,32,128]{2,1,0:T(8,128)S(1)} %get-tuple-element.7), channel_id=1, source_target_pairs={{0,1},{1,0},{2,3},{3,2},{4,5},{5,4},{6,7},{7,6},{8,9},{9,8},{10,11... | collective-permute-start | bytes 393224 | tf_op jit(solution)/shard_map/ppermute | solution.py:340

commit v20 on v19

--- a/solution.py
+++ b/solution.py
@@ -320,8 +320,9 @@
     plane = freq * blocks // 4
     order = [
         z * plane + d
-        for z in (3, 2, 0, 1)
+        for planes in ((3, 2), (0,), (1,))
         for core in reversed(range(blocks))
+        for z in planes
         for d in reversed(range(core, plane, blocks))
     ]
     me = lax.axis_index("blk").astype(jnp.int32)

time: 41.1 us -> 41.5 us (level)
  waiting for transfers between devices: 25 us -> 25.5 us
    all_to_all x1, waiting for transfers between devices: 23.7 us -> 24.2 us  [split_channels(): lax.all_to_all(sent, axes, split_axis=0, concat_axis=0, axis_index_groups...]
where the time goes in v20:
time: 41.5 us; the launch traced here: 41.3 us
  waiting for transfers between devices  25.5 us (61%)
  starting transfers between devices  7.69 us (19%)
  Pallas kernels  7.56 us (18%)
    all_to_all x1, waiting for transfers between devices, split_channels(): lax.all_to_all(sent, axes, split_axis=0, concat_axis=0, axis_index_groups...  24.2 us
    all_to_all x1, starting transfers between devices, split_channels(): lax.all_to_all(sent, axes, split_axis=0, concat_axis=0, axis_index_groups...  7.3 us
    pallas_call x1, Pallas kernels, channelize(): pl.pallas_call(channelize_kernel, out_shape=jax.ShapeDtypeStruct((FRAME,...  5.09 us
    pallas_call x2, Pallas kernels, place(): pl.pallas_call(functools.partial(place_kernel, own=base is None), out_sha...  1.6 us
    pallas_call x1, Pallas kernels, correlate(): pl.pallas_call(functools.partial(correlate_kernel, order=order), out_shap...  0.87 us
  transfers between devices with their start and end apart: 3, of which 3 were waited for; matrix products, arithmetic and copies ran while one was open for 1% of the time, Pallas kernels for 2%

profile of v20, /device:TPU:0, one launch (start us, length us, event | category | flops | bytes accessed | tf_op | source)
XLA Modules:
  0.0 41.3 jit_solution(8977960189674994445)
XLA Ops:
  0.0 5.1 %shard_map.64 = bf16[512,1024]{1,0:T(8,128)(2,1)} custom-call(s32[2]{0:T(128)} %flags_hbm.1, bf16[4184,128]{1,0:T(8,128)(2,1)} %bitcast.9, f32[12,512]{1,0:T(8,128)} %constant.41.clone.taps_hbm, bf16[512,512]{1,0:T(8,128)(2,1)} %constant.40.clone.table_hbm), custom_call_target="tpu_custom_call" | custom-call | flops 549453824 | bytes 2097152 | tf_op jit(solution)/shard_map/pallas_call | solution.py:191
  5.1 0.0 copy-start
  5.1 0.0 copy-start.1
  5.1 7.3 %all-to-all-start = ((bf16[32,16,1024]{2,1,0:T(8,128)(2,1)}), bf16[32,16,1024]{2,1,0:T(8,128)(2,1)S(1)}, u32[]{:S(2)}, u32[]{:S(2)}) async-start(bf16[32,16,1024]{2,1,0:T(8,128)(2,1)} %bitcast.8), calls=%async_computation | async-start | bytes 2097152 | tf_op jit(solution)/shard_map/all_to_all | solution.py:336
  12.4 0.0 copy-done
  12.4 0.3 collective-permute-start
  12.8 0.1 add.50
  12.8 0.8 %collective-permute-done = s32[1,32]{1,0:T(1,128)S(1)} collective-permute-done((s32[1,32]{1,0:T(1,128)S(1)}, s32[1,32]{1,0:T(1,128)S(1)}, u32[]{:S(2)}, u32[]{:S(2)}) %collective-permute-start) | collective-permute-done | bytes 160 | tf_op jit(solution)/shard_map/ppermute | solution.py:329
  13.6 0.0 copy-done.1
  13.7 0.1 select_reduce_fusion
  13.8 0.1 add.48
  13.9 0.1 fusion.pick_ref
  14.0 24.2 %all-to-all-done = bf16[32,16,1024]{2,1,0:T(8,128)(2,1)S(1)} async-done(((bf16[32,16,1024]{2,1,0:T(8,128)(2,1)}), bf16[32,16,1024]{2,1,0:T(8,128)(2,1)S(1)}, u32[]{:S(2)}, u32[]{:S(2)}) %all-to-all-start) | async-done | bytes 1048608 | tf_op jit(solution)/shard_map/all_to_all | solution.py:336
  38.2 0.9 %shard_map.65 = (f32[8,32,128]{2,1,0:T(8,128)S(1)}, f32[8,32,128]{2,1,0:T(8,128)S(1)}) custom-call(bf16[2,256,256]{2,1,0:T(8,128)(2,1)S(1)} %fusion.pick_ref, bf16[512,1024]{1,0:T(8,128)(2,1)S(1)} %bitcast.7), custom_call_target="tpu_custom_call" | custom-call | flops 268435456 | bytes 2097152 | tf_op jit(solution)/shard_map/pallas_call | solution.py:266
  39.1 0.1 collective-permute-start.1
  39.2 0.8 %shard_map.66.refs_0_ = f32[16,2,32,64]{3,2,1,0:T(8,128)} custom-call(f32[8,32,128]{2,1,0:T(8,128)S(1)} %get-tuple-element.8.packed_ref), custom_call_target="tpu_custom_call" | custom-call | bytes 262144 | tf_op jit(solution)/shard_map/pallas_call | solution.py:301
  40.0 0.5 %collective-permute-done.1.packed_ref = f32[8,32,128]{2,1,0:T(8,128)S(1)} collective-permute-done((f32[8,32,128]{2,1,0:T(8,128)S(1)}, f32[8,32,128]{2,1,0:T(8,128)S(1)}, u32[]{:S(2)}, u32[]{:S(2)}) %collective-permute-start.1) | collective-permute-done | bytes 131104 | tf_op jit(solution)/shard_map/ppermute | solution.py:341
  40.5 0.8 %shard_map.67 = f32[16,2,32,64]{3,2,1,0:T(8,128)} custom-call(f32[8,32,128]{2,1,0:T(8,128)S(1)} %collective-permute-done.1.packed_ref, f32[16,2,32,64]{3,2,1,0:T(8,128)} %shard_map.66.refs_0_), custom_call_target="tpu_custom_call", output_to_operand_aliasing={{}: (1, {})} | custom-call | bytes 262144 | tf_op jit(solution)/shard_map/pallas_call | solution.py:301
  (5 shorter events, 0.1 us)
Async XLA Ops:
  5.1 7.3 %copy-start = (s32[1,32]{1,0:T(1,128)S(1)}, s32[1,32]{1,0:T(1,128)}, u32[]{:S(2)}) copy-start(s32[1,32]{1,0:T(1,128)} %param.7) | copy-start | bytes 388
  5.1 8.5 %copy-start.1 = (s32[2,16]{1,0:T(2,128)S(1)}, s32[2,16]{1,0:T(2,128)}, u32[]{:S(2)}) copy-start(s32[2,16]{1,0:T(2,128)} %constant.42.clone) | copy-start | bytes 388
  5.1 33.1 %all-to-all-start = ((bf16[32,16,1024]{2,1,0:T(8,128)(2,1)}), bf16[32,16,1024]{2,1,0:T(8,128)(2,1)S(1)}, u32[]{:S(2)}, u32[]{:S(2)}) async-start(bf16[32,16,1024]{2,1,0:T(8,128)(2,1)} %bitcast.8), calls=%async_computation | async-start | bytes 2097152 | tf_op jit(solution)/shard_map/all_to_all | solution.py:336
  12.4 1.2 %collective-permute-start = (s32[1,32]{1,0:T(1,128)S(1)}, s32[1,32]{1,0:T(1,128)S(1)}, u32[]{:S(2)}, u32[]{:S(2)}) collective-permute-start(s32[1,32]{1,0:T(1,128)S(1)} %copy-done), channel_id=1, source_target_pairs={{0,1},{1,0},{2,3},{3,2},{4,5},{5,4},{6,7},{7,6},{8,9},{9,8},{10,11... | collective-permute-start | bytes 392 | tf_op jit(solution)/shard_map/ppermute | solution.py:329
  39.1 1.4 %collective-permute-start.1 = (f32[8,32,128]{2,1,0:T(8,128)S(1)}, f32[8,32,128]{2,1,0:T(8,128)S(1)}, u32[]{:S(2)}, u32[]{:S(2)}) collective-permute-start(f32[8,32,128]{2,1,0:T(8,128)S(1)} %get-tuple-element.7), channel_id=1, source_target_pairs={{0,1},{1,0},{2,3},{3,2},{4,5},{5,4},{6,7},{7,6},{8,9},{9,8},{10,11... | collective-permute-start | bytes 393224 | tf_op jit(solution)/shard_map/ppermute | solution.py:341

commit v21 on v19

--- a/solution.py
+++ b/solution.py
@@ -75,7 +75,7 @@
         return pl.ds(edges[n] * spread, (edges[n + 1] - edges[n]) * spread)
 
     chunks = len(edges) - 1
-    loads = [load(x_hbm.at[span(n)], held.at[span(n)], n) for n in range(chunks)]
+    loads = [load(x_hbm.at[span(n)], held.at[span(n)], n) for n in range(chunks - 1)]
     load_taps = load(taps_hbm, taps_all, chunks)
     load_flags = load(flags_hbm, flags, chunks + 2)
 
@@ -113,14 +113,15 @@
                 both = jnp.concatenate(out[b : b + 2], axis=0).astype(jnp.bfloat16)
                 fir[i, pl.ds(g * GROUP + (first + b) * SUB, 2 * SUB), cols] = both
 
-    def transform(g, i):
+    def transform(g, i, points=pl.ds(0, FRAME), add=False):
         part = pl.ds(g * GROUP, GROUP)
-        spectra[i, :, part] = lax.dot_general(
-            table[...],
-            fir[i, part, :],
+        product = lax.dot_general(
+            table[:, points],
+            fir[i, part, points],
             (((1,), (1,)), ((), ())),
             preferred_element_type=jnp.float32,
         )
+        spectra[i, :, part] = spectra[i, :, part] + product if add else product
 
     def rate(i):
         good = (1 - flags[i]).astype(jnp.float32)
@@ -151,6 +152,7 @@
         return copy
 
     loads[0].wait()
+    loads.append(load(x_hbm.at[span(chunks - 1)], held.at[span(chunks - 1)], chunks - 1))
     convert(0)
     load_taps.wait()
     loads[1].wait()
@@ -165,12 +167,15 @@
     for i in range(inputs):
         transform(0, i)
     convert(2)
+    halves = pl.ds(0, FRAME // 2), pl.ds(FRAME // 2, FRAME // 2)
     for i in range(inputs):
         if i > 0:
             transform(1, i - 1)
         for j in range(FRAME // LANES):
+            if i == inputs - 1 and j == FRAME // LANES // 2:
+                transform(1, i, halves[0])
             filter_group(1, i, j)
-    transform(1, inputs - 1)
+    transform(1, inputs - 1, halves[1], add=True)
     for i in range(inputs):
         rate(i)
     copies = [pack(piece) for piece in range(pieces)]

time: 41.1 us -> 41.1 us (level)
  no operation moved by 1% of the time
where the time goes in v21:
time: 41.1 us; the launch traced here: 40.8 us
  waiting for transfers between devices  25 us (61%)
  starting transfers between devices  7.7 us (19%)
  Pallas kernels  7.57 us (18%)
    all_to_all x1, waiting for transfers between devices, split_channels(): lax.all_to_all(sent, axes, split_axis=0, concat_axis=0, axis_index_groups...  23.7 us
    all_to_all x1, starting transfers between devices, split_channels(): lax.all_to_all(sent, axes, split_axis=0, concat_axis=0, axis_index_groups...  7.31 us
    pallas_call x1, Pallas kernels, channelize(): pl.pallas_call(channelize_kernel, out_shape=jax.ShapeDtypeStruct((FRAME,...  5.1 us
    pallas_call x2, Pallas kernels, place(): pl.pallas_call(functools.partial(place_kernel, own=base is None), out_sha...  1.6 us
    pallas_call x1, Pallas kernels, correlate(): pl.pallas_call(functools.partial(correlate_kernel, order=order), out_shap...  0.87 us
  transfers between devices with their start and end apart: 3, of which 3 were waited for; matrix products, arithmetic and copies ran while one was open for 1% of the time, Pallas kernels for 2%

profile of v21, /device:TPU:0, one launch (start us, length us, event | category | flops | bytes accessed | tf_op | source)
XLA Modules:
  0.0 40.8 jit_solution(662842499615839561)
XLA Ops:
  0.0 5.1 %shard_map.64 = bf16[512,1024]{1,0:T(8,128)(2,1)} custom-call(s32[2]{0:T(128)} %flags_hbm.1, bf16[4184,128]{1,0:T(8,128)(2,1)} %bitcast.9, f32[12,512]{1,0:T(8,128)} %constant.41.clone.taps_hbm, bf16[512,512]{1,0:T(8,128)(2,1)} %constant.40.clone.table_hbm), custom_call_target="tpu_custom_call" | custom-call | flops 549453824 | bytes 2097152 | tf_op jit(solution)/shard_map/pallas_call | solution.py:196
  5.1 0.0 copy-start
  5.1 0.0 copy-start.1
  5.1 7.3 %all-to-all-start = ((bf16[32,16,1024]{2,1,0:T(8,128)(2,1)}), bf16[32,16,1024]{2,1,0:T(8,128)(2,1)S(1)}, u32[]{:S(2)}, u32[]{:S(2)}) async-start(bf16[32,16,1024]{2,1,0:T(8,128)(2,1)} %bitcast.8), calls=%async_computation | async-start | bytes 2097152 | tf_op jit(solution)/shard_map/all_to_all | solution.py:340
  12.5 0.0 copy-done
  12.5 0.3 collective-permute-start
  12.8 0.1 add.50
  12.9 0.8 %collective-permute-done = s32[1,32]{1,0:T(1,128)S(1)} collective-permute-done((s32[1,32]{1,0:T(1,128)S(1)}, s32[1,32]{1,0:T(1,128)S(1)}, u32[]{:S(2)}, u32[]{:S(2)}) %collective-permute-start) | collective-permute-done | bytes 160 | tf_op jit(solution)/shard_map/ppermute | solution.py:333
  13.7 0.0 copy-done.1
  13.7 0.1 select_reduce_fusion
  13.8 0.1 add.48
  13.9 0.1 fusion.pick_ref
  14.0 23.7 %all-to-all-done = bf16[32,16,1024]{2,1,0:T(8,128)(2,1)S(1)} async-done(((bf16[32,16,1024]{2,1,0:T(8,128)(2,1)}), bf16[32,16,1024]{2,1,0:T(8,128)(2,1)S(1)}, u32[]{:S(2)}, u32[]{:S(2)}) %all-to-all-start) | async-done | bytes 1048608 | tf_op jit(solution)/shard_map/all_to_all | solution.py:340
  37.8 0.9 %shard_map.65 = (f32[8,32,128]{2,1,0:T(8,128)S(1)}, f32[8,32,128]{2,1,0:T(8,128)S(1)}) custom-call(bf16[2,256,256]{2,1,0:T(8,128)(2,1)S(1)} %fusion.pick_ref, bf16[512,1024]{1,0:T(8,128)(2,1)S(1)} %bitcast.7), custom_call_target="tpu_custom_call" | custom-call | flops 268435456 | bytes 2097152 | tf_op jit(solution)/shard_map/pallas_call | solution.py:271
  38.6 0.1 collective-permute-start.1
  38.7 0.8 %shard_map.66.refs_0_ = f32[16,2,32,64]{3,2,1,0:T(8,128)} custom-call(f32[8,32,128]{2,1,0:T(8,128)S(1)} %get-tuple-element.8.packed_ref), custom_call_target="tpu_custom_call" | custom-call | bytes 262144 | tf_op jit(solution)/shard_map/pallas_call | solution.py:306
  39.5 0.5 %collective-permute-done.1.packed_ref = f32[8,32,128]{2,1,0:T(8,128)S(1)} collective-permute-done((f32[8,32,128]{2,1,0:T(8,128)S(1)}, f32[8,32,128]{2,1,0:T(8,128)S(1)}, u32[]{:S(2)}, u32[]{:S(2)}) %collective-permute-start.1) | collective-permute-done | bytes 131104 | tf_op jit(solution)/shard_map/ppermute | solution.py:345
  40.1 0.8 %shard_map.67 = f32[16,2,32,64]{3,2,1,0:T(8,128)} custom-call(f32[8,32,128]{2,1,0:T(8,128)S(1)} %collective-permute-done.1.packed_ref, f32[16,2,32,64]{3,2,1,0:T(8,128)} %shard_map.66.refs_0_), custom_call_target="tpu_custom_call", output_to_operand_aliasing={{}: (1, {})} | custom-call | bytes 262144 | tf_op jit(solution)/shard_map/pallas_call | solution.py:306
  (5 shorter events, 0.1 us)
Async XLA Ops:
  5.1 7.3 %copy-start = (s32[1,32]{1,0:T(1,128)S(1)}, s32[1,32]{1,0:T(1,128)}, u32[]{:S(2)}) copy-start(s32[1,32]{1,0:T(1,128)} %param.7) | copy-start | bytes 388
  5.1 8.5 %copy-start.1 = (s32[2,16]{1,0:T(2,128)S(1)}, s32[2,16]{1,0:T(2,128)}, u32[]{:S(2)}) copy-start(s32[2,16]{1,0:T(2,128)} %constant.42.clone) | copy-start | bytes 388
  5.1 32.6 %all-to-all-start = ((bf16[32,16,1024]{2,1,0:T(8,128)(2,1)}), bf16[32,16,1024]{2,1,0:T(8,128)(2,1)S(1)}, u32[]{:S(2)}, u32[]{:S(2)}) async-start(bf16[32,16,1024]{2,1,0:T(8,128)(2,1)} %bitcast.8), calls=%async_computation | async-start | bytes 2097152 | tf_op jit(solution)/shard_map/all_to_all | solution.py:340
  12.5 1.2 %collective-permute-start = (s32[1,32]{1,0:T(1,128)S(1)}, s32[1,32]{1,0:T(1,128)S(1)}, u32[]{:S(2)}, u32[]{:S(2)}) collective-permute-start(s32[1,32]{1,0:T(1,128)S(1)} %copy-done), channel_id=1, source_target_pairs={{0,1},{1,0},{2,3},{3,2},{4,5},{5,4},{6,7},{7,6},{8,9},{9,8},{10,11... | collective-permute-start | bytes 392 | tf_op jit(solution)/shard_map/ppermute | solution.py:333
  38.6 1.4 %collective-permute-start.1 = (f32[8,32,128]{2,1,0:T(8,128)S(1)}, f32[8,32,128]{2,1,0:T(8,128)S(1)}, u32[]{:S(2)}, u32[]{:S(2)}) collective-permute-start(f32[8,32,128]{2,1,0:T(8,128)S(1)} %get-tuple-element.7), channel_id=1, source_target_pairs={{0,1},{1,0},{2,3},{3,2},{4,5},{5,4},{6,7},{7,6},{8,9},{9,8},{10,11... | collective-permute-start | bytes 393224 | tf_op jit(solution)/shard_map/ppermute | solution.py:345

commit v22 on v19

--- a/solution.py
+++ b/solution.py
@@ -95,20 +95,22 @@
             first = (inputs * j + i) * PITCH + g * GROUP + b
             return wide[pl.ds(first, SUB, stride=STRIDE), :]
 
+        window = []
+
         def total(first, count):
-            window = [take(first + b) for b in range(count + TAPS - 1)]
-            out = [taps[0] * window[b] for b in range(count)]
+            while len(window) < first + count + TAPS - 1:
+                window.append(take(len(window)))
+            out = [taps[0] * window[first + b] for b in range(count)]
             for t in range(1, TAPS):
-                out = [out[b] + taps[t] * window[b + t] for b in range(count)]
+                out = [out[b] + taps[t] * window[first + b + t] for b in range(count)]
             return out
 
-        extra = total(STEP, 1)[0]
         for first in range(0, STEP, SUB):
-            out = total(first, SUB)
-            for b in range(SUB):
-                past = first + b - (STEP - SUB + 1)
-                if past >= 0:
-                    out[b] = jnp.where(last, pltpu.roll(extra, SUB - 1 - past, 0), out[b])
+            final = first + SUB == STEP
+            out = total(first, SUB + 1 if final else SUB)
+            for m in range(SUB - 1 if final else 0):
+                moved = pltpu.roll(out[SUB], SUB - 1 - m, 0)
+                out[m + 1] = jnp.where(last, moved, out[m + 1])
             for b in range(0, SUB, 2):
                 both = jnp.concatenate(out[b : b + 2], axis=0).astype(jnp.bfloat16)
                 fir[i, pl.ds(g * GROUP + (first + b) * SUB, 2 * SUB), cols] = both

time: 41.1 us -> 41.1 us (level)
  no operation moved by 1% of the time
where the time goes in v22:
time: 41.1 us; the launch traced here: 40.8 us
  waiting for transfers between devices  25 us (61%)
  starting transfers between devices  7.7 us (19%)
  Pallas kernels  7.56 us (18%)
    all_to_all x1, waiting for transfers between devices, split_channels(): lax.all_to_all(sent, axes, split_axis=0, concat_axis=0, axis_index_groups...  23.7 us
    all_to_all x1, starting transfers between devices, split_channels(): lax.all_to_all(sent, axes, split_axis=0, concat_axis=0, axis_index_groups...  7.31 us
    pallas_call x1, Pallas kernels, channelize(): pl.pallas_call(channelize_kernel, out_shape=jax.ShapeDtypeStruct((FRAME,...  5.09 us
    pallas_call x2, Pallas kernels, place(): pl.pallas_call(functools.partial(place_kernel, own=base is None), out_sha...  1.6 us
    pallas_call x1, Pallas kernels, correlate(): pl.pallas_call(functools.partial(correlate_kernel, order=order), out_shap...  0.87 us
  transfers between devices with their start and end apart: 3, of which 3 were waited for; matrix products, arithmetic and copies ran while one was open for 1% of the time, Pallas kernels for 2%

profile of v22, /device:TPU:0, one launch (start us, length us, event | category | flops | bytes accessed | tf_op | source)
XLA Modules:
  0.0 40.8 jit_solution(7025495371223007228)
XLA Ops:
  0.0 5.1 %shard_map.64 = bf16[512,1024]{1,0:T(8,128)(2,1)} custom-call(s32[2]{0:T(128)} %flags_hbm.1, bf16[4184,128]{1,0:T(8,128)(2,1)} %bitcast.9, f32[12,512]{1,0:T(8,128)} %constant.41.clone.taps_hbm, bf16[512,512]{1,0:T(8,128)(2,1)} %constant.40.clone.table_hbm), custom_call_target="tpu_custom_call" | custom-call | flops 549453824 | bytes 2097152 | tf_op jit(solution)/shard_map/pallas_call | solution.py:193
  5.1 0.0 copy-start
  5.1 0.0 copy-start.1
  5.1 7.3 %all-to-all-start = ((bf16[32,16,1024]{2,1,0:T(8,128)(2,1)}), bf16[32,16,1024]{2,1,0:T(8,128)(2,1)S(1)}, u32[]{:S(2)}, u32[]{:S(2)}) async-start(bf16[32,16,1024]{2,1,0:T(8,128)(2,1)} %bitcast.8), calls=%async_computation | async-start | bytes 2097152 | tf_op jit(solution)/shard_map/all_to_all | solution.py:337
  12.4 0.0 copy-done
  12.4 0.3 collective-permute-start
  12.8 0.1 add.50
  12.8 0.8 %collective-permute-done = s32[1,32]{1,0:T(1,128)S(1)} collective-permute-done((s32[1,32]{1,0:T(1,128)S(1)}, s32[1,32]{1,0:T(1,128)S(1)}, u32[]{:S(2)}, u32[]{:S(2)}) %collective-permute-start) | collective-permute-done | bytes 160 | tf_op jit(solution)/shard_map/ppermute | solution.py:330
  13.6 0.0 copy-done.1
  13.7 0.1 select_reduce_fusion
  13.8 0.1 add.48
  13.9 0.1 fusion.pick_ref
  14.0 23.7 %all-to-all-done = bf16[32,16,1024]{2,1,0:T(8,128)(2,1)S(1)} async-done(((bf16[32,16,1024]{2,1,0:T(8,128)(2,1)}), bf16[32,16,1024]{2,1,0:T(8,128)(2,1)S(1)}, u32[]{:S(2)}, u32[]{:S(2)}) %all-to-all-start) | async-done | bytes 1048608 | tf_op jit(solution)/shard_map/all_to_all | solution.py:337
  37.7 0.9 %shard_map.65 = (f32[8,32,128]{2,1,0:T(8,128)S(1)}, f32[8,32,128]{2,1,0:T(8,128)S(1)}) custom-call(bf16[2,256,256]{2,1,0:T(8,128)(2,1)S(1)} %fusion.pick_ref, bf16[512,1024]{1,0:T(8,128)(2,1)S(1)} %bitcast.7), custom_call_target="tpu_custom_call" | custom-call | flops 268435456 | bytes 2097152 | tf_op jit(solution)/shard_map/pallas_call | solution.py:268
  38.6 0.1 collective-permute-start.1
  38.7 0.8 %shard_map.66.refs_0_ = f32[16,2,32,64]{3,2,1,0:T(8,128)} custom-call(f32[8,32,128]{2,1,0:T(8,128)S(1)} %get-tuple-element.8.packed_ref), custom_call_target="tpu_custom_call" | custom-call | bytes 262144 | tf_op jit(solution)/shard_map/pallas_call | solution.py:303
  39.5 0.5 %collective-permute-done.1.packed_ref = f32[8,32,128]{2,1,0:T(8,128)S(1)} collective-permute-done((f32[8,32,128]{2,1,0:T(8,128)S(1)}, f32[8,32,128]{2,1,0:T(8,128)S(1)}, u32[]{:S(2)}, u32[]{:S(2)}) %collective-permute-start.1) | collective-permute-done | bytes 131104 | tf_op jit(solution)/shard_map/ppermute | solution.py:342
  40.0 0.8 %shard_map.67 = f32[16,2,32,64]{3,2,1,0:T(8,128)} custom-call(f32[8,32,128]{2,1,0:T(8,128)S(1)} %collective-permute-done.1.packed_ref, f32[16,2,32,64]{3,2,1,0:T(8,128)} %shard_map.66.refs_0_), custom_call_target="tpu_custom_call", output_to_operand_aliasing={{}: (1, {})} | custom-call | bytes 262144 | tf_op jit(solution)/shard_map/pallas_call | solution.py:303
  (5 shorter events, 0.1 us)
Async XLA Ops:
  5.1 7.3 %copy-start = (s32[1,32]{1,0:T(1,128)S(1)}, s32[1,32]{1,0:T(1,128)}, u32[]{:S(2)}) copy-start(s32[1,32]{1,0:T(1,128)} %param.7) | copy-start | bytes 388
  5.1 8.5 %copy-start.1 = (s32[2,16]{1,0:T(2,128)S(1)}, s32[2,16]{1,0:T(2,128)}, u32[]{:S(2)}) copy-start(s32[2,16]{1,0:T(2,128)} %constant.42.clone) | copy-start | bytes 388
  5.1 32.6 %all-to-all-start = ((bf16[32,16,1024]{2,1,0:T(8,128)(2,1)}), bf16[32,16,1024]{2,1,0:T(8,128)(2,1)S(1)}, u32[]{:S(2)}, u32[]{:S(2)}) async-start(bf16[32,16,1024]{2,1,0:T(8,128)(2,1)} %bitcast.8), calls=%async_computation | async-start | bytes 2097152 | tf_op jit(solution)/shard_map/all_to_all | solution.py:337
  12.4 1.2 %collective-permute-start = (s32[1,32]{1,0:T(1,128)S(1)}, s32[1,32]{1,0:T(1,128)S(1)}, u32[]{:S(2)}, u32[]{:S(2)}) collective-permute-start(s32[1,32]{1,0:T(1,128)S(1)} %copy-done), channel_id=1, source_target_pairs={{0,1},{1,0},{2,3},{3,2},{4,5},{5,4},{6,7},{7,6},{8,9},{9,8},{10,11... | collective-permute-start | bytes 392 | tf_op jit(solution)/shard_map/ppermute | solution.py:330
  38.6 1.4 %collective-permute-start.1 = (f32[8,32,128]{2,1,0:T(8,128)S(1)}, f32[8,32,128]{2,1,0:T(8,128)S(1)}, u32[]{:S(2)}, u32[]{:S(2)}) collective-permute-start(f32[8,32,128]{2,1,0:T(8,128)S(1)} %get-tuple-element.7), channel_id=1, source_target_pairs={{0,1},{1,0},{2,3},{3,2},{4,5},{5,4},{6,7},{7,6},{8,9},{9,8},{10,11... | collective-permute-start | bytes 393224 | tf_op jit(solution)/shard_map/ppermute | solution.py:342

commit v23 on v22

--- a/solution.py
+++ b/solution.py
@@ -78,6 +78,7 @@
     loads = [load(x_hbm.at[span(n)], held.at[span(n)], n) for n in range(chunks)]
     load_taps = load(taps_hbm, taps_all, chunks)
     load_flags = load(flags_hbm, flags, chunks + 2)
+    load_table = load(table_hbm, table, chunks + 1)
 
     def convert(n):
         for f in range(edges[n], edges[n + 1], 2):
@@ -152,18 +153,13 @@
         copy.start()
         return copy
 
-    loads[0].wait()
+    for copy in [*loads, load_taps, load_flags, load_table]:
+        copy.wait()
     convert(0)
-    load_taps.wait()
-    loads[1].wait()
-    load_table = load(table_hbm, table, chunks + 1)
     convert(1)
     for i in range(inputs):
         for j in range(FRAME // LANES):
             filter_group(0, i, j)
-    loads[2].wait()
-    load_table.wait()
-    load_flags.wait()
     for i in range(inputs):
         transform(0, i)
     convert(2)

time: 41.1 us -> 41.4 us (level)
  no operation moved by 1% of the time
where the time goes in v23:
time: 41.4 us; the launch traced here: 41.2 us
  waiting for transfers between devices  25 us (60%)
  Pallas kernels  7.9 us (19%)
  starting transfers between devices  7.69 us (19%)
    all_to_all x1, waiting for transfers between devices, split_channels(): lax.all_to_all(sent, axes, split_axis=0, concat_axis=0, axis_index_groups...  23.7 us
    all_to_all x1, starting transfers between devices, split_channels(): lax.all_to_all(sent, axes, split_axis=0, concat_axis=0, axis_index_groups...  7.3 us
    pallas_call x1, Pallas kernels, channelize(): pl.pallas_call(channelize_kernel, out_shape=jax.ShapeDtypeStruct((FRAME,...  5.44 us
    pallas_call x2, Pallas kernels, place(): pl.pallas_call(functools.partial(place_kernel, own=base is None), out_sha...  1.6 us
    pallas_call x1, Pallas kernels, correlate(): pl.pallas_call(functools.partial(correlate_kernel, order=order), out_shap...  0.87 us
  transfers between devices with their start and end apart: 3, of which 3 were waited for; matrix products, arithmetic and copies ran while one was open for 1% of the time, Pallas kernels for 2%

profile of v23, /device:TPU:0, one launch (start us, length us, event | category | flops | bytes accessed | tf_op | source)
XLA Modules:
  0.0 41.2 jit_solution(8008690454583076942)
XLA Ops:
  0.0 5.4 %shard_map.64 = bf16[512,1024]{1,0:T(8,128)(2,1)} custom-call(s32[2]{0:T(128)} %flags_hbm.1, bf16[4184,128]{1,0:T(8,128)(2,1)} %bitcast.9, f32[12,512]{1,0:T(8,128)} %constant.41.clone.taps_hbm, bf16[512,512]{1,0:T(8,128)(2,1)} %constant.40.clone.table_hbm), custom_call_target="tpu_custom_call" | custom-call | flops 549453824 | bytes 2097152 | tf_op jit(solution)/shard_map/pallas_call | solution.py:189
  5.4 0.0 copy-start
  5.5 0.0 copy-start.1
  5.5 7.3 %all-to-all-start = ((bf16[32,16,1024]{2,1,0:T(8,128)(2,1)}), bf16[32,16,1024]{2,1,0:T(8,128)(2,1)S(1)}, u32[]{:S(2)}, u32[]{:S(2)}) async-start(bf16[32,16,1024]{2,1,0:T(8,128)(2,1)} %bitcast.8), calls=%async_computation | async-start | bytes 2097152 | tf_op jit(solution)/shard_map/all_to_all | solution.py:333
  12.8 0.0 copy-done
  12.8 0.3 collective-permute-start
  13.1 0.1 add.50
  13.2 0.8 %collective-permute-done = s32[1,32]{1,0:T(1,128)S(1)} collective-permute-done((s32[1,32]{1,0:T(1,128)S(1)}, s32[1,32]{1,0:T(1,128)S(1)}, u32[]{:S(2)}, u32[]{:S(2)}) %collective-permute-start) | collective-permute-done | bytes 160 | tf_op jit(solution)/shard_map/ppermute | solution.py:326
  14.0 0.0 copy-done.1
  14.0 0.1 select_reduce_fusion
  14.1 0.1 add.48
  14.2 0.1 fusion.pick_ref
  14.4 23.7 %all-to-all-done = bf16[32,16,1024]{2,1,0:T(8,128)(2,1)S(1)} async-done(((bf16[32,16,1024]{2,1,0:T(8,128)(2,1)}), bf16[32,16,1024]{2,1,0:T(8,128)(2,1)S(1)}, u32[]{:S(2)}, u32[]{:S(2)}) %all-to-all-start) | async-done | bytes 1048608 | tf_op jit(solution)/shard_map/all_to_all | solution.py:333
  38.1 0.9 %shard_map.65 = (f32[8,32,128]{2,1,0:T(8,128)S(1)}, f32[8,32,128]{2,1,0:T(8,128)S(1)}) custom-call(bf16[2,256,256]{2,1,0:T(8,128)(2,1)S(1)} %fusion.pick_ref, bf16[512,1024]{1,0:T(8,128)(2,1)S(1)} %bitcast.7), custom_call_target="tpu_custom_call" | custom-call | flops 268435456 | bytes 2097152 | tf_op jit(solution)/shard_map/pallas_call | solution.py:264
  39.0 0.1 collective-permute-start.1
  39.0 0.8 %shard_map.66.refs_0_ = f32[16,2,32,64]{3,2,1,0:T(8,128)} custom-call(f32[8,32,128]{2,1,0:T(8,128)S(1)} %get-tuple-element.8.packed_ref), custom_call_target="tpu_custom_call" | custom-call | bytes 262144 | tf_op jit(solution)/shard_map/pallas_call | solution.py:299
  39.9 0.5 %collective-permute-done.1.packed_ref = f32[8,32,128]{2,1,0:T(8,128)S(1)} collective-permute-done((f32[8,32,128]{2,1,0:T(8,128)S(1)}, f32[8,32,128]{2,1,0:T(8,128)S(1)}, u32[]{:S(2)}, u32[]{:S(2)}) %collective-permute-start.1) | collective-permute-done | bytes 131104 | tf_op jit(solution)/shard_map/ppermute | solution.py:338
  40.4 0.8 %shard_map.67 = f32[16,2,32,64]{3,2,1,0:T(8,128)} custom-call(f32[8,32,128]{2,1,0:T(8,128)S(1)} %collective-permute-done.1.packed_ref, f32[16,2,32,64]{3,2,1,0:T(8,128)} %shard_map.66.refs_0_), custom_call_target="tpu_custom_call", output_to_operand_aliasing={{}: (1, {})} | custom-call | bytes 262144 | tf_op jit(solution)/shard_map/pallas_call | solution.py:299
  (5 shorter events, 0.1 us)
Async XLA Ops:
  5.4 7.3 %copy-start = (s32[1,32]{1,0:T(1,128)S(1)}, s32[1,32]{1,0:T(1,128)}, u32[]{:S(2)}) copy-start(s32[1,32]{1,0:T(1,128)} %param.7) | copy-start | bytes 388
  5.5 8.5 %copy-start.1 = (s32[2,16]{1,0:T(2,128)S(1)}, s32[2,16]{1,0:T(2,128)}, u32[]{:S(2)}) copy-start(s32[2,16]{1,0:T(2,128)} %constant.42.clone) | copy-start | bytes 388
  5.5 32.6 %all-to-all-start = ((bf16[32,16,1024]{2,1,0:T(8,128)(2,1)}), bf16[32,16,1024]{2,1,0:T(8,128)(2,1)S(1)}, u32[]{:S(2)}, u32[]{:S(2)}) async-start(bf16[32,16,1024]{2,1,0:T(8,128)(2,1)} %bitcast.8), calls=%async_computation | async-start | bytes 2097152 | tf_op jit(solution)/shard_map/all_to_all | solution.py:333
  12.8 1.2 %collective-permute-start = (s32[1,32]{1,0:T(1,128)S(1)}, s32[1,32]{1,0:T(1,128)S(1)}, u32[]{:S(2)}, u32[]{:S(2)}) collective-permute-start(s32[1,32]{1,0:T(1,128)S(1)} %copy-done), channel_id=1, source_target_pairs={{0,1},{1,0},{2,3},{3,2},{4,5},{5,4},{6,7},{7,6},{8,9},{9,8},{10,11... | collective-permute-start | bytes 392 | tf_op jit(solution)/shard_map/ppermute | solution.py:326
  39.0 1.4 %collective-permute-start.1 = (f32[8,32,128]{2,1,0:T(8,128)S(1)}, f32[8,32,128]{2,1,0:T(8,128)S(1)}, u32[]{:S(2)}, u32[]{:S(2)}) collective-permute-start(f32[8,32,128]{2,1,0:T(8,128)S(1)} %get-tuple-element.7), channel_id=1, source_target_pairs={{0,1},{1,0},{2,3},{3,2},{4,5},{5,4},{6,7},{7,6},{8,9},{9,8},{10,11... | collective-permute-start | bytes 393224 | tf_op jit(solution)/shard_map/ppermute | solution.py:338

commit v24 on v22

--- a/solution.py
+++ b/solution.py
@@ -61,7 +61,7 @@
     frames = SPEC + TAPS - 1
     spread = inputs * FRAME // LANES
     groups = SPEC // GROUP
-    pieces = sems.shape[0]
+    pieces = sems.shape[1]
     rows = FRAME // pieces
     last = lax.broadcasted_iota(jnp.int32, (SUB, LANES), 0) == SUB - 1
     edges = [0, GROUP // 2] + [g * GROUP + TAPS for g in range(1, groups)] + [frames]
@@ -142,13 +142,15 @@
         scale = jnp.concatenate([scale] * (SPEC // LANES), axis=1)
         return pairs * scale.reshape(rows // (2 * SUB), 1, SUB, SPEC)
 
-    def pack(piece):
-        place = pl.ds(piece * rows, rows)
-        parts = [scaled(i, piece) for i in range(inputs)]
+    def pack(i, piece):
+        part = scaled(i, piece).astype(jnp.bfloat16)
         for p in range(2):
-            both = jnp.concatenate([part[:, p] for part in parts], axis=1)
-            result[place, pl.ds(p * SPEC, SPEC)] = both.astype(jnp.bfloat16).reshape(rows, SPEC)
-        copy = pltpu.make_async_copy(result.at[place], out_hbm.at[place], sems.at[piece])
+            place = (pl.ds(piece * rows // 2, rows // 2), pl.ds((2 * i + p) * SPEC, SPEC))
+            result[place] = part[:, p].reshape(rows // 2, SPEC)
+
+    def store(i, piece):
+        place = (pl.ds(piece * rows // 2, rows // 2), pl.ds(2 * i * SPEC, 2 * SPEC))
+        copy = pltpu.make_async_copy(result.at[place], out_hbm.at[place], sems.at[i, piece])
         copy.start()
         return copy
 
@@ -167,15 +169,22 @@
     for i in range(inputs):
         transform(0, i)
     convert(2)
+    copies = []
     for i in range(inputs):
         if i > 0:
             transform(1, i - 1)
         for j in range(FRAME // LANES):
             filter_group(1, i, j)
+        if i > 0:
+            rate(i - 1)
+            for piece in range(pieces):
+                pack(i - 1, piece)
+            copies += [store(i - 1, piece) for piece in range(pieces)]
     transform(1, inputs - 1)
-    for i in range(inputs):
-        rate(i)
-    copies = [pack(piece) for piece in range(pieces)]
+    rate(inputs - 1)
+    for piece in range(pieces):
+        pack(inputs - 1, piece)
+        copies.append(store(inputs - 1, piece))
     for copy in copies:
         copy.wait()
 
@@ -192,7 +201,7 @@
     hbm = pl.BlockSpec(memory_space=pltpu.HBM)
     return pl.pallas_call(
         channelize_kernel,
-        out_shape=jax.ShapeDtypeStruct((FRAME, inputs * SPEC), jnp.bfloat16),
+        out_shape=jax.ShapeDtypeStruct((CH, inputs * 2 * SPEC), jnp.bfloat16),
         in_specs=[hbm] * 4,
         out_specs=hbm,
         scratch_shapes=[
@@ -204,9 +213,9 @@
             pltpu.VMEM((inputs, SPEC, FRAME), jnp.bfloat16),
             pltpu.VMEM((inputs, FRAME, SPEC), jnp.float32),
             pltpu.VMEM((inputs, CH, LANES), jnp.float32),
-            pltpu.VMEM((FRAME, inputs * SPEC), jnp.bfloat16),
+            pltpu.VMEM((CH, inputs * 2 * SPEC), jnp.bfloat16),
             pltpu.SemaphoreType.DMA((SPEC // GROUP + 4,)),
-            pltpu.SemaphoreType.DMA((8,)),
+            pltpu.SemaphoreType.DMA((inputs, 4)),
         ],
         cost_estimate=pl.CostEstimate(
             flops=2 * inputs * SPEC * FRAME * (FRAME + TAPS),
@@ -220,13 +229,16 @@
     share, block, _ = own_ref.shape
     blocks = pick_ref.shape[0]
     width = blocks * block
-    held = arrived_ref.shape[0] // len(order)
     first = lax.axis_index("blk") == 0
     lane = lax.broadcasted_iota(jnp.int32, (width, 2 * width), 1)
     sign = jnp.where(lane < width, 1.0 / SPEC, -1.0 / SPEC)
     for n in range(blocks):
         places = [place for place, device in enumerate(order) if device % blocks == n]
-        rows = [arrived_ref[pl.ds(place * held, held), :] for place in places]
+        rows = [
+            arrived_ref[pl.ds(place * share, 2 * share), pl.ds(2 * i * SPEC, 2 * SPEC)]
+            for i in range(arrived_ref.shape[1] // (2 * SPEC))
+            for place in places[::2]
+        ]
         slots[n] = jnp.dot(
             pick_ref[n], jnp.concatenate(rows, axis=0), preferred_element_type=jnp.float32
         ).astype(jnp.bfloat16)
@@ -254,7 +266,7 @@
     known = jnp.asarray(np.stack(rank), dtype=jnp.int32)
     match = device[:, :, None] == jnp.arange(known.shape[1], dtype=jnp.int32)
     place = jnp.sum(jnp.where(match, known[:, None, :], 0), axis=2)
-    start = ((place * inputs + held) * share)[:, None, :]
+    start = ((held * known.shape[1] + place) * share)[:, None, :]
     chan = jnp.arange(share, dtype=jnp.int32)[:, None]
     target = (start + chan).reshape(blocks, share * block, 1)
     column = lax.broadcasted_iota(jnp.int32, (1, 1, known.shape[1] * inputs * share), 2)

time: 41.1 us -> 41.1 us (level)
  no operation moved by 1% of the time
where the time goes in v24:
time: 41.1 us; the launch traced here: 40.9 us
  waiting for transfers between devices  25 us (61%)
  starting transfers between devices  7.69 us (19%)
  Pallas kernels  7.59 us (18%)
    all_to_all x1, waiting for transfers between devices, split_channels(): lax.all_to_all(sent, axes, split_axis=0, concat_axis=0, axis_index_groups...  23.7 us
    all_to_all x1, starting transfers between devices, split_channels(): lax.all_to_all(sent, axes, split_axis=0, concat_axis=0, axis_index_groups...  7.31 us
    pallas_call x1, Pallas kernels, channelize(): pl.pallas_call(channelize_kernel, out_shape=jax.ShapeDtypeStruct((CH, inp...  5.12 us
    pallas_call x2, Pallas kernels, place(): pl.pallas_call(functools.partial(place_kernel, own=base is None), out_sha...  1.6 us
    pallas_call x1, Pallas kernels, correlate(): pl.pallas_call(functools.partial(correlate_kernel, order=order), out_shap...  0.87 us
  transfers between devices with their start and end apart: 3, of which 3 were waited for; matrix products, arithmetic and copies ran while one was open for 1% of the time, Pallas kernels for 2%

profile of v24, /device:TPU:0, one launch (start us, length us, event | category | flops | bytes accessed | tf_op | source)
XLA Modules:
  0.0 40.9 jit_solution(12582678024114359762)
XLA Ops:
  0.0 5.1 %shard_map.64 = bf16[256,2048]{1,0:T(8,128)(2,1)} custom-call(s32[2]{0:T(128)} %flags_hbm.1, bf16[4184,128]{1,0:T(8,128)(2,1)} %bitcast.9, f32[12,512]{1,0:T(8,128)} %constant.42.clone.taps_hbm, bf16[512,512]{1,0:T(8,128)(2,1)} %constant.41.clone.table_hbm), custom_call_target="tpu_custom_call" | custom-call | flops 549453824 | bytes 2097152 | tf_op jit(solution)/shard_map/pallas_call | solution.py:202
  5.1 0.0 copy-start
  5.1 0.0 copy-start.1
  5.2 7.3 %all-to-all-start = ((bf16[32,8,2048]{2,1,0:T(8,128)(2,1)}), bf16[32,8,2048]{2,1,0:T(8,128)(2,1)S(1)}, u32[]{:S(2)}, u32[]{:S(2)}) async-start(bf16[32,8,2048]{2,1,0:T(8,128)(2,1)} %bitcast.8), calls=%async_computation | async-start | bytes 2097152 | tf_op jit(solution)/shard_map/all_to_all | solution.py:349
  12.5 0.0 copy-done
  12.5 0.3 collective-permute-start
  12.8 0.1 add.50
  12.9 0.8 %collective-permute-done = s32[1,32]{1,0:T(1,128)S(1)} collective-permute-done((s32[1,32]{1,0:T(1,128)S(1)}, s32[1,32]{1,0:T(1,128)S(1)}, u32[]{:S(2)}, u32[]{:S(2)}) %collective-permute-start) | collective-permute-done | bytes 160 | tf_op jit(solution)/shard_map/ppermute | solution.py:342
  13.7 0.0 copy-done.1
  13.7 0.1 select_reduce_fusion
  13.8 0.1 add.48
  13.9 0.1 fusion.pick_ref
  14.0 23.7 %all-to-all-done = bf16[32,8,2048]{2,1,0:T(8,128)(2,1)S(1)} async-done(((bf16[32,8,2048]{2,1,0:T(8,128)(2,1)}), bf16[32,8,2048]{2,1,0:T(8,128)(2,1)S(1)}, u32[]{:S(2)}, u32[]{:S(2)}) %all-to-all-start) | async-done | bytes 1048608 | tf_op jit(solution)/shard_map/all_to_all | solution.py:349
  37.8 0.9 %shard_map.65 = (f32[8,32,128]{2,1,0:T(8,128)S(1)}, f32[8,32,128]{2,1,0:T(8,128)S(1)}) custom-call(bf16[2,256,256]{2,1,0:T(8,128)(2,1)S(1)} %fusion.pick_ref, bf16[256,2048]{1,0:T(8,128)(2,1)S(1)} %bitcast.7), custom_call_target="tpu_custom_call" | custom-call | flops 268435456 | bytes 2097152 | tf_op jit(solution)/shard_map/pallas_call | solution.py:280
  38.6 0.1 collective-permute-start.1
  38.7 0.8 %shard_map.66.refs_0_ = f32[16,2,32,64]{3,2,1,0:T(8,128)} custom-call(f32[8,32,128]{2,1,0:T(8,128)S(1)} %get-tuple-element.8.packed_ref), custom_call_target="tpu_custom_call" | custom-call | bytes 262144 | tf_op jit(solution)/shard_map/pallas_call | solution.py:315
  39.5 0.5 %collective-permute-done.1.packed_ref = f32[8,32,128]{2,1,0:T(8,128)S(1)} collective-permute-done((f32[8,32,128]{2,1,0:T(8,128)S(1)}, f32[8,32,128]{2,1,0:T(8,128)S(1)}, u32[]{:S(2)}, u32[]{:S(2)}) %collective-permute-start.1) | collective-permute-done | bytes 131104 | tf_op jit(solution)/shard_map/ppermute | solution.py:354
  40.1 0.8 %shard_map.67 = f32[16,2,32,64]{3,2,1,0:T(8,128)} custom-call(f32[8,32,128]{2,1,0:T(8,128)S(1)} %collective-permute-done.1.packed_ref, f32[16,2,32,64]{3,2,1,0:T(8,128)} %shard_map.66.refs_0_), custom_call_target="tpu_custom_call", output_to_operand_aliasing={{}: (1, {})} | custom-call | bytes 262144 | tf_op jit(solution)/shard_map/pallas_call | solution.py:315
  (5 shorter events, 0.1 us)
Async XLA Ops:
  5.1 7.3 %copy-start = (s32[1,32]{1,0:T(1,128)S(1)}, s32[1,32]{1,0:T(1,128)}, u32[]{:S(2)}) copy-start(s32[1,32]{1,0:T(1,128)} %param.7) | copy-start | bytes 388
  5.1 8.5 %copy-start.1 = (s32[2,16]{1,0:T(2,128)S(1)}, s32[2,16]{1,0:T(2,128)}, u32[]{:S(2)}) copy-start(s32[2,16]{1,0:T(2,128)} %constant.43.clone) | copy-start | bytes 388
  5.2 32.6 %all-to-all-start = ((bf16[32,8,2048]{2,1,0:T(8,128)(2,1)}), bf16[32,8,2048]{2,1,0:T(8,128)(2,1)S(1)}, u32[]{:S(2)}, u32[]{:S(2)}) async-start(bf16[32,8,2048]{2,1,0:T(8,128)(2,1)} %bitcast.8), calls=%async_computation | async-start | bytes 2097152 | tf_op jit(solution)/shard_map/all_to_all | solution.py:349
  12.5 1.2 %collective-permute-start = (s32[1,32]{1,0:T(1,128)S(1)}, s32[1,32]{1,0:T(1,128)S(1)}, u32[]{:S(2)}, u32[]{:S(2)}) collective-permute-start(s32[1,32]{1,0:T(1,128)S(1)} %copy-done), channel_id=1, source_target_pairs={{0,1},{1,0},{2,3},{3,2},{4,5},{5,4},{6,7},{7,6},{8,9},{9,8},{10,11... | collective-permute-start | bytes 392 | tf_op jit(solution)/shard_map/ppermute | solution.py:342
  38.6 1.4 %collective-permute-start.1 = (f32[8,32,128]{2,1,0:T(8,128)S(1)}, f32[8,32,128]{2,1,0:T(8,128)S(1)}, u32[]{:S(2)}, u32[]{:S(2)}) collective-permute-start(f32[8,32,128]{2,1,0:T(8,128)S(1)} %get-tuple-element.7), channel_id=1, source_target_pairs={{0,1},{1,0},{2,3},{3,2},{4,5},{5,4},{6,7},{7,6},{8,9},{9,8},{10,11... | collective-permute-start | bytes 393224 | tf_op jit(solution)/shard_map/ppermute | solution.py:354

commit v25 on v24

--- a/solution.py
+++ b/solution.py
@@ -336,7 +336,8 @@
         z * plane + d
         for z in (3, 2, 0, 1)
         for core in reversed(range(blocks))
-        for d in reversed(range(core, plane, blocks))
+        for half in reversed(range(blocks))
+        for d in reversed(range(core + half * blocks, plane, 2 * blocks))
     ]
     me = lax.axis_index("blk").astype(jnp.int32)
     partner = lax.ppermute(slot_order, "blk", SWAP)

time: 41.1 us -> 41.1 us (level)
  no operation moved by 1% of the time
where the time goes in v25:
time: 41.1 us; the launch traced here: 40.9 us
  waiting for transfers between devices  25 us (61%)
  starting transfers between devices  7.69 us (19%)
  Pallas kernels  7.59 us (18%)
    all_to_all x1, waiting for transfers between devices, split_channels(): lax.all_to_all(sent, axes, split_axis=0, concat_axis=0, axis_index_groups...  23.7 us
    all_to_all x1, starting transfers between devices, split_channels(): lax.all_to_all(sent, axes, split_axis=0, concat_axis=0, axis_index_groups...  7.31 us
    pallas_call x1, Pallas kernels, channelize(): pl.pallas_call(channelize_kernel, out_shape=jax.ShapeDtypeStruct((CH, inp...  5.12 us
    pallas_call x2, Pallas kernels, place(): pl.pallas_call(functools.partial(place_kernel, own=base is None), out_sha...  1.6 us
    pallas_call x1, Pallas kernels, correlate(): pl.pallas_call(functools.partial(correlate_kernel, order=order), out_shap...  0.87 us
  transfers between devices with their start and end apart: 3, of which 3 were waited for; matrix products, arithmetic and copies ran while one was open for 1% of the time, Pallas kernels for 2%

profile of v25, /device:TPU:0, one launch (start us, length us, event | category | flops | bytes accessed | tf_op | source)
XLA Modules:
  0.0 40.9 jit_solution(15119254070750325111)
XLA Ops:
  0.0 5.1 %shard_map.64 = bf16[256,2048]{1,0:T(8,128)(2,1)} custom-call(s32[2]{0:T(128)} %flags_hbm.1, bf16[4184,128]{1,0:T(8,128)(2,1)} %bitcast.9, f32[12,512]{1,0:T(8,128)} %constant.42.clone.taps_hbm, bf16[512,512]{1,0:T(8,128)(2,1)} %constant.41.clone.table_hbm), custom_call_target="tpu_custom_call" | custom-call | flops 549453824 | bytes 2097152 | tf_op jit(solution)/shard_map/pallas_call | solution.py:202
  5.1 0.0 copy-start
  5.1 0.0 copy-start.1
  5.2 7.3 %all-to-all-start = ((bf16[32,8,2048]{2,1,0:T(8,128)(2,1)}), bf16[32,8,2048]{2,1,0:T(8,128)(2,1)S(1)}, u32[]{:S(2)}, u32[]{:S(2)}) async-start(bf16[32,8,2048]{2,1,0:T(8,128)(2,1)} %bitcast.8), calls=%async_computation | async-start | bytes 2097152 | tf_op jit(solution)/shard_map/all_to_all | solution.py:350
  12.5 0.0 copy-done
  12.5 0.3 collective-permute-start
  12.8 0.1 add.50
  12.9 0.8 %collective-permute-done = s32[1,32]{1,0:T(1,128)S(1)} collective-permute-done((s32[1,32]{1,0:T(1,128)S(1)}, s32[1,32]{1,0:T(1,128)S(1)}, u32[]{:S(2)}, u32[]{:S(2)}) %collective-permute-start) | collective-permute-done | bytes 160 | tf_op jit(solution)/shard_map/ppermute | solution.py:343
  13.7 0.0 copy-done.1
  13.7 0.1 select_reduce_fusion
  13.8 0.1 add.48
  13.9 0.1 fusion.pick_ref
  14.0 23.7 %all-to-all-done = bf16[32,8,2048]{2,1,0:T(8,128)(2,1)S(1)} async-done(((bf16[32,8,2048]{2,1,0:T(8,128)(2,1)}), bf16[32,8,2048]{2,1,0:T(8,128)(2,1)S(1)}, u32[]{:S(2)}, u32[]{:S(2)}) %all-to-all-start) | async-done | bytes 1048608 | tf_op jit(solution)/shard_map/all_to_all | solution.py:350
  37.8 0.9 %shard_map.65 = (f32[8,32,128]{2,1,0:T(8,128)S(1)}, f32[8,32,128]{2,1,0:T(8,128)S(1)}) custom-call(bf16[2,256,256]{2,1,0:T(8,128)(2,1)S(1)} %fusion.pick_ref, bf16[256,2048]{1,0:T(8,128)(2,1)S(1)} %bitcast.7), custom_call_target="tpu_custom_call" | custom-call | flops 268435456 | bytes 2097152 | tf_op jit(solution)/shard_map/pallas_call | solution.py:280
  38.6 0.1 collective-permute-start.1
  38.7 0.8 %shard_map.66.refs_0_ = f32[16,2,32,64]{3,2,1,0:T(8,128)} custom-call(f32[8,32,128]{2,1,0:T(8,128)S(1)} %get-tuple-element.8.packed_ref), custom_call_target="tpu_custom_call" | custom-call | bytes 262144 | tf_op jit(solution)/shard_map/pallas_call | solution.py:315
  39.5 0.5 %collective-permute-done.1.packed_ref = f32[8,32,128]{2,1,0:T(8,128)S(1)} collective-permute-done((f32[8,32,128]{2,1,0:T(8,128)S(1)}, f32[8,32,128]{2,1,0:T(8,128)S(1)}, u32[]{:S(2)}, u32[]{:S(2)}) %collective-permute-start.1) | collective-permute-done | bytes 131104 | tf_op jit(solution)/shard_map/ppermute | solution.py:355
  40.1 0.8 %shard_map.67 = f32[16,2,32,64]{3,2,1,0:T(8,128)} custom-call(f32[8,32,128]{2,1,0:T(8,128)S(1)} %collective-permute-done.1.packed_ref, f32[16,2,32,64]{3,2,1,0:T(8,128)} %shard_map.66.refs_0_), custom_call_target="tpu_custom_call", output_to_operand_aliasing={{}: (1, {})} | custom-call | bytes 262144 | tf_op jit(solution)/shard_map/pallas_call | solution.py:315
  (5 shorter events, 0.1 us)
Async XLA Ops:
  5.1 7.3 %copy-start = (s32[1,32]{1,0:T(1,128)S(1)}, s32[1,32]{1,0:T(1,128)}, u32[]{:S(2)}) copy-start(s32[1,32]{1,0:T(1,128)} %param.7) | copy-start | bytes 388
  5.1 8.5 %copy-start.1 = (s32[2,16]{1,0:T(2,128)S(1)}, s32[2,16]{1,0:T(2,128)}, u32[]{:S(2)}) copy-start(s32[2,16]{1,0:T(2,128)} %constant.43.clone) | copy-start | bytes 388
  5.2 32.6 %all-to-all-start = ((bf16[32,8,2048]{2,1,0:T(8,128)(2,1)}), bf16[32,8,2048]{2,1,0:T(8,128)(2,1)S(1)}, u32[]{:S(2)}, u32[]{:S(2)}) async-start(bf16[32,8,2048]{2,1,0:T(8,128)(2,1)} %bitcast.8), calls=%async_computation | async-start | bytes 2097152 | tf_op jit(solution)/shard_map/all_to_all | solution.py:350
  12.5 1.2 %collective-permute-start = (s32[1,32]{1,0:T(1,128)S(1)}, s32[1,32]{1,0:T(1,128)S(1)}, u32[]{:S(2)}, u32[]{:S(2)}) collective-permute-start(s32[1,32]{1,0:T(1,128)S(1)} %copy-done), channel_id=1, source_target_pairs={{0,1},{1,0},{2,3},{3,2},{4,5},{5,4},{6,7},{7,6},{8,9},{9,8},{10,11... | collective-permute-start | bytes 392 | tf_op jit(solution)/shard_map/ppermute | solution.py:343
  38.6 1.4 %collective-permute-start.1 = (f32[8,32,128]{2,1,0:T(8,128)S(1)}, f32[8,32,128]{2,1,0:T(8,128)S(1)}, u32[]{:S(2)}, u32[]{:S(2)}) collective-permute-start(f32[8,32,128]{2,1,0:T(8,128)S(1)} %get-tuple-element.7), channel_id=1, source_target_pairs={{0,1},{1,0},{2,3},{3,2},{4,5},{5,4},{6,7},{7,6},{8,9},{9,8},{10,11... | collective-permute-start | bytes 393224 | tf_op jit(solution)/shard_map/ppermute | solution.py:355

commit v26 on v24

--- a/solution.py
+++ b/solution.py
@@ -332,11 +332,11 @@
     inputs, block = samples.shape[0], slot_order.shape[1]
     axes = ("freq", "blk")
     plane = freq * blocks // 4
+    near = [6, 2, 4, 0, 7, 3, 5, 1]
     order = [
         z * plane + d
         for z in (3, 2, 0, 1)
-        for core in reversed(range(blocks))
-        for d in reversed(range(core, plane, blocks))
+        for d in (near if z == 0 else [7, 5, 3, 1, 6, 4, 2, 0])
     ]
     me = lax.axis_index("blk").astype(jnp.int32)
     partner = lax.ppermute(slot_order, "blk", SWAP)

time: 41.1 us -> 40.9 us (level)
  no operation moved by 1% of the time
where the time goes in v26:
time: 40.9 us; the launch traced here: 40.6 us
  waiting for transfers between devices  24.7 us (60%)
  starting transfers between devices  7.8 us (19%)
  Pallas kernels  7.58 us (19%)
    all_to_all x1, waiting for transfers between devices, split_channels(): lax.all_to_all(sent, axes, split_axis=0, concat_axis=0, axis_index_groups...  23.5 us
    all_to_all x1, starting transfers between devices, split_channels(): lax.all_to_all(sent, axes, split_axis=0, concat_axis=0, axis_index_groups...  7.31 us
    pallas_call x1, Pallas kernels, channelize(): pl.pallas_call(channelize_kernel, out_shape=jax.ShapeDtypeStruct((CH, inp...  5.12 us
    pallas_call x2, Pallas kernels, place(): pl.pallas_call(functools.partial(place_kernel, own=base is None), out_sha...  1.6 us
    pallas_call x1, Pallas kernels, correlate(): pl.pallas_call(functools.partial(correlate_kernel, order=order), out_shap...  0.87 us
  transfers between devices with their start and end apart: 3, of which 3 were waited for; matrix products, arithmetic and copies ran while one was open for 1% of the time, Pallas kernels for 2%

profile of v26, /device:TPU:0, one launch (start us, length us, event | category | flops | bytes accessed | tf_op | source)
XLA Modules:
  0.0 40.6 jit_solution(17413971618070143162)
XLA Ops:
  0.0 5.1 %shard_map.64 = bf16[256,2048]{1,0:T(8,128)(2,1)} custom-call(s32[2]{0:T(128)} %flags_hbm.1, bf16[4184,128]{1,0:T(8,128)(2,1)} %bitcast.9, f32[12,512]{1,0:T(8,128)} %constant.42.clone.taps_hbm, bf16[512,512]{1,0:T(8,128)(2,1)} %constant.41.clone.table_hbm), custom_call_target="tpu_custom_call" | custom-call | flops 549453824 | bytes 2097152 | tf_op jit(solution)/shard_map/pallas_call | solution.py:202
  5.1 0.0 copy-start
  5.1 0.0 copy-start.1
  5.2 7.3 %all-to-all-start = ((bf16[32,8,2048]{2,1,0:T(8,128)(2,1)}), bf16[32,8,2048]{2,1,0:T(8,128)(2,1)S(1)}, u32[]{:S(2)}, u32[]{:S(2)}) async-start(bf16[32,8,2048]{2,1,0:T(8,128)(2,1)} %bitcast.8), calls=%async_computation | async-start | bytes 2097152 | tf_op jit(solution)/shard_map/all_to_all | solution.py:349
  12.5 0.0 copy-done
  12.5 0.3 collective-permute-start
  12.8 0.1 add.50
  12.9 0.8 %collective-permute-done = s32[1,32]{1,0:T(1,128)S(1)} collective-permute-done((s32[1,32]{1,0:T(1,128)S(1)}, s32[1,32]{1,0:T(1,128)S(1)}, u32[]{:S(2)}, u32[]{:S(2)}) %collective-permute-start) | collective-permute-done | bytes 160 | tf_op jit(solution)/shard_map/ppermute | solution.py:342
  13.7 0.0 copy-done.1
  13.7 0.1 select_reduce_fusion
  13.8 0.1 add.48
  13.9 0.1 fusion.pick_ref
  14.0 23.5 %all-to-all-done = bf16[32,8,2048]{2,1,0:T(8,128)(2,1)S(1)} async-done(((bf16[32,8,2048]{2,1,0:T(8,128)(2,1)}), bf16[32,8,2048]{2,1,0:T(8,128)(2,1)S(1)}, u32[]{:S(2)}, u32[]{:S(2)}) %all-to-all-start) | async-done | bytes 1048608 | tf_op jit(solution)/shard_map/all_to_all | solution.py:349
  37.5 0.9 %shard_map.65 = (f32[8,32,128]{2,1,0:T(8,128)S(1)}, f32[8,32,128]{2,1,0:T(8,128)S(1)}) custom-call(bf16[2,256,256]{2,1,0:T(8,128)(2,1)S(1)} %fusion.pick_ref, bf16[256,2048]{1,0:T(8,128)(2,1)S(1)} %bitcast.7), custom_call_target="tpu_custom_call" | custom-call | flops 268435456 | bytes 2097152 | tf_op jit(solution)/shard_map/pallas_call | solution.py:280
  38.4 0.2 collective-permute-start.1
  38.6 0.8 %shard_map.66.refs_0_ = f32[16,2,32,64]{3,2,1,0:T(8,128)} custom-call(f32[8,32,128]{2,1,0:T(8,128)S(1)} %get-tuple-element.8.packed_ref), custom_call_target="tpu_custom_call" | custom-call | bytes 262144 | tf_op jit(solution)/shard_map/pallas_call | solution.py:315
  39.4 0.4 %collective-permute-done.1.packed_ref = f32[8,32,128]{2,1,0:T(8,128)S(1)} collective-permute-done((f32[8,32,128]{2,1,0:T(8,128)S(1)}, f32[8,32,128]{2,1,0:T(8,128)S(1)}, u32[]{:S(2)}, u32[]{:S(2)}) %collective-permute-start.1) | collective-permute-done | bytes 131104 | tf_op jit(solution)/shard_map/ppermute | solution.py:354
  39.8 0.8 %shard_map.67 = f32[16,2,32,64]{3,2,1,0:T(8,128)} custom-call(f32[8,32,128]{2,1,0:T(8,128)S(1)} %collective-permute-done.1.packed_ref, f32[16,2,32,64]{3,2,1,0:T(8,128)} %shard_map.66.refs_0_), custom_call_target="tpu_custom_call", output_to_operand_aliasing={{}: (1, {})} | custom-call | bytes 262144 | tf_op jit(solution)/shard_map/pallas_call | solution.py:315
  (5 shorter events, 0.1 us)
Async XLA Ops:
  5.1 7.3 %copy-start = (s32[1,32]{1,0:T(1,128)S(1)}, s32[1,32]{1,0:T(1,128)}, u32[]{:S(2)}) copy-start(s32[1,32]{1,0:T(1,128)} %param.7) | copy-start | bytes 388
  5.1 8.5 %copy-start.1 = (s32[2,16]{1,0:T(2,128)S(1)}, s32[2,16]{1,0:T(2,128)}, u32[]{:S(2)}) copy-start(s32[2,16]{1,0:T(2,128)} %constant.43.clone) | copy-start | bytes 388
  5.2 32.4 %all-to-all-start = ((bf16[32,8,2048]{2,1,0:T(8,128)(2,1)}), bf16[32,8,2048]{2,1,0:T(8,128)(2,1)S(1)}, u32[]{:S(2)}, u32[]{:S(2)}) async-start(bf16[32,8,2048]{2,1,0:T(8,128)(2,1)} %bitcast.8), calls=%async_computation | async-start | bytes 2097152 | tf_op jit(solution)/shard_map/all_to_all | solution.py:349
  12.5 1.2 %collective-permute-start = (s32[1,32]{1,0:T(1,128)S(1)}, s32[1,32]{1,0:T(1,128)S(1)}, u32[]{:S(2)}, u32[]{:S(2)}) collective-permute-start(s32[1,32]{1,0:T(1,128)S(1)} %copy-done), channel_id=1, source_target_pairs={{0,1},{1,0},{2,3},{3,2},{4,5},{5,4},{6,7},{7,6},{8,9},{9,8},{10,11... | collective-permute-start | bytes 392 | tf_op jit(solution)/shard_map/ppermute | solution.py:342
  38.4 1.4 %collective-permute-start.1 = (f32[8,32,128]{2,1,0:T(8,128)S(1)}, f32[8,32,128]{2,1,0:T(8,128)S(1)}, u32[]{:S(2)}, u32[]{:S(2)}) collective-permute-start(f32[8,32,128]{2,1,0:T(8,128)S(1)} %get-tuple-element.7), channel_id=1, source_target_pairs={{0,1},{1,0},{2,3},{3,2},{4,5},{5,4},{6,7},{7,6},{8,9},{9,8},{10,11... | collective-permute-start | bytes 393224 | tf_op jit(solution)/shard_map/ppermute | solution.py:354

commit v27 on v24

--- a/solution.py
+++ b/solution.py
@@ -334,7 +334,7 @@
     plane = freq * blocks // 4
     order = [
         z * plane + d
-        for z in (3, 2, 0, 1)
+        for z in (2, 3, 0, 1)
         for core in reversed(range(blocks))
         for d in reversed(range(core, plane, blocks))
     ]

time: 41.1 us -> 42.1 us (1.024)
  waiting for transfers between devices: 25 us -> 26 us
    all_to_all x1, waiting for transfers between devices: 23.7 us -> 24.7 us  [split_channels(): lax.all_to_all(sent, axes, split_axis=0, concat_axis=0, axis_index_groups...]
where the time goes in v27:
time: 42.1 us; the launch traced here: 41.8 us
  waiting for transfers between devices  26 us (62%)
  starting transfers between devices  7.69 us (18%)
  Pallas kernels  7.59 us (18%)
    all_to_all x1, waiting for transfers between devices, split_channels(): lax.all_to_all(sent, axes, split_axis=0, concat_axis=0, axis_index_groups...  24.7 us
    all_to_all x1, starting transfers between devices, split_channels(): lax.all_to_all(sent, axes, split_axis=0, concat_axis=0, axis_index_groups...  7.31 us
    pallas_call x1, Pallas kernels, channelize(): pl.pallas_call(channelize_kernel, out_shape=jax.ShapeDtypeStruct((CH, inp...  5.12 us
    pallas_call x2, Pallas kernels, place(): pl.pallas_call(functools.partial(place_kernel, own=base is None), out_sha...  1.6 us
    pallas_call x1, Pallas kernels, correlate(): pl.pallas_call(functools.partial(correlate_kernel, order=order), out_shap...  0.87 us
  transfers between devices with their start and end apart: 3, of which 3 were waited for; matrix products, arithmetic and copies ran while one was open for 1% of the time, Pallas kernels for 2%

profile of v27, /device:TPU:0, one launch (start us, length us, event | category | flops | bytes accessed | tf_op | source)
XLA Modules:
  0.0 41.8 jit_solution(16153807542972102448)
XLA Ops:
  0.0 5.1 %shard_map.64 = bf16[256,2048]{1,0:T(8,128)(2,1)} custom-call(s32[2]{0:T(128)} %flags_hbm.1, bf16[4184,128]{1,0:T(8,128)(2,1)} %bitcast.9, f32[12,512]{1,0:T(8,128)} %constant.42.clone.taps_hbm, bf16[512,512]{1,0:T(8,128)(2,1)} %constant.41.clone.table_hbm), custom_call_target="tpu_custom_call" | custom-call | flops 549453824 | bytes 2097152 | tf_op jit(solution)/shard_map/pallas_call | solution.py:202
  5.1 0.0 copy-start
  5.1 0.0 copy-start.1
  5.2 7.3 %all-to-all-start = ((bf16[32,8,2048]{2,1,0:T(8,128)(2,1)}), bf16[32,8,2048]{2,1,0:T(8,128)(2,1)S(1)}, u32[]{:S(2)}, u32[]{:S(2)}) async-start(bf16[32,8,2048]{2,1,0:T(8,128)(2,1)} %bitcast.8), calls=%async_computation | async-start | bytes 2097152 | tf_op jit(solution)/shard_map/all_to_all | solution.py:349
  12.5 0.0 copy-done
  12.5 0.3 collective-permute-start
  12.8 0.1 add.50
  12.9 0.8 %collective-permute-done = s32[1,32]{1,0:T(1,128)S(1)} collective-permute-done((s32[1,32]{1,0:T(1,128)S(1)}, s32[1,32]{1,0:T(1,128)S(1)}, u32[]{:S(2)}, u32[]{:S(2)}) %collective-permute-start) | collective-permute-done | bytes 160 | tf_op jit(solution)/shard_map/ppermute | solution.py:342
  13.7 0.0 copy-done.1
  13.7 0.1 select_reduce_fusion
  13.8 0.1 add.48
  13.9 0.1 fusion.pick_ref
  14.0 24.7 %all-to-all-done = bf16[32,8,2048]{2,1,0:T(8,128)(2,1)S(1)} async-done(((bf16[32,8,2048]{2,1,0:T(8,128)(2,1)}), bf16[32,8,2048]{2,1,0:T(8,128)(2,1)S(1)}, u32[]{:S(2)}, u32[]{:S(2)}) %all-to-all-start) | async-done | bytes 1048608 | tf_op jit(solution)/shard_map/all_to_all | solution.py:349
  38.7 0.9 %shard_map.65 = (f32[8,32,128]{2,1,0:T(8,128)S(1)}, f32[8,32,128]{2,1,0:T(8,128)S(1)}) custom-call(bf16[2,256,256]{2,1,0:T(8,128)(2,1)S(1)} %fusion.pick_ref, bf16[256,2048]{1,0:T(8,128)(2,1)S(1)} %bitcast.7), custom_call_target="tpu_custom_call" | custom-call | flops 268435456 | bytes 2097152 | tf_op jit(solution)/shard_map/pallas_call | solution.py:280
  39.6 0.1 collective-permute-start.1
  39.7 0.8 %shard_map.66.refs_0_ = f32[16,2,32,64]{3,2,1,0:T(8,128)} custom-call(f32[8,32,128]{2,1,0:T(8,128)S(1)} %get-tuple-element.8.packed_ref), custom_call_target="tpu_custom_call" | custom-call | bytes 262144 | tf_op jit(solution)/shard_map/pallas_call | solution.py:315
  40.5 0.5 %collective-permute-done.1.packed_ref = f32[8,32,128]{2,1,0:T(8,128)S(1)} collective-permute-done((f32[8,32,128]{2,1,0:T(8,128)S(1)}, f32[8,32,128]{2,1,0:T(8,128)S(1)}, u32[]{:S(2)}, u32[]{:S(2)}) %collective-permute-start.1) | collective-permute-done | bytes 131104 | tf_op jit(solution)/shard_map/ppermute | solution.py:354
  41.0 0.8 %shard_map.67 = f32[16,2,32,64]{3,2,1,0:T(8,128)} custom-call(f32[8,32,128]{2,1,0:T(8,128)S(1)} %collective-permute-done.1.packed_ref, f32[16,2,32,64]{3,2,1,0:T(8,128)} %shard_map.66.refs_0_), custom_call_target="tpu_custom_call", output_to_operand_aliasing={{}: (1, {})} | custom-call | bytes 262144 | tf_op jit(solution)/shard_map/pallas_call | solution.py:315
  (5 shorter events, 0.1 us)
Async XLA Ops:
  5.1 7.3 %copy-start = (s32[1,32]{1,0:T(1,128)S(1)}, s32[1,32]{1,0:T(1,128)}, u32[]{:S(2)}) copy-start(s32[1,32]{1,0:T(1,128)} %param.7) | copy-start | bytes 388
  5.1 8.5 %copy-start.1 = (s32[2,16]{1,0:T(2,128)S(1)}, s32[2,16]{1,0:T(2,128)}, u32[]{:S(2)}) copy-start(s32[2,16]{1,0:T(2,128)} %constant.43.clone) | copy-start | bytes 388
  5.2 33.6 %all-to-all-start = ((bf16[32,8,2048]{2,1,0:T(8,128)(2,1)}), bf16[32,8,2048]{2,1,0:T(8,128)(2,1)S(1)}, u32[]{:S(2)}, u32[]{:S(2)}) async-start(bf16[32,8,2048]{2,1,0:T(8,128)(2,1)} %bitcast.8), calls=%async_computation | async-start | bytes 2097152 | tf_op jit(solution)/shard_map/all_to_all | solution.py:349
  12.5 1.2 %collective-permute-start = (s32[1,32]{1,0:T(1,128)S(1)}, s32[1,32]{1,0:T(1,128)S(1)}, u32[]{:S(2)}, u32[]{:S(2)}) collective-permute-start(s32[1,32]{1,0:T(1,128)S(1)} %copy-done), channel_id=1, source_target_pairs={{0,1},{1,0},{2,3},{3,2},{4,5},{5,4},{6,7},{7,6},{8,9},{9,8},{10,11... | collective-permute-start | bytes 392 | tf_op jit(solution)/shard_map/ppermute | solution.py:342
  39.6 1.4 %collective-permute-start.1 = (f32[8,32,128]{2,1,0:T(8,128)S(1)}, f32[8,32,128]{2,1,0:T(8,128)S(1)}, u32[]{:S(2)}, u32[]{:S(2)}) collective-permute-start(f32[8,32,128]{2,1,0:T(8,128)S(1)} %get-tuple-element.7), channel_id=1, source_target_pairs={{0,1},{1,0},{2,3},{3,2},{4,5},{5,4},{6,7},{7,6},{8,9},{9,8},{10,11... | collective-permute-start | bytes 393224 | tf_op jit(solution)/shard_map/ppermute | solution.py:354

commit v28 on v24

--- a/solution.py
+++ b/solution.py
@@ -115,14 +115,15 @@
                 both = jnp.concatenate(out[b : b + 2], axis=0).astype(jnp.bfloat16)
                 fir[i, pl.ds(g * GROUP + (first + b) * SUB, 2 * SUB), cols] = both
 
-    def transform(g, i):
+    def transform(g, i, points=pl.ds(0, FRAME), add=False):
         part = pl.ds(g * GROUP, GROUP)
-        spectra[i, :, part] = lax.dot_general(
-            table[...],
-            fir[i, part, :],
+        product = lax.dot_general(
+            table[:, points],
+            fir[i, part, points],
             (((1,), (1,)), ((), ())),
             preferred_element_type=jnp.float32,
         )
+        spectra[i, :, part] = spectra[i, :, part] + product if add else product
 
     def rate(i):
         good = (1 - flags[i]).astype(jnp.float32)
@@ -169,18 +170,21 @@
     for i in range(inputs):
         transform(0, i)
     convert(2)
+    halves = pl.ds(0, FRAME // 2), pl.ds(FRAME // 2, FRAME // 2)
     copies = []
     for i in range(inputs):
         if i > 0:
             transform(1, i - 1)
         for j in range(FRAME // LANES):
+            if i == inputs - 1 and j == FRAME // LANES // 2:
+                transform(1, i, halves[0])
             filter_group(1, i, j)
         if i > 0:
             rate(i - 1)
             for piece in range(pieces):
                 pack(i - 1, piece)
             copies += [store(i - 1, piece) for piece in range(pieces)]
-    transform(1, inputs - 1)
+    transform(1, inputs - 1, halves[1], add=True)
     rate(inputs - 1)
     for piece in range(pieces):
         pack(inputs - 1, piece)

time: 41.1 us -> 41.1 us (level)
  no operation moved by 1% of the time
where the time goes in v28:
time: 41.1 us; the launch traced here: 40.9 us
  waiting for transfers between devices  25 us (61%)
  starting transfers between devices  7.69 us (19%)
  Pallas kernels  7.59 us (18%)
    all_to_all x1, waiting for transfers between devices, split_channels(): lax.all_to_all(sent, axes, split_axis=0, concat_axis=0, axis_index_groups...  23.7 us
    all_to_all x1, starting transfers between devices, split_channels(): lax.all_to_all(sent, axes, split_axis=0, concat_axis=0, axis_index_groups...  7.31 us
    pallas_call x1, Pallas kernels, channelize(): pl.pallas_call(channelize_kernel, out_shape=jax.ShapeDtypeStruct((CH, inp...  5.12 us
    pallas_call x2, Pallas kernels, place(): pl.pallas_call(functools.partial(place_kernel, own=base is None), out_sha...  1.6 us
    pallas_call x1, Pallas kernels, correlate(): pl.pallas_call(functools.partial(correlate_kernel, order=order), out_shap...  0.87 us
  transfers between devices with their start and end apart: 3, of which 3 were waited for; matrix products, arithmetic and copies ran while one was open for 1% of the time, Pallas kernels for 2%

profile of v28, /device:TPU:0, one launch (start us, length us, event | category | flops | bytes accessed | tf_op | source)
XLA Modules:
  0.0 40.9 jit_solution(12582678024114359762)
XLA Ops:
  0.0 5.1 %shard_map.64 = bf16[256,2048]{1,0:T(8,128)(2,1)} custom-call(s32[2]{0:T(128)} %flags_hbm.1, bf16[4184,128]{1,0:T(8,128)(2,1)} %bitcast.9, f32[12,512]{1,0:T(8,128)} %constant.42.clone.taps_hbm, bf16[512,512]{1,0:T(8,128)(2,1)} %constant.41.clone.table_hbm), custom_call_target="tpu_custom_call" | custom-call | flops 549453824 | bytes 2097152 | tf_op jit(solution)/shard_map/pallas_call | solution.py:206
  5.1 0.0 copy-start
  5.1 0.0 copy-start.1
  5.2 7.3 %all-to-all-start = ((bf16[32,8,2048]{2,1,0:T(8,128)(2,1)}), bf16[32,8,2048]{2,1,0:T(8,128)(2,1)S(1)}, u32[]{:S(2)}, u32[]{:S(2)}) async-start(bf16[32,8,2048]{2,1,0:T(8,128)(2,1)} %bitcast.8), calls=%async_computation | async-start | bytes 2097152 | tf_op jit(solution)/shard_map/all_to_all | solution.py:353
  12.5 0.0 copy-done
  12.5 0.3 collective-permute-start
  12.8 0.1 add.50
  12.9 0.8 %collective-permute-done = s32[1,32]{1,0:T(1,128)S(1)} collective-permute-done((s32[1,32]{1,0:T(1,128)S(1)}, s32[1,32]{1,0:T(1,128)S(1)}, u32[]{:S(2)}, u32[]{:S(2)}) %collective-permute-start) | collective-permute-done | bytes 160 | tf_op jit(solution)/shard_map/ppermute | solution.py:346
  13.7 0.0 copy-done.1
  13.7 0.1 select_reduce_fusion
  13.8 0.1 add.48
  13.9 0.1 fusion.pick_ref
  14.0 23.7 %all-to-all-done = bf16[32,8,2048]{2,1,0:T(8,128)(2,1)S(1)} async-done(((bf16[32,8,2048]{2,1,0:T(8,128)(2,1)}), bf16[32,8,2048]{2,1,0:T(8,128)(2,1)S(1)}, u32[]{:S(2)}, u32[]{:S(2)}) %all-to-all-start) | async-done | bytes 1048608 | tf_op jit(solution)/shard_map/all_to_all | solution.py:353
  37.8 0.9 %shard_map.65 = (f32[8,32,128]{2,1,0:T(8,128)S(1)}, f32[8,32,128]{2,1,0:T(8,128)S(1)}) custom-call(bf16[2,256,256]{2,1,0:T(8,128)(2,1)S(1)} %fusion.pick_ref, bf16[256,2048]{1,0:T(8,128)(2,1)S(1)} %bitcast.7), custom_call_target="tpu_custom_call" | custom-call | flops 268435456 | bytes 2097152 | tf_op jit(solution)/shard_map/pallas_call | solution.py:284
  38.6 0.1 collective-permute-start.1
  38.7 0.8 %shard_map.66.refs_0_ = f32[16,2,32,64]{3,2,1,0:T(8,128)} custom-call(f32[8,32,128]{2,1,0:T(8,128)S(1)} %get-tuple-element.8.packed_ref), custom_call_target="tpu_custom_call" | custom-call | bytes 262144 | tf_op jit(solution)/shard_map/pallas_call | solution.py:319
  39.5 0.5 %collective-permute-done.1.packed_ref = f32[8,32,128]{2,1,0:T(8,128)S(1)} collective-permute-done((f32[8,32,128]{2,1,0:T(8,128)S(1)}, f32[8,32,128]{2,1,0:T(8,128)S(1)}, u32[]{:S(2)}, u32[]{:S(2)}) %collective-permute-start.1) | collective-permute-done | bytes 131104 | tf_op jit(solution)/shard_map/ppermute | solution.py:358
  40.1 0.8 %shard_map.67 = f32[16,2,32,64]{3,2,1,0:T(8,128)} custom-call(f32[8,32,128]{2,1,0:T(8,128)S(1)} %collective-permute-done.1.packed_ref, f32[16,2,32,64]{3,2,1,0:T(8,128)} %shard_map.66.refs_0_), custom_call_target="tpu_custom_call", output_to_operand_aliasing={{}: (1, {})} | custom-call | bytes 262144 | tf_op jit(solution)/shard_map/pallas_call | solution.py:319
  (5 shorter events, 0.1 us)
Async XLA Ops:
  5.1 7.3 %copy-start = (s32[1,32]{1,0:T(1,128)S(1)}, s32[1,32]{1,0:T(1,128)}, u32[]{:S(2)}) copy-start(s32[1,32]{1,0:T(1,128)} %param.7) | copy-start | bytes 388
  5.1 8.5 %copy-start.1 = (s32[2,16]{1,0:T(2,128)S(1)}, s32[2,16]{1,0:T(2,128)}, u32[]{:S(2)}) copy-start(s32[2,16]{1,0:T(2,128)} %constant.43.clone) | copy-start | bytes 388
  5.2 32.6 %all-to-all-start = ((bf16[32,8,2048]{2,1,0:T(8,128)(2,1)}), bf16[32,8,2048]{2,1,0:T(8,128)(2,1)S(1)}, u32[]{:S(2)}, u32[]{:S(2)}) async-start(bf16[32,8,2048]{2,1,0:T(8,128)(2,1)} %bitcast.8), calls=%async_computation | async-start | bytes 2097152 | tf_op jit(solution)/shard_map/all_to_all | solution.py:353
  12.5 1.2 %collective-permute-start = (s32[1,32]{1,0:T(1,128)S(1)}, s32[1,32]{1,0:T(1,128)S(1)}, u32[]{:S(2)}, u32[]{:S(2)}) collective-permute-start(s32[1,32]{1,0:T(1,128)S(1)} %copy-done), channel_id=1, source_target_pairs={{0,1},{1,0},{2,3},{3,2},{4,5},{5,4},{6,7},{7,6},{8,9},{9,8},{10,11... | collective-permute-start | bytes 392 | tf_op jit(solution)/shard_map/ppermute | solution.py:346
  38.6 1.4 %collective-permute-start.1 = (f32[8,32,128]{2,1,0:T(8,128)S(1)}, f32[8,32,128]{2,1,0:T(8,128)S(1)}, u32[]{:S(2)}, u32[]{:S(2)}) collective-permute-start(f32[8,32,128]{2,1,0:T(8,128)S(1)} %get-tuple-element.7), channel_id=1, source_target_pairs={{0,1},{1,0},{2,3},{3,2},{4,5},{5,4},{6,7},{7,6},{8,9},{9,8},{10,11... | collective-permute-start | bytes 393224 | tf_op jit(solution)/shard_map/ppermute | solution.py:358
